TPU v7x, 32 devices: a whole 2x2x4 slice. The times are simulated.
32 devices in a mesh: groups: 2 (over y), seq: 2 (over x), frame: 4 (over z), cfg: 2 (over core).
Axes of the slice: x: 2, y: 2, z: 4, core: 2. Of those that a mesh axis runs over, the one named last changes fastest.
Arguments:
- qkv: bfloat16 [2, 4096, 3, 4096], P('cfg', ('groups', 'frame', 'seq')), parts along dimension 1, may hold values from -108 to 108, as said below
- timestep: int32 [2], P('groups'), parts along dimension 0, may hold values from 0 to 999
- windows: int32 [32], replicated, may hold values from 0 to 2
- segments: int32 [16], P('groups'), parts along dimension 0, may hold values from 0 to 3, never falling along the last dimension, each value on 1 to 4 neighbouring positions
Outputs:
- guided: bfloat16 [4096, 16, 256], P(('groups', 'frame', 'seq'), 'cfg'), parts along dimension 0
There are 2 independent parts, one for each index of `groups`. A program takes and returns all parts, laid end to end along the dimension named above; an argument that names none is the same for every part. Nothing has to cross between parts.
Inputs may be any that keep to these rules, and one draw needn't show every extreme that they name: Entries of qkv lie in this range. `segments`: shot numbers never fall from one frame to the next.
All inputs are finite; a program needn't handle non-finite values.
Results may differ from a plain program's by a relative error of at most 0.0053.
Values may be sent and summed in bfloat16 or wider, within the bound.
No kernel may reach another device: no remote copies, remote signals or barrier semaphores. Data moves between devices by JAX's collectives and lax.ppermute only.
A program may use at most 128 MiB of HBM per device.

v0:
```python
import math

import jax
import jax.numpy as jnp
from jax import lax
from jax.sharding import PartitionSpec as P

HD = 128
F_DEV = 2
W_MAX = 2


def padded_2(block, sides, width):
    for axis, dim in sides:
        count = lax.axis_size(axis)
        forward = [(i, i + 1) for i in range(count - 1)]
        backward = [(target, source) for source, target in forward]
        low = lax.ppermute(
            lax.slice_in_dim(block, block.shape[dim] - width, None, axis=dim), axis, forward
        )
        high = lax.ppermute(lax.slice_in_dim(block, 0, width, axis=dim), axis, backward)
        block = jnp.concatenate([low, block, high], axis=dim)
    return block


def attend(block, head_windows, seg_pad, first_frame):
    count_blocks = block.shape[0]
    branches = block.shape[1]
    rows_block = block.shape[2]
    columns = block.shape[4]
    heads_here = columns // HD
    per_frame = count_blocks // F_DEV
    reach = W_MAX * per_frame
    span = 2 * W_MAX + 1
    scale = 1.0 / math.sqrt(HD)
    pairs = block[:, :, :, 1:]
    padded = padded_2(pairs, (("frame", 0),), reach)
    queries = block[:, :, :, 0].reshape(count_blocks, branches, rows_block, heads_here, HD)
    offsets = jnp.arange(span, dtype=jnp.int32) - W_MAX
    within_reach = jnp.abs(offsets)[None, None, :] <= head_windows[:, :, None]
    results = []
    for frame_number in range(F_DEV):
        query = queries[frame_number * per_frame : (frame_number + 1) * per_frame]
        window_rows = padded[frame_number * per_frame : frame_number * per_frame + span * per_frame]
        window_rows = window_rows.reshape(span * per_frame, branches, rows_block, 2, heads_here, HD)
        key_rows = window_rows[:, :, :, 0]
        value_rows = window_rows[:, :, :, 1]
        here = first_frame + frame_number
        shots = lax.dynamic_slice_in_dim(seg_pad, here, span, 0)
        own_shot = lax.dynamic_index_in_dim(seg_pad, here + W_MAX, 0, keepdims=False)
        allowed = within_reach & (shots == own_shot)[None, None, :]
        allowed = jnp.repeat(allowed, per_frame, axis=2)
        scores = (
            jnp.einsum("sbthd,ubrhd->bhstur", query, key_rows, preferred_element_type=jnp.float32)
            * scale
        )
        scores = jnp.where(allowed[:, :, None, None, :, None], scores, -1e30)
        highest = jnp.max(scores, axis=(4, 5), keepdims=True)
        expd = jnp.exp(scores - highest)
        totals = jnp.sum(expd, axis=(4, 5))
        weights = expd.astype(jnp.bfloat16)
        mixed = jnp.einsum(
            "bhstur,ubrhd->sbthd", weights, value_rows, preferred_element_type=jnp.float32
        )
        mixed = mixed / jnp.transpose(totals, (2, 0, 3, 1))[..., None]
        results.append(mixed.astype(jnp.bfloat16))
    return jnp.concatenate(results, axis=0)


def body(qkv, timestep, windows, segments):
    first_frame = lax.axis_index("frame") * F_DEV
    fill = jnp.full((W_MAX,), -1, jnp.int32)
    seg_pad = jnp.concatenate([fill, segments, fill])
    strength = 1.0 + 4.0 * timestep[0].astype(jnp.float32) / 999.0
    seq_count = lax.axis_size("seq")
    cfg_count = lax.axis_size("cfg")
    spread = lax.all_to_all(qkv, ("seq", "cfg"), split_axis=3, concat_axis=0, tiled=True)
    columns = spread.shape[3]
    heads_here = columns // HD
    block = spread.reshape(seq_count, cfg_count, spread.shape[1], 3, columns)
    start_head = (lax.axis_index("seq") * cfg_count + lax.axis_index("cfg")) * heads_here
    head_windows = lax.dynamic_slice_in_dim(windows, start_head, heads_here, 0).reshape(
        1, heads_here
    )
    attended = attend(block, head_windows, seg_pad, first_frame)
    cond = attended[:, 0].astype(jnp.float32)
    uncond = attended[:, 1].astype(jnp.float32)
    guided = (uncond + strength * (cond - uncond)).astype(jnp.bfloat16)
    own_rows = lax.all_to_all(guided, "seq", split_axis=0, concat_axis=3, tiled=True)
    return own_rows[0]


def solution(mesh):
    return jax.shard_map(
        body,
        mesh=mesh,
        in_specs=(P("cfg", ("groups", "frame", "seq"), None, None), P("groups"), P(), P("groups")),
        out_specs=P(("groups", "frame", "seq"), "cfg", None),
        check_vma=False,
    )
```

profile of v0, /device:TPU:0, one launch (start us, length us, event | category | flops | bytes accessed | tf_op | source)
XLA Modules:
  0.0 343.5 jit_solution(6959180274236141472)
XLA Ops:
  0.0 13.1 %copy.21 = bf16[1,256,3,4096]{1,2,0,3:T(4,128)(2,1)} copy(bf16[1,256,3,4096]{3,1,2,0:T(8,128)(2,1)} %param.4) | data formatting | bytes 12582912 | tf_op args[0]
  13.1 97.8 %all_to_all.30 = bf16[1,256,3,4096]{1,2,0,3:T(4,128)(2,1)S(1)} all-to-all(bf16[1,256,3,4096]{1,2,0,3:T(4,128)(2,1)} %copy.21), channel_id=1, replica_groups=mesh['groups'=2,'seq'=2,'frame'=4,'cfg'=2] {'seq','cfg'}, dimensions={3} | all-to-all | bytes 12582912 | tf_op jit(solution)/shard_map/all_to_all | solution.py:77
  111.0 3.7 %copy.22 = bf16[1,256,3,4,1024]{1,4,2,3,0:T(8,128)(2,1)} copy(bf16[1,256,3,4,1024]{1,2,4,3,0:T(4,128)(2,1)S(1)} %bitcast.109) | data formatting | bytes 12582912 | tf_op jit(solution)/shard_map/all_to_all | solution.py:77
  114.6 4.5 %slice.49 = bf16[2,2,256,2,1024]{2,4,3,1,0:T(8,128)(2,1)} slice(bf16[2,2,256,3,1024]{2,4,3,1,0:T(8,128)(2,1)} %bitcast.110), slice={[0:2], [0:2], [0:256], [1:3], [0:1024]} | slice | bytes 8388608 | tf_op jit(solution)/shard_map/slice | solution.py:36
  119.1 1.3 collective-permute-start.1
  120.4 6.9 %collective-permute-start = (bf16[2,2,256,2,1024]{2,4,3,1,0:T(8,128)(2,1)}, bf16[2,2,256,2,1024]{2,4,3,1,0:T(8,128)(2,1)}, u32[]{:S(2)}, u32[]{:S(2)}) collective-permute-start(bf16[2,2,256,2,1024]{2,4,3,1,0:T(8,128)(2,1)} %slice.49), channel_id=1, source_target_pairs={{0,2},{2,4},{4,6},{1,3},{3,5},{5,7},{8,10},{10,12},{12,14},{9,11},... | collective-permute-start | bytes 12582920 | tf_op jit(solution)/shard_map/ppermute | solution.py:18
  128.1 0.6 fusion.35
  128.8 1.3 dynamic-slice_compare_fusion
  130.2 1.7 fusion.34
  131.9 82.1 %collective-permute-done.1 = bf16[2,2,256,2,1024]{2,4,3,1,0:T(8,128)(2,1)} collective-permute-done((bf16[2,2,256,2,1024]{2,4,3,1,0:T(8,128)(2,1)}, bf16[2,2,256,2,1024]{2,4,3,1,0:T(8,128)(2,1)}, u32[]{:S(2)}, u32[]{:S(2)}) %collective-permute-start.1) | collective-permute-done | bytes 4194336 | tf_op jit(solution)/shard_map/ppermute | solution.py:21
  213.9 1.2 collective-permute-done
  215.1 6.3 %pad_maximum_fusion = bf16[6,2,256,2,1024]{2,4,3,1,0:T(8,128)(2,1)S(1)} fusion(bf16[2,2,256,2,1024]{2,4,3,1,0:T(8,128)(2,1)} %collective-permute-done.1, bf16[2,2,256,2,1024]{2,4,3,1,0:T(8,128)(2,1)} %slice.49, bf16[2,2,256,2,1024]{2,4,3,1,0:T(8,128)(2,1)} %collective-permute-done), kind=kLoop, calls=%fused_computation.12 | loop fusion | flops 12582912 | bytes 25165824 | tf_op jit(solution)/shard_map/concatenate | solution.py:22
  221.4 7.4 %fusion.31 = (bf16[5,2,256,2,1024]{2,4,3,1,0:T(8,128)(2,1)}, bf16[5,2,256,2,1024]{2,4,3,1,0:T(8,128)(2,1)}) fusion(bf16[6,2,256,2,1024]{2,4,3,1,0:T(8,128)(2,1)S(1)} %pad_maximum_fusion), kind=kLoop, calls=%fused_computation.47 | loop fusion | bytes 41943040 | tf_op jit(solution)/shard_map/slice | solution.py:44
  228.8 9.7 %fusion.33 = (bf16[5,2,256,1,8,128]{2,5,4,3,1,0:T(8,128)(2,1)}, bf16[5,2,256,1,8,128]{2,5,4,3,1,0:T(8,128)(2,1)}) fusion(bf16[5,2,256,2,8,128]{2,5,4,3,1,0:T(8,128)(2,1)} %bitcast.108), kind=kLoop, calls=%fused_computation.49 | loop fusion | bytes 20971520 | tf_op jit(solution)/shard_map/slice | solution.py:47
  238.4 8.0 %copy.44 = bf16[5,2,256,1,8,128]{5,2,0,4,1,3:T(8,128)(2,1)} copy(bf16[5,2,256,1,8,128]{2,5,4,3,1,0:T(8,128)(2,1)} %get-tuple-element.10) | data formatting | bytes 10485760
  246.4 9.6 %fusion.32 = (bf16[5,2,256,1,8,128]{2,5,4,3,1,0:T(8,128)(2,1)}, bf16[5,2,256,1,8,128]{2,5,4,3,1,0:T(8,128)(2,1)}) fusion(bf16[5,2,256,2,8,128]{2,5,4,3,1,0:T(8,128)(2,1)} %bitcast.107), kind=kLoop, calls=%fused_computation.48 | loop fusion | bytes 20971520 | tf_op jit(solution)/shard_map/slice | solution.py:47
  256.0 7.9 %copy.46 = bf16[5,2,256,1,8,128]{5,2,0,4,1,3:T(8,128)(2,1)} copy(bf16[5,2,256,1,8,128]{2,5,4,3,1,0:T(8,128)(2,1)} %get-tuple-element.8) | data formatting | bytes 10485760
  263.9 12.4 %bitcast_reduce_fusion.1 = (f32[2,8,256]{2,1,0:T(8,128)S(1)}, f32[2,8,5,256,256]{4,3,2,1,0:T(8,128)}) fusion(pred[8,5]{1,0:T(8,128)(4,1)S(1)} %get-tuple-element.14, bf16[2,256,8,128,1]{1,3,4,2,0:T(8,128)(2,1)S(1)} %bitcast.113, bf16[5,2,256,1,8,128]{5,2,0,4,1,3:T(8,128)(2,1)} %copy.44), kind=kOutput, calls=%fused_computation.4 | convolution fusion | flops 1357901824 | bytes 27279400 | tf_op jit(solution)/shard_map/sbthd,ubrhd->bhstur/dot_general | solution.py:54
  276.3 4.8 %bitcast_reduce_fusion = (f32[2,8,256]{2,1,0:T(8,128)S(1)}, f32[2,8,5,256,256]{4,3,2,1,0:T(8,128)S(1)}) fusion(pred[8,5]{1,0:T(8,128)(4,1)S(1)} %get-tuple-element.13, bf16[2,256,8,128,1]{1,3,4,2,0:T(8,128)(2,1)S(1)} %bitcast.112, bf16[5,2,256,1,8,128]{5,2,0,4,1,3:T(8,128)(2,1)} %copy.46), kind=kOutput, calls=%fused_computation.1 | convolution fusion | flops 1357901824 | bytes 27279400 | tf_op jit(solution)/shard_map/sbthd,ubrhd->bhstur/dot_general | solution.py:54
  281.2 18.6 %fusion.2 = (f32[2,8,256]{2,1,0:T(8,128)S(1)}, f32[2,8,256]{2,1,0:T(8,128)S(1)}) fusion(f32[2,8,5,256,256]{4,3,2,1,0:T(8,128)} %get-tuple-element.20, f32[2,8,256]{2,1,0:T(8,128)S(1)} %get-tuple-element.19, pred[8,5]{1,0:T(8,128)(4,1)S(1)} %get-tuple-element.14, f32[2,8,256]{2,1,0:T(8,128)S(1)} %get-tuple-element.21, ...), kind=kLoop, calls=%fused_computation.8 | loop fusion | flops 41934848 | bytes 42008656 | tf_op jit(solution)/shard_map/reduce_sum | solution.py:60
  299.8 13.2 %fusion.19 = bf16[1,2,256,8,128]{2,4,3,1,0:T(8,128)(2,1)S(1)} fusion(f32[2,8,5,256,256]{4,3,2,1,0:T(8,128)} %get-tuple-element.20, f32[2,8,256]{2,1,0:T(8,128)S(1)} %get-tuple-element.19, pred[8,5]{1,0:T(8,128)(4,1)S(1)} %get-tuple-element.14, bf16[5,2,256,1,8,128]{2,5,4,3,1,0:T(8,128)(2,1)} %get-tuple-element.9, f32[2,256,8]{1,2,0:T(8,128)S(1)} %bitcast.116), kind=kOutput, calls=%fused_computation.32 | convolution fusion | flops 1364197376 | bytes 27295784 | tf_op jit(solution)/shard_map/bhstur,ubrhd->sbthd/dot_general | solution.py:62
  313.0 13.2 %fusion.18 = bf16[1,2,256,8,128]{2,4,3,1,0:T(8,128)(2,1)S(1)} fusion(f32[2,8,5,256,256]{4,3,2,1,0:T(8,128)} %copy-done, f32[2,8,256]{2,1,0:T(8,128)S(1)} %get-tuple-element.21, pred[8,5]{1,0:T(8,128)(4,1)S(1)} %get-tuple-element.13, bf16[5,2,256,1,8,128]{2,5,4,3,1,0:T(8,128)(2,1)} %get-tuple-element.7, f32[2,256,8]{1,2,0:T(8,128)S(1)} %bitcast.115), kind=kOutput, calls=%fused_computation.30 | convolution fusion | flops 1364197376 | bytes 27295784 | tf_op jit(solution)/shard_map/bhstur,ubrhd->sbthd/dot_general | solution.py:62
  326.7 15.0 %all_to_all.31 = bf16[2,256,8,128]{1,3,2,0:T(8,128)(2,1)S(1)} all-to-all(bf16[2,256,8,128]{1,3,2,0:T(8,128)(2,1)S(1)} %fusion.17), channel_id=1, replica_groups=mesh['groups'=2,'seq'=2,'frame'=4,'cfg'=2] {'seq'}, dimensions={0} | all-to-all | bytes 2097152 | tf_op jit(solution)/shard_map/all_to_all | solution.py:89
  341.8 1.8 copy.32
  (12 shorter events, 0.7 us)
Async XLA Ops:
  111.0 17.0 %copy-start.1 = (s32[32]{0:T(128)S(1)}, s32[32]{0:T(128)}, u32[]{:S(2)}) copy-start(s32[32]{0:T(128)} %param.6) | copy-start | bytes 388
  111.0 17.1 %copy-start.2 = (s32[8]{0:T(128)S(1)}, s32[8]{0:T(128)}, u32[]{:S(2)}) copy-start(s32[8]{0:T(128)} %param.7) | copy-start | bytes 100
  119.1 94.8 %collective-permute-start.1 = (bf16[2,2,256,2,1024]{2,4,3,1,0:T(8,128)(2,1)}, bf16[2,2,256,2,1024]{2,4,3,1,0:T(8,128)(2,1)}, u32[]{:S(2)}, u32[]{:S(2)}) collective-permute-start(bf16[2,2,256,2,1024]{2,4,3,1,0:T(8,128)(2,1)} %slice.49), channel_id=1, source_target_pairs={{2,0},{4,2},{6,4},{3,1},{5,3},{7,5},{10,8},{12,10},{14,12},{11,9},... | collective-permute-start | bytes 12582920 | tf_op jit(solution)/shard_map/ppermute | solution.py:21
  120.4 94.7 %collective-permute-start = (bf16[2,2,256,2,1024]{2,4,3,1,0:T(8,128)(2,1)}, bf16[2,2,256,2,1024]{2,4,3,1,0:T(8,128)(2,1)}, u32[]{:S(2)}, u32[]{:S(2)}) collective-permute-start(bf16[2,2,256,2,1024]{2,4,3,1,0:T(8,128)(2,1)} %slice.49), channel_id=1, source_target_pairs={{0,2},{2,4},{4,6},{1,3},{3,5},{5,7},{8,10},{10,12},{12,14},{9,11},... | collective-permute-start | bytes 12582920 | tf_op jit(solution)/shard_map/ppermute | solution.py:18
  281.1 18.6 %copy-start = (f32[2,8,5,256,256]{4,3,2,1,0:T(8,128)}, f32[2,8,5,256,256]{4,3,2,1,0:T(8,128)S(1)}, u32[]{:S(2)}) copy-start(f32[2,8,5,256,256]{4,3,2,1,0:T(8,128)S(1)} %get-tuple-element.22) | copy-start | bytes 62914564
where the time goes:
time: 346 us; the launch traced here: 344 us
  blocking collectives  113 us (33%)
  waiting for transfers between devices  83.3 us (24%)
  local copies, waits for them, and re-layouts  68 us (20%)
  matrix products  43.7 us (13%)
  other arithmetic  26.8 us (8%)
  starting transfers between devices  8.19 us (2%)
    all_to_all x1, blocking collectives, body(): lax.all_to_all(qkv, ('seq', 'cfg'), split_axis=3, concat_axis=0, tiled=True)  97.8 us
    ppermute x1, waiting for transfers between devices, padded_2(): lax.ppermute(lax.slice_in_dim(block, 0, width, axis=dim), axis, backward)  82.1 us
    unnamed x9, local copies, waits for them, and re-layouts  29 us
    dot_general x2, matrix products, attend(): jnp.einsum('bhstur,ubrhd->sbthd', weights, value_rows, preferred_element_...  26.5 us
    slice x2, local copies, waits for them, and re-layouts, attend(): value_rows = window_rows[:, :, :, 1]  19.3 us
    reduce_sum x1, other arithmetic, attend(): totals = jnp.sum(expd, axis=(4, 5))  18.6 us
    dot_general x2, matrix products, attend(): jnp.einsum('sbthd,ubrhd->bhstur', query, key_rows, preferred_element_type...  17.2 us
    all_to_all x1, blocking collectives, body(): lax.all_to_all(guided, 'seq', split_axis=0, concat_axis=3, tiled=True)  15 us
  transfers between devices with their start and end apart: 2, of which 2 were waited for; matrix products, arithmetic and copies ran while one was open for 1% of the time, Pallas kernels for 0%

commit v1 on v0

--- a/solution.py
+++ b/solution.py
@@ -1,8 +1,11 @@
+import functools
 import math
 
 import jax
 import jax.numpy as jnp
 from jax import lax
+from jax.experimental import pallas as pl
+from jax.experimental.pallas import tpu as pltpu
 from jax.sharding import PartitionSpec as P
 
 HD = 128
@@ -89,10 +92,377 @@
     own_rows = lax.all_to_all(guided, "seq", split_axis=0, concat_axis=3, tiled=True)
     return own_rows[0]
 
+LOG2E = 1.4426950408889634
+MASKED = -1e30
+BF16 = jnp.bfloat16
+F32 = jnp.float32
+VMEM_BYTES = 32 * 1024 * 1024
+
+
+def whole(space=pltpu.VMEM):
+    return pl.BlockSpec(memory_space=space)
+
+
+def pack_kernel(planes, count, heads_ref, x_ref, out_ref, sems):
+    copies = []
+    for j in range(count):
+        start = pl.multiple_of(heads_ref[j] * HD, HD)
+        for k, plane in enumerate(planes):
+            copies.append(
+                pltpu.make_async_copy(
+                    x_ref.at[plane, :, pl.ds(start, HD)],
+                    out_ref.at[j, k],
+                    sems.at[j * len(planes) + k],
+                )
+            )
+    for copy in copies:
+        copy.start()
+    for copy in copies:
+        copy.wait()
+
+
+def pack(x3, heads, planes):
+    count = heads.shape[0]
+    rows = x3.shape[1]
+    return pl.pallas_call(
+        functools.partial(pack_kernel, planes, count),
+        out_shape=jax.ShapeDtypeStruct((count, len(planes), rows, HD), x3.dtype),
+        grid_spec=pltpu.PrefetchScalarGridSpec(
+            num_scalar_prefetch=1,
+            grid=(1,),
+            in_specs=[whole(pl.ANY)],
+            out_specs=whole(pl.ANY),
+            scratch_shapes=[pltpu.SemaphoreType.DMA((count * len(planes),))],
+        ),
+        compiler_params=pltpu.CompilerParams(vmem_limit_bytes=VMEM_BYTES),
+        cost_estimate=pl.CostEstimate(
+            flops=0, bytes_accessed=4 * count * len(planes) * rows * HD, transcendentals=0
+        ),
+        name="pack_heads",
+    )(heads, x3)
+
+
+def softmax_mix(q, keys, values, biases):
+    factor = LOG2E / math.sqrt(HD)
+    scores = []
+    for key, bias in zip(keys, biases):
+        score = lax.dot_general(
+            q, key, (((1,), (1,)), ((), ())), preferred_element_type=F32
+        )
+        scores.append(score if bias is None else score + bias)
+    top = functools.reduce(
+        jnp.maximum, [jnp.max(score, axis=1, keepdims=True) for score in scores]
+    )
+    total = None
+    mixed = None
+    for score, value in zip(scores, values):
+        expd = jnp.exp2((score - top) * factor)
+        part = jnp.sum(expd, axis=1, keepdims=True)
+        prod = jnp.dot(expd.astype(BF16), value, preferred_element_type=F32)
+        total = part if total is None else total + part
+        mixed = prod if mixed is None else mixed + prod
+    return (mixed / total).astype(BF16)
+
+
+def attend_kernel(count_src, masked, halves, heads_ref, flags_ref, scal_ref, q_ref, *refs):
+    slot = pl.program_id(0)
+    if masked:
+        kv_refs, out_refs = refs[:count_src], refs[count_src:]
+        keys = [ref[0, 0] for ref in kv_refs]
+        values = [ref[0, 1] for ref in kv_refs]
+        biases = [
+            jnp.where(flags_ref[slot * count_src + k] != 0, 0.0, MASKED).astype(F32)
+            for k in range(count_src)
+        ]
+    else:
+        keys, values, out_refs = [refs[0][0]], [refs[1][0]], refs[2:]
+        biases = [None]
+    out = softmax_mix(q_ref[0], keys, values, biases)
+    if halves:
+        half = out.shape[0] // 2
+        low, high = out[:half], out[half:]
+        first = scal_ref[0] == 0
+        out_refs[0][0] = jnp.where(first, low, high)
+        out_refs[1][0] = jnp.where(first, high, low)
+    else:
+        out_refs[0][0] = out
+
+
+def attend_slots(q, q_is_x3, sources, flags, heads, scal, halves):
+    count = heads.shape[0]
+    rows = q.shape[1] if q_is_x3 else q.shape[-2]
+    if q_is_x3:
+        q_spec = pl.BlockSpec((1, rows, HD), lambda i, h, fl, sc: (0, 0, h[i]))
+    else:
+        q_spec = pl.BlockSpec((1, rows, HD), lambda i, h, fl, sc: (i, 0, 0))
+    args = [q]
+    specs = [q_spec]
+    masked = sources is not None
+    if masked:
+        count_src = len(sources)
+        for array, first in sources:
+            args.append(array)
+            specs.append(
+                pl.BlockSpec(
+                    (1, 2, rows, HD), functools.partial(lambda o, i, h, fl, sc: (i + o, 0, 0, 0), first)
+                )
+            )
+    else:
+        count_src = 1
+        for plane in (1, 2):
+            args.append(q)
+            specs.append(
+                pl.BlockSpec(
+                    (1, rows, HD), functools.partial(lambda p, i, h, fl, sc: (p, 0, h[i]), plane)
+                )
+            )
+    if halves:
+        out_shape = [jax.ShapeDtypeStruct((count, rows // 2, HD), BF16)] * 2
+        out_specs = [pl.BlockSpec((1, rows // 2, HD), lambda i, h, fl, sc: (i, 0, 0))] * 2
+    else:
+        out_shape = jax.ShapeDtypeStruct((count, rows, HD), BF16)
+        out_specs = pl.BlockSpec((1, rows, HD), lambda i, h, fl, sc: (i, 0, 0))
+    return pl.pallas_call(
+        functools.partial(attend_kernel, count_src, masked, halves),
+        out_shape=out_shape,
+        grid_spec=pltpu.PrefetchScalarGridSpec(
+            num_scalar_prefetch=3, grid=(count,), in_specs=specs, out_specs=out_specs
+        ),
+        compiler_params=pltpu.CompilerParams(vmem_limit_bytes=VMEM_BYTES),
+        cost_estimate=pl.CostEstimate(
+            flops=8 * count * count_src * rows * rows * HD,
+            bytes_accessed=2 * count * (count_src * 2 + 2) * rows * HD,
+            transcendentals=count * count_src * rows * rows,
+        ),
+        name="attend",
+    )(heads, flags.reshape(-1), scal, *args)
+
+
+def blend(cond, uncond, strength):
+    cond = cond.astype(F32)
+    uncond = uncond.astype(F32)
+    return (uncond + strength * (cond - uncond)).astype(BF16)
+
+
+def assemble_kernel(sizes, pos_ref, scal_ref, strength_ref, *refs):
+    chunks, local = sizes
+    count = len(chunks)
+    own, peer = refs[: count + 1], refs[count + 1 : 2 * count + 2]
+    kept, moved = refs[2 * count + 2 : 3 * count + 2], refs[3 * count + 2 : 4 * count + 2]
+    out_ref = refs[-1]
+    branch, column = scal_ref[0], scal_ref[1]
+    strength = strength_ref[0]
+    exchanged = 2 * sum(chunks)
+
+    def mix(mine_ref, other_ref, index):
+        mine, other = mine_ref[index], other_ref[index]
+        first = branch == 0
+        return blend(jnp.where(first, mine, other), jnp.where(first, other, mine), strength)
+
+    def one(t, carry):
+        p = pos_ref[t]
+        slot = lax.shift_right_logical(p, 1)
+        here = jnp.bitwise_and(p, 1) == column
+        is_local = p >= exchanged
+        first = 0
+        for k, size in enumerate(chunks):
+            inside = jnp.logical_and(slot >= first, slot < first + size)
+            inside = jnp.logical_and(inside, jnp.logical_not(is_local))
+            index = jnp.clip(slot - first, 0, size - 1)
+
+            @pl.when(jnp.logical_and(inside, here))
+            def _(k=k, index=index):
+                out_ref[t] = mix(own[k], peer[k], index)
+
+            @pl.when(jnp.logical_and(inside, jnp.logical_not(here)))
+            def _(k=k, index=index):
+                half = kept[k].shape[1]
+                low_here = branch == 0
+                mine, other = kept[k][index], moved[k][index]
+                out_ref[t, :half] = jnp.where(low_here, mine, other)
+                out_ref[t, half:] = jnp.where(low_here, other, mine)
+
+            first += size
+        if local:
+            index = jnp.clip(p - exchanged, 0, local - 1)
+
+            @pl.when(is_local)
+            def _():
+                out_ref[t] = mix(own[count], peer[count], index)
+
+        return carry
+
+    lax.fori_loop(0, pos_ref.shape[0], one, 0)
+
+
+def ranked_body(rungs, qkv, timestep, windows, segments):
+    rows = qkv.shape[1]
+    heads = windows.shape[0]
+    seq_count = lax.axis_size("seq")
+    frame_count = lax.axis_size("frame")
+    cfg_count = lax.axis_size("cfg")
+    column = lax.axis_index("seq").astype(jnp.int32)
+    block = lax.axis_index("frame").astype(jnp.int32)
+    branch = lax.axis_index("cfg").astype(jnp.int32)
+    strength = 1.0 + 4.0 * timestep.astype(F32) / 999.0
+    x3 = jnp.transpose(qkv[0], (1, 0, 2))
+
+    ids = jnp.arange(heads, dtype=jnp.int32)
+    ahead = (windows[None, :] > windows[:, None]) | (
+        (windows[None, :] == windows[:, None]) & (ids[None, :] < ids[:, None])
+    )
+    rank = jnp.sum(ahead.astype(jnp.int32), axis=1)
+    order = jnp.sum(jnp.where(rank[None, :] == ids[:, None], ids[None, :], 0), axis=1)
+    sorted_windows = jnp.sum(
+        jnp.where(rank[None, :] == ids[:, None], windows[None, :], 0), axis=1
+    )
+    by_column = order.reshape(heads // 2, 2)
+    mine = lax.dynamic_index_in_dim(by_column, column, 1, keepdims=False)
+    theirs = lax.dynamic_index_in_dim(by_column, 1 - column, 1, keepdims=False)
+    my_windows = lax.dynamic_index_in_dim(
+        sorted_windows.reshape(heads // 2, 2), column, 1, keepdims=False
+    )
+
+    own_frame = 2 * block + column
+    sign = 1 - 2 * column
+    fill = jnp.full((W_MAX,), -1, jnp.int32)
+    seg_pad = jnp.concatenate([fill, segments, fill])
+    steps = {"O": 0, "X": 1, "NO": 2, "NR": -1, "FO": -2, "FR": 3}
+    shot = {
+        name: lax.dynamic_index_in_dim(
+            seg_pad, own_frame + step * sign + W_MAX, 0, keepdims=False
+        )
+        for name, step in steps.items()
+    }
+    own_names = ("FO", "NR", "O", "X", "NO")
+    across_names = ("NR", "O", "X", "NO", "FR")
+    distances = (2, 1, 0, 1, 2)
+
+    def flags_of(names, own):
+        columns = [
+            (my_windows >= distance) & (shot[name] == shot[own])
+            for name, distance in zip(names, distances)
+        ]
+        return jnp.stack(columns, axis=1).astype(jnp.int32)
+
+    flags_own = flags_of(own_names, "O")
+    flags_across = flags_of(across_names, "X")
+    scal = jnp.stack([branch, column])
+
+    per_half = heads // (seq_count * cfg_count)
+    first_out = branch * per_half
+    rank_grid = rank.reshape(seq_count, heads // seq_count)
+    pos = lax.dynamic_slice_in_dim(rank_grid, first_out, per_half, 1).reshape(-1)
+
+    grid_axes = ("seq", "frame")
+    last = frame_count - 1
+    apart = [(i, i - 1) for i in range(1, frame_count)] + [
+        (frame_count + i, frame_count + i + 1) for i in range(last)
+    ]
+    onward = [(i, i + 1) for i in range(last)] + [
+        (frame_count + i, frame_count + i - 1) for i in range(1, frame_count)
+    ]
+    swap = [(0, 1), (1, 0)]
+
+    def attempt(rung, x3, strength, mine, theirs, order, flags_own, flags_across, scal, pos):
+        exchanged, wide = rung
+        slots, far = exchanged // 2, wide // 2
+        local = heads - exchanged
+        bounds = [(0, far)] if far == slots else [(0, far), (far, slots)]
+        bounds = [(lo, hi) for lo, hi in bounds if hi > lo]
+        kv_out = [pack(x3, theirs[lo:hi], (1, 2)) for lo, hi in bounds]
+        kv_own = [pack(x3, mine[lo:hi], (1, 2)) for lo, hi in bounds]
+        q_out = [pack(x3, theirs[lo:hi], (0,)) for lo, hi in bounds]
+        kv_across = [lax.ppermute(a, "seq", swap) for a in kv_out]
+        near_own = [lax.ppermute(a, grid_axes, apart) for a in kv_own]
+        far_own = lax.ppermute(kv_own[0], grid_axes, onward)
+        q_across = [lax.ppermute(a, "seq", swap) for a in q_out]
+        near_across = [lax.ppermute(a, grid_axes, onward) for a in kv_across]
+        far_across = lax.ppermute(kv_across[0], grid_axes, apart)
+        own, kept, moved = [], [], []
+        for k, (lo, hi) in enumerate(bounds):
+            sources = {
+                "O": kv_own[k],
+                "X": kv_across[k],
+                "NO": near_own[k],
+                "NR": near_across[k],
+                "FO": far_own,
+                "FR": far_across,
+            }
+            cut = slice(0, 5) if k == 0 else slice(1, 4)
+            own.append(
+                attend_slots(
+                    x3,
+                    True,
+                    [(sources[name], 0) for name in own_names[cut]],
+                    flags_own[lo:hi, cut],
+                    mine[lo:hi],
+                    scal,
+                    False,
+                )
+            )
+            keep, send = attend_slots(
+                q_across[k].reshape(hi - lo, rows, HD),
+                False,
+                [(sources[name], 0) for name in across_names[cut]],
+                flags_across[lo:hi, cut],
+                mine[lo:hi],
+                scal,
+                True,
+            )
+            got = lax.ppermute(send, "cfg", swap)
+            first = scal[0] == 0
+            mixed = blend(jnp.where(first, keep, got), jnp.where(first, got, keep), strength[0])
+            kept.append(lax.ppermute(mixed, "seq", swap))
+            moved.append(lax.ppermute(kept[-1], "cfg", swap))
+        if local:
+            own.append(attend_slots(x3, True, None, mine[:1], order[exchanged:], scal, False))
+        peer = [lax.ppermute(a, "cfg", swap) for a in own]
+        if not local:
+            own, peer = own + own[:1], peer + peer[:1]
+        arrays = [*own, *peer, *kept, *moved]
+        return pl.pallas_call(
+            functools.partial(assemble_kernel, ([hi - lo for lo, hi in bounds], local)),
+            out_shape=jax.ShapeDtypeStruct((pos.shape[0], rows, HD), BF16),
+            in_specs=[whole(pltpu.SMEM)] * 3 + [whole()] * len(arrays),
+            out_specs=whole(),
+            compiler_params=pltpu.CompilerParams(vmem_limit_bytes=VMEM_BYTES),
+            name="assemble",
+        )(pos, scal, strength, *arrays)
+
+    many = jnp.sum((windows >= 1).astype(jnp.int32))
+    most = jnp.sum((windows >= 2).astype(jnp.int32))
+    index = jnp.int32(len(rungs) - 1)
+    for k in reversed(range(len(rungs) - 1)):
+        fits = (many <= rungs[k][0]) & (most <= rungs[k][1])
+        index = jnp.where(fits, jnp.int32(k), index)
+    out = lax.switch(
+        index,
+        [functools.partial(attempt, rung) for rung in rungs],
+        x3, strength, mine, theirs, order, flags_own, flags_across, scal, pos,
+    )
+    out = out.reshape(seq_count, per_half, rows, HD)
+    return jnp.transpose(out, (2, 1, 0, 3)).reshape(rows, per_half, seq_count * HD)
+
+
+def rungs_of(heads):
+    third = heads // 3
+    return ((2 * third + 2, third), (2 * third + 2, 2 * third + 2), (heads, heads))
+
 
 def solution(mesh):
+    sizes = dict(mesh.shape)
+
+    def whole_body(qkv, timestep, windows, segments):
+        tokens_here = qkv.shape[1]
+        frames_here = segments.shape[0] // sizes["frame"]
+        one_frame = frames_here == sizes["seq"]
+        if sizes["seq"] == 2 and sizes["cfg"] == 2 and one_frame and tokens_here % 32 == 0:
+            return ranked_body(rungs_of(windows.shape[0]), qkv, timestep, windows, segments)
+        return body(qkv, timestep, windows, segments)
+
     return jax.shard_map(
-        body,
+        whole_body,
         mesh=mesh,
         in_specs=(P("cfg", ("groups", "frame", "seq"), None, None), P("groups"), P(), P("groups")),
         out_specs=P(("groups", "frame", "seq"), "cfg", None),

time: 346 us -> 149 us (0.43)
  blocking collectives: 113 us -> 0 us
  local copies, waits for them, and re-layouts: 68 us -> 5.46 us
  matrix products: 43.7 us -> 0 us
  Pallas kernels: 0 us -> 40.5 us
  waiting for transfers between devices: 83.3 us -> 54.3 us
  starting transfers between devices: 8.19 us -> 29.8 us
  other arithmetic: 26.8 us -> 5.65 us
  between operations: 0.75 us -> 11.9 us
    all_to_all x2 -> x0, blocking collectives: 113 us -> none  [the longest x1 97.8 us: body(): lax.all_to_all(qkv, ('seq', 'cfg'), split_axis=3, concat_axis=0, tiled=True)]
    dot_general x4 -> x0, matrix products: 43.7 us -> none  [the longest x2 26.5 us: attend(): jnp.einsum('bhstur,ubrhd->sbthd', weights, value_rows, preferred_element_...]
    pallas_call x0 -> x12, Pallas kernels: none -> 40.5 us  [the longest x5 31.3 us: attend_slots(): pl.pallas_call(functools.partial(attend_kernel, count_src, masked, halves...]
    slice x5 -> x7, local copies, waits for them, and re-layouts: 32.8 us -> 1.04 us  [the longest x1 0.75 us: attempt(): order[exchanged:]]
    ppermute x2 -> x19, waiting for transfers between devices: 83.3 us -> 54.3 us  [the longest x2 35.7 us: attempt(): q_across = [lax.ppermute(a, 'seq', swap) for a in q_out]]
    unnamed x9 -> x0, local copies, waits for them, and re-layouts: 29 us -> none
    ppermute x2 -> x19, starting transfers between devices: 8.19 us -> 29.8 us  [the longest x2 6.75 us: attempt(): near_across = [lax.ppermute(a, grid_axes, onward) for a in kv_across]]
    reduce_sum x1 -> x3, other arithmetic: 18.6 us -> 3.01 us  [the longest x1 1.33 us: ranked_body(): most = jnp.sum((windows >= 2).astype(jnp.int32))]
  transfers between devices with their start and end apart: 2 -> 19, of which waited for: 2 -> 5; matrix products, arithmetic and copies ran while one was open for 1% -> 2% of each run, Pallas kernels for 0% -> 25%
where the time goes in v1:
time: 149 us; the launch traced here: 148 us
  waiting for transfers between devices  54.3 us (36%)
  Pallas kernels  40.5 us (27%)
  starting transfers between devices  29.8 us (20%)
  between operations  11.9 us (8%)
  other arithmetic  5.65 us (4%)
  local copies, waits for them, and re-layouts  5.46 us (4%)
    ppermute x2, waiting for transfers between devices, attempt(): q_across = [lax.ppermute(a, 'seq', swap) for a in q_out]  35.7 us
    pallas_call x5, Pallas kernels, attend_slots(): pl.pallas_call(functools.partial(attend_kernel, count_src, masked, halves...  31.3 us
    ppermute x1, waiting for transfers between devices, attempt(): far_across = lax.ppermute(kv_across[0], grid_axes, apart)  7.92 us
    pallas_call x6, Pallas kernels, pack(): pl.pallas_call(functools.partial(pack_kernel, planes, count), out_shape=j...  7.58 us
    ppermute x2, starting transfers between devices, attempt(): near_across = [lax.ppermute(a, grid_axes, onward) for a in kv_across]  6.75 us
    ppermute x2, starting transfers between devices, attempt(): kv_across = [lax.ppermute(a, 'seq', swap) for a in kv_out]  6.18 us
    ppermute x1, starting transfers between devices, attempt(): far_own = lax.ppermute(kv_own[0], grid_axes, onward)  5.39 us
    ppermute x2, waiting for transfers between devices, attempt(): kept.append(lax.ppermute(mixed, 'seq', swap))  4.64 us
  transfers between devices with their start and end apart: 19, of which 5 were waited for; matrix products, arithmetic and copies ran while one was open for 2% of the time, Pallas kernels for 25%

profile of v1, /device:TPU:0, one launch (start us, length us, event | category | flops | bytes accessed | tf_op | source)
XLA Modules:
  0.0 148.2 jit_solution(17019947191443068741)
XLA Ops:
  15.1 1.3 fusion.11
  18.4 128.2 %conditional.1 = (bf16[16,256,128]{2,1,0:T(8,128)(2,1)S(1)}) conditional(s32[]{:T(128)} %clamp.3, (s32[16]{0:T(128)S(1)}, s32[16,5]{1,0:T(8,128)}, bf16[3,256,4096]{2,1,0:T(8,128)(2,1)}, s32[16]{0:T(128)S(1)}, s32[2]{0:T(128)S(1)}, /*index=5*/s32[32]{0:T(128)S(1)}, s32[]{:T(128)}, s32[16,5]{1,0:T(8,128)S(1)}, f32[1]{0:T(128)}, ...), branch_computations={%region_5.6_spmd, %region_6.7_spmd, %region_7.8_spmd} | conditional | flops 10739515392 | bytes 119016824 | solution.py:439
  19.0 2.1 %pack_heads.15.refs_1_.refs_0_ = bf16[6,2,256,128]{3,2,1,0:T(8,128)(2,1)S(1)} custom-call(s32[6]{0:T(128)S(1)} %slice.35.heads_ref, bf16[3,256,4096]{2,1,0:T(8,128)(2,1)} %get-tuple-element.72.x_ref.q_ref.refs_0_.refs_1_), custom_call_target="tpu_custom_call" | custom-call | bytes 1572864 | tf_op jit(solution)/shard_map/cond/branch_0_fun/pack_heads/pallas_call | solution.py:127
  21.1 1.4 collective-permute-start.14
  23.5 6.1 %collective-permute-start.4 = (bf16[6,2,256,128]{3,2,1,0:T(8,128)(2,1)S(1)}, bf16[6,2,256,128]{3,2,1,0:T(8,128)(2,1)S(1)}, u32[]{:S(2)}, u32[]{:S(2)}) collective-permute-start(bf16[6,2,256,128]{3,2,1,0:T(8,128)(2,1)S(1)} %pack_heads.14), channel_id=1, source_target_pairs={{0,8},{8,0},{1,9},{9,1},{2,10},{10,2},{3,11},{11,3},{4,12},{12,4},... | collective-permute-start | bytes 2359304 | tf_op jit(solution)/shard_map/cond/branch_0_fun/ppermute | solution.py:376
  29.6 1.5 pack_heads.13
  31.8 2.1 %collective-permute-start.13 = (bf16[6,1,256,128]{3,2,0,1:T(8,128)(2,1)S(1)}, bf16[6,1,256,128]{3,2,0,1:T(8,128)(2,1)}, u32[]{:S(2)}, u32[]{:S(2)}) collective-permute-start(bf16[6,1,256,128]{3,2,0,1:T(8,128)(2,1)S(1)} %bitcast.39), channel_id=1, source_target_pairs={{0,8},{8,0},{1,9},{9,1},{2,10},{10,2},{3,11},{11,3},{4,12},{12,4},... | collective-permute-start | bytes 1179656 | tf_op jit(solution)/shard_map/cond/branch_0_fun/ppermute | solution.py:379
  34.8 35.7 %collective-permute-done.13 = bf16[6,1,256,128]{3,2,0,1:T(8,128)(2,1)} collective-permute-done((bf16[6,1,256,128]{3,2,0,1:T(8,128)(2,1)S(1)}, bf16[6,1,256,128]{3,2,0,1:T(8,128)(2,1)}, u32[]{:S(2)}, u32[]{:S(2)}) %collective-permute-start.13) | collective-permute-done | bytes 393248 | tf_op jit(solution)/shard_map/cond/branch_0_fun/ppermute | solution.py:379
  70.6 5.9 %attend.14 = (bf16[6,128,128]{2,1,0:T(8,128)(2,1)S(1)}, bf16[6,128,128]{2,1,0:T(8,128)(2,1)S(1)}) custom-call(s32[6]{0:T(128)S(1)} %slice.35.heads_ref, s32[18]{0:T(128)S(1)} %reshape.51.flags_ref, s32[2]{0:T(128)S(1)} %get-tuple-element.68.scal_ref, bf16[6,256,128]{2,1,0:T(8,128)(2,1)} %bitcast.4.q_ref, ...), custom_call_target="tpu_custom_call" | custom-call | flops 1207959552 | bytes 3145728 | tf_op jit(solution)/shard_map/cond/branch_0_fun/attend/pallas_call | solution.py:225
  76.6 1.8 %pack_heads.12.refs_2_.refs_1_ = bf16[5,2,256,128]{3,2,1,0:T(8,128)(2,1)S(1)} custom-call(s32[5]{0:T(128)S(1)} %bitcast.49, bf16[3,256,4096]{2,1,0:T(8,128)(2,1)} %get-tuple-element.72.x_ref.q_ref.refs_0_.refs_1_), custom_call_target="tpu_custom_call" | custom-call | bytes 1310720 | tf_op jit(solution)/shard_map/cond/branch_0_fun/pack_heads/pallas_call | solution.py:127
  79.7 5.4 %collective-permute-start.2 = (bf16[5,2,256,128]{3,2,1,0:T(8,128)(2,1)}, bf16[5,2,256,128]{3,2,1,0:T(8,128)(2,1)}, u32[]{:S(2)}, u32[]{:S(2)}) collective-permute-start(bf16[5,2,256,128]{3,2,1,0:T(8,128)(2,1)} %collective-permute-done.1.refs_3_.refs_2_), channel_id=1, source_target_pairs={{0,2},{2,4},{4,6},{10,8},{12,10},{14,12},{1,3},{3,5},{5,7},{11,9},... | collective-permute-start | bytes 1966088 | tf_op jit(solution)/shard_map/cond/branch_0_fun/ppermute | solution.py:380
  86.4 5.4 %collective-permute-start = (bf16[5,2,256,128]{3,2,1,0:T(8,128)(2,1)S(1)}, bf16[5,2,256,128]{3,2,1,0:T(8,128)(2,1)}, u32[]{:S(2)}, u32[]{:S(2)}) collective-permute-start(bf16[5,2,256,128]{3,2,1,0:T(8,128)(2,1)S(1)} %pack_heads.12.refs_2_.refs_1_), channel_id=1, source_target_pairs={{0,2},{2,4},{4,6},{10,8},{12,10},{14,12},{1,3},{3,5},{5,7},{11,9},... | collective-permute-start | bytes 1966088 | tf_op jit(solution)/shard_map/cond/branch_0_fun/ppermute | solution.py:378
  91.8 1.3 collective-permute-start.5
  94.2 8.0 %attend.12.refs_2_ = bf16[10,256,128]{2,1,0:T(8,128)(2,1)S(1)} custom-call(s32[10]{0:T(128)S(1)} %slice.38.heads_ref, s32[1]{0:T(128)S(1)} %bitcast.50, s32[2]{0:T(128)} %copy-done.6, bf16[3,256,4096]{2,1,0:T(8,128)(2,1)} %get-tuple-element.72.x_ref.q_ref.refs_0_.refs_1_, bf16[3,256,4096]{2,1,0:T(8,128)(2,1)} %get-tuple-element.72.x_ref.q_ref.refs_0_.refs_1_, ...), custom_call_target="tpu_custom_call" | custom-call | flops 671088640 | bytes 2621440 | tf_op jit(solution)/shard_map/cond/branch_0_fun/attend/pallas_call | solution.py:225
  103.6 7.9 %collective-permute-done.10.refs_4_ = bf16[5,2,256,128]{3,2,1,0:T(8,128)(2,1)} collective-permute-done((bf16[5,2,256,128]{3,2,1,0:T(8,128)(2,1)}, bf16[5,2,256,128]{3,2,1,0:T(8,128)(2,1)}, u32[]{:S(2)}, u32[]{:S(2)}) %collective-permute-start.10) | collective-permute-done | bytes 655392 | tf_op jit(solution)/shard_map/cond/branch_0_fun/ppermute | solution.py:381
  111.5 6.5 %attend.13 = (bf16[5,128,128]{2,1,0:T(8,128)(2,1)S(1)}, bf16[5,128,128]{2,1,0:T(8,128)(2,1)S(1)}) custom-call(s32[5]{0:T(128)S(1)} %bitcast.51, s32[25]{0:T(128)S(1)} %reshape.49.flags_ref, s32[2]{0:T(128)S(1)} %copy-done.7, bf16[5,256,128]{2,1,0:T(8,128)(2,1)} %bitcast.1.q_ref, bf16[5,2,256,128]{3,2,1,0:T(8,128)(2,1)} %collective-permute-done.2.refs_1_.refs_0_, ...), custom_call_target="tpu_custom_call" | custom-call | flops 1677721600 | bytes 3932160 | tf_op jit(solution)/shard_map/cond/branch_0_fun/attend/pallas_call | solution.py:225
  118.2 6.3 %attend.10.refs_0_ = bf16[5,256,128]{2,1,0:T(8,128)(2,1)S(1)} custom-call(s32[5]{0:T(128)S(1)} %bitcast.52, s32[25]{0:T(128)S(1)} %reshape.47.flags_ref, s32[2]{0:T(128)S(1)} %copy-done.7, bf16[3,256,4096]{2,1,0:T(8,128)(2,1)} %get-tuple-element.72.x_ref.q_ref.refs_0_.refs_1_, bf16[5,2,256,128]{3,2,1,0:T(8,128)(2,1)} %collective-permute-done.refs_0_, ...), custom_call_target="tpu_custom_call" | custom-call | flops 1677721600 | bytes 3932160 | tf_op jit(solution)/shard_map/cond/branch_0_fun/attend/pallas_call | solution.py:225
  125.1 4.6 %collective-permute-done.5.refs_0_ = bf16[6,2,256,128]{3,2,1,0:T(8,128)(2,1)S(1)} collective-permute-done((bf16[6,2,256,128]{3,2,1,0:T(8,128)(2,1)S(1)}, bf16[6,2,256,128]{3,2,1,0:T(8,128)(2,1)S(1)}, u32[]{:S(2)}, u32[]{:S(2)}) %collective-permute-start.5) | collective-permute-done | bytes 786464 | tf_op jit(solution)/shard_map/cond/branch_0_fun/ppermute | solution.py:380
  129.7 4.5 %attend.11.refs_1_ = bf16[6,256,128]{2,1,0:T(8,128)(2,1)S(1)} custom-call(s32[6]{0:T(128)S(1)} %slice.35.heads_ref, s32[18]{0:T(128)S(1)} %reshape.48.flags_ref, s32[2]{0:T(128)S(1)} %copy-done.7, bf16[3,256,4096]{2,1,0:T(8,128)(2,1)S(1)} %bitcast.45, bf16[6,2,256,128]{3,2,1,0:T(8,128)(2,1)S(1)} %collective-permute-done.5.refs_0_, ...), custom_call_target="tpu_custom_call" | custom-call | flops 1207959552 | bytes 3145728 | tf_op jit(solution)/shard_map/cond/branch_0_fun/attend/pallas_call | solution.py:225
  134.4 4.1 %collective-permute-start.12 = (bf16[5,128,128]{2,1,0:T(8,128)(2,1)S(1)}, bf16[5,128,128]{2,1,0:T(8,128)(2,1)S(1)}, u32[]{:S(2)}, u32[]{:S(2)}) collective-permute-start(bf16[5,128,128]{2,1,0:T(8,128)(2,1)S(1)} %fusion.3), channel_id=1, source_target_pairs={{0,8},{8,0},{1,9},{9,1},{2,10},{10,2},{3,11},{11,3},{4,12},{12,4},... | collective-permute-start | bytes 491528 | tf_op jit(solution)/shard_map/cond/branch_0_fun/ppermute | solution.py:416
  138.6 4.6 %collective-permute-done.12.refs_6_ = bf16[5,128,128]{2,1,0:T(8,128)(2,1)S(1)} collective-permute-done((bf16[5,128,128]{2,1,0:T(8,128)(2,1)S(1)}, bf16[5,128,128]{2,1,0:T(8,128)(2,1)S(1)}, u32[]{:S(2)}, u32[]{:S(2)}) %collective-permute-start.12) | collective-permute-done | bytes 163872 | tf_op jit(solution)/shard_map/cond/branch_0_fun/ppermute | solution.py:416
  143.3 1.4 collective-permute-done.17.refs_8_
  144.7 1.6 %assemble.3 = bf16[16,256,128]{2,1,0:T(8,128)(2,1)S(1)} custom-call(s32[16]{0:T(128)S(1)} %copy-done.12, s32[2]{0:T(128)S(1)} %copy-done.7, f32[1]{0:T(128)} %get-tuple-element.69.strength_ref, bf16[5,256,128]{2,1,0:T(8,128)(2,1)S(1)} %attend.10.refs_0_, bf16[6,256,128]{2,1,0:T(8,128)(2,1)S(1)} %attend.11.refs_1_, bf16[10,256,128]{2,1,0:T(8,128)(2,1)S(1)} %attend.12.refs_2_, ...), custom_call_target="tpu_custom_call" | custom-call | tf_op jit(solution)/shard_map/cond/branch_0_fun/assemble/pallas_call | solution.py:424
  146.6 1.6 %copy.21 = bf16[2,8,256,128]{3,1,0,2:T(8,128)(2,1)} copy(bf16[2,8,256,128]{3,2,1,0:T(8,128)(2,1)S(1)} %bitcast.46) | data formatting | bytes 2097152 | tf_op jit(solution)/shard_map/reshape | solution.py:444
  (77 shorter events, 14.5 us)
Async XLA Ops:
  18.4 52.1 %copy-start.6 = (s32[2]{0:T(128)}, s32[2]{0:T(128)S(1)}, u32[]{:S(2)}) copy-start(s32[2]{0:T(128)S(1)} %get-tuple-element.68.scal_ref) | copy-start | bytes 28 | tf_op jit(solution)/shard_map/cond
  21.1 49.5 %collective-permute-start.14 = (bf16[6,2,256,128]{3,2,1,0:T(8,128)(2,1)S(1)}, bf16[6,2,256,128]{3,2,1,0:T(8,128)(2,1)}, u32[]{:S(2)}, u32[]{:S(2)}) collective-permute-start(bf16[6,2,256,128]{3,2,1,0:T(8,128)(2,1)S(1)} %pack_heads.15.refs_1_.refs_0_), channel_id=1, source_target_pairs={{2,0},{4,2},{6,4},{8,10},{10,12},{12,14},{3,1},{5,3},{7,5},{9,11},... | collective-permute-start | bytes 2359304 | tf_op jit(solution)/shard_map/cond/branch_0_fun/ppermute | solution.py:377
  23.5 47.1 %collective-permute-start.4 = (bf16[6,2,256,128]{3,2,1,0:T(8,128)(2,1)S(1)}, bf16[6,2,256,128]{3,2,1,0:T(8,128)(2,1)S(1)}, u32[]{:S(2)}, u32[]{:S(2)}) collective-permute-start(bf16[6,2,256,128]{3,2,1,0:T(8,128)(2,1)S(1)} %pack_heads.14), channel_id=1, source_target_pairs={{0,8},{8,0},{1,9},{9,1},{2,10},{10,2},{3,11},{11,3},{4,12},{12,4},... | collective-permute-start | bytes 2359304 | tf_op jit(solution)/shard_map/cond/branch_0_fun/ppermute | solution.py:376
  31.0 48.7 %collective-permute-start.1 = (bf16[5,2,256,128]{3,2,1,0:T(8,128)(2,1)}, bf16[5,2,256,128]{3,2,1,0:T(8,128)(2,1)}, u32[]{:S(2)}, u32[]{:S(2)}) collective-permute-start(bf16[5,2,256,128]{3,2,1,0:T(8,128)(2,1)} %pack_heads.13), channel_id=1, source_target_pairs={{0,8},{8,0},{1,9},{9,1},{2,10},{10,2},{3,11},{11,3},{4,12},{12,4},... | collective-permute-start | bytes 1966088 | tf_op jit(solution)/shard_map/cond/branch_0_fun/ppermute | solution.py:376
  31.8 38.7 %collective-permute-start.13 = (bf16[6,1,256,128]{3,2,0,1:T(8,128)(2,1)S(1)}, bf16[6,1,256,128]{3,2,0,1:T(8,128)(2,1)}, u32[]{:S(2)}, u32[]{:S(2)}) collective-permute-start(bf16[6,1,256,128]{3,2,0,1:T(8,128)(2,1)S(1)} %bitcast.39), channel_id=1, source_target_pairs={{0,8},{8,0},{1,9},{9,1},{2,10},{10,2},{3,11},{11,3},{4,12},{12,4},... | collective-permute-start | bytes 1179656 | tf_op jit(solution)/shard_map/cond/branch_0_fun/ppermute | solution.py:379
  34.6 51.8 %collective-permute-start.9 = (bf16[5,1,256,128]{3,2,0,1:T(8,128)(2,1)S(1)}, bf16[5,1,256,128]{3,2,0,1:T(8,128)(2,1)}, u32[]{:S(2)}, u32[]{:S(2)}) collective-permute-start(bf16[5,1,256,128]{3,2,0,1:T(8,128)(2,1)S(1)} %bitcast.40), channel_id=1, source_target_pairs={{0,8},{8,0},{1,9},{9,1},{2,10},{10,2},{3,11},{11,3},{4,12},{12,4},... | collective-permute-start | bytes 983048 | tf_op jit(solution)/shard_map/cond/branch_0_fun/ppermute | solution.py:379
  76.5 15.3 %collective-permute-start.15 = (bf16[6,128,128]{2,1,0:T(8,128)(2,1)S(1)}, bf16[6,128,128]{2,1,0:T(8,128)(2,1)}, u32[]{:S(2)}, u32[]{:S(2)}) collective-permute-start(bf16[6,128,128]{2,1,0:T(8,128)(2,1)S(1)} %get-tuple-element.79), channel_id=1, source_target_pairs={{0,1},{1,0},{2,3},{3,2},{4,5},{5,4},{6,7},{7,6},{8,9},{9,8},{10,11... | collective-permute-start | bytes 589832 | tf_op jit(solution)/shard_map/cond/branch_0_fun/ppermute | solution.py:413
  76.6 16.6 %copy-start.3 = (s32[16,5]{1,0:T(8,128)S(1)}, s32[16,5]{1,0:T(8,128)}, u32[]{:S(2)}) copy-start(s32[16,5]{1,0:T(8,128)} %get-tuple-element.71) | copy-start | bytes 964 | tf_op jit(solution)/shard_map/cond
  78.4 24.9 %collective-permute-start.3 = (bf16[5,2,256,128]{3,2,1,0:T(8,128)(2,1)S(1)}, bf16[5,2,256,128]{3,2,1,0:T(8,128)(2,1)}, u32[]{:S(2)}, u32[]{:S(2)}) collective-permute-start(bf16[5,2,256,128]{3,2,1,0:T(8,128)(2,1)S(1)} %pack_heads.12.refs_2_.refs_1_), channel_id=1, source_target_pairs={{2,0},{4,2},{6,4},{8,10},{10,12},{12,14},{3,1},{5,3},{7,5},{9,11},... | collective-permute-start | bytes 1966088 | tf_op jit(solution)/shard_map/cond/branch_0_fun/ppermute | solution.py:377
  79.7 23.7 %collective-permute-start.2 = (bf16[5,2,256,128]{3,2,1,0:T(8,128)(2,1)}, bf16[5,2,256,128]{3,2,1,0:T(8,128)(2,1)}, u32[]{:S(2)}, u32[]{:S(2)}) collective-permute-start(bf16[5,2,256,128]{3,2,1,0:T(8,128)(2,1)} %collective-permute-done.1.refs_3_.refs_2_), channel_id=1, source_target_pairs={{0,2},{2,4},{4,6},{10,8},{12,10},{14,12},{1,3},{3,5},{5,7},{11,9},... | collective-permute-start | bytes 1966088 | tf_op jit(solution)/shard_map/cond/branch_0_fun/ppermute | solution.py:380
  85.1 26.4 %collective-permute-start.10 = (bf16[5,2,256,128]{3,2,1,0:T(8,128)(2,1)}, bf16[5,2,256,128]{3,2,1,0:T(8,128)(2,1)}, u32[]{:S(2)}, u32[]{:S(2)}) collective-permute-start(bf16[5,2,256,128]{3,2,1,0:T(8,128)(2,1)} %collective-permute-done.1.refs_3_.refs_2_), channel_id=1, source_target_pairs={{2,0},{4,2},{6,4},{8,10},{10,12},{12,14},{3,1},{5,3},{7,5},{9,11},... | collective-permute-start | bytes 1966088 | tf_op jit(solution)/shard_map/cond/branch_0_fun/ppermute | solution.py:381
  86.4 31.8 %collective-permute-start = (bf16[5,2,256,128]{3,2,1,0:T(8,128)(2,1)S(1)}, bf16[5,2,256,128]{3,2,1,0:T(8,128)(2,1)}, u32[]{:S(2)}, u32[]{:S(2)}) collective-permute-start(bf16[5,2,256,128]{3,2,1,0:T(8,128)(2,1)S(1)} %pack_heads.12.refs_2_.refs_1_), channel_id=1, source_target_pairs={{0,2},{2,4},{4,6},{10,8},{12,10},{14,12},{1,3},{3,5},{5,7},{11,9},... | collective-permute-start | bytes 1966088 | tf_op jit(solution)/shard_map/cond/branch_0_fun/ppermute | solution.py:378
  91.8 37.9 %collective-permute-start.5 = (bf16[6,2,256,128]{3,2,1,0:T(8,128)(2,1)S(1)}, bf16[6,2,256,128]{3,2,1,0:T(8,128)(2,1)S(1)}, u32[]{:S(2)}, u32[]{:S(2)}) collective-permute-start(bf16[6,2,256,128]{3,2,1,0:T(8,128)(2,1)S(1)} %collective-permute-done.4.refs_2_.refs_1_), channel_id=1, source_target_pairs={{0,2},{2,4},{4,6},{10,8},{12,10},{14,12},{1,3},{3,5},{5,7},{11,9},... | collective-permute-start | bytes 2359304 | tf_op jit(solution)/shard_map/cond/branch_0_fun/ppermute | solution.py:380
  94.2 17.3 %copy-start.7 = (s32[2]{0:T(128)S(1)}, s32[2]{0:T(128)}, u32[]{:S(2)}) copy-start(s32[2]{0:T(128)} %copy-done.6) | copy-start | bytes 28 | tf_op jit(solution)/shard_map/cond
  103.3 40.0 %collective-permute-start.8 = (bf16[10,256,128]{2,1,0:T(8,128)(2,1)S(1)}, bf16[10,256,128]{2,1,0:T(8,128)(2,1)S(1)}, u32[]{:S(2)}, u32[]{:S(2)}) collective-permute-start(bf16[10,256,128]{2,1,0:T(8,128)(2,1)S(1)} %attend.12.refs_2_), channel_id=1, source_target_pairs={{0,1},{1,0},{2,3},{3,2},{4,5},{5,4},{6,7},{7,6},{8,9},{9,8},{10,11... | collective-permute-start | bytes 1966088 | tf_op jit(solution)/shard_map/cond/branch_0_fun/ppermute | solution.py:420
  103.4 35.0 %collective-permute-start.16 = (bf16[6,128,128]{2,1,0:T(8,128)(2,1)S(1)}, bf16[6,128,128]{2,1,0:T(8,128)(2,1)S(1)}, u32[]{:S(2)}, u32[]{:S(2)}) collective-permute-start(bf16[6,128,128]{2,1,0:T(8,128)(2,1)S(1)} %fusion.1), channel_id=1, source_target_pairs={{0,8},{8,0},{1,9},{9,1},{2,10},{10,2},{3,11},{11,3},{4,12},{12,4},... | collective-permute-start | bytes 589832 | tf_op jit(solution)/shard_map/cond/branch_0_fun/ppermute | solution.py:416
  111.5 18.1 %slice-start = ((s8[6291456]{0:T(1024)(128)(4,1)}), s8[4194304]{0:T(1024)(128)(4,1)S(1)}, s32[]{:S(2)}) async-start(s8[6291456]{0:T(1024)(128)(4,1)} %bitcast.44), calls=%async_computation | async-start | bytes 8388608 | tf_op jit(solution)/shard_map/cond
  118.1 16.1 %collective-permute-start.11 = (bf16[5,128,128]{2,1,0:T(8,128)(2,1)S(1)}, bf16[5,128,128]{2,1,0:T(8,128)(2,1)S(1)}, u32[]{:S(2)}, u32[]{:S(2)}) collective-permute-start(bf16[5,128,128]{2,1,0:T(8,128)(2,1)S(1)} %get-tuple-element.77), channel_id=1, source_target_pairs={{0,1},{1,0},{2,3},{3,2},{4,5},{5,4},{6,7},{7,6},{8,9},{9,8},{10,11... | collective-permute-start | bytes 491528 | tf_op jit(solution)/shard_map/cond/branch_0_fun/ppermute | solution.py:413
  124.5 20.2 %copy-start.12 = (s32[16]{0:T(128)S(1)}, s32[16]{0:T(128)}, u32[]{:S(2)}) copy-start(s32[16]{0:T(128)} %get-tuple-element.66.pos_ref) | copy-start | bytes 196 | tf_op jit(solution)/shard_map/cond
  124.5 18.8 %collective-permute-start.6 = (bf16[5,256,128]{2,1,0:T(8,128)(2,1)S(1)}, bf16[5,256,128]{2,1,0:T(8,128)(2,1)S(1)}, u32[]{:S(2)}, u32[]{:S(2)}) collective-permute-start(bf16[5,256,128]{2,1,0:T(8,128)(2,1)S(1)} %attend.10.refs_0_), channel_id=1, source_target_pairs={{0,1},{1,0},{2,3},{3,2},{4,5},{5,4},{6,7},{7,6},{8,9},{9,8},{10,11... | collective-permute-start | bytes 983048 | tf_op jit(solution)/shard_map/cond/branch_0_fun/ppermute | solution.py:420
  134.2 10.5 %collective-permute-start.7 = (bf16[6,256,128]{2,1,0:T(8,128)(2,1)S(1)}, bf16[6,256,128]{2,1,0:T(8,128)(2,1)S(1)}, u32[]{:S(2)}, u32[]{:S(2)}) collective-permute-start(bf16[6,256,128]{2,1,0:T(8,128)(2,1)S(1)} %attend.11.refs_1_), channel_id=1, source_target_pairs={{0,1},{1,0},{2,3},{3,2},{4,5},{5,4},{6,7},{7,6},{8,9},{9,8},{10,11... | collective-permute-start | bytes 1179656 | tf_op jit(solution)/shard_map/cond/branch_0_fun/ppermute | solution.py:420
  134.4 8.9 %collective-permute-start.12 = (bf16[5,128,128]{2,1,0:T(8,128)(2,1)S(1)}, bf16[5,128,128]{2,1,0:T(8,128)(2,1)S(1)}, u32[]{:S(2)}, u32[]{:S(2)}) collective-permute-start(bf16[5,128,128]{2,1,0:T(8,128)(2,1)S(1)} %fusion.3), channel_id=1, source_target_pairs={{0,8},{8,0},{1,9},{9,1},{2,10},{10,2},{3,11},{11,3},{4,12},{12,4},... | collective-permute-start | bytes 491528 | tf_op jit(solution)/shard_map/cond/branch_0_fun/ppermute | solution.py:416
  138.4 4.9 %collective-permute-start.18 = (bf16[6,128,128]{2,1,0:T(8,128)(2,1)S(1)}, bf16[6,128,128]{2,1,0:T(8,128)(2,1)S(1)}, u32[]{:S(2)}, u32[]{:S(2)}) collective-permute-start(bf16[6,128,128]{2,1,0:T(8,128)(2,1)S(1)} %collective-permute-done.16.refs_7_), channel_id=1, source_target_pairs={{0,1},{1,0},{2,3},{3,2},{4,5},{5,4},{6,7},{7,6},{8,9},{9,8},{10,11... | collective-permute-start | bytes 589832 | tf_op jit(solution)/shard_map/cond/branch_0_fun/ppermute | solution.py:417
  143.3 1.4 collective-permute-start.17
  (3 other events, 15.8 us)

commit v2 on v0

--- a/solution.py
+++ b/solution.py
@@ -1,8 +1,11 @@
+import functools
 import math
 
 import jax
 import jax.numpy as jnp
 from jax import lax
+from jax.experimental import pallas as pl
+from jax.experimental.pallas import tpu as pltpu
 from jax.sharding import PartitionSpec as P
 
 HD = 128
@@ -89,10 +92,496 @@
     own_rows = lax.all_to_all(guided, "seq", split_axis=0, concat_axis=3, tiled=True)
     return own_rows[0]
 
+LOG2E = 1.4426950408889634
+MASKED = -1e30
+BF16 = jnp.bfloat16
+F32 = jnp.float32
+VMEM_BYTES = 32 * 1024 * 1024
+SWAP = ((0, 1), (1, 0))
+STEPS = {"O": 0, "X": 1, "NO": 2, "NR": -1, "FO": -2, "FR": 3}
+OWN_SOURCES = ("FO", "NR", "O", "X", "NO")
+ACROSS_SOURCES = ("NR", "O", "X", "NO", "FR")
+DISTANCES = (2, 1, 0, 1, 2)
+
+
+def whole(space=pltpu.VMEM):
+    return pl.BlockSpec(memory_space=space)
+
+
+def params():
+    return pltpu.CompilerParams(vmem_limit_bytes=VMEM_BYTES)
+
+
+class Layout:
+    def __init__(self, heads, outs):
+        self.mine = 0
+        self.theirs = heads // 2
+        self.order = heads
+        self.rank = 2 * heads
+        self.reach = 3 * heads
+        self.my_reach = 4 * heads
+        self.pos = self.my_reach + heads // 2
+        self.own_match = self.pos + outs
+        self.across_match = self.own_match + len(DISTANCES)
+        self.branch = self.across_match + len(DISTANCES)
+        self.column = self.branch + 1
+        self.rung = self.column + 1
+        self.size = self.rung + 1
+
+
+def plan_kernel(at, rungs, split, place_ref, windows_ref, segments_ref, plan_ref):
+    heads = windows_ref.shape[0]
+    frames = segments_ref.shape[0]
+    column, block, branch = place_ref[0], place_ref[1], place_ref[2]
+    reach = [windows_ref[h] for h in range(heads)]
+    wide = [(w >= 2).astype(jnp.int32) for w in reach]
+    some = [(w >= 1).astype(jnp.int32) for w in reach]
+    most = functools.reduce(lambda a, b: a + b, wide)
+    many = functools.reduce(lambda a, b: a + b, some)
+    next_wide, next_some, next_none = jnp.int32(0), most, many
+    for h in range(heads):
+        spot = jnp.where(wide[h] == 1, next_wide, jnp.where(some[h] == 1, next_some, next_none))
+        next_wide = next_wide + wide[h]
+        next_some = next_some + some[h] - wide[h]
+        next_none = next_none + 1 - some[h]
+        plan_ref[at.order + spot] = jnp.int32(h)
+        plan_ref[at.rank + h] = spot
+        plan_ref[at.reach + spot] = reach[h]
+    for j in range(heads // 2):
+        plan_ref[at.mine + j] = plan_ref[at.order + 2 * j + column]
+        plan_ref[at.theirs + j] = plan_ref[at.order + 2 * j + 1 - column]
+        plan_ref[at.my_reach + j] = plan_ref[at.reach + 2 * j + column]
+    columns, cores = split
+    per_half = heads // (columns * cores)
+    for t in range(columns * per_half):
+        head = (t // per_half) * (heads // columns) + branch * per_half + t % per_half
+        plan_ref[at.pos + t] = plan_ref[at.rank + head]
+    own_frame = 2 * block + column
+    sign = 1 - 2 * column
+
+    def shot(name):
+        frame = own_frame + STEPS[name] * sign
+        inside = jnp.logical_and(frame >= 0, frame < frames)
+        return jnp.where(inside, segments_ref[jnp.clip(frame, 0, frames - 1)], -1)
+
+    for first, names, query in (
+        (at.own_match, OWN_SOURCES, "O"),
+        (at.across_match, ACROSS_SOURCES, "X"),
+    ):
+        for k, name in enumerate(names):
+            plan_ref[first + k] = (shot(name) == shot(query)).astype(jnp.int32)
+    plan_ref[at.branch] = branch
+    plan_ref[at.column] = column
+    index = jnp.int32(len(rungs) - 1)
+    for k in reversed(range(len(rungs) - 1)):
+        fits = jnp.logical_and(many <= rungs[k][0], most <= rungs[k][1])
+        index = jnp.where(fits, jnp.int32(k), index)
+    plan_ref[at.rung] = index
+
+
+def pack_kernel(jobs, count_in, plan_ref, x_ref, *refs):
+    outs, sems = refs[count_in:-1], refs[-1]
+    copies = []
+    for out_ref, (first, count, planes) in zip(outs, jobs):
+        for j in range(count):
+            start = pl.multiple_of(plan_ref[first + j] * HD, HD)
+            for k, plane in enumerate(planes):
+                copies.append(
+                    pltpu.make_async_copy(
+                        x_ref.at[plane, :, pl.ds(start, HD)],
+                        out_ref.at[j, k],
+                        sems.at[len(copies)],
+                    )
+                )
+    for copy in copies:
+        copy.start()
+    for copy in copies:
+        copy.wait()
+
+
+def pack(plan, x3, jobs, after):
+    rows = x3.shape[1]
+    total = sum(count * len(planes) for _, count, planes in jobs)
+    return pl.pallas_call(
+        functools.partial(pack_kernel, jobs, len(after)),
+        out_shape=[
+            jax.ShapeDtypeStruct((count, len(planes), rows, HD), x3.dtype)
+            for _, count, planes in jobs
+        ],
+        grid_spec=pltpu.PrefetchScalarGridSpec(
+            num_scalar_prefetch=1,
+            grid=(1,),
+            in_specs=[whole(pl.ANY)] * (1 + len(after)),
+            out_specs=[whole(pl.ANY)] * len(jobs),
+            scratch_shapes=[pltpu.SemaphoreType.DMA((total,))],
+        ),
+        compiler_params=params(),
+        cost_estimate=pl.CostEstimate(
+            flops=0, bytes_accessed=4 * total * rows * HD, transcendentals=0
+        ),
+        name="pack_heads",
+    )(plan, x3, *after)
+
+
+def gate_kernel(*refs):
+    del refs
+
+
+def gate(values, after):
+    count = len(values)
+    return pl.pallas_call(
+        gate_kernel,
+        out_shape=[jax.ShapeDtypeStruct(v.shape, v.dtype) for v in values],
+        in_specs=[whole(pl.ANY)] * (count + len(after)),
+        out_specs=[whole(pl.ANY)] * count,
+        input_output_aliases={i: i for i in range(count)},
+        compiler_params=params(),
+        name="gate",
+    )(*values, *after)
+
+
+def softmax_mix(q, keys, values, biases):
+    factor = LOG2E / math.sqrt(HD)
+    scores = []
+    for key, bias in zip(keys, biases):
+        score = lax.dot_general(q, key, (((1,), (1,)), ((), ())), preferred_element_type=F32)
+        scores.append(score if bias is None else score + bias)
+    top = jnp.max(functools.reduce(jnp.maximum, scores), axis=1, keepdims=True)
+    expd = [jnp.exp2((score - top) * factor) for score in scores]
+    total = jnp.sum(functools.reduce(jnp.add, expd), axis=1, keepdims=True)
+    mixed = functools.reduce(
+        jnp.add,
+        [
+            jnp.dot(e.astype(BF16), value, preferred_element_type=F32)
+            for e, value in zip(expd, values)
+        ],
+    )
+    return (mixed / total).astype(BF16)
+
+
+def attend_kernel(spec, plan_ref, q_ref, *refs):
+    count, sources, gathered, heads_at, reach_at, match_at, distances, branch_at, halves = spec
+    kv_refs = refs[:sources]
+    refs = refs[sources:]
+    if gathered:
+        outs, (held, sems) = refs[:-2], refs[-2:]
+        outs = outs[-1:]
+        copies = []
+        planes = held.shape[1]
+        for j in range(count):
+            start = pl.multiple_of(plan_ref[heads_at + j] * HD, HD)
+            for k in range(planes):
+                copies.append(
+                    pltpu.make_async_copy(
+                        q_ref.at[k, :, pl.ds(start, HD)], held.at[j, k], sems.at[j * planes + k]
+                    )
+                )
+        for copy in copies:
+            copy.start()
+        for copy in copies:
+            copy.wait()
+    else:
+        outs = refs[-2:] if halves else refs[-1:]
+    for j in range(count):
+        if gathered:
+            q = held[j, 0]
+        else:
+            q = q_ref[j, 0]
+        if sources:
+            keys = [ref[j, 0] for ref in kv_refs]
+            values = [ref[j, 1] for ref in kv_refs]
+            reach = plan_ref[reach_at + j]
+            biases = []
+            for k, distance in enumerate(distances):
+                seen = jnp.logical_and(reach >= distance, plan_ref[match_at + k] != 0)
+                biases.append(jnp.where(seen, 0.0, MASKED).astype(F32))
+        else:
+            keys, values, biases = [held[j, 1]], [held[j, 2]], [None]
+        out = softmax_mix(q, keys, values, biases)
+        if halves:
+            half = out.shape[0] // 2
+            low, high = out[:half], out[half:]
+            first = plan_ref[branch_at] == 0
+            outs[0][j] = jnp.where(first, low, high)
+            outs[1][j] = jnp.where(first, high, low)
+        else:
+            outs[0][j] = out
+
+
+def attend_slots(plan, at, q, sources, heads_at, first, count, match_at, distances, after):
+    rows = q.shape[-2]
+    gathered = q.ndim == 3
+    spec = (
+        count,
+        len(sources),
+        gathered,
+        heads_at,
+        at.my_reach + first,
+        match_at,
+        distances,
+        at.branch,
+        not gathered,
+    )
+    kv_specs, kvs = [], []
+    for array, offset in sources:
+        kvs.append(array)
+        if array.shape[0] == count:
+            kv_specs.append(whole())
+        else:
+            kv_specs.append(
+                pl.BlockSpec(
+                    (pl.Element(count), pl.Element(2), pl.Element(rows), pl.Element(HD)),
+                    functools.partial(lambda o, i, plan: (o, 0, 0, 0), offset),
+                )
+            )
+    scratch = []
+    if gathered:
+        planes = 1 if sources else 3
+        scratch = [
+            pltpu.VMEM((count, planes, rows, HD), BF16),
+            pltpu.SemaphoreType.DMA((count * planes,)),
+        ]
+        out_shape = jax.ShapeDtypeStruct((count, rows, HD), BF16)
+        out_specs = whole()
+    else:
+        out_shape = [jax.ShapeDtypeStruct((count, rows // 2, HD), BF16)] * 2
+        out_specs = [whole()] * 2
+    blocks = count * max(1, len(sources))
+    return pl.pallas_call(
+        functools.partial(attend_kernel, spec),
+        out_shape=out_shape,
+        grid_spec=pltpu.PrefetchScalarGridSpec(
+            num_scalar_prefetch=1,
+            grid=(1,),
+            in_specs=[whole(pl.ANY) if gathered else whole()]
+            + kv_specs
+            + [whole(pl.ANY)] * len(after),
+            out_specs=out_specs,
+            scratch_shapes=scratch,
+        ),
+        compiler_params=params(),
+        cost_estimate=pl.CostEstimate(
+            flops=8 * blocks * rows * rows * HD,
+            bytes_accessed=4 * (blocks + count) * rows * HD,
+            transcendentals=blocks * rows * rows,
+        ),
+        name="attend",
+    )(plan, q, *kvs, *after)
+
+
+def blend(cond, uncond, strength):
+    cond = cond.astype(F32)
+    uncond = uncond.astype(F32)
+    return (uncond + strength * (cond - uncond)).astype(BF16)
+
+
+def assemble_kernel(at, chunks, local, plan_ref, strength_ref, *refs):
+    count = len(chunks)
+    own, peer = refs[: count + 1], refs[count + 1 : 2 * count + 2]
+    kept, moved = refs[2 * count + 2 : 3 * count + 2], refs[3 * count + 2 : 4 * count + 2]
+    out_ref = refs[-1]
+    branch, column = plan_ref[at.branch], plan_ref[at.column]
+    strength = strength_ref[0]
+    exchanged = 2 * sum(chunks)
+
+    def mix(mine_ref, other_ref, index):
+        mine, other = mine_ref[index], other_ref[index]
+        first = branch == 0
+        return blend(jnp.where(first, mine, other), jnp.where(first, other, mine), strength)
+
+    def one(t, carry):
+        p = plan_ref[at.pos + t]
+        slot = lax.shift_right_logical(p, 1)
+        here = jnp.bitwise_and(p, 1) == column
+        is_local = p >= exchanged
+        first = 0
+        for k, size in enumerate(chunks):
+            inside = jnp.logical_and(slot >= first, slot < first + size)
+            inside = jnp.logical_and(inside, jnp.logical_not(is_local))
+            index = jnp.clip(slot - first, 0, size - 1)
+
+            @pl.when(jnp.logical_and(inside, here))
+            def _(k=k, index=index):
+                out_ref[t] = mix(own[k], peer[k], index)
+
+            @pl.when(jnp.logical_and(inside, jnp.logical_not(here)))
+            def _(k=k, index=index):
+                half = kept[k].shape[1]
+                low_here = branch == 0
+                mine, other = kept[k][index], moved[k][index]
+                out_ref[t, :half] = jnp.where(low_here, mine, other)
+                out_ref[t, half:] = jnp.where(low_here, other, mine)
+
+            first += size
+        if local:
+            index = jnp.clip(p - exchanged, 0, local - 1)
+
+            @pl.when(is_local)
+            def _():
+                out_ref[t] = mix(own[count], peer[count], index)
+
+        return carry
+
+    lax.fori_loop(0, out_ref.shape[0], one, 0)
+
+
+def ranked_body(rungs, qkv, timestep, windows, segments):
+    rows = qkv.shape[1]
+    heads = windows.shape[0]
+    seq_count = lax.axis_size("seq")
+    frame_count = lax.axis_size("frame")
+    cfg_count = lax.axis_size("cfg")
+    per_half = heads // (seq_count * cfg_count)
+    outs = seq_count * per_half
+    at = Layout(heads, outs)
+    strength = 1.0 + 4.0 * timestep.astype(F32) / 999.0
+    x3 = jnp.transpose(qkv[0], (1, 0, 2))
+    place = jnp.stack([lax.axis_index(a).astype(jnp.int32) for a in ("seq", "frame", "cfg")])
+    plan = pl.pallas_call(
+        functools.partial(plan_kernel, at, rungs, (seq_count, cfg_count)),
+        out_shape=jax.ShapeDtypeStruct((at.size,), jnp.int32),
+        in_specs=[whole(pltpu.SMEM)] * 3,
+        out_specs=whole(pltpu.SMEM),
+        name="plan",
+    )(place, windows, segments)
+
+    grid_axes = ("seq", "frame")
+    last = frame_count - 1
+    apart = [(i, i - 1) for i in range(1, frame_count)] + [
+        (frame_count + i, frame_count + i + 1) for i in range(last)
+    ]
+    onward = [(i, i + 1) for i in range(last)] + [
+        (frame_count + i, frame_count + i - 1) for i in range(1, frame_count)
+    ]
+
+    def attempt(rung, plan, x3, strength):
+        exchanged, wide = rung
+        slots, far = exchanged // 2, wide // 2
+        local = heads - exchanged
+        bounds = [(lo, hi) for lo, hi in ((0, far), (far, slots)) if hi > lo]
+        two = len(bounds) == 2
+
+        def cross(a):
+            return lax.ppermute(a, "seq", SWAP)
+
+        def mate(a):
+            return lax.ppermute(a, "cfg", SWAP)
+
+        (kv_out0,) = pack(plan, x3, [(at.theirs, far, (1, 2))], [])
+        across = [cross(kv_out0)]
+        kv_own, kv_far = pack(
+            plan, x3, [(at.mine, slots, (1, 2)), (at.mine, far, (1, 2))], [kv_out0]
+        )
+        near_own = lax.ppermute(kv_own, grid_axes, apart)
+        far_own = lax.ppermute(kv_far, grid_axes, onward)
+        jobs = [(at.theirs, far, (0,))]
+        if two:
+            jobs += [(at.theirs + far, slots - far, (0,)), (at.theirs + far, slots - far, (1, 2))]
+        q_out = list(pack(plan, x3, jobs, [kv_own]))
+        if two:
+            across.append(cross(q_out.pop()))
+        done = [q_out[0]]
+        if local:
+            own_local = attend_slots(
+                plan, at, x3, [], at.order + exchanged, 0, local, 0, (), done
+            )
+            peer_local = mate(own_local)
+            done = [own_local]
+        across[0], q_out[0] = gate([across[0], q_out[0]], [*done, far_own])
+        near_across = [lax.ppermute(across[0], grid_axes, onward)]
+        far_across = lax.ppermute(across[0], grid_axes, apart)
+        q_across = [cross(q_out[0])]
+        done = [across[0]]
+        if two:
+            across[1], q_out[1] = gate([across[1], q_out[1]], [*done, near_own])
+            near_across.append(lax.ppermute(across[1], grid_axes, onward))
+            q_across.append(cross(q_out[1]))
+            done = [across[1]]
+
+        def sources_of(k, names):
+            lo = bounds[k][0]
+            arrays = {
+                "O": (kv_own, lo),
+                "X": (across[k], 0),
+                "NO": (near_own, lo),
+                "NR": (near_across[k], 0),
+                "FO": (far_own, 0),
+                "FR": (far_across, 0),
+            }
+            return [arrays[name] for name in names]
+
+        def cut(k):
+            return slice(0, 5) if k == 0 else slice(1, 4)
+
+        own, kept, moved = [], [], []
+
+        def attend_own(k, after):
+            lo, hi = bounds[k]
+            own.append(
+                attend_slots(
+                    plan, at, x3, sources_of(k, OWN_SOURCES[cut(k)]), at.mine + lo, lo, hi - lo,
+                    at.own_match + cut(k).start, DISTANCES[cut(k)], after,
+                )
+            )
+            return [own[-1]]
+
+        def attend_across(k, after):
+            lo, hi = bounds[k]
+            keep, send = attend_slots(
+                plan, at, q_across[k], sources_of(k, ACROSS_SOURCES[cut(k)]), 0, lo, hi - lo,
+                at.across_match + cut(k).start, DISTANCES[cut(k)], after,
+            )
+            got = mate(send)
+            first = plan[at.branch] == 0
+            mixed = blend(jnp.where(first, keep, got), jnp.where(first, got, keep), strength[0])
+            kept.append(cross(mixed))
+            moved.append(mate(kept[-1]))
+            return [keep]
+
+        done = attend_own(0, done)
+        done = attend_across(0, done)
+        if two:
+            done = attend_across(1, done)
+            done = attend_own(1, done)
+        peer = [mate(a) for a in own]
+        if local:
+            own, peer = own + [own_local], peer + [peer_local]
+        else:
+            own, peer = own + own[:1], peer + peer[:1]
+        arrays = [*own, *peer, *kept, *moved]
+        return pl.pallas_call(
+            functools.partial(assemble_kernel, at, [hi - lo for lo, hi in bounds], local),
+            out_shape=jax.ShapeDtypeStruct((outs, rows, HD), BF16),
+            in_specs=[whole(pltpu.SMEM)] * 2 + [whole()] * len(arrays),
+            out_specs=whole(),
+            compiler_params=params(),
+            name="assemble",
+        )(plan, strength, *arrays)
+
+    out = lax.switch(
+        plan[at.rung], [functools.partial(attempt, rung) for rung in rungs], plan, x3, strength
+    )
+    out = out.reshape(seq_count, per_half, rows, HD)
+    return jnp.transpose(out, (2, 1, 0, 3)).reshape(rows, per_half, seq_count * HD)
+
+
+def rungs_of(heads):
+    third = heads // 3
+    return ((2 * third + 2, third), (2 * third + 2, 2 * third + 2), (heads, heads))
+
 
 def solution(mesh):
+    sizes = dict(mesh.shape)
+
+    def whole_body(qkv, timestep, windows, segments):
+        frames_here = segments.shape[0] // sizes["frame"]
+        one_frame = frames_here == sizes["seq"]
+        if sizes["seq"] == 2 and sizes["cfg"] == 2 and one_frame and qkv.shape[1] % 32 == 0:
+            return ranked_body(rungs_of(windows.shape[0]), qkv, timestep, windows, segments)
+        return body(qkv, timestep, windows, segments)
+
     return jax.shard_map(
-        body,
+        whole_body,
         mesh=mesh,
         in_specs=(P("cfg", ("groups", "frame", "seq"), None, None), P("groups"), P(), P("groups")),
         out_specs=P(("groups", "frame", "seq"), "cfg", None),

time: 346 us -> 86.8 us (0.25)
  blocking collectives: 113 us -> 0 us
  local copies, waits for them, and re-layouts: 68 us -> 3.91 us
  waiting for transfers between devices: 83.3 us -> 28.8 us
  matrix products: 43.7 us -> 0 us
  other arithmetic: 26.8 us -> 0.85 us
  Pallas kernels: 0 us -> 24.7 us
  starting transfers between devices: 8.19 us -> 25.6 us
    all_to_all x2 -> x0, blocking collectives: 113 us -> none  [the longest x1 97.8 us: body(): lax.all_to_all(qkv, ('seq', 'cfg'), split_axis=3, concat_axis=0, tiled=True)]
    ppermute x2 -> x18, waiting for transfers between devices: 83.3 us -> 28.8 us  [the longest x6 19.5 us: cross(): return lax.ppermute(a, 'seq', SWAP)]
    dot_general x4 -> x0, matrix products: 43.7 us -> none  [the longest x2 26.5 us: attend(): jnp.einsum('bhstur,ubrhd->sbthd', weights, value_rows, preferred_element_...]
    slice x5 -> x2, local copies, waits for them, and re-layouts: 32.8 us -> 1.19 us  [the longest x1 0.61 us: attend_across(): first = plan[at.branch] == 0]
    unnamed x9 -> x0, local copies, waits for them, and re-layouts: 29 us -> none
    pallas_call x0 -> x12, Pallas kernels: none -> 24.7 us  [the longest x5 16.5 us: attend_slots(): pl.pallas_call(functools.partial(attend_kernel, spec), out_shape=out_shap...]
    reduce_sum x1 -> x0, other arithmetic: 18.6 us -> none  [attend(): totals = jnp.sum(expd, axis=(4, 5))]
    ppermute x2 -> x18, starting transfers between devices: 8.19 us -> 25.6 us  [the longest x6 7.49 us: cross(): return lax.ppermute(a, 'seq', SWAP)]
  transfers between devices with their start and end apart: 2 -> 18, of which waited for: 2 -> 7; matrix products, arithmetic and copies ran while one was open for 1% -> 1% of each run, Pallas kernels for 0% -> 20%
where the time goes in v2:
time: 86.8 us; the launch traced here: 86.5 us
  waiting for transfers between devices  28.8 us (33%)
  starting transfers between devices  25.6 us (29%)
  Pallas kernels  24.7 us (28%)
  local copies, waits for them, and re-layouts  3.91 us (5%)
  loops' own time  1.37 us (2%)
  between operations  1.32 us (2%)
    ppermute x6, waiting for transfers between devices, cross(): return lax.ppermute(a, 'seq', SWAP)  19.5 us
    pallas_call x5, Pallas kernels, attend_slots(): pl.pallas_call(functools.partial(attend_kernel, spec), out_shape=out_shap...  16.5 us
    ppermute x1, waiting for transfers between devices, attempt(): far_own = lax.ppermute(kv_far, grid_axes, onward)  7.85 us
    ppermute x6, starting transfers between devices, cross(): return lax.ppermute(a, 'seq', SWAP)  7.49 us
    ppermute x1, starting transfers between devices, attempt(): far_own = lax.ppermute(kv_far, grid_axes, onward)  5.6 us
    ppermute x1, starting transfers between devices, attempt(): near_across.append(lax.ppermute(across[1], grid_axes, onward))  4.78 us
    pallas_call x3, Pallas kernels, pack(): pl.pallas_call(functools.partial(pack_kernel, jobs, len(after)), out_shap...  4.69 us
    ppermute x1, starting transfers between devices, attempt(): near_across = [lax.ppermute(across[0], grid_axes, onward)]  3.93 us
  transfers between devices with their start and end apart: 18, of which 7 were waited for; matrix products, arithmetic and copies ran while one was open for 1% of the time, Pallas kernels for 20%

profile of v2, /device:TPU:0, one launch (start us, length us, event | category | flops | bytes accessed | tf_op | source)
XLA Modules:
  0.0 86.5 jit_solution(1817836962392454291)
XLA Ops:
  0.7 1.8 %plan.1 = s32[173]{0:T(256)S(1)} custom-call(s32[3]{0:T(128)} %pad_add_fusion.place_ref, s32[32]{0:T(128)} %windows_ref.1, s32[8]{0:T(128)} %segments_ref.1), custom_call_target="tpu_custom_call" | custom-call | tf_op jit(solution)/shard_map/plan/pallas_call | solution.py:440
  4.3 80.5 %conditional.1 = (bf16[16,256,128]{2,1,0:T(8,128)(2,1)S(1)}) conditional(s32[]{:T(128)} %bitcast.9, (s32[173]{0:T(256)S(1)}, bf16[3,256,4096]{2,1,0:T(8,128)(2,1)}, f32[1]{0:T(128)}) %tuple.18, (s32[173]{0:T(256)S(1)}, bf16[3,256,4096]{2,1,0:T(8,128)(2,1)}, f32[1]{0:T(128)}) %tuple.19, (s32[173]{0:T(256)S(1)}, ...), branch_computations={%region_0.1_spmd, %region_1.2_spmd, %region_2.3_spmd} | conditional | flops 10739515392 | bytes 125305288 | solution.py:561
  4.4 2.0 %pack_heads.9.refs_0_ = bf16[5,2,256,128]{3,2,1,0:T(8,128)(2,1)S(1)} custom-call(s32[173]{0:T(256)S(1)} %get-tuple-element.26.plan_ref, bf16[3,256,4096]{2,1,0:T(8,128)(2,1)} %get-tuple-element.29.x_ref.q_ref), custom_call_target="tpu_custom_call" | custom-call | bytes 1310720 | tf_op jit(solution)/shard_map/cond/branch_0_fun/pack_heads/pallas_call | solution.py:205
  7.5 1.5 %pack_heads.10 = (bf16[11,2,256,128]{3,2,1,0:T(8,128)(2,1)S(1)}, bf16[5,2,256,128]{3,2,1,0:T(8,128)(2,1)S(1)}) custom-call(s32[173]{0:T(256)S(1)} %get-tuple-element.26.plan_ref, bf16[3,256,4096]{2,1,0:T(8,128)(2,1)S(1)} %copy-done, bf16[5,2,256,128]{3,2,1,0:T(8,128)(2,1)S(1)} %pack_heads.9.refs_0_), custom_call_target="tpu_custom_call" | custom-call | bytes 4194304 | tf_op jit(solution)/shard_map/cond/branch_0_fun/pack_heads/pallas_call | solution.py:205
  8.9 1.3 %collective-permute-start.3 = (bf16[11,2,256,128]{3,2,1,0:T(8,128)(2,1)S(1)}, bf16[11,2,256,128]{3,2,1,0:T(8,128)(2,1)S(1)}, u32[]{:S(2)}, u32[]{:S(2)}) collective-permute-start(bf16[11,2,256,128]{3,2,1,0:T(8,128)(2,1)S(1)} %get-tuple-element.31.refs_0_.refs_2_.refs_1_), channel_id=1, source_target_pairs={{2,0},{4,2},{6,4},{8,10},{10,12},{12,14},{3,1},{5,3},{7,5},{9,11},... | collective-permute-start | bytes 4325384 | tf_op jit(solution)/shard_map/cond/branch_0_fun/ppermute | solution.py:475
  10.2 5.6 %collective-permute-start = (bf16[5,2,256,128]{3,2,1,0:T(8,128)(2,1)S(1)}, bf16[5,2,256,128]{3,2,1,0:T(8,128)(2,1)S(1)}, u32[]{:S(2)}, u32[]{:S(2)}) collective-permute-start(bf16[5,2,256,128]{3,2,1,0:T(8,128)(2,1)S(1)} %get-tuple-element.30), channel_id=1, source_target_pairs={{0,2},{2,4},{4,6},{10,8},{12,10},{14,12},{1,3},{3,5},{5,7},{11,9},... | collective-permute-start | bytes 1966088 | tf_op jit(solution)/shard_map/cond/branch_0_fun/ppermute | solution.py:476
  16.8 1.2 %pack_heads.11 = (bf16[5,1,256,128]{3,2,1,0:T(8,128)(2,1)S(1)}, bf16[6,1,256,128]{3,2,1,0:T(8,128)(2,1)S(1)}, bf16[6,2,256,128]{3,2,1,0:T(8,128)(2,1)S(1)}) custom-call(s32[173]{0:T(256)S(1)} %get-tuple-element.26.plan_ref, bf16[3,256,4096]{2,1,0:T(8,128)(2,1)S(1)} %copy-done, bf16[11,2,256,128]{3,2,1,0:T(8,128)(2,1)S(1)} %get-tuple-element.31.refs_0_.refs_2_.refs_1_), custom_call_target="tpu_custom_call" | custom-call | bytes 3014656 | tf_op jit(solution)/shard_map/cond/branch_0_fun/pack_heads/pallas_call | solution.py:205
  19.2 2.7 %attend.10.refs_2_ = bf16[10,256,128]{2,1,0:T(8,128)(2,1)S(1)} custom-call(s32[173]{0:T(256)S(1)} %get-tuple-element.26.plan_ref, bf16[3,256,4096]{2,1,0:T(8,128)(2,1)S(1)} %copy-done, bf16[5,1,256,128]{3,2,1,0:T(8,128)(2,1)S(1)} %get-tuple-element.32.refs_0_.refs_1_), custom_call_target="tpu_custom_call" | custom-call | flops 671088640 | bytes 2621440 | tf_op jit(solution)/shard_map/cond/branch_0_fun/attend/pallas_call | solution.py:350
  21.9 7.9 %collective-permute-done.refs_3_.refs_0_ = bf16[5,2,256,128]{3,2,1,0:T(8,128)(2,1)S(1)} collective-permute-done((bf16[5,2,256,128]{3,2,1,0:T(8,128)(2,1)S(1)}, bf16[5,2,256,128]{3,2,1,0:T(8,128)(2,1)S(1)}, u32[]{:S(2)}, u32[]{:S(2)}) %collective-permute-start) | collective-permute-done | bytes 655392 | tf_op jit(solution)/shard_map/cond/branch_0_fun/ppermute | solution.py:476
  29.8 3.8 %collective-permute-done.1.refs_0_ = bf16[5,2,256,128]{3,2,1,0:T(8,128)(2,1)S(1)} collective-permute-done((bf16[5,2,256,128]{3,2,1,0:T(8,128)(2,1)S(1)}, bf16[5,2,256,128]{3,2,1,0:T(8,128)(2,1)S(1)}, u32[]{:S(2)}, u32[]{:S(2)}) %collective-permute-start.1) | collective-permute-done | bytes 655392 | tf_op jit(solution)/shard_map/cond/branch_0_fun/ppermute | solution.py:465
  33.6 3.9 %collective-permute-start.2 = (bf16[5,2,256,128]{3,2,1,0:T(8,128)(2,1)S(1)}, bf16[5,2,256,128]{3,2,1,0:T(8,128)(2,1)S(1)}, u32[]{:S(2)}, u32[]{:S(2)}) collective-permute-start(bf16[5,2,256,128]{3,2,1,0:T(8,128)(2,1)S(1)} %get-tuple-element.33.refs_2_.refs_3_), channel_id=1, source_target_pairs={{0,2},{2,4},{4,6},{10,8},{12,10},{14,12},{1,3},{3,5},{5,7},{11,9},... | collective-permute-start | bytes 1966088 | tf_op jit(solution)/shard_map/cond/branch_0_fun/ppermute | solution.py:491
  37.5 1.3 %collective-permute-start.8 = (bf16[5,2,256,128]{3,2,1,0:T(8,128)(2,1)S(1)}, bf16[5,2,256,128]{3,2,1,0:T(8,128)(2,1)S(1)}, u32[]{:S(2)}, u32[]{:S(2)}) collective-permute-start(bf16[5,2,256,128]{3,2,1,0:T(8,128)(2,1)S(1)} %get-tuple-element.33.refs_2_.refs_3_), channel_id=1, source_target_pairs={{2,0},{4,2},{6,4},{8,10},{10,12},{12,14},{3,1},{5,3},{7,5},{9,11},... | collective-permute-start | bytes 1966088 | tf_op jit(solution)/shard_map/cond/branch_0_fun/ppermute | solution.py:492
  38.8 2.3 %collective-permute-start.7 = (bf16[5,1,256,128]{3,2,1,0:T(8,128)(2,1)S(1)}, bf16[5,1,256,128]{3,2,1,0:T(8,128)(2,1)S(1)}, u32[]{:S(2)}, u32[]{:S(2)}) collective-permute-start(bf16[5,1,256,128]{3,2,1,0:T(8,128)(2,1)S(1)} %get-tuple-element.38), channel_id=1, source_target_pairs={{0,8},{8,0},{1,9},{9,1},{2,10},{10,2},{3,11},{11,3},{4,12},{12,4},... | collective-permute-start | bytes 983048 | tf_op jit(solution)/shard_map/cond/branch_0_fun/ppermute | solution.py:465
  41.1 9.3 %collective-permute-done.4.refs_0_ = bf16[6,2,256,128]{3,2,1,0:T(8,128)(2,1)S(1)} collective-permute-done((bf16[6,2,256,128]{3,2,1,0:T(8,128)(2,1)S(1)}, bf16[6,2,256,128]{3,2,1,0:T(8,128)(2,1)S(1)}, u32[]{:S(2)}, u32[]{:S(2)}) %collective-permute-start.4) | collective-permute-done | bytes 786464 | tf_op jit(solution)/shard_map/cond/branch_0_fun/ppermute | solution.py:465
  51.3 4.8 %collective-permute-start.5 = (bf16[6,2,256,128]{3,2,1,0:T(8,128)(2,1)S(1)}, bf16[6,2,256,128]{3,2,1,0:T(8,128)(2,1)S(1)}, u32[]{:S(2)}, u32[]{:S(2)}) collective-permute-start(bf16[6,2,256,128]{3,2,1,0:T(8,128)(2,1)S(1)} %get-tuple-element.36.refs_5_.refs_1_.refs_2_), channel_id=1, source_target_pairs={{0,2},{2,4},{4,6},{10,8},{12,10},{14,12},{1,3},{3,5},{5,7},{11,9},... | collective-permute-start | bytes 2359304 | tf_op jit(solution)/shard_map/cond/branch_0_fun/ppermute | solution.py:497
  56.1 3.7 %attend.11.refs_5_.refs_0_ = bf16[5,256,128]{2,1,0:T(8,128)(2,1)S(1)} custom-call(s32[173]{0:T(256)S(1)} %get-tuple-element.26.plan_ref, bf16[3,256,4096]{2,1,0:T(8,128)(2,1)S(1)} %copy-done, bf16[5,2,256,128]{3,2,1,0:T(8,128)(2,1)S(1)} %collective-permute-done.refs_3_.refs_0_, bf16[5,2,256,128]{3,2,1,0:T(8,128)(2,1)S(1)} %collective-permute-done.2.refs_1_.refs_0_, ...), custom_call_target="tpu_custom_call" | custom-call | flops 1677721600 | bytes 3932160 | tf_op jit(solution)/shard_map/cond/branch_0_fun/attend/pallas_call | solution.py:350
  59.9 3.6 %attend.12 = (bf16[5,128,128]{2,1,0:T(8,128)(2,1)S(1)}, bf16[5,128,128]{2,1,0:T(8,128)(2,1)S(1)}) custom-call(s32[173]{0:T(256)S(1)} %get-tuple-element.26.plan_ref, bf16[5,1,256,128]{3,2,1,0:T(8,128)(2,1)S(1)} %collective-permute-done.7.q_ref, bf16[5,2,256,128]{3,2,1,0:T(8,128)(2,1)S(1)} %collective-permute-done.2.refs_1_.refs_0_, ...), custom_call_target="tpu_custom_call" | custom-call | flops 1677721600 | bytes 3932160 | tf_op jit(solution)/shard_map/cond/branch_0_fun/attend/pallas_call | solution.py:350
  64.4 3.1 %attend.13 = (bf16[6,128,128]{2,1,0:T(8,128)(2,1)S(1)}, bf16[6,128,128]{2,1,0:T(8,128)(2,1)S(1)}) custom-call(s32[173]{0:T(256)S(1)} %get-tuple-element.26.plan_ref, bf16[6,1,256,128]{3,2,1,0:T(8,128)(2,1)S(1)} %collective-permute-done.6.q_ref, bf16[11,2,256,128]{3,2,1,0:T(8,128)(2,1)S(1)} %get-tuple-element.31.refs_0_.refs_2_.refs_1_, ...), custom_call_target="tpu_custom_call" | custom-call | flops 1207959552 | bytes 3145728 | tf_op jit(solution)/shard_map/cond/branch_0_fun/attend/pallas_call | solution.py:350
  71.0 3.3 %attend.14.refs_1_ = bf16[6,256,128]{2,1,0:T(8,128)(2,1)S(1)} custom-call(s32[173]{0:T(256)S(1)} %get-tuple-element.26.plan_ref, bf16[3,256,4096]{2,1,0:T(8,128)(2,1)S(1)} %copy-done, bf16[6,2,256,128]{3,2,1,0:T(8,128)(2,1)S(1)} %collective-permute-done.5.refs_0_, bf16[11,2,256,128]{3,2,1,0:T(8,128)(2,1)S(1)} %get-tuple-element.31.refs_0_.refs_2_.refs_1_, ...), custom_call_target="tpu_custom_call" | custom-call | flops 1207959552 | bytes 3145728 | tf_op jit(solution)/shard_map/cond/branch_0_fun/attend/pallas_call | solution.py:350
  75.7 1.3 %collective-permute-done.15.refs_7_ = bf16[6,128,128]{2,1,0:T(8,128)(2,1)S(1)} collective-permute-done((bf16[6,128,128]{2,1,0:T(8,128)(2,1)S(1)}, bf16[6,128,128]{2,1,0:T(8,128)(2,1)S(1)}, u32[]{:S(2)}, u32[]{:S(2)}) %collective-permute-start.15) | collective-permute-done | bytes 196640 | tf_op jit(solution)/shard_map/cond/branch_0_fun/ppermute | solution.py:465
  77.0 4.2 %collective-permute-done.13.refs_6_ = bf16[5,128,128]{2,1,0:T(8,128)(2,1)S(1)} collective-permute-done((bf16[5,128,128]{2,1,0:T(8,128)(2,1)S(1)}, bf16[5,128,128]{2,1,0:T(8,128)(2,1)S(1)}, u32[]{:S(2)}, u32[]{:S(2)}) %collective-permute-start.13) | collective-permute-done | bytes 163872 | tf_op jit(solution)/shard_map/cond/branch_0_fun/ppermute | solution.py:465
  81.2 1.4 %collective-permute-done.16.refs_8_ = bf16[5,128,128]{2,1,0:T(8,128)(2,1)S(1)} collective-permute-done((bf16[5,128,128]{2,1,0:T(8,128)(2,1)S(1)}, bf16[5,128,128]{2,1,0:T(8,128)(2,1)S(1)}, u32[]{:S(2)}, u32[]{:S(2)}) %collective-permute-start.16) | collective-permute-done | bytes 163872 | tf_op jit(solution)/shard_map/cond/branch_0_fun/ppermute | solution.py:468
  82.6 1.7 %assemble.3 = bf16[16,256,128]{2,1,0:T(8,128)(2,1)S(1)} custom-call(s32[173]{0:T(256)S(1)} %get-tuple-element.26.plan_ref, f32[1]{0:T(128)} %get-tuple-element.28.strength_ref, bf16[5,256,128]{2,1,0:T(8,128)(2,1)S(1)} %attend.11.refs_5_.refs_0_, bf16[6,256,128]{2,1,0:T(8,128)(2,1)S(1)} %attend.14.refs_1_, bf16[10,256,128]{2,1,0:T(8,128)(2,1)S(1)} %attend.10.refs_2_, ...), custom_call_target="tpu_custom_call" | custom-call | tf_op jit(solution)/shard_map/cond/branch_0_fun/assemble/pallas_call | solution.py:552
  84.9 1.6 %copy.15 = bf16[2,8,256,128]{3,1,0,2:T(8,128)(2,1)} copy(bf16[2,8,256,128]{3,2,1,0:T(8,128)(2,1)S(1)} %bitcast.22) | data formatting | bytes 2097152 | tf_op jit(solution)/shard_map/reshape | solution.py:564
  (33 shorter events, 10.5 us)
Async XLA Ops:
  4.4 3.1 %copy-start = (bf16[3,256,4096]{2,1,0:T(8,128)(2,1)S(1)}, bf16[3,256,4096]{2,1,0:T(8,128)(2,1)}, u32[]{:S(2)}) copy-start(bf16[3,256,4096]{2,1,0:T(8,128)(2,1)} %get-tuple-element.29.x_ref.q_ref) | copy-start | bytes 18874372 | tf_op jit(solution)/shard_map/cond
  8.9 41.5 %collective-permute-start.3 = (bf16[11,2,256,128]{3,2,1,0:T(8,128)(2,1)S(1)}, bf16[11,2,256,128]{3,2,1,0:T(8,128)(2,1)S(1)}, u32[]{:S(2)}, u32[]{:S(2)}) collective-permute-start(bf16[11,2,256,128]{3,2,1,0:T(8,128)(2,1)S(1)} %get-tuple-element.31.refs_0_.refs_2_.refs_1_), channel_id=1, source_target_pairs={{2,0},{4,2},{6,4},{8,10},{10,12},{12,14},{3,1},{5,3},{7,5},{9,11},... | collective-permute-start | bytes 4325384 | tf_op jit(solution)/shard_map/cond/branch_0_fun/ppermute | solution.py:475
  10.2 19.5 %collective-permute-start = (bf16[5,2,256,128]{3,2,1,0:T(8,128)(2,1)S(1)}, bf16[5,2,256,128]{3,2,1,0:T(8,128)(2,1)S(1)}, u32[]{:S(2)}, u32[]{:S(2)}) collective-permute-start(bf16[5,2,256,128]{3,2,1,0:T(8,128)(2,1)S(1)} %get-tuple-element.30), channel_id=1, source_target_pairs={{0,2},{2,4},{4,6},{10,8},{12,10},{14,12},{1,3},{3,5},{5,7},{11,9},... | collective-permute-start | bytes 1966088 | tf_op jit(solution)/shard_map/cond/branch_0_fun/ppermute | solution.py:476
  15.8 17.7 %collective-permute-start.1 = (bf16[5,2,256,128]{3,2,1,0:T(8,128)(2,1)S(1)}, bf16[5,2,256,128]{3,2,1,0:T(8,128)(2,1)S(1)}, u32[]{:S(2)}, u32[]{:S(2)}) collective-permute-start(bf16[5,2,256,128]{3,2,1,0:T(8,128)(2,1)S(1)} %pack_heads.9.refs_0_), channel_id=1, source_target_pairs={{0,8},{8,0},{1,9},{9,1},{2,10},{10,2},{3,11},{11,3},{4,12},{12,4},... | collective-permute-start | bytes 1966088 | tf_op jit(solution)/shard_map/cond/branch_0_fun/ppermute | solution.py:465
  18.0 32.4 %collective-permute-start.4 = (bf16[6,2,256,128]{3,2,1,0:T(8,128)(2,1)S(1)}, bf16[6,2,256,128]{3,2,1,0:T(8,128)(2,1)S(1)}, u32[]{:S(2)}, u32[]{:S(2)}) collective-permute-start(bf16[6,2,256,128]{3,2,1,0:T(8,128)(2,1)S(1)} %get-tuple-element.34), channel_id=1, source_target_pairs={{0,8},{8,0},{1,9},{9,1},{2,10},{10,2},{3,11},{11,3},{4,12},{12,4},... | collective-permute-start | bytes 2359304 | tf_op jit(solution)/shard_map/cond/branch_0_fun/ppermute | solution.py:465
  33.6 22.6 %collective-permute-start.2 = (bf16[5,2,256,128]{3,2,1,0:T(8,128)(2,1)S(1)}, bf16[5,2,256,128]{3,2,1,0:T(8,128)(2,1)S(1)}, u32[]{:S(2)}, u32[]{:S(2)}) collective-permute-start(bf16[5,2,256,128]{3,2,1,0:T(8,128)(2,1)S(1)} %get-tuple-element.33.refs_2_.refs_3_), channel_id=1, source_target_pairs={{0,2},{2,4},{4,6},{10,8},{12,10},{14,12},{1,3},{3,5},{5,7},{11,9},... | collective-permute-start | bytes 1966088 | tf_op jit(solution)/shard_map/cond/branch_0_fun/ppermute | solution.py:491
  37.5 22.4 %collective-permute-start.8 = (bf16[5,2,256,128]{3,2,1,0:T(8,128)(2,1)S(1)}, bf16[5,2,256,128]{3,2,1,0:T(8,128)(2,1)S(1)}, u32[]{:S(2)}, u32[]{:S(2)}) collective-permute-start(bf16[5,2,256,128]{3,2,1,0:T(8,128)(2,1)S(1)} %get-tuple-element.33.refs_2_.refs_3_), channel_id=1, source_target_pairs={{2,0},{4,2},{6,4},{8,10},{10,12},{12,14},{3,1},{5,3},{7,5},{9,11},... | collective-permute-start | bytes 1966088 | tf_op jit(solution)/shard_map/cond/branch_0_fun/ppermute | solution.py:492
  38.8 21.1 %collective-permute-start.7 = (bf16[5,1,256,128]{3,2,1,0:T(8,128)(2,1)S(1)}, bf16[5,1,256,128]{3,2,1,0:T(8,128)(2,1)S(1)}, u32[]{:S(2)}, u32[]{:S(2)}) collective-permute-start(bf16[5,1,256,128]{3,2,1,0:T(8,128)(2,1)S(1)} %get-tuple-element.38), channel_id=1, source_target_pairs={{0,8},{8,0},{1,9},{9,1},{2,10},{10,2},{3,11},{11,3},{4,12},{12,4},... | collective-permute-start | bytes 983048 | tf_op jit(solution)/shard_map/cond/branch_0_fun/ppermute | solution.py:465
  50.4 14.0 %collective-permute-start.6 = (bf16[6,1,256,128]{3,2,1,0:T(8,128)(2,1)S(1)}, bf16[6,1,256,128]{3,2,1,0:T(8,128)(2,1)S(1)}, u32[]{:S(2)}, u32[]{:S(2)}) collective-permute-start(bf16[6,1,256,128]{3,2,1,0:T(8,128)(2,1)S(1)} %get-tuple-element.37), channel_id=1, source_target_pairs={{0,8},{8,0},{1,9},{9,1},{2,10},{10,2},{3,11},{11,3},{4,12},{12,4},... | collective-permute-start | bytes 1179656 | tf_op jit(solution)/shard_map/cond/branch_0_fun/ppermute | solution.py:465
  51.3 19.7 %collective-permute-start.5 = (bf16[6,2,256,128]{3,2,1,0:T(8,128)(2,1)S(1)}, bf16[6,2,256,128]{3,2,1,0:T(8,128)(2,1)S(1)}, u32[]{:S(2)}, u32[]{:S(2)}) collective-permute-start(bf16[6,2,256,128]{3,2,1,0:T(8,128)(2,1)S(1)} %get-tuple-element.36.refs_5_.refs_1_.refs_2_), channel_id=1, source_target_pairs={{0,2},{2,4},{4,6},{10,8},{12,10},{14,12},{1,3},{3,5},{5,7},{11,9},... | collective-permute-start | bytes 2359304 | tf_op jit(solution)/shard_map/cond/branch_0_fun/ppermute | solution.py:497
  67.5 2.4 %collective-permute-start.14 = (bf16[6,128,128]{2,1,0:T(8,128)(2,1)S(1)}, bf16[6,128,128]{2,1,0:T(8,128)(2,1)S(1)}, u32[]{:S(2)}, u32[]{:S(2)}) collective-permute-start(bf16[6,128,128]{2,1,0:T(8,128)(2,1)S(1)} %get-tuple-element.42), channel_id=1, source_target_pairs={{0,1},{1,0},{2,3},{3,2},{4,5},{5,4},{6,7},{7,6},{8,9},{9,8},{10,11... | collective-permute-start | bytes 589832 | tf_op jit(solution)/shard_map/cond/branch_0_fun/ppermute | solution.py:468
  67.6 13.6 %collective-permute-start.11 = (bf16[10,256,128]{2,1,0:T(8,128)(2,1)S(1)}, bf16[10,256,128]{2,1,0:T(8,128)(2,1)S(1)}, u32[]{:S(2)}, u32[]{:S(2)}) collective-permute-start(bf16[10,256,128]{2,1,0:T(8,128)(2,1)S(1)} %attend.10.refs_2_), channel_id=1, source_target_pairs={{0,1},{1,0},{2,3},{3,2},{4,5},{5,4},{6,7},{7,6},{8,9},{9,8},{10,11... | collective-permute-start | bytes 1966088 | tf_op jit(solution)/shard_map/cond/branch_0_fun/ppermute | solution.py:468
  69.3 11.9 %collective-permute-start.9 = (bf16[5,256,128]{2,1,0:T(8,128)(2,1)S(1)}, bf16[5,256,128]{2,1,0:T(8,128)(2,1)S(1)}, u32[]{:S(2)}, u32[]{:S(2)}) collective-permute-start(bf16[5,256,128]{2,1,0:T(8,128)(2,1)S(1)} %attend.11.refs_5_.refs_0_), channel_id=1, source_target_pairs={{0,1},{1,0},{2,3},{3,2},{4,5},{5,4},{6,7},{7,6},{8,9},{9,8},{10,11... | collective-permute-start | bytes 983048 | tf_op jit(solution)/shard_map/cond/branch_0_fun/ppermute | solution.py:468
  69.5 5.0 %collective-permute-start.12 = (bf16[5,128,128]{2,1,0:T(8,128)(2,1)S(1)}, bf16[5,128,128]{2,1,0:T(8,128)(2,1)S(1)}, u32[]{:S(2)}, u32[]{:S(2)}) collective-permute-start(bf16[5,128,128]{2,1,0:T(8,128)(2,1)S(1)} %get-tuple-element.41), channel_id=1, source_target_pairs={{0,1},{1,0},{2,3},{3,2},{4,5},{5,4},{6,7},{7,6},{8,9},{9,8},{10,11... | collective-permute-start | bytes 491528 | tf_op jit(solution)/shard_map/cond/branch_0_fun/ppermute | solution.py:468
  70.0 7.0 %collective-permute-start.15 = (bf16[6,128,128]{2,1,0:T(8,128)(2,1)S(1)}, bf16[6,128,128]{2,1,0:T(8,128)(2,1)S(1)}, u32[]{:S(2)}, u32[]{:S(2)}) collective-permute-start(bf16[6,128,128]{2,1,0:T(8,128)(2,1)S(1)} %fusion.1), channel_id=1, source_target_pairs={{0,8},{8,0},{1,9},{9,1},{2,10},{10,2},{3,11},{11,3},{4,12},{12,4},... | collective-permute-start | bytes 589832 | tf_op jit(solution)/shard_map/cond/branch_0_fun/ppermute | solution.py:465
  74.4 8.2 %collective-permute-start.10 = (bf16[6,256,128]{2,1,0:T(8,128)(2,1)S(1)}, bf16[6,256,128]{2,1,0:T(8,128)(2,1)S(1)}, u32[]{:S(2)}, u32[]{:S(2)}) collective-permute-start(bf16[6,256,128]{2,1,0:T(8,128)(2,1)S(1)} %attend.14.refs_1_), channel_id=1, source_target_pairs={{0,1},{1,0},{2,3},{3,2},{4,5},{5,4},{6,7},{7,6},{8,9},{9,8},{10,11... | collective-permute-start | bytes 1179656 | tf_op jit(solution)/shard_map/cond/branch_0_fun/ppermute | solution.py:468
  74.5 6.7 %collective-permute-start.13 = (bf16[5,128,128]{2,1,0:T(8,128)(2,1)S(1)}, bf16[5,128,128]{2,1,0:T(8,128)(2,1)S(1)}, u32[]{:S(2)}, u32[]{:S(2)}) collective-permute-start(bf16[5,128,128]{2,1,0:T(8,128)(2,1)S(1)} %fusion.3), channel_id=1, source_target_pairs={{0,8},{8,0},{1,9},{9,1},{2,10},{10,2},{3,11},{11,3},{4,12},{12,4},... | collective-permute-start | bytes 491528 | tf_op jit(solution)/shard_map/cond/branch_0_fun/ppermute | solution.py:465
  77.0 5.6 %collective-permute-start.17 = (bf16[6,128,128]{2,1,0:T(8,128)(2,1)S(1)}, bf16[6,128,128]{2,1,0:T(8,128)(2,1)S(1)}, u32[]{:S(2)}, u32[]{:S(2)}) collective-permute-start(bf16[6,128,128]{2,1,0:T(8,128)(2,1)S(1)} %collective-permute-done.15.refs_7_), channel_id=1, source_target_pairs={{0,1},{1,0},{2,3},{3,2},{4,5},{5,4},{6,7},{7,6},{8,9},{9,8},{10,11... | collective-permute-start | bytes 589832 | tf_op jit(solution)/shard_map/cond/branch_0_fun/ppermute | solution.py:468
  81.2 1.4 %collective-permute-start.16 = (bf16[5,128,128]{2,1,0:T(8,128)(2,1)S(1)}, bf16[5,128,128]{2,1,0:T(8,128)(2,1)S(1)}, u32[]{:S(2)}, u32[]{:S(2)}) collective-permute-start(bf16[5,128,128]{2,1,0:T(8,128)(2,1)S(1)} %collective-permute-done.13.refs_6_), channel_id=1, source_target_pairs={{0,1},{1,0},{2,3},{3,2},{4,5},{5,4},{6,7},{7,6},{8,9},{9,8},{10,11... | collective-permute-start | bytes 491528 | tf_op jit(solution)/shard_map/cond/branch_0_fun/ppermute | solution.py:468

commit v3 on v2

--- a/solution.py
+++ b/solution.py
@@ -97,7 +97,9 @@
 BF16 = jnp.bfloat16
 F32 = jnp.float32
 VMEM_BYTES = 32 * 1024 * 1024
+PLAN_VMEM_BYTES = 60 * 1024 * 1024
 SWAP = ((0, 1), (1, 0))
+COSTS = {"pack": 1e10, "attend": 1e9, "mix": 1e8, "gate": 1e9}
 STEPS = {"O": 0, "X": 1, "NO": 2, "NR": -1, "FO": -2, "FR": 3}
 OWN_SOURCES = ("FO", "NR", "O", "X", "NO")
 ACROSS_SOURCES = ("NR", "O", "X", "NO", "FR")
@@ -108,8 +110,12 @@
     return pl.BlockSpec(memory_space=space)
 
 
-def params():
-    return pltpu.CompilerParams(vmem_limit_bytes=VMEM_BYTES)
+def cost(kind):
+    return pl.CostEstimate(flops=int(COSTS[kind]), bytes_accessed=1, transcendentals=0)
+
+
+def params(limit=VMEM_BYTES):
+    return pltpu.CompilerParams(vmem_limit_bytes=limit)
 
 
 class Layout:
@@ -125,14 +131,24 @@
         self.across_match = self.own_match + len(DISTANCES)
         self.branch = self.across_match + len(DISTANCES)
         self.column = self.branch + 1
-        self.rung = self.column + 1
-        self.size = self.rung + 1
-
-
-def plan_kernel(at, rungs, split, place_ref, windows_ref, segments_ref, plan_ref):
+        self.step = self.column + 1
+        self.size = self.step + 1
+
+
+def plan_kernel(
+    at, rungs, split, windows_in, segments_in, step_in, x_ref, plan_ref, rung_ref, kv_ref, own_ref,
+    windows_ref, segments_ref, step_ref, in_sems, sems,
+):
+    get_windows = pltpu.make_async_copy(windows_in, windows_ref, in_sems.at[0])
+    get_segments = pltpu.make_async_copy(segments_in, segments_ref, in_sems.at[1])
+    get_windows.start()
+    get_segments.start()
+    get_step = pltpu.make_async_copy(step_in, step_ref, in_sems.at[2])
+    get_step.start()
     heads = windows_ref.shape[0]
     frames = segments_ref.shape[0]
-    column, block, branch = place_ref[0], place_ref[1], place_ref[2]
+    column, block, branch = (lax.axis_index(a).astype(jnp.int32) for a in ("seq", "frame", "cfg"))
+    get_windows.wait()
     reach = [windows_ref[h] for h in range(heads)]
     wide = [(w >= 2).astype(jnp.int32) for w in reach]
     some = [(w >= 1).astype(jnp.int32) for w in reach]
@@ -147,6 +163,17 @@
         plan_ref[at.order + spot] = jnp.int32(h)
         plan_ref[at.rank + h] = spot
         plan_ref[at.reach + spot] = reach[h]
+    copies = []
+    for out_ref, side in ((kv_ref, 1 - column), (own_ref, column)):
+        for j in range(out_ref.shape[0]):
+            start = pl.multiple_of(plan_ref[at.order + 2 * j + side] * HD, HD)
+            for k in range(2):
+                copies.append(
+                    pltpu.make_async_copy(
+                        x_ref.at[k + 1, :, pl.ds(start, HD)], out_ref.at[j, k], sems.at[len(copies)]
+                    )
+                )
+                copies[-1].start()
     for j in range(heads // 2):
         plan_ref[at.mine + j] = plan_ref[at.order + 2 * j + column]
         plan_ref[at.theirs + j] = plan_ref[at.order + 2 * j + 1 - column]
@@ -158,6 +185,10 @@
         plan_ref[at.pos + t] = plan_ref[at.rank + head]
     own_frame = 2 * block + column
     sign = 1 - 2 * column
+
+    get_segments.wait()
+    get_step.wait()
+    plan_ref[at.step] = step_ref[0]
 
     def shot(name):
         frame = own_frame + STEPS[name] * sign
@@ -176,7 +207,9 @@
     for k in reversed(range(len(rungs) - 1)):
         fits = jnp.logical_and(many <= rungs[k][0], most <= rungs[k][1])
         index = jnp.where(fits, jnp.int32(k), index)
-    plan_ref[at.rung] = index
+    rung_ref[0] = index
+    for copy in copies:
+        copy.wait()
 
 
 def pack_kernel(jobs, count_in, plan_ref, x_ref, *refs):
@@ -216,9 +249,7 @@
             scratch_shapes=[pltpu.SemaphoreType.DMA((total,))],
         ),
         compiler_params=params(),
-        cost_estimate=pl.CostEstimate(
-            flops=0, bytes_accessed=4 * total * rows * HD, transcendentals=0
-        ),
+        cost_estimate=cost("pack"),
         name="pack_heads",
     )(plan, x3, *after)
 
@@ -236,6 +267,7 @@
         out_specs=[whole(pl.ANY)] * count,
         input_output_aliases={i: i for i in range(count)},
         compiler_params=params(),
+        cost_estimate=cost("gate"),
         name="gate",
     )(*values, *after)
 
@@ -308,6 +340,15 @@
             outs[0][j] = out
 
 
+def slot_spec(array, first, count):
+    if array.shape[0] == count:
+        return whole()
+    block = (count, *array.shape[1:])
+    return pl.BlockSpec(
+        tuple(pl.Element(size) for size in block), lambda i, plan: (first, 0, 0, 0)
+    )
+
+
 def attend_slots(plan, at, q, sources, heads_at, first, count, match_at, distances, after):
     rows = q.shape[-2]
     gathered = q.ndim == 3
@@ -325,15 +366,7 @@
     kv_specs, kvs = [], []
     for array, offset in sources:
         kvs.append(array)
-        if array.shape[0] == count:
-            kv_specs.append(whole())
-        else:
-            kv_specs.append(
-                pl.BlockSpec(
-                    (pl.Element(count), pl.Element(2), pl.Element(rows), pl.Element(HD)),
-                    functools.partial(lambda o, i, plan: (o, 0, 0, 0), offset),
-                )
-            )
+        kv_specs.append(slot_spec(array, offset, count))
     scratch = []
     if gathered:
         planes = 1 if sources else 3
@@ -346,25 +379,20 @@
     else:
         out_shape = [jax.ShapeDtypeStruct((count, rows // 2, HD), BF16)] * 2
         out_specs = [whole()] * 2
-    blocks = count * max(1, len(sources))
     return pl.pallas_call(
         functools.partial(attend_kernel, spec),
         out_shape=out_shape,
         grid_spec=pltpu.PrefetchScalarGridSpec(
             num_scalar_prefetch=1,
             grid=(1,),
-            in_specs=[whole(pl.ANY) if gathered else whole()]
+            in_specs=[whole(pl.ANY) if gathered else slot_spec(q, first, count)]
             + kv_specs
             + [whole(pl.ANY)] * len(after),
             out_specs=out_specs,
             scratch_shapes=scratch,
         ),
         compiler_params=params(),
-        cost_estimate=pl.CostEstimate(
-            flops=8 * blocks * rows * rows * HD,
-            bytes_accessed=4 * (blocks + count) * rows * HD,
-            transcendentals=blocks * rows * rows,
-        ),
+        cost_estimate=cost("attend"),
         name="attend",
     )(plan, q, *kvs, *after)
 
@@ -375,54 +403,110 @@
     return (uncond + strength * (cond - uncond)).astype(BF16)
 
 
-def assemble_kernel(at, chunks, local, plan_ref, strength_ref, *refs):
-    count = len(chunks)
-    own, peer = refs[: count + 1], refs[count + 1 : 2 * count + 2]
-    kept, moved = refs[2 * count + 2 : 3 * count + 2], refs[3 * count + 2 : 4 * count + 2]
+def strength_of(at, plan_ref):
+    step = jnp.full((1, HD), plan_ref[at.step], jnp.int32).astype(F32)
+    return 1.0 + 4.0 * step / 999.0
+
+
+def mix_kernel(at, plan_ref, mine_ref, other_ref, *refs):
     out_ref = refs[-1]
+    strength = strength_of(at, plan_ref)
+    first = plan_ref[at.branch] == 0
+    for j in range(out_ref.shape[0]):
+        mine, other = mine_ref[j], other_ref[j]
+        out_ref[j] = blend(
+            jnp.where(first, mine, other), jnp.where(first, other, mine), strength
+        )
+
+
+def mix_cores(plan, at, mine, other, after):
+    return pl.pallas_call(
+        functools.partial(mix_kernel, at),
+        out_shape=jax.ShapeDtypeStruct(mine.shape, mine.dtype),
+        in_specs=[whole(pltpu.SMEM)] + [whole()] * 2 + [whole(pl.ANY)] * len(after),
+        out_specs=whole(),
+        compiler_params=params(),
+        cost_estimate=cost("mix"),
+        name="mix",
+    )(plan, mine, other, *after)
+
+
+def assemble_kernel(at, own_places, raw_places, places, local, plan_ref, *refs):
+    count, own_count, raw_count = len(places), len(own_places), len(raw_places)
+    own, refs = refs[:own_count], refs[own_count:]
+    mine_refs, refs = refs[:raw_count], refs[raw_count:]
+    other_refs, refs = refs[:raw_count], refs[raw_count:]
+    strength = strength_of(at, plan_ref)
+    kept, moved = refs[:count], refs[count : 2 * count]
+    local_ref = refs[2 * count] if local else None
+    out_ref, held, turned, sems = refs[-4:]
     branch, column = plan_ref[at.branch], plan_ref[at.column]
-    strength = strength_ref[0]
-    exchanged = 2 * sum(chunks)
-
-    def mix(mine_ref, other_ref, index):
-        mine, other = mine_ref[index], other_ref[index]
-        first = branch == 0
-        return blend(jnp.where(first, mine, other), jnp.where(first, other, mine), strength)
+    exchanged = 2 * sum(size for _, size in places)
 
     def one(t, carry):
         p = plan_ref[at.pos + t]
         slot = lax.shift_right_logical(p, 1)
         here = jnp.bitwise_and(p, 1) == column
         is_local = p >= exchanged
-        first = 0
-        for k, size in enumerate(chunks):
+
+        def place(first, size):
             inside = jnp.logical_and(slot >= first, slot < first + size)
             inside = jnp.logical_and(inside, jnp.logical_not(is_local))
-            index = jnp.clip(slot - first, 0, size - 1)
+            return inside, jnp.clip(slot - first, 0, size - 1)
+
+        for k, (first, size) in enumerate(own_places):
+            inside, index = place(first, size)
 
             @pl.when(jnp.logical_and(inside, here))
             def _(k=k, index=index):
-                out_ref[t] = mix(own[k], peer[k], index)
+                held[t] = own[k][index]
+
+        for k, (first, size) in enumerate(raw_places):
+            inside, index = place(first, size)
+
+            @pl.when(jnp.logical_and(inside, here))
+            def _(k=k, index=index):
+                mine, other = mine_refs[k][index], other_refs[k][index]
+                is_cond = branch == 0
+                held[t] = blend(
+                    jnp.where(is_cond, mine, other), jnp.where(is_cond, other, mine), strength
+                )
+
+        for k, (first, size) in enumerate(places):
+            inside, index = place(first, size)
 
             @pl.when(jnp.logical_and(inside, jnp.logical_not(here)))
             def _(k=k, index=index):
                 half = kept[k].shape[1]
                 low_here = branch == 0
                 mine, other = kept[k][index], moved[k][index]
-                out_ref[t, :half] = jnp.where(low_here, mine, other)
-                out_ref[t, half:] = jnp.where(low_here, other, mine)
-
-            first += size
+                held[t, :half] = jnp.where(low_here, mine, other)
+                held[t, half:] = jnp.where(low_here, other, mine)
+
         if local:
             index = jnp.clip(p - exchanged, 0, local - 1)
 
             @pl.when(is_local)
             def _():
-                out_ref[t] = mix(own[count], peer[count], index)
+                held[t] = local_ref[index]
 
         return carry
 
-    lax.fori_loop(0, out_ref.shape[0], one, 0)
+    lax.fori_loop(0, held.shape[0], one, 0)
+    per_half = turned.shape[1]
+    half = turned.shape[0] // 2
+    copies = []
+    for r in range(2):
+        tokens = slice(r * half, (r + 1) * half)
+        for s in range(held.shape[0] // per_half):
+            part = held[s * per_half : (s + 1) * per_half, tokens]
+            turned[tokens, :, s * HD : (s + 1) * HD] = jnp.swapaxes(part, 0, 1)
+        copies.append(
+            pltpu.make_async_copy(turned.at[tokens], out_ref.at[tokens], sems.at[r])
+        )
+        copies[-1].start()
+    for copy in copies:
+        copy.wait()
 
 
 def ranked_body(rungs, qkv, timestep, windows, segments):
@@ -434,16 +518,28 @@
     per_half = heads // (seq_count * cfg_count)
     outs = seq_count * per_half
     at = Layout(heads, outs)
-    strength = 1.0 + 4.0 * timestep.astype(F32) / 999.0
     x3 = jnp.transpose(qkv[0], (1, 0, 2))
-    place = jnp.stack([lax.axis_index(a).astype(jnp.int32) for a in ("seq", "frame", "cfg")])
-    plan = pl.pallas_call(
+    lead, base = rungs[0][1] // 2, rungs[0][0] // 2
+    plan, rung, kv_lead, kv_base = pl.pallas_call(
         functools.partial(plan_kernel, at, rungs, (seq_count, cfg_count)),
-        out_shape=jax.ShapeDtypeStruct((at.size,), jnp.int32),
-        in_specs=[whole(pltpu.SMEM)] * 3,
-        out_specs=whole(pltpu.SMEM),
+        out_shape=[
+            jax.ShapeDtypeStruct((at.size,), jnp.int32),
+            jax.ShapeDtypeStruct((1,), jnp.int32),
+            jax.ShapeDtypeStruct((lead, 2, rows, HD), BF16),
+            jax.ShapeDtypeStruct((base, 2, rows, HD), BF16),
+        ],
+        in_specs=[whole(pltpu.HBM)] * 3 + [whole(pl.ANY)],
+        out_specs=[whole(pltpu.SMEM)] * 2 + [whole(pl.ANY)] * 2,
+        scratch_shapes=[
+            pltpu.SMEM(windows.shape, jnp.int32),
+            pltpu.SMEM(segments.shape, jnp.int32),
+            pltpu.SMEM(timestep.shape, jnp.int32),
+            pltpu.SemaphoreType.DMA((3,)),
+            pltpu.SemaphoreType.DMA((2 * (lead + base),)),
+        ],
+        compiler_params=params(PLAN_VMEM_BYTES),
         name="plan",
-    )(place, windows, segments)
+    )(windows, segments, timestep, x3)
 
     grid_axes = ("seq", "frame")
     last = frame_count - 1
@@ -454,12 +550,15 @@
         (frame_count + i, frame_count + i - 1) for i in range(1, frame_count)
     ]
 
-    def attempt(rung, plan, x3, strength):
+    def attempt(rung, plan, x3, kv_lead, kv_base):
         exchanged, wide = rung
         slots, far = exchanged // 2, wide // 2
         local = heads - exchanged
-        bounds = [(lo, hi) for lo, hi in ((0, far), (far, slots)) if hi > lo]
-        two = len(bounds) == 2
+        bounds = [(0, lead), (lead, base)]
+        if slots > base:
+            bounds.append((base, slots))
+        chunks = range(len(bounds))
+        reaches = [far >= hi for _, hi in bounds]
 
         def cross(a):
             return lax.ppermute(a, "seq", SWAP)
@@ -467,102 +566,112 @@
         def mate(a):
             return lax.ppermute(a, "cfg", SWAP)
 
-        (kv_out0,) = pack(plan, x3, [(at.theirs, far, (1, 2))], [])
-        across = [cross(kv_out0)]
-        kv_own, kv_far = pack(
-            plan, x3, [(at.mine, slots, (1, 2)), (at.mine, far, (1, 2))], [kv_out0]
-        )
-        near_own = lax.ppermute(kv_own, grid_axes, apart)
+        def mix(mine, other, after):
+            return mix_cores(plan, at, mine, other, after)
+
+        across = [cross(kv_lead)]
+        near_base = lax.ppermute(kv_base, grid_axes, apart)
+        jobs = [(at.mine, far, (1, 2)), (at.theirs, slots, (0,))]
+        jobs += [(at.theirs + lo, hi - lo, (1, 2)) for lo, hi in bounds[1:]]
+        jobs += [(at.mine + lo, hi - lo, (1, 2)) for lo, hi in bounds[2:]]
+        kv_far, queries, *rest = pack(plan, x3, jobs, [kv_base])
         far_own = lax.ppermute(kv_far, grid_axes, onward)
-        jobs = [(at.theirs, far, (0,))]
-        if two:
-            jobs += [(at.theirs + far, slots - far, (0,)), (at.theirs + far, slots - far, (1, 2))]
-        q_out = list(pack(plan, x3, jobs, [kv_own]))
-        if two:
-            across.append(cross(q_out.pop()))
-        done = [q_out[0]]
+        across += [cross(a) for a in rest[: len(bounds) - 1]]
+        kv_more = rest[len(bounds) - 1 :]
+        near_more = [lax.ppermute(a, grid_axes, apart) for a in kv_more]
+        done = [rest[0]]
         if local:
             own_local = attend_slots(
                 plan, at, x3, [], at.order + exchanged, 0, local, 0, (), done
             )
             peer_local = mate(own_local)
             done = [own_local]
-        across[0], q_out[0] = gate([across[0], q_out[0]], [*done, far_own])
-        near_across = [lax.ppermute(across[0], grid_axes, onward)]
-        far_across = lax.ppermute(across[0], grid_axes, apart)
-        q_across = [cross(q_out[0])]
-        done = [across[0]]
-        if two:
-            across[1], q_out[1] = gate([across[1], q_out[1]], [*done, near_own])
-            near_across.append(lax.ppermute(across[1], grid_axes, onward))
-            q_across.append(cross(q_out[1]))
-            done = [across[1]]
-
-        def sources_of(k, names):
-            lo = bounds[k][0]
+
+        near_across, far_across, guided = [], [], []
+        (across[0],) = gate([across[0]], done)
+        near_across.append(lax.ppermute(across[0], grid_axes, onward))
+        (queries,) = gate([queries], [across[0], far_own])
+        q_across = cross(queries)
+        done = [queries]
+        if local:
+            guided = [mix(own_local, peer_local, done)]
+            done = guided
+        for k in chunks[1:]:
+            (across[k],) = gate([across[k]], done)
+            done = [across[k]]
+        (late,) = gate([across[0]], [across[1]])
+        far_across.append(lax.ppermute(late, grid_axes, apart))
+        for k in chunks[1:]:
+            near_across.append(lax.ppermute(across[k], grid_axes, onward))
+            far_across.append(
+                lax.ppermute(across[k], grid_axes, apart) if reaches[k] else None
+            )
+
+        def attend_chunk(k, q, names, heads_at, match_at, after):
+            lo, hi = bounds[k]
             arrays = {
-                "O": (kv_own, lo),
+                "O": (kv_more[0], 0) if lo == base else (kv_base, lo),
                 "X": (across[k], 0),
-                "NO": (near_own, lo),
+                "NO": (near_more[0], 0) if lo == base else (near_base, lo),
                 "NR": (near_across[k], 0),
-                "FO": (far_own, 0),
-                "FR": (far_across, 0),
+                "FO": (far_own, lo),
+                "FR": (far_across[k], 0),
             }
-            return [arrays[name] for name in names]
-
-        def cut(k):
-            return slice(0, 5) if k == 0 else slice(1, 4)
-
-        own, kept, moved = [], [], []
+            cut = slice(0, 5) if reaches[k] else slice(1, 4)
+            sources = [arrays[name] for name in names[cut]]
+            return attend_slots(
+                plan, at, q, sources, heads_at + lo, lo, hi - lo,
+                match_at + cut.start, DISTANCES[cut], after,
+            )
 
         def attend_own(k, after):
+            return attend_chunk(k, x3, OWN_SOURCES, at.mine, at.own_match, after)
+
+        def attend_across(k, after):
+            return attend_chunk(k, q_across, ACROSS_SOURCES, 0, at.across_match, after)
+
+        own, kept = {}, {}
+        own[0] = attend_own(0, done)
+        keep, send = attend_across(1, [own[0]])
+        got = mate(send)
+        end = mix(own[0], mate(own[0]), [keep])
+        mixed = mix(keep, got, [end])
+        for last_k, k in zip((1, *chunks[2:]), (*chunks[2:], 0)):
+            kept[last_k] = cross(mixed)
+            keep, send = attend_across(k, [mixed])
+            mixed = mix(keep, mate(send), [])
+        kept[0] = cross(mixed)
+        raw = []
+        for k in chunks[1:]:
             lo, hi = bounds[k]
-            own.append(
-                attend_slots(
-                    plan, at, x3, sources_of(k, OWN_SOURCES[cut(k)]), at.mine + lo, lo, hi - lo,
-                    at.own_match + cut(k).start, DISTANCES[cut(k)], after,
-                )
-            )
-            return [own[-1]]
-
-        def attend_across(k, after):
-            lo, hi = bounds[k]
-            keep, send = attend_slots(
-                plan, at, q_across[k], sources_of(k, ACROSS_SOURCES[cut(k)]), 0, lo, hi - lo,
-                at.across_match + cut(k).start, DISTANCES[cut(k)], after,
-            )
-            got = mate(send)
-            first = plan[at.branch] == 0
-            mixed = blend(jnp.where(first, keep, got), jnp.where(first, got, keep), strength[0])
-            kept.append(cross(mixed))
-            moved.append(mate(kept[-1]))
-            return [keep]
-
-        done = attend_own(0, done)
-        done = attend_across(0, done)
-        if two:
-            done = attend_across(1, done)
-            done = attend_own(1, done)
-        peer = [mate(a) for a in own]
-        if local:
-            own, peer = own + [own_local], peer + [peer_local]
-        else:
-            own, peer = own + own[:1], peer + peer[:1]
-        arrays = [*own, *peer, *kept, *moved]
+            own[k] = attend_own(k, [mixed, kept[1]])
+            middle = (hi - lo) // 2
+            raw += [(lo, own[k][:middle]), (lo + middle, own[k][middle:])]
+        others = [mate(a) for _, a in raw]
+        own_places = ((0, lead),)
+        raw_places = tuple((lo, a.shape[0]) for lo, a in raw)
+        arrays = [end, *[a for _, a in raw], *others]
+        arrays += [kept[k] for k in chunks] + [mate(kept[k]) for k in chunks] + guided
+        places = tuple((lo, hi - lo) for lo, hi in bounds)
         return pl.pallas_call(
-            functools.partial(assemble_kernel, at, [hi - lo for lo, hi in bounds], local),
-            out_shape=jax.ShapeDtypeStruct((outs, rows, HD), BF16),
-            in_specs=[whole(pltpu.SMEM)] * 2 + [whole()] * len(arrays),
-            out_specs=whole(),
+            functools.partial(assemble_kernel, at, own_places, raw_places, places, local),
+            out_shape=jax.ShapeDtypeStruct((rows, per_half, seq_count * HD), BF16),
+            in_specs=[whole(pltpu.SMEM)] + [whole()] * len(arrays),
+            out_specs=whole(pltpu.HBM),
+            scratch_shapes=[
+                pltpu.VMEM((outs, rows, HD), BF16),
+                pltpu.VMEM((rows, per_half, seq_count * HD), BF16),
+                pltpu.SemaphoreType.DMA((2,)),
+            ],
             compiler_params=params(),
             name="assemble",
-        )(plan, strength, *arrays)
-
-    out = lax.switch(
-        plan[at.rung], [functools.partial(attempt, rung) for rung in rungs], plan, x3, strength
+        )(plan, *arrays)
+
+    return lax.switch(
+        rung[0],
+        [functools.partial(attempt, rung) for rung in rungs],
+        plan, x3, kv_lead, kv_base,
     )
-    out = out.reshape(seq_count, per_half, rows, HD)
-    return jnp.transpose(out, (2, 1, 0, 3)).reshape(rows, per_half, seq_count * HD)
 
 
 def rungs_of(heads):

time: 86.8 us -> 79.4 us (0.915)
  waiting for transfers between devices: 28.8 us -> 23.2 us
  Pallas kernels: 24.7 us -> 27.8 us
  local copies, waits for them, and re-layouts: 3.91 us -> 1.05 us
    ppermute x6 -> x5, waiting for transfers between devices: 19.5 us -> 15.5 us  [cross(): return lax.ppermute(a, 'seq', SWAP)]
    ppermute x1, waiting for transfers between devices: 7.85 us -> 4.15 us  [attempt(): far_own = lax.ppermute(kv_far, grid_axes, onward)]
    pallas_call x1 -> x5, Pallas kernels: 1.71 us -> 4.99 us  [the longest x4 2.89 us: mix_cores(): pl.pallas_call(functools.partial(mix_kernel, at), out_shape=jax.ShapeDtyp...]
    ppermute x7 -> x8, waiting for transfers between devices: 1.4 us -> 3.46 us  [mate(): return lax.ppermute(a, 'cfg', SWAP)]
    pallas_call x3 -> x1, Pallas kernels: 4.69 us -> 2.75 us  [pack(): pl.pallas_call(functools.partial(pack_kernel, jobs, len(after)), out_shap...]
    pallas_call x1, Pallas kernels: 1.8 us -> 3.57 us  [ranked_body(): pl.pallas_call(functools.partial(plan_kernel, at, rungs, (seq_count, cfg_...]
    reshape x1 -> x0, local copies, waits for them, and re-layouts: 1.65 us -> none  [ranked_body(): out = out.reshape(seq_count, per_half, rows, HD)]
    slice x2 -> x1, local copies, waits for them, and re-layouts: 1.19 us -> 0.03 us  [attempt(): raw += [(lo, own[k][:middle]), (lo + middle, own[k][middle:])]]
  transfers between devices with their start and end apart: 18 -> 18, of which waited for: 7 -> 8; matrix products, arithmetic and copies ran while one was open for 1% -> 0% of each run, Pallas kernels for 20% -> 28%
where the time goes in v3:
time: 79.4 us; the launch traced here: 79.1 us
  Pallas kernels  27.8 us (35%)
  starting transfers between devices  24.9 us (31%)
  waiting for transfers between devices  23.2 us (29%)
  between operations  1.33 us (2%)
  local copies, waits for them, and re-layouts  1.05 us (1%)
  loops' own time  0.81 us (1%)
    pallas_call x5, Pallas kernels, attend_slots(): pl.pallas_call(functools.partial(attend_kernel, spec), out_shape=out_shap...  16.5 us
    ppermute x5, waiting for transfers between devices, cross(): return lax.ppermute(a, 'seq', SWAP)  15.5 us
    ppermute x5, starting transfers between devices, cross(): return lax.ppermute(a, 'seq', SWAP)  7.88 us
    ppermute x1, starting transfers between devices, attempt(): near_across.append(lax.ppermute(across[k], grid_axes, onward))  4.91 us
    ppermute x1, starting transfers between devices, attempt(): far_own = lax.ppermute(kv_far, grid_axes, onward)  4.59 us
    ppermute x1, waiting for transfers between devices, attempt(): far_own = lax.ppermute(kv_far, grid_axes, onward)  4.15 us
    ppermute x1, starting transfers between devices, attempt(): near_across.append(lax.ppermute(across[0], grid_axes, onward))  4.08 us
    pallas_call x1, Pallas kernels, ranked_body(): pl.pallas_call(functools.partial(plan_kernel, at, rungs, (seq_count, cfg_...  3.57 us
  transfers between devices with their start and end apart: 18, of which 8 were waited for; matrix products, arithmetic and copies ran while one was open for 0% of the time, Pallas kernels for 28%

profile of v3, /device:TPU:0, one launch (start us, length us, event | category | flops | bytes accessed | tf_op | source)
XLA Modules:
  0.0 79.1 jit_solution(111246517209525516)
XLA Ops:
  0.7 3.6 %plan.1 = (s32[173]{0:T(256)S(1)}, s32[1]{0:T(128)}, bf16[5,2,256,128]{3,2,1,0:T(8,128)(2,1)S(1)}, bf16[11,2,256,128]{3,2,1,0:T(8,128)(2,1)S(1)}) custom-call(s32[32]{0:T(128)} %windows_in.1, s32[8]{0:T(128)} %segments_in.1, s32[1]{0:T(128)S(6)} %copy.37.step_in, bf16[3,256,4096]{2,1,0:T(8,128)(2,1)} %bitcast.4), custom_call_target="tpu_custom_call" | custom-call | tf_op jit(solution)/shard_map/plan/pallas_call | solution.py:523
  4.9 73.2 %conditional.1 = (bf16[256,8,256]{2,1,0:T(8,128)(2,1)S(1)}) conditional(s32[]{:T(128)} %bitcast.2, (s32[173]{0:T(256)S(1)}, bf16[3,256,4096]{2,1,0:T(8,128)(2,1)}, bf16[11,2,256,128]{3,2,1,0:T(8,128)(2,1)S(1)}, bf16[5,2,256,128]{3,2,1,0:T(8,128)(2,1)S(1)}) %tuple.24, (s32[173]{0:T(256)S(1)}, bf16[3,256,4096]{2,1,0:T(8,128)(2,1)}, ...), branch_computations={%region_0.0_spmd, %region_1.0_spmd, %region_2.0_spmd} | conditional | flops 21399994368 | bytes 78251120 | solution.py:670
  4.9 3.0 %collective-permute-start.1 = (bf16[5,2,256,128]{3,2,1,0:T(8,128)(2,1)S(1)}, bf16[5,2,256,128]{3,2,1,0:T(8,128)(2,1)S(1)}, u32[]{:S(2)}, u32[]{:S(2)}) collective-permute-start(bf16[5,2,256,128]{3,2,1,0:T(8,128)(2,1)S(1)} %get-tuple-element.37), channel_id=1, source_target_pairs={{0,8},{8,0},{1,9},{9,1},{2,10},{10,2},{3,11},{11,3},{4,12},{12,4},... | collective-permute-start | bytes 1966088 | tf_op jit(solution)/shard_map/cond/branch_0_fun/ppermute | solution.py:564
  7.9 1.3 %collective-permute-start.3 = (bf16[11,2,256,128]{3,2,1,0:T(8,128)(2,1)S(1)}, bf16[11,2,256,128]{3,2,1,0:T(8,128)(2,1)S(1)}, u32[]{:S(2)}, u32[]{:S(2)}) collective-permute-start(bf16[11,2,256,128]{3,2,1,0:T(8,128)(2,1)S(1)} %get-tuple-element.35.refs_0_.refs_2_.refs_1_), channel_id=1, source_target_pairs={{2,0},{4,2},{6,4},{8,10},{10,12},{12,14},{3,1},{5,3},{7,5},{9,11},... | collective-permute-start | bytes 4325384 | tf_op jit(solution)/shard_map/cond/branch_0_fun/ppermute | solution.py:573
  9.2 2.8 %pack_heads.3 = (bf16[5,2,256,128]{3,2,1,0:T(8,128)(2,1)S(1)}, bf16[11,1,256,128]{3,2,1,0:T(8,128)(2,1)S(1)}, bf16[6,2,256,128]{3,2,1,0:T(8,128)(2,1)S(1)}) custom-call(s32[173]{0:T(256)S(1)} %get-tuple-element.32.plan_ref, bf16[3,256,4096]{2,1,0:T(8,128)(2,1)} %get-tuple-element.34.x_ref.q_ref, ...), custom_call_target="tpu_custom_call" | custom-call | flops 10000000000 | bytes 1 | tf_op jit(solution)/shard_map/cond/branch_0_fun/pack_heads/pallas_call | solution.py:238
  12.0 4.6 %collective-permute-start = (bf16[5,2,256,128]{3,2,1,0:T(8,128)(2,1)S(1)}, bf16[5,2,256,128]{3,2,1,0:T(8,128)(2,1)S(1)}, u32[]{:S(2)}, u32[]{:S(2)}) collective-permute-start(bf16[5,2,256,128]{3,2,1,0:T(8,128)(2,1)S(1)} %get-tuple-element.36), channel_id=1, source_target_pairs={{0,2},{2,4},{4,6},{10,8},{12,10},{14,12},{1,3},{3,5},{5,7},{11,9},... | collective-permute-start | bytes 1966088 | tf_op jit(solution)/shard_map/cond/branch_0_fun/ppermute | solution.py:578
  16.7 2.7 %attend.16.refs_1_.mine_ref = bf16[10,256,128]{2,1,0:T(8,128)(2,1)S(1)} custom-call(s32[173]{0:T(256)S(1)} %get-tuple-element.32.plan_ref, bf16[3,256,4096]{2,1,0:T(8,128)(2,1)S(1)} %bitcast.9, bf16[6,2,256,128]{3,2,1,0:T(8,128)(2,1)S(1)} %get-tuple-element.38.refs_0_), custom_call_target="tpu_custom_call" | custom-call | flops 1000000000 | bytes 1 | tf_op jit(solution)/shard_map/cond/branch_0_fun/attend/pallas_call | solution.py:382
  19.5 4.0 %collective-permute-done.1.refs_0_ = bf16[5,2,256,128]{3,2,1,0:T(8,128)(2,1)S(1)} collective-permute-done((bf16[5,2,256,128]{3,2,1,0:T(8,128)(2,1)S(1)}, bf16[5,2,256,128]{3,2,1,0:T(8,128)(2,1)S(1)}, u32[]{:S(2)}, u32[]{:S(2)}) %collective-permute-start.1) | collective-permute-done | bytes 655392 | tf_op jit(solution)/shard_map/cond/branch_0_fun/ppermute | solution.py:564
  23.5 4.1 %collective-permute-start.2 = (bf16[5,2,256,128]{3,2,1,0:T(8,128)(2,1)S(1)}, bf16[5,2,256,128]{3,2,1,0:T(8,128)(2,1)S(1)}, u32[]{:S(2)}, u32[]{:S(2)}) collective-permute-start(bf16[5,2,256,128]{3,2,1,0:T(8,128)(2,1)S(1)} %gate.13.refs_1_.refs_3_.refs_2_), channel_id=1, source_target_pairs={{0,2},{2,4},{4,6},{10,8},{12,10},{14,12},{1,3},{3,5},{5,7},{11,9},... | collective-permute-start | bytes 1966088 | tf_op jit(solution)/shard_map/cond/branch_0_fun/ppermute | solution.py:592
  27.5 4.2 %collective-permute-done.refs_2_.refs_0_ = bf16[5,2,256,128]{3,2,1,0:T(8,128)(2,1)S(1)} collective-permute-done((bf16[5,2,256,128]{3,2,1,0:T(8,128)(2,1)S(1)}, bf16[5,2,256,128]{3,2,1,0:T(8,128)(2,1)S(1)}, u32[]{:S(2)}, u32[]{:S(2)}) %collective-permute-start) | collective-permute-done | bytes 655392 | tf_op jit(solution)/shard_map/cond/branch_0_fun/ppermute | solution.py:578
  31.7 2.7 %collective-permute-start.7 = (bf16[11,1,256,128]{3,2,1,0:T(8,128)(2,1)S(1)}, bf16[11,1,256,128]{3,2,1,0:T(8,128)(2,1)S(1)}, u32[]{:S(2)}, u32[]{:S(2)}) collective-permute-start(bf16[11,1,256,128]{3,2,1,0:T(8,128)(2,1)S(1)} %gate.14.refs_0_), channel_id=1, source_target_pairs={{0,8},{8,0},{1,9},{9,1},{2,10},{10,2},{3,11},{11,3},{4,12},{12,4},... | collective-permute-start | bytes 2162696 | tf_op jit(solution)/shard_map/cond/branch_0_fun/ppermute | solution.py:564
  35.3 5.0 %collective-permute-done.4.refs_0_ = bf16[6,2,256,128]{3,2,1,0:T(8,128)(2,1)S(1)} collective-permute-done((bf16[6,2,256,128]{3,2,1,0:T(8,128)(2,1)S(1)}, bf16[6,2,256,128]{3,2,1,0:T(8,128)(2,1)S(1)}, u32[]{:S(2)}, u32[]{:S(2)}) %collective-permute-start.4) | collective-permute-done | bytes 786464 | tf_op jit(solution)/shard_map/cond/branch_0_fun/ppermute | solution.py:564
  40.3 1.3 %collective-permute-start.9 = (bf16[5,2,256,128]{3,2,1,0:T(8,128)(2,1)S(1)}, bf16[5,2,256,128]{3,2,1,0:T(8,128)(2,1)S(1)}, u32[]{:S(2)}, u32[]{:S(2)}) collective-permute-start(bf16[5,2,256,128]{3,2,1,0:T(8,128)(2,1)S(1)} %gate.16), channel_id=1, source_target_pairs={{2,0},{4,2},{6,4},{8,10},{10,12},{12,14},{3,1},{5,3},{7,5},{9,11},... | collective-permute-start | bytes 1966088 | tf_op jit(solution)/shard_map/cond/branch_0_fun/ppermute | solution.py:603
  41.6 4.9 %collective-permute-start.8 = (bf16[6,2,256,128]{3,2,1,0:T(8,128)(2,1)S(1)}, bf16[6,2,256,128]{3,2,1,0:T(8,128)(2,1)S(1)}, u32[]{:S(2)}, u32[]{:S(2)}) collective-permute-start(bf16[6,2,256,128]{3,2,1,0:T(8,128)(2,1)S(1)} %gate.15.refs_5_.refs_1_.refs_2_), channel_id=1, source_target_pairs={{0,2},{2,4},{4,6},{10,8},{12,10},{14,12},{1,3},{3,5},{5,7},{11,9},... | collective-permute-start | bytes 2359304 | tf_op jit(solution)/shard_map/cond/branch_0_fun/ppermute | solution.py:605
  46.5 3.7 %attend.17.refs_3_.mine_ref = bf16[5,256,128]{2,1,0:T(8,128)(2,1)S(1)} custom-call(s32[173]{0:T(256)S(1)} %get-tuple-element.32.plan_ref, bf16[3,256,4096]{2,1,0:T(8,128)(2,1)S(1)} %bitcast.9, bf16[5,2,256,128]{3,2,1,0:T(8,128)(2,1)S(1)} %collective-permute-done.refs_2_.refs_0_, bf16[5,2,256,128]{3,2,1,0:T(8,128)(2,1)S(1)} %collective-permute-done.2.refs_1_.refs_0_, ...), custom_call_target="tpu_custom_call" | custom-call | flops 1000000000 | bytes 1 | tf_op jit(solution)/shard_map/cond/branch_0_fun/attend/pallas_call | solution.py:382
  50.4 4.6 %collective-permute-done.7.q_ref = bf16[11,1,256,128]{3,2,1,0:T(8,128)(2,1)S(1)} collective-permute-done((bf16[11,1,256,128]{3,2,1,0:T(8,128)(2,1)S(1)}, bf16[11,1,256,128]{3,2,1,0:T(8,128)(2,1)S(1)}, u32[]{:S(2)}, u32[]{:S(2)}) %collective-permute-start.7) | collective-permute-done | bytes 720928 | tf_op jit(solution)/shard_map/cond/branch_0_fun/ppermute | solution.py:564
  54.9 3.1 %attend.18 = (bf16[6,128,128]{2,1,0:T(8,128)(2,1)S(1)}, bf16[6,128,128]{2,1,0:T(8,128)(2,1)S(1)}) custom-call(s32[173]{0:T(256)S(1)} %get-tuple-element.32.plan_ref, bf16[11,1,256,128]{3,2,1,0:T(8,128)(2,1)S(1)} %collective-permute-done.7.q_ref, bf16[11,2,256,128]{3,2,1,0:T(8,128)(2,1)S(1)} %get-tuple-element.35.refs_0_.refs_2_.refs_1_, ...), custom_call_target="tpu_custom_call" | custom-call | flops 1000000000 | bytes 1 | tf_op jit(solution)/shard_map/cond/branch_0_fun/attend/pallas_call | solution.py:382
  60.2 1.8 %collective-permute-start.12 = (bf16[6,128,128]{2,1,0:T(8,128)(2,1)S(1)}, bf16[6,128,128]{2,1,0:T(8,128)(2,1)S(1)}, u32[]{:S(2)}, u32[]{:S(2)}) collective-permute-start(bf16[6,128,128]{2,1,0:T(8,128)(2,1)S(1)} %mix.14.refs_5_), channel_id=1, source_target_pairs={{0,8},{8,0},{1,9},{9,1},{2,10},{10,2},{3,11},{11,3},{4,12},{12,4},... | collective-permute-start | bytes 589832 | tf_op jit(solution)/shard_map/cond/branch_0_fun/ppermute | solution.py:564
  62.0 3.6 %attend.19 = (bf16[5,128,128]{2,1,0:T(8,128)(2,1)S(1)}, bf16[5,128,128]{2,1,0:T(8,128)(2,1)S(1)}) custom-call(s32[173]{0:T(256)S(1)} %get-tuple-element.32.plan_ref, bf16[11,1,256,128]{3,2,1,0:T(8,128)(2,1)S(1)} %collective-permute-done.7.q_ref, bf16[5,2,256,128]{3,2,1,0:T(8,128)(2,1)S(1)} %collective-permute-done.2.refs_1_.refs_0_, ...), custom_call_target="tpu_custom_call" | custom-call | flops 1000000000 | bytes 1 | tf_op jit(solution)/shard_map/cond/branch_0_fun/attend/pallas_call | solution.py:382
  65.7 1.4 %collective-permute-done.11.other_ref = bf16[5,128,128]{2,1,0:T(8,128)(2,1)S(1)} collective-permute-done((bf16[5,128,128]{2,1,0:T(8,128)(2,1)S(1)}, bf16[5,128,128]{2,1,0:T(8,128)(2,1)S(1)}, u32[]{:S(2)}, u32[]{:S(2)}) %collective-permute-start.11) | collective-permute-done | bytes 163872 | tf_op jit(solution)/shard_map/cond/branch_0_fun/ppermute | solution.py:567
  68.1 3.3 %attend.20 = bf16[6,256,128]{2,1,0:T(8,128)(2,1)S(1)} custom-call(s32[173]{0:T(256)S(1)} %get-tuple-element.32.plan_ref, bf16[3,256,4096]{2,1,0:T(8,128)(2,1)S(1)} %bitcast.9, bf16[6,2,256,128]{3,2,1,0:T(8,128)(2,1)S(1)} %collective-permute-done.8.refs_0_, bf16[11,2,256,128]{3,2,1,0:T(8,128)(2,1)S(1)} %get-tuple-element.35.refs_0_.refs_2_.refs_1_, ...), custom_call_target="tpu_custom_call" | custom-call | flops 1000000000 | bytes 1 | tf_op jit(solution)/shard_map/cond/branch_0_fun/attend/pallas_call | solution.py:382
  72.1 1.9 %collective-permute-done.15.refs_5_ = bf16[5,128,128]{2,1,0:T(8,128)(2,1)S(1)} collective-permute-done((bf16[5,128,128]{2,1,0:T(8,128)(2,1)S(1)}, bf16[5,128,128]{2,1,0:T(8,128)(2,1)S(1)}, u32[]{:S(2)}, u32[]{:S(2)}) %collective-permute-start.15) | collective-permute-done | bytes 163872 | tf_op jit(solution)/shard_map/cond/branch_0_fun/ppermute | solution.py:564
  74.1 1.4 %collective-permute-done.16.refs_7_ = bf16[5,128,128]{2,1,0:T(8,128)(2,1)S(1)} collective-permute-done((bf16[5,128,128]{2,1,0:T(8,128)(2,1)S(1)}, bf16[5,128,128]{2,1,0:T(8,128)(2,1)S(1)}, u32[]{:S(2)}, u32[]{:S(2)}) %collective-permute-start.16) | collective-permute-done | bytes 163872 | tf_op jit(solution)/shard_map/cond/branch_0_fun/ppermute | solution.py:567
  75.5 2.1 %assemble.3 = bf16[256,8,256]{2,1,0:T(8,128)(2,1)S(1)} custom-call(s32[173]{0:T(256)S(1)} %get-tuple-element.32.plan_ref, bf16[5,256,128]{2,1,0:T(8,128)(2,1)S(1)} %mix.13.refs_0_, bf16[3,256,128]{2,1,0:T(8,128)(2,1)S(1)} %get-tuple-element.80.refs_1_, bf16[3,256,128]{2,1,0:T(8,128)(2,1)S(1)} %get-tuple-element.79.refs_2_, ...), custom_call_target="tpu_custom_call" | custom-call | tf_op jit(solution)/shard_map/cond/branch_0_fun/assemble/pallas_call | solution.py:656
  (38 shorter events, 6.0 us)
Async XLA Ops:
  4.9 18.6 %collective-permute-start.1 = (bf16[5,2,256,128]{3,2,1,0:T(8,128)(2,1)S(1)}, bf16[5,2,256,128]{3,2,1,0:T(8,128)(2,1)S(1)}, u32[]{:S(2)}, u32[]{:S(2)}) collective-permute-start(bf16[5,2,256,128]{3,2,1,0:T(8,128)(2,1)S(1)} %get-tuple-element.37), channel_id=1, source_target_pairs={{0,8},{8,0},{1,9},{9,1},{2,10},{10,2},{3,11},{11,3},{4,12},{12,4},... | collective-permute-start | bytes 1966088 | tf_op jit(solution)/shard_map/cond/branch_0_fun/ppermute | solution.py:564
  7.9 38.6 %collective-permute-start.3 = (bf16[11,2,256,128]{3,2,1,0:T(8,128)(2,1)S(1)}, bf16[11,2,256,128]{3,2,1,0:T(8,128)(2,1)S(1)}, u32[]{:S(2)}, u32[]{:S(2)}) collective-permute-start(bf16[11,2,256,128]{3,2,1,0:T(8,128)(2,1)S(1)} %get-tuple-element.35.refs_0_.refs_2_.refs_1_), channel_id=1, source_target_pairs={{2,0},{4,2},{6,4},{8,10},{10,12},{12,14},{3,1},{5,3},{7,5},{9,11},... | collective-permute-start | bytes 4325384 | tf_op jit(solution)/shard_map/cond/branch_0_fun/ppermute | solution.py:573
  9.2 7.5 %slice-start = ((s8[6291456]{0:T(1024)(128)(4,1)}), s8[4194304]{0:T(1024)(128)(4,1)S(1)}, s32[]{:S(2)}) async-start(s8[6291456]{0:T(1024)(128)(4,1)} %bitcast.8), calls=%async_computation | async-start | bytes 8388608 | tf_op jit(solution)/shard_map/cond
  9.2 7.5 %slice-start.1 = ((s8[6291456]{0:T(1024)(128)(4,1)}), s8[2097152]{0:T(1024)(128)(4,1)S(1)}, s32[]{:S(2)}) async-start(s8[6291456]{0:T(1024)(128)(4,1)} %bitcast.8), calls=%async_computation.1 | async-start | bytes 4194304 | tf_op jit(solution)/shard_map/cond
  12.0 19.7 %collective-permute-start = (bf16[5,2,256,128]{3,2,1,0:T(8,128)(2,1)S(1)}, bf16[5,2,256,128]{3,2,1,0:T(8,128)(2,1)S(1)}, u32[]{:S(2)}, u32[]{:S(2)}) collective-permute-start(bf16[5,2,256,128]{3,2,1,0:T(8,128)(2,1)S(1)} %get-tuple-element.36), channel_id=1, source_target_pairs={{0,2},{2,4},{4,6},{10,8},{12,10},{14,12},{1,3},{3,5},{5,7},{11,9},... | collective-permute-start | bytes 1966088 | tf_op jit(solution)/shard_map/cond/branch_0_fun/ppermute | solution.py:578
  16.6 23.7 %collective-permute-start.4 = (bf16[6,2,256,128]{3,2,1,0:T(8,128)(2,1)S(1)}, bf16[6,2,256,128]{3,2,1,0:T(8,128)(2,1)S(1)}, u32[]{:S(2)}, u32[]{:S(2)}) collective-permute-start(bf16[6,2,256,128]{3,2,1,0:T(8,128)(2,1)S(1)} %get-tuple-element.38.refs_0_), channel_id=1, source_target_pairs={{0,8},{8,0},{1,9},{9,1},{2,10},{10,2},{3,11},{11,3},{4,12},{12,4},... | collective-permute-start | bytes 2359304 | tf_op jit(solution)/shard_map/cond/branch_0_fun/ppermute | solution.py:564
  19.4 15.0 %collective-permute-start.5 = (bf16[10,256,128]{2,1,0:T(8,128)(2,1)S(1)}, bf16[10,256,128]{2,1,0:T(8,128)(2,1)S(1)}, u32[]{:S(2)}, u32[]{:S(2)}) collective-permute-start(bf16[10,256,128]{2,1,0:T(8,128)(2,1)S(1)} %attend.16.refs_1_.mine_ref), channel_id=1, source_target_pairs={{0,1},{1,0},{2,3},{3,2},{4,5},{5,4},{6,7},{7,6},{8,9},{9,8},{10,11... | collective-permute-start | bytes 1966088 | tf_op jit(solution)/shard_map/cond/branch_0_fun/ppermute | solution.py:567
  23.5 23.1 %collective-permute-start.2 = (bf16[5,2,256,128]{3,2,1,0:T(8,128)(2,1)S(1)}, bf16[5,2,256,128]{3,2,1,0:T(8,128)(2,1)S(1)}, u32[]{:S(2)}, u32[]{:S(2)}) collective-permute-start(bf16[5,2,256,128]{3,2,1,0:T(8,128)(2,1)S(1)} %gate.13.refs_1_.refs_3_.refs_2_), channel_id=1, source_target_pairs={{0,2},{2,4},{4,6},{10,8},{12,10},{14,12},{1,3},{3,5},{5,7},{11,9},... | collective-permute-start | bytes 1966088 | tf_op jit(solution)/shard_map/cond/branch_0_fun/ppermute | solution.py:592
  31.7 23.2 %collective-permute-start.7 = (bf16[11,1,256,128]{3,2,1,0:T(8,128)(2,1)S(1)}, bf16[11,1,256,128]{3,2,1,0:T(8,128)(2,1)S(1)}, u32[]{:S(2)}, u32[]{:S(2)}) collective-permute-start(bf16[11,1,256,128]{3,2,1,0:T(8,128)(2,1)S(1)} %gate.14.refs_0_), channel_id=1, source_target_pairs={{0,8},{8,0},{1,9},{9,1},{2,10},{10,2},{3,11},{11,3},{4,12},{12,4},... | collective-permute-start | bytes 2162696 | tf_op jit(solution)/shard_map/cond/branch_0_fun/ppermute | solution.py:564
  40.3 21.7 %collective-permute-start.9 = (bf16[5,2,256,128]{3,2,1,0:T(8,128)(2,1)S(1)}, bf16[5,2,256,128]{3,2,1,0:T(8,128)(2,1)S(1)}, u32[]{:S(2)}, u32[]{:S(2)}) collective-permute-start(bf16[5,2,256,128]{3,2,1,0:T(8,128)(2,1)S(1)} %gate.16), channel_id=1, source_target_pairs={{2,0},{4,2},{6,4},{8,10},{10,12},{12,14},{3,1},{5,3},{7,5},{9,11},... | collective-permute-start | bytes 1966088 | tf_op jit(solution)/shard_map/cond/branch_0_fun/ppermute | solution.py:603
  41.6 26.5 %collective-permute-start.8 = (bf16[6,2,256,128]{3,2,1,0:T(8,128)(2,1)S(1)}, bf16[6,2,256,128]{3,2,1,0:T(8,128)(2,1)S(1)}, u32[]{:S(2)}, u32[]{:S(2)}) collective-permute-start(bf16[6,2,256,128]{3,2,1,0:T(8,128)(2,1)S(1)} %gate.15.refs_5_.refs_1_.refs_2_), channel_id=1, source_target_pairs={{0,2},{2,4},{4,6},{10,8},{12,10},{14,12},{1,3},{3,5},{5,7},{11,9},... | collective-permute-start | bytes 2359304 | tf_op jit(solution)/shard_map/cond/branch_0_fun/ppermute | solution.py:605
  50.3 7.9 %collective-permute-start.6 = (bf16[5,256,128]{2,1,0:T(8,128)(2,1)S(1)}, bf16[5,256,128]{2,1,0:T(8,128)(2,1)S(1)}, u32[]{:S(2)}, u32[]{:S(2)}) collective-permute-start(bf16[5,256,128]{2,1,0:T(8,128)(2,1)S(1)} %attend.17.refs_3_.mine_ref), channel_id=1, source_target_pairs={{0,1},{1,0},{2,3},{3,2},{4,5},{5,4},{6,7},{7,6},{8,9},{9,8},{10,11... | collective-permute-start | bytes 983048 | tf_op jit(solution)/shard_map/cond/branch_0_fun/ppermute | solution.py:567
  58.1 1.5 %collective-permute-start.10 = (bf16[6,128,128]{2,1,0:T(8,128)(2,1)S(1)}, bf16[6,128,128]{2,1,0:T(8,128)(2,1)S(1)}, u32[]{:S(2)}, u32[]{:S(2)}) collective-permute-start(bf16[6,128,128]{2,1,0:T(8,128)(2,1)S(1)} %get-tuple-element.41), channel_id=1, source_target_pairs={{0,1},{1,0},{2,3},{3,2},{4,5},{5,4},{6,7},{7,6},{8,9},{9,8},{10,11... | collective-permute-start | bytes 589832 | tf_op jit(solution)/shard_map/cond/branch_0_fun/ppermute | solution.py:567
  60.2 7.9 %collective-permute-start.12 = (bf16[6,128,128]{2,1,0:T(8,128)(2,1)S(1)}, bf16[6,128,128]{2,1,0:T(8,128)(2,1)S(1)}, u32[]{:S(2)}, u32[]{:S(2)}) collective-permute-start(bf16[6,128,128]{2,1,0:T(8,128)(2,1)S(1)} %mix.14.refs_5_), channel_id=1, source_target_pairs={{0,8},{8,0},{1,9},{9,1},{2,10},{10,2},{3,11},{11,3},{4,12},{12,4},... | collective-permute-start | bytes 589832 | tf_op jit(solution)/shard_map/cond/branch_0_fun/ppermute | solution.py:564
  65.6 1.5 %collective-permute-start.11 = (bf16[5,128,128]{2,1,0:T(8,128)(2,1)S(1)}, bf16[5,128,128]{2,1,0:T(8,128)(2,1)S(1)}, u32[]{:S(2)}, u32[]{:S(2)}) collective-permute-start(bf16[5,128,128]{2,1,0:T(8,128)(2,1)S(1)} %get-tuple-element.43), channel_id=1, source_target_pairs={{0,1},{1,0},{2,3},{3,2},{4,5},{5,4},{6,7},{7,6},{8,9},{9,8},{10,11... | collective-permute-start | bytes 491528 | tf_op jit(solution)/shard_map/cond/branch_0_fun/ppermute | solution.py:567
  67.7 6.3 %collective-permute-start.15 = (bf16[5,128,128]{2,1,0:T(8,128)(2,1)S(1)}, bf16[5,128,128]{2,1,0:T(8,128)(2,1)S(1)}, u32[]{:S(2)}, u32[]{:S(2)}) collective-permute-start(bf16[5,128,128]{2,1,0:T(8,128)(2,1)S(1)} %mix.15.refs_3_), channel_id=1, source_target_pairs={{0,8},{8,0},{1,9},{9,1},{2,10},{10,2},{3,11},{11,3},{4,12},{12,4},... | collective-permute-start | bytes 491528 | tf_op jit(solution)/shard_map/cond/branch_0_fun/ppermute | solution.py:564
  71.5 2.6 %collective-permute-start.13 = (bf16[3,256,128]{2,1,0:T(8,128)(2,1)S(1)}, bf16[3,256,128]{2,1,0:T(8,128)(2,1)S(1)}, u32[]{:S(2)}, u32[]{:S(2)}) collective-permute-start(bf16[3,256,128]{2,1,0:T(8,128)(2,1)S(1)} %get-tuple-element.80.refs_1_), channel_id=1, source_target_pairs={{0,1},{1,0},{2,3},{3,2},{4,5},{5,4},{6,7},{7,6},{8,9},{9,8},{10,11... | collective-permute-start | bytes 589832 | tf_op jit(solution)/shard_map/cond/branch_0_fun/ppermute | solution.py:567
  71.5 2.5 %collective-permute-start.14 = (bf16[3,256,128]{2,1,0:T(8,128)(2,1)S(1)}, bf16[3,256,128]{2,1,0:T(8,128)(2,1)S(1)}, u32[]{:S(2)}, u32[]{:S(2)}) collective-permute-start(bf16[3,256,128]{2,1,0:T(8,128)(2,1)S(1)} %get-tuple-element.79.refs_2_), channel_id=1, source_target_pairs={{0,1},{1,0},{2,3},{3,2},{4,5},{5,4},{6,7},{7,6},{8,9},{9,8},{10,11... | collective-permute-start | bytes 589832 | tf_op jit(solution)/shard_map/cond/branch_0_fun/ppermute | solution.py:567
  72.0 2.0 %collective-permute-start.17 = (bf16[6,128,128]{2,1,0:T(8,128)(2,1)S(1)}, bf16[6,128,128]{2,1,0:T(8,128)(2,1)S(1)}, u32[]{:S(2)}, u32[]{:S(2)}) collective-permute-start(bf16[6,128,128]{2,1,0:T(8,128)(2,1)S(1)} %collective-permute-done.12.refs_4_.refs_6_), channel_id=1, source_target_pairs={{0,1},{1,0},{2,3},{3,2},{4,5},{5,4},{6,7},{7,6},{8,9},{9,8},{10,11... | collective-permute-start | bytes 589832 | tf_op jit(solution)/shard_map/cond/branch_0_fun/ppermute | solution.py:567
  74.1 1.4 %collective-permute-start.16 = (bf16[5,128,128]{2,1,0:T(8,128)(2,1)S(1)}, bf16[5,128,128]{2,1,0:T(8,128)(2,1)S(1)}, u32[]{:S(2)}, u32[]{:S(2)}) collective-permute-start(bf16[5,128,128]{2,1,0:T(8,128)(2,1)S(1)} %collective-permute-done.15.refs_5_), channel_id=1, source_target_pairs={{0,1},{1,0},{2,3},{3,2},{4,5},{5,4},{6,7},{7,6},{8,9},{9,8},{10,11... | collective-permute-start | bytes 491528 | tf_op jit(solution)/shard_map/cond/branch_0_fun/ppermute | solution.py:567
  78.1 1.0 %copy-start = (bf16[256,8,256]{2,1,0:T(8,128)(2,1)}, bf16[256,8,256]{2,1,0:T(8,128)(2,1)S(1)}, u32[]{:S(2)}) copy-start(bf16[256,8,256]{2,1,0:T(8,128)(2,1)S(1)} %get-tuple-element.213) | copy-start | bytes 3145732

commit v4 on v3

--- a/solution.py
+++ b/solution.py
@@ -99,7 +99,7 @@
 VMEM_BYTES = 32 * 1024 * 1024
 PLAN_VMEM_BYTES = 60 * 1024 * 1024
 SWAP = ((0, 1), (1, 0))
-COSTS = {"pack": 1e10, "attend": 1e9, "mix": 1e8, "gate": 1e9}
+COSTS = {"pack": 1e10, "local": 3e9, "own": 3e9, "across": 3e9, "mix": 1e8, "gate": 1e9}
 STEPS = {"O": 0, "X": 1, "NO": 2, "NR": -1, "FO": -2, "FR": 3}
 OWN_SOURCES = ("FO", "NR", "O", "X", "NO")
 ACROSS_SOURCES = ("NR", "O", "X", "NO", "FR")
@@ -215,9 +215,9 @@
 def pack_kernel(jobs, count_in, plan_ref, x_ref, *refs):
     outs, sems = refs[count_in:-1], refs[-1]
     copies = []
-    for out_ref, (first, count, planes) in zip(outs, jobs):
-        for j in range(count):
-            start = pl.multiple_of(plan_ref[first + j] * HD, HD)
+    for out_ref, (spots, planes) in zip(outs, jobs):
+        for j, spot in enumerate(spots):
+            start = pl.multiple_of(plan_ref[spot] * HD, HD)
             for k, plane in enumerate(planes):
                 copies.append(
                     pltpu.make_async_copy(
@@ -234,12 +234,12 @@
 
 def pack(plan, x3, jobs, after):
     rows = x3.shape[1]
-    total = sum(count * len(planes) for _, count, planes in jobs)
+    total = sum(len(spots) * len(planes) for spots, planes in jobs)
     return pl.pallas_call(
         functools.partial(pack_kernel, jobs, len(after)),
         out_shape=[
-            jax.ShapeDtypeStruct((count, len(planes), rows, HD), x3.dtype)
-            for _, count, planes in jobs
+            jax.ShapeDtypeStruct((len(spots), len(planes), rows, HD), x3.dtype)
+            for spots, planes in jobs
         ],
         grid_spec=pltpu.PrefetchScalarGridSpec(
             num_scalar_prefetch=1,
@@ -349,7 +349,7 @@
     )
 
 
-def attend_slots(plan, at, q, sources, heads_at, first, count, match_at, distances, after):
+def attend_slots(plan, at, q, q_offset, sources, heads_at, first, count, match_at, distances, after):
     rows = q.shape[-2]
     gathered = q.ndim == 3
     spec = (
@@ -385,14 +385,14 @@
         grid_spec=pltpu.PrefetchScalarGridSpec(
             num_scalar_prefetch=1,
             grid=(1,),
-            in_specs=[whole(pl.ANY) if gathered else slot_spec(q, first, count)]
+            in_specs=[whole(pl.ANY) if gathered else slot_spec(q, q_offset, count)]
             + kv_specs
             + [whole(pl.ANY)] * len(after),
             out_specs=out_specs,
             scratch_shapes=scratch,
         ),
         compiler_params=params(),
-        cost_estimate=cost("attend"),
+        cost_estimate=cost("local" if not sources else "own" if gathered else "across"),
         name="attend",
     )(plan, q, *kvs, *after)
 
@@ -571,91 +571,119 @@
 
         across = [cross(kv_lead)]
         near_base = lax.ppermute(kv_base, grid_axes, apart)
-        jobs = [(at.mine, far, (1, 2)), (at.theirs, slots, (0,))]
-        jobs += [(at.theirs + lo, hi - lo, (1, 2)) for lo, hi in bounds[1:]]
-        jobs += [(at.mine + lo, hi - lo, (1, 2)) for lo, hi in bounds[2:]]
-        kv_far, queries, *rest = pack(plan, x3, jobs, [kv_base])
-        far_own = lax.ppermute(kv_far, grid_axes, onward)
+        (kv_far,) = pack(plan, x3, [(range(at.mine, at.mine + lead), (1, 2))], [kv_base])
+        far_own = [lax.ppermute(kv_far, grid_axes, onward)]
+        split = (lead + base) // 2
+        parts = [(lead, split, 1), (0, lead, 0)]
+        parts += [(lo, hi, k) for k, (lo, hi) in enumerate(bounds) if k > 1] + [(split, base, 1)]
+        later = [slot for lo, hi, _ in parts[1:] for slot in range(lo, hi)]
+        jobs = [
+            ([at.theirs + slot for slot in slots_of], (0,))
+            for slots_of in (range(lead, split), later)
+        ]
+        jobs += [(range(at.theirs + lo, at.theirs + hi), (1, 2)) for lo, hi in bounds[1:]]
+        jobs += [(range(at.mine + lo, at.mine + hi), (1, 2)) for lo, hi in bounds[2:]]
+        jobs += [(range(at.mine + lead, at.mine + far), (1, 2))] if far > lead else []
+        q_early, q_late, *rest = pack(plan, x3, jobs, [kv_far])
         across += [cross(a) for a in rest[: len(bounds) - 1]]
-        kv_more = rest[len(bounds) - 1 :]
+        more = rest[len(bounds) - 1 :]
+        if far > lead:
+            far_own.append(lax.ppermute(more.pop(), grid_axes, onward))
+        kv_more = more
         near_more = [lax.ppermute(a, grid_axes, apart) for a in kv_more]
         done = [rest[0]]
         if local:
             own_local = attend_slots(
-                plan, at, x3, [], at.order + exchanged, 0, local, 0, (), done
+                plan, at, x3, 0, [], at.order + exchanged, 0, local, 0, (), done
             )
             peer_local = mate(own_local)
             done = [own_local]
 
-        near_across, far_across, guided = [], [], []
+        near_across, far_across, guided = {}, {}, []
         (across[0],) = gate([across[0]], done)
-        near_across.append(lax.ppermute(across[0], grid_axes, onward))
-        (queries,) = gate([queries], [across[0], far_own])
-        q_across = cross(queries)
-        done = [queries]
+        near_across[0] = lax.ppermute(across[0], grid_axes, onward)
+        (q_early,) = gate([q_early], [across[0], *far_own])
+        done = [q_early]
+        q_early = cross(q_early)
         if local:
             guided = [mix(own_local, peer_local, done)]
             done = guided
+        (late,) = gate([across[0]], done)
+        far_across[0] = lax.ppermute(late, grid_axes, apart)
+        (across[1],) = gate([across[1]], [late, *done])
+        (q_late,) = gate([q_late], [across[1]])
+        done = [near_across[0], q_late]
+        q_late = cross(q_late)
         for k in chunks[1:]:
             (across[k],) = gate([across[k]], done)
             done = [across[k]]
-        (late,) = gate([across[0]], [across[1]])
-        far_across.append(lax.ppermute(late, grid_axes, apart))
-        for k in chunks[1:]:
-            near_across.append(lax.ppermute(across[k], grid_axes, onward))
-            far_across.append(
-                lax.ppermute(across[k], grid_axes, apart) if reaches[k] else None
-            )
-
-        def attend_chunk(k, q, names, heads_at, match_at, after):
-            lo, hi = bounds[k]
+            near_across[k] = lax.ppermute(across[k], grid_axes, onward)
+            if reaches[k]:
+                far_across[k] = lax.ppermute(across[k], grid_axes, apart)
+
+        def attend_part(k, lo, hi, q, q_offset, names, heads_at, match_at, after):
+            skip = lo - bounds[k][0]
             arrays = {
-                "O": (kv_more[0], 0) if lo == base else (kv_base, lo),
-                "X": (across[k], 0),
-                "NO": (near_more[0], 0) if lo == base else (near_base, lo),
-                "NR": (near_across[k], 0),
-                "FO": (far_own, lo),
-                "FR": (far_across[k], 0),
+                "O": (kv_more[0], skip) if k > 1 else (kv_base, lo),
+                "X": (across[k], skip),
+                "NO": (near_more[0], skip) if k > 1 else (near_base, lo),
+                "NR": (near_across[k], skip),
+                "FO": (far_own[min(k, 1)], max(lo - lead, 0)) if reaches[k] else None,
+                "FR": (far_across.get(k), skip),
             }
             cut = slice(0, 5) if reaches[k] else slice(1, 4)
             sources = [arrays[name] for name in names[cut]]
             return attend_slots(
-                plan, at, q, sources, heads_at + lo, lo, hi - lo,
+                plan, at, q, q_offset, sources, heads_at + lo, lo, hi - lo,
                 match_at + cut.start, DISTANCES[cut], after,
             )
 
         def attend_own(k, after):
-            return attend_chunk(k, x3, OWN_SOURCES, at.mine, at.own_match, after)
-
-        def attend_across(k, after):
-            return attend_chunk(k, q_across, ACROSS_SOURCES, 0, at.across_match, after)
-
-        own, kept = {}, {}
+            return attend_part(
+                k, *bounds[k], x3, 0, OWN_SOURCES, at.mine, at.own_match, after
+            )
+
+        def attend_across(part, after):
+            lo, hi, k = parts[part]
+            q = q_late if part else q_early
+            offset = later.index(lo) if part else 0
+            return attend_part(
+                k, lo, hi, q, offset, ACROSS_SOURCES, 0, at.across_match, after
+            )
+
+        own, kept = {}, []
         own[0] = attend_own(0, done)
-        keep, send = attend_across(1, [own[0]])
+        keep, send = attend_across(0, [own[0]])
         got = mate(send)
         end = mix(own[0], mate(own[0]), [keep])
         mixed = mix(keep, got, [end])
-        for last_k, k in zip((1, *chunks[2:]), (*chunks[2:], 0)):
-            kept[last_k] = cross(mixed)
-            keep, send = attend_across(k, [mixed])
-            mixed = mix(keep, mate(send), [])
-        kept[0] = cross(mixed)
+        kept.append(cross(mixed))
+        waiting = []
+        done = [mixed]
+        for part in range(1, len(parts)):
+            keep, send = attend_across(part, done)
+            waiting.append((keep, mate(send)))
+            done = [keep]
+        done.append(kept[0])
+        for keep, got in waiting:
+            mixed = mix(keep, got, done)
+            kept.append(cross(mixed))
+            done = [mixed]
         raw = []
         for k in chunks[1:]:
             lo, hi = bounds[k]
-            own[k] = attend_own(k, [mixed, kept[1]])
+            own[k] = attend_own(k, [mixed, kept[0]])
             middle = (hi - lo) // 2
             raw += [(lo, own[k][:middle]), (lo + middle, own[k][middle:])]
         others = [mate(a) for _, a in raw]
         own_places = ((0, lead),)
         raw_places = tuple((lo, a.shape[0]) for lo, a in raw)
         arrays = [end, *[a for _, a in raw], *others]
-        arrays += [kept[k] for k in chunks] + [mate(kept[k]) for k in chunks] + guided
-        places = tuple((lo, hi - lo) for lo, hi in bounds)
+        arrays += kept + [mate(a) for a in kept] + guided
+        places = tuple((lo, hi - lo) for lo, hi, _ in parts)
         return pl.pallas_call(
             functools.partial(assemble_kernel, at, own_places, raw_places, places, local),
-            out_shape=jax.ShapeDtypeStruct((rows, per_half, seq_count * HD), BF16),
+            out_shape=pltpu.HBM((rows, per_half, seq_count * HD), BF16),
             in_specs=[whole(pltpu.SMEM)] + [whole()] * len(arrays),
             out_specs=whole(pltpu.HBM),
             scratch_shapes=[

time: 79.4 us -> 77.3 us (0.974)
  waiting for transfers between devices: 23.2 us -> 15.8 us
  starting transfers between devices: 24.9 us -> 28.4 us
  Pallas kernels: 27.8 us -> 30.4 us
  local copies, waits for them, and re-layouts: 1.05 us -> 0.08 us
    ppermute x5 -> x7, waiting for transfers between devices: 15.5 us -> 8.89 us  [cross(): return lax.ppermute(a, 'seq', SWAP)]
    ppermute x5 -> x7, starting transfers between devices: 7.88 us -> 10 us  [cross(): return lax.ppermute(a, 'seq', SWAP)]
    ppermute x8 -> x10, waiting for transfers between devices: 3.46 us -> 1.53 us  [mate(): return lax.ppermute(a, 'cfg', SWAP)]
    ppermute x8 -> x10, starting transfers between devices: 0.93 us -> 2.41 us  [mate(): return lax.ppermute(a, 'cfg', SWAP)]
    ppermute x4, waiting for transfers between devices: 4.16 us -> 5.34 us  [the longest x1 3.48 us: attempt(): far_own = [lax.ppermute(kv_far, grid_axes, onward)]]
    unnamed x2 -> x0, local copies, waits for them, and re-layouts: 0.96 us -> none
    pallas_call x5 -> x6, Pallas kernels: 16.5 us -> 17.3 us  [attend_slots(): pl.pallas_call(functools.partial(attend_kernel, spec), out_shape=out_shap...]
    pallas_call x4 -> x5, Pallas kernels: 2.89 us -> 3.44 us  [mix_cores(): pl.pallas_call(functools.partial(mix_kernel, at), out_shape=jax.ShapeDtyp...]
  transfers between devices with their start and end apart: 18 -> 22, of which waited for: 8 -> 10; matrix products, arithmetic and copies ran while one was open for 0% -> 0% of each run, Pallas kernels for 28% -> 31%
where the time goes in v4:
time: 77.3 us; the launch traced here: 76.9 us
  Pallas kernels  30.4 us (39%)
  starting transfers between devices  28.4 us (37%)
  waiting for transfers between devices  15.8 us (20%)
  between operations  1.53 us (2%)
  loops' own time  0.81 us (1%)
    pallas_call x6, Pallas kernels, attend_slots(): pl.pallas_call(functools.partial(attend_kernel, spec), out_shape=out_shap...  17.3 us
    ppermute x7, starting transfers between devices, cross(): return lax.ppermute(a, 'seq', SWAP)  10 us
    ppermute x7, waiting for transfers between devices, cross(): return lax.ppermute(a, 'seq', SWAP)  8.89 us
    ppermute x1, starting transfers between devices, attempt(): far_own = [lax.ppermute(kv_far, grid_axes, onward)]  4.72 us
    ppermute x1, starting transfers between devices, attempt(): near_across[k] = lax.ppermute(across[k], grid_axes, onward)  4.6 us
    ppermute x1, starting transfers between devices, attempt(): near_across[0] = lax.ppermute(across[0], grid_axes, onward)  4.08 us
    pallas_call x1, Pallas kernels, ranked_body(): pl.pallas_call(functools.partial(plan_kernel, at, rungs, (seq_count, cfg_...  3.57 us
    ppermute x1, waiting for transfers between devices, attempt(): far_own = [lax.ppermute(kv_far, grid_axes, onward)]  3.48 us
  transfers between devices with their start and end apart: 22, of which 10 were waited for; matrix products, arithmetic and copies ran while one was open for 0% of the time, Pallas kernels for 31%

profile of v4, /device:TPU:0, one launch (start us, length us, event | category | flops | bytes accessed | tf_op | source)
XLA Modules:
  0.0 76.9 jit_solution(9922729120578051089)
XLA Ops:
  0.7 3.6 %plan.1 = (s32[173]{0:T(256)S(1)}, s32[1]{0:T(128)}, bf16[5,2,256,128]{3,2,1,0:T(8,128)(2,1)S(1)}, bf16[11,2,256,128]{3,2,1,0:T(8,128)(2,1)S(1)}) custom-call(s32[32]{0:T(128)} %windows_in.1, s32[8]{0:T(128)} %segments_in.1, s32[1]{0:T(128)S(6)} %copy.49.step_in, bf16[3,256,4096]{2,1,0:T(8,128)(2,1)} %bitcast.4), custom_call_target="tpu_custom_call" | custom-call | tf_op jit(solution)/shard_map/plan/pallas_call | solution.py:523
  4.9 71.8 %conditional.1 = (bf16[256,8,256]{2,1,0:T(8,128)(2,1)}) conditional(s32[]{:T(128)} %bitcast.2, (s32[173]{0:T(256)S(1)}, bf16[3,256,4096]{2,1,0:T(8,128)(2,1)}, bf16[11,2,256,128]{3,2,1,0:T(8,128)(2,1)S(1)}, bf16[5,2,256,128]{3,2,1,0:T(8,128)(2,1)S(1)}) %tuple.24, (s32[173]{0:T(256)S(1)}, bf16[3,256,4096]{2,1,0:T(8,128)(2,1)}, ...), branch_computations={%region_0.0_spmd, %region_1.0_spmd, %region_2.0_spmd} | conditional | flops 48499998720 | bytes 84542760 | solution.py:698
  4.9 3.0 %collective-permute-start.1 = (bf16[5,2,256,128]{3,2,1,0:T(8,128)(2,1)S(1)}, bf16[5,2,256,128]{3,2,1,0:T(8,128)(2,1)S(1)}, u32[]{:S(2)}, u32[]{:S(2)}) collective-permute-start(bf16[5,2,256,128]{3,2,1,0:T(8,128)(2,1)S(1)} %get-tuple-element.36), channel_id=1, source_target_pairs={{0,8},{8,0},{1,9},{9,1},{2,10},{10,2},{3,11},{11,3},{4,12},{12,4},... | collective-permute-start | bytes 1966088 | tf_op jit(solution)/shard_map/cond/branch_0_fun/ppermute | solution.py:564
  7.9 1.3 %collective-permute-start.3 = (bf16[11,2,256,128]{3,2,1,0:T(8,128)(2,1)S(1)}, bf16[11,2,256,128]{3,2,1,0:T(8,128)(2,1)S(1)}, u32[]{:S(2)}, u32[]{:S(2)}) collective-permute-start(bf16[11,2,256,128]{3,2,1,0:T(8,128)(2,1)S(1)} %get-tuple-element.35.refs_0_.refs_2_.refs_1_), channel_id=1, source_target_pairs={{2,0},{4,2},{6,4},{8,10},{10,12},{12,14},{3,1},{5,3},{7,5},{9,11},... | collective-permute-start | bytes 4325384 | tf_op jit(solution)/shard_map/cond/branch_0_fun/ppermute | solution.py:573
  9.2 2.0 %pack_heads.6.refs_0_ = bf16[5,2,256,128]{3,2,1,0:T(8,128)(2,1)S(1)} custom-call(s32[173]{0:T(256)S(1)} %get-tuple-element.32.plan_ref, bf16[3,256,4096]{2,1,0:T(8,128)(2,1)} %get-tuple-element.34.x_ref.q_ref, bf16[11,2,256,128]{3,2,1,0:T(8,128)(2,1)S(1)} %get-tuple-element.35.refs_0_.refs_2_.refs_1_), custom_call_target="tpu_custom_call" | custom-call | flops 10000000000 | bytes 1 | tf_op jit(solution)/shard_map/cond/branch_0_fun/pack_heads/pallas_call | solution.py:238
  11.2 4.7 %collective-permute-start = (bf16[5,2,256,128]{3,2,1,0:T(8,128)(2,1)S(1)}, bf16[5,2,256,128]{3,2,1,0:T(8,128)(2,1)S(1)}, u32[]{:S(2)}, u32[]{:S(2)}) collective-permute-start(bf16[5,2,256,128]{3,2,1,0:T(8,128)(2,1)S(1)} %pack_heads.6.refs_0_), channel_id=1, source_target_pairs={{0,2},{2,4},{4,6},{10,8},{12,10},{14,12},{1,3},{3,5},{5,7},{11,9},... | collective-permute-start | bytes 1966088 | tf_op jit(solution)/shard_map/cond/branch_0_fun/ppermute | solution.py:575
  16.0 1.2 %pack_heads.7 = (bf16[3,1,256,128]{3,2,1,0:T(8,128)(2,1)S(1)}, bf16[8,1,256,128]{3,2,1,0:T(8,128)(2,1)S(1)}, bf16[6,2,256,128]{3,2,1,0:T(8,128)(2,1)S(1)}) custom-call(s32[173]{0:T(256)S(1)} %get-tuple-element.32.plan_ref, bf16[3,256,4096]{2,1,0:T(8,128)(2,1)S(1)} %copy-done, bf16[5,2,256,128]{3,2,1,0:T(8,128)(2,1)S(1)} %pack_heads.6.refs_0_), custom_call_target="tpu_custom_call" | custom-call | flops 10000000000 | bytes 1 | tf_op jit(solution)/shard_map/cond/branch_0_fun/pack_heads/pallas_call | solution.py:238
  17.3 2.7 %attend.19.refs_1_.mine_ref = bf16[10,256,128]{2,1,0:T(8,128)(2,1)S(1)} custom-call(s32[173]{0:T(256)S(1)} %get-tuple-element.32.plan_ref, bf16[3,256,4096]{2,1,0:T(8,128)(2,1)S(1)} %copy-done, bf16[6,2,256,128]{3,2,1,0:T(8,128)(2,1)S(1)} %get-tuple-element.37.refs_0_), custom_call_target="tpu_custom_call" | custom-call | flops 3000000000 | bytes 1 | tf_op jit(solution)/shard_map/cond/branch_0_fun/attend/pallas_call | solution.py:382
  20.0 3.4 %collective-permute-done.1.refs_0_ = bf16[5,2,256,128]{3,2,1,0:T(8,128)(2,1)S(1)} collective-permute-done((bf16[5,2,256,128]{3,2,1,0:T(8,128)(2,1)S(1)}, bf16[5,2,256,128]{3,2,1,0:T(8,128)(2,1)S(1)}, u32[]{:S(2)}, u32[]{:S(2)}) %collective-permute-start.1) | collective-permute-done | bytes 655392 | tf_op jit(solution)/shard_map/cond/branch_0_fun/ppermute | solution.py:564
  23.5 4.1 %collective-permute-start.2 = (bf16[5,2,256,128]{3,2,1,0:T(8,128)(2,1)S(1)}, bf16[5,2,256,128]{3,2,1,0:T(8,128)(2,1)S(1)}, u32[]{:S(2)}, u32[]{:S(2)}) collective-permute-start(bf16[5,2,256,128]{3,2,1,0:T(8,128)(2,1)S(1)} %gate.19.refs_1_.refs_3_.refs_2_), channel_id=1, source_target_pairs={{0,2},{2,4},{4,6},{10,8},{12,10},{14,12},{1,3},{3,5},{5,7},{11,9},... | collective-permute-start | bytes 1966088 | tf_op jit(solution)/shard_map/cond/branch_0_fun/ppermute | solution.py:604
  27.6 3.5 %collective-permute-done.refs_2_.refs_0_ = bf16[5,2,256,128]{3,2,1,0:T(8,128)(2,1)S(1)} collective-permute-done((bf16[5,2,256,128]{3,2,1,0:T(8,128)(2,1)S(1)}, bf16[5,2,256,128]{3,2,1,0:T(8,128)(2,1)S(1)}, u32[]{:S(2)}, u32[]{:S(2)}) %collective-permute-start) | collective-permute-done | bytes 655392 | tf_op jit(solution)/shard_map/cond/branch_0_fun/ppermute | solution.py:575
  31.1 2.7 %collective-permute-start.7 = (bf16[3,1,256,128]{3,2,1,0:T(8,128)(2,1)S(1)}, bf16[3,1,256,128]{3,2,1,0:T(8,128)(2,1)S(1)}, u32[]{:S(2)}, u32[]{:S(2)}) collective-permute-start(bf16[3,1,256,128]{3,2,1,0:T(8,128)(2,1)S(1)} %gate.20.refs_0_), channel_id=1, source_target_pairs={{0,8},{8,0},{1,9},{9,1},{2,10},{10,2},{3,11},{11,3},{4,12},{12,4},... | collective-permute-start | bytes 589832 | tf_op jit(solution)/shard_map/cond/branch_0_fun/ppermute | solution.py:564
  34.6 1.3 %collective-permute-start.10 = (bf16[5,2,256,128]{3,2,1,0:T(8,128)(2,1)S(1)}, bf16[5,2,256,128]{3,2,1,0:T(8,128)(2,1)S(1)}, u32[]{:S(2)}, u32[]{:S(2)}) collective-permute-start(bf16[5,2,256,128]{3,2,1,0:T(8,128)(2,1)S(1)} %gate.21.refs_1_), channel_id=1, source_target_pairs={{2,0},{4,2},{6,4},{8,10},{10,12},{12,14},{3,1},{5,3},{7,5},{9,11},... | collective-permute-start | bytes 1966088 | tf_op jit(solution)/shard_map/cond/branch_0_fun/ppermute | solution.py:612
  35.9 4.4 %collective-permute-done.4.refs_0_ = bf16[6,2,256,128]{3,2,1,0:T(8,128)(2,1)S(1)} collective-permute-done((bf16[6,2,256,128]{3,2,1,0:T(8,128)(2,1)S(1)}, bf16[6,2,256,128]{3,2,1,0:T(8,128)(2,1)S(1)}, u32[]{:S(2)}, u32[]{:S(2)}) %collective-permute-start.4) | collective-permute-done | bytes 786464 | tf_op jit(solution)/shard_map/cond/branch_0_fun/ppermute | solution.py:564
  40.3 2.1 %collective-permute-start.9 = (bf16[8,1,256,128]{3,2,1,0:T(8,128)(2,1)S(1)}, bf16[8,1,256,128]{3,2,1,0:T(8,128)(2,1)S(1)}, u32[]{:S(2)}, u32[]{:S(2)}) collective-permute-start(bf16[8,1,256,128]{3,2,1,0:T(8,128)(2,1)S(1)} %gate.23.refs_2_), channel_id=1, source_target_pairs={{0,8},{8,0},{1,9},{9,1},{2,10},{10,2},{3,11},{11,3},{4,12},{12,4},... | collective-permute-start | bytes 1572872 | tf_op jit(solution)/shard_map/cond/branch_0_fun/ppermute | solution.py:564
  42.4 1.0 %collective-permute-done.2.refs_1_.refs_0_ = bf16[5,2,256,128]{3,2,1,0:T(8,128)(2,1)S(1)} collective-permute-done((bf16[5,2,256,128]{3,2,1,0:T(8,128)(2,1)S(1)}, bf16[5,2,256,128]{3,2,1,0:T(8,128)(2,1)S(1)}, u32[]{:S(2)}, u32[]{:S(2)}) %collective-permute-start.2) | collective-permute-done | bytes 655392 | tf_op jit(solution)/shard_map/cond/branch_0_fun/ppermute | solution.py:604
  43.4 4.6 %collective-permute-start.8 = (bf16[6,2,256,128]{3,2,1,0:T(8,128)(2,1)S(1)}, bf16[6,2,256,128]{3,2,1,0:T(8,128)(2,1)S(1)}, u32[]{:S(2)}, u32[]{:S(2)}) collective-permute-start(bf16[6,2,256,128]{3,2,1,0:T(8,128)(2,1)S(1)} %gate.24.refs_5_.refs_1_.refs_2_), channel_id=1, source_target_pairs={{0,2},{2,4},{4,6},{10,8},{12,10},{14,12},{1,3},{3,5},{5,7},{11,9},... | collective-permute-start | bytes 2359304 | tf_op jit(solution)/shard_map/cond/branch_0_fun/ppermute | solution.py:620
  48.0 3.7 %attend.20.refs_3_.mine_ref = bf16[5,256,128]{2,1,0:T(8,128)(2,1)S(1)} custom-call(s32[173]{0:T(256)S(1)} %get-tuple-element.32.plan_ref, bf16[3,256,4096]{2,1,0:T(8,128)(2,1)S(1)} %copy-done, bf16[5,2,256,128]{3,2,1,0:T(8,128)(2,1)S(1)} %collective-permute-done.refs_2_.refs_0_, bf16[5,2,256,128]{3,2,1,0:T(8,128)(2,1)S(1)} %collective-permute-done.2.refs_1_.refs_0_, ...), custom_call_target="tpu_custom_call" | custom-call | flops 3000000000 | bytes 1 | tf_op jit(solution)/shard_map/cond/branch_0_fun/attend/pallas_call | solution.py:382
  51.8 2.0 %attend.21 = (bf16[3,128,128]{2,1,0:T(8,128)(2,1)S(1)}, bf16[3,128,128]{2,1,0:T(8,128)(2,1)S(1)}) custom-call(s32[173]{0:T(256)S(1)} %get-tuple-element.32.plan_ref, bf16[3,1,256,128]{3,2,1,0:T(8,128)(2,1)S(1)} %collective-permute-done.7.q_ref, bf16[11,2,256,128]{3,2,1,0:T(8,128)(2,1)S(1)} %get-tuple-element.35.refs_0_.refs_2_.refs_1_, ...), custom_call_target="tpu_custom_call" | custom-call | flops 3000000000 | bytes 1 | tf_op jit(solution)/shard_map/cond/branch_0_fun/attend/pallas_call | solution.py:382
  56.9 3.6 %attend.22 = (bf16[5,128,128]{2,1,0:T(8,128)(2,1)S(1)}, bf16[5,128,128]{2,1,0:T(8,128)(2,1)S(1)}) custom-call(s32[173]{0:T(256)S(1)} %get-tuple-element.32.plan_ref, bf16[8,1,256,128]{3,2,1,0:T(8,128)(2,1)S(1)} %collective-permute-done.9.q_ref, bf16[5,2,256,128]{3,2,1,0:T(8,128)(2,1)S(1)} %collective-permute-done.2.refs_1_.refs_0_, ...), custom_call_target="tpu_custom_call" | custom-call | flops 3000000000 | bytes 1 | tf_op jit(solution)/shard_map/cond/branch_0_fun/attend/pallas_call | solution.py:382
  60.5 2.0 %attend.23 = (bf16[3,128,128]{2,1,0:T(8,128)(2,1)S(1)}, bf16[3,128,128]{2,1,0:T(8,128)(2,1)S(1)}) custom-call(s32[173]{0:T(256)S(1)} %get-tuple-element.32.plan_ref, bf16[8,1,256,128]{3,2,1,0:T(8,128)(2,1)S(1)} %collective-permute-done.9.q_ref, bf16[11,2,256,128]{3,2,1,0:T(8,128)(2,1)S(1)} %get-tuple-element.35.refs_0_.refs_2_.refs_1_, ...), custom_call_target="tpu_custom_call" | custom-call | flops 3000000000 | bytes 1 | tf_op jit(solution)/shard_map/cond/branch_0_fun/attend/pallas_call | solution.py:382
  63.7 1.2 %collective-permute-start.17 = (bf16[5,128,128]{2,1,0:T(8,128)(2,1)S(1)}, bf16[5,128,128]{2,1,0:T(8,128)(2,1)S(1)}, u32[]{:S(2)}, u32[]{:S(2)}) collective-permute-start(bf16[5,128,128]{2,1,0:T(8,128)(2,1)S(1)} %mix.18.refs_0_), channel_id=1, source_target_pairs={{0,8},{8,0},{1,9},{9,1},{2,10},{10,2},{3,11},{11,3},{4,12},{12,4},... | collective-permute-start | bytes 491528 | tf_op jit(solution)/shard_map/cond/branch_0_fun/ppermute | solution.py:564
  66.5 3.3 %attend.24 = bf16[6,256,128]{2,1,0:T(8,128)(2,1)S(1)} custom-call(s32[173]{0:T(256)S(1)} %get-tuple-element.32.plan_ref, bf16[3,256,4096]{2,1,0:T(8,128)(2,1)S(1)} %copy-done, bf16[6,2,256,128]{3,2,1,0:T(8,128)(2,1)S(1)} %collective-permute-done.8.refs_0_, bf16[11,2,256,128]{3,2,1,0:T(8,128)(2,1)S(1)} %get-tuple-element.35.refs_0_.refs_2_.refs_1_, ...), custom_call_target="tpu_custom_call" | custom-call | flops 3000000000 | bytes 1 | tf_op jit(solution)/shard_map/cond/branch_0_fun/attend/pallas_call | solution.py:382
  73.4 2.8 %assemble.3 = bf16[256,8,256]{2,1,0:T(8,128)(2,1)} custom-call(s32[173]{0:T(256)S(1)} %get-tuple-element.32.plan_ref, bf16[5,256,128]{2,1,0:T(8,128)(2,1)S(1)} %mix.16.refs_0_, bf16[3,256,128]{2,1,0:T(8,128)(2,1)S(1)} %get-tuple-element.88.refs_1_, bf16[3,256,128]{2,1,0:T(8,128)(2,1)S(1)} %get-tuple-element.87.refs_2_, ...), custom_call_target="tpu_custom_call" | custom-call | tf_op jit(solution)/shard_map/cond/branch_0_fun/assemble/pallas_call | solution.py:684
  (46 shorter events, 10.5 us)
Async XLA Ops:
  4.9 18.6 %collective-permute-start.1 = (bf16[5,2,256,128]{3,2,1,0:T(8,128)(2,1)S(1)}, bf16[5,2,256,128]{3,2,1,0:T(8,128)(2,1)S(1)}, u32[]{:S(2)}, u32[]{:S(2)}) collective-permute-start(bf16[5,2,256,128]{3,2,1,0:T(8,128)(2,1)S(1)} %get-tuple-element.36), channel_id=1, source_target_pairs={{0,8},{8,0},{1,9},{9,1},{2,10},{10,2},{3,11},{11,3},{4,12},{12,4},... | collective-permute-start | bytes 1966088 | tf_op jit(solution)/shard_map/cond/branch_0_fun/ppermute | solution.py:564
  7.9 40.1 %collective-permute-start.3 = (bf16[11,2,256,128]{3,2,1,0:T(8,128)(2,1)S(1)}, bf16[11,2,256,128]{3,2,1,0:T(8,128)(2,1)S(1)}, u32[]{:S(2)}, u32[]{:S(2)}) collective-permute-start(bf16[11,2,256,128]{3,2,1,0:T(8,128)(2,1)S(1)} %get-tuple-element.35.refs_0_.refs_2_.refs_1_), channel_id=1, source_target_pairs={{2,0},{4,2},{6,4},{8,10},{10,12},{12,14},{3,1},{5,3},{7,5},{9,11},... | collective-permute-start | bytes 4325384 | tf_op jit(solution)/shard_map/cond/branch_0_fun/ppermute | solution.py:573
  9.2 6.8 %copy-start = (bf16[3,256,4096]{2,1,0:T(8,128)(2,1)S(1)}, bf16[3,256,4096]{2,1,0:T(8,128)(2,1)}, u32[]{:S(2)}) copy-start(bf16[3,256,4096]{2,1,0:T(8,128)(2,1)} %get-tuple-element.34.x_ref.q_ref) | copy-start | bytes 18874372 | tf_op jit(solution)/shard_map/cond
  11.2 19.9 %collective-permute-start = (bf16[5,2,256,128]{3,2,1,0:T(8,128)(2,1)S(1)}, bf16[5,2,256,128]{3,2,1,0:T(8,128)(2,1)S(1)}, u32[]{:S(2)}, u32[]{:S(2)}) collective-permute-start(bf16[5,2,256,128]{3,2,1,0:T(8,128)(2,1)S(1)} %pack_heads.6.refs_0_), channel_id=1, source_target_pairs={{0,2},{2,4},{4,6},{10,8},{12,10},{14,12},{1,3},{3,5},{5,7},{11,9},... | collective-permute-start | bytes 1966088 | tf_op jit(solution)/shard_map/cond/branch_0_fun/ppermute | solution.py:575
  17.2 23.1 %collective-permute-start.4 = (bf16[6,2,256,128]{3,2,1,0:T(8,128)(2,1)S(1)}, bf16[6,2,256,128]{3,2,1,0:T(8,128)(2,1)S(1)}, u32[]{:S(2)}, u32[]{:S(2)}) collective-permute-start(bf16[6,2,256,128]{3,2,1,0:T(8,128)(2,1)S(1)} %get-tuple-element.37.refs_0_), channel_id=1, source_target_pairs={{0,8},{8,0},{1,9},{9,1},{2,10},{10,2},{3,11},{11,3},{4,12},{12,4},... | collective-permute-start | bytes 2359304 | tf_op jit(solution)/shard_map/cond/branch_0_fun/ppermute | solution.py:564
  20.0 13.8 %collective-permute-start.5 = (bf16[10,256,128]{2,1,0:T(8,128)(2,1)S(1)}, bf16[10,256,128]{2,1,0:T(8,128)(2,1)S(1)}, u32[]{:S(2)}, u32[]{:S(2)}) collective-permute-start(bf16[10,256,128]{2,1,0:T(8,128)(2,1)S(1)} %attend.19.refs_1_.mine_ref), channel_id=1, source_target_pairs={{0,1},{1,0},{2,3},{3,2},{4,5},{5,4},{6,7},{7,6},{8,9},{9,8},{10,11... | collective-permute-start | bytes 1966088 | tf_op jit(solution)/shard_map/cond/branch_0_fun/ppermute | solution.py:567
  23.5 19.9 %collective-permute-start.2 = (bf16[5,2,256,128]{3,2,1,0:T(8,128)(2,1)S(1)}, bf16[5,2,256,128]{3,2,1,0:T(8,128)(2,1)S(1)}, u32[]{:S(2)}, u32[]{:S(2)}) collective-permute-start(bf16[5,2,256,128]{3,2,1,0:T(8,128)(2,1)S(1)} %gate.19.refs_1_.refs_3_.refs_2_), channel_id=1, source_target_pairs={{0,2},{2,4},{4,6},{10,8},{12,10},{14,12},{1,3},{3,5},{5,7},{11,9},... | collective-permute-start | bytes 1966088 | tf_op jit(solution)/shard_map/cond/branch_0_fun/ppermute | solution.py:604
  31.1 20.7 %collective-permute-start.7 = (bf16[3,1,256,128]{3,2,1,0:T(8,128)(2,1)S(1)}, bf16[3,1,256,128]{3,2,1,0:T(8,128)(2,1)S(1)}, u32[]{:S(2)}, u32[]{:S(2)}) collective-permute-start(bf16[3,1,256,128]{3,2,1,0:T(8,128)(2,1)S(1)} %gate.20.refs_0_), channel_id=1, source_target_pairs={{0,8},{8,0},{1,9},{9,1},{2,10},{10,2},{3,11},{11,3},{4,12},{12,4},... | collective-permute-start | bytes 589832 | tf_op jit(solution)/shard_map/cond/branch_0_fun/ppermute | solution.py:564
  34.6 22.2 %collective-permute-start.10 = (bf16[5,2,256,128]{3,2,1,0:T(8,128)(2,1)S(1)}, bf16[5,2,256,128]{3,2,1,0:T(8,128)(2,1)S(1)}, u32[]{:S(2)}, u32[]{:S(2)}) collective-permute-start(bf16[5,2,256,128]{3,2,1,0:T(8,128)(2,1)S(1)} %gate.21.refs_1_), channel_id=1, source_target_pairs={{2,0},{4,2},{6,4},{8,10},{10,12},{12,14},{3,1},{5,3},{7,5},{9,11},... | collective-permute-start | bytes 1966088 | tf_op jit(solution)/shard_map/cond/branch_0_fun/ppermute | solution.py:612
  40.3 15.7 %collective-permute-start.9 = (bf16[8,1,256,128]{3,2,1,0:T(8,128)(2,1)S(1)}, bf16[8,1,256,128]{3,2,1,0:T(8,128)(2,1)S(1)}, u32[]{:S(2)}, u32[]{:S(2)}) collective-permute-start(bf16[8,1,256,128]{3,2,1,0:T(8,128)(2,1)S(1)} %gate.23.refs_2_), channel_id=1, source_target_pairs={{0,8},{8,0},{1,9},{9,1},{2,10},{10,2},{3,11},{11,3},{4,12},{12,4},... | collective-permute-start | bytes 1572872 | tf_op jit(solution)/shard_map/cond/branch_0_fun/ppermute | solution.py:564
  43.4 23.2 %collective-permute-start.8 = (bf16[6,2,256,128]{3,2,1,0:T(8,128)(2,1)S(1)}, bf16[6,2,256,128]{3,2,1,0:T(8,128)(2,1)S(1)}, u32[]{:S(2)}, u32[]{:S(2)}) collective-permute-start(bf16[6,2,256,128]{3,2,1,0:T(8,128)(2,1)S(1)} %gate.24.refs_5_.refs_1_.refs_2_), channel_id=1, source_target_pairs={{0,2},{2,4},{4,6},{10,8},{12,10},{14,12},{1,3},{3,5},{5,7},{11,9},... | collective-permute-start | bytes 2359304 | tf_op jit(solution)/shard_map/cond/branch_0_fun/ppermute | solution.py:620
  51.7 2.6 %collective-permute-start.6 = (bf16[5,256,128]{2,1,0:T(8,128)(2,1)S(1)}, bf16[5,256,128]{2,1,0:T(8,128)(2,1)S(1)}, u32[]{:S(2)}, u32[]{:S(2)}) collective-permute-start(bf16[5,256,128]{2,1,0:T(8,128)(2,1)S(1)} %attend.20.refs_3_.mine_ref), channel_id=1, source_target_pairs={{0,1},{1,0},{2,3},{3,2},{4,5},{5,4},{6,7},{7,6},{8,9},{9,8},{10,11... | collective-permute-start | bytes 983048 | tf_op jit(solution)/shard_map/cond/branch_0_fun/ppermute | solution.py:567
  53.8 1.5 %collective-permute-start.11 = (bf16[3,128,128]{2,1,0:T(8,128)(2,1)S(1)}, bf16[3,128,128]{2,1,0:T(8,128)(2,1)S(1)}, u32[]{:S(2)}, u32[]{:S(2)}) collective-permute-start(bf16[3,128,128]{2,1,0:T(8,128)(2,1)S(1)} %get-tuple-element.41), channel_id=1, source_target_pairs={{0,1},{1,0},{2,3},{3,2},{4,5},{5,4},{6,7},{7,6},{8,9},{9,8},{10,11... | collective-permute-start | bytes 294920 | tf_op jit(solution)/shard_map/cond/branch_0_fun/ppermute | solution.py:567
  55.9 7.2 %collective-permute-start.14 = (bf16[3,128,128]{2,1,0:T(8,128)(2,1)S(1)}, bf16[3,128,128]{2,1,0:T(8,128)(2,1)S(1)}, u32[]{:S(2)}, u32[]{:S(2)}) collective-permute-start(bf16[3,128,128]{2,1,0:T(8,128)(2,1)S(1)} %mix.17.refs_5_), channel_id=1, source_target_pairs={{0,8},{8,0},{1,9},{9,1},{2,10},{10,2},{3,11},{11,3},{4,12},{12,4},... | collective-permute-start | bytes 294920 | tf_op jit(solution)/shard_map/cond/branch_0_fun/ppermute | solution.py:564
  60.5 2.6 %collective-permute-start.13 = (bf16[5,128,128]{2,1,0:T(8,128)(2,1)S(1)}, bf16[5,128,128]{2,1,0:T(8,128)(2,1)S(1)}, u32[]{:S(2)}, u32[]{:S(2)}) collective-permute-start(bf16[5,128,128]{2,1,0:T(8,128)(2,1)S(1)} %get-tuple-element.45), channel_id=1, source_target_pairs={{0,1},{1,0},{2,3},{3,2},{4,5},{5,4},{6,7},{7,6},{8,9},{9,8},{10,11... | collective-permute-start | bytes 491528 | tf_op jit(solution)/shard_map/cond/branch_0_fun/ppermute | solution.py:567
  62.5 2.4 %collective-permute-start.12 = (bf16[3,128,128]{2,1,0:T(8,128)(2,1)S(1)}, bf16[3,128,128]{2,1,0:T(8,128)(2,1)S(1)}, u32[]{:S(2)}, u32[]{:S(2)}) collective-permute-start(bf16[3,128,128]{2,1,0:T(8,128)(2,1)S(1)} %get-tuple-element.44), channel_id=1, source_target_pairs={{0,1},{1,0},{2,3},{3,2},{4,5},{5,4},{6,7},{7,6},{8,9},{9,8},{10,11... | collective-permute-start | bytes 294920 | tf_op jit(solution)/shard_map/cond/branch_0_fun/ppermute | solution.py:567
  63.7 7.1 %collective-permute-start.17 = (bf16[5,128,128]{2,1,0:T(8,128)(2,1)S(1)}, bf16[5,128,128]{2,1,0:T(8,128)(2,1)S(1)}, u32[]{:S(2)}, u32[]{:S(2)}) collective-permute-start(bf16[5,128,128]{2,1,0:T(8,128)(2,1)S(1)} %mix.18.refs_0_), channel_id=1, source_target_pairs={{0,8},{8,0},{1,9},{9,1},{2,10},{10,2},{3,11},{11,3},{4,12},{12,4},... | collective-permute-start | bytes 491528 | tf_op jit(solution)/shard_map/cond/branch_0_fun/ppermute | solution.py:564
  65.6 6.5 %collective-permute-start.18 = (bf16[3,128,128]{2,1,0:T(8,128)(2,1)S(1)}, bf16[3,128,128]{2,1,0:T(8,128)(2,1)S(1)}, u32[]{:S(2)}, u32[]{:S(2)}) collective-permute-start(bf16[3,128,128]{2,1,0:T(8,128)(2,1)S(1)} %mix.19.refs_3_), channel_id=1, source_target_pairs={{0,8},{8,0},{1,9},{9,1},{2,10},{10,2},{3,11},{11,3},{4,12},{12,4},... | collective-permute-start | bytes 294920 | tf_op jit(solution)/shard_map/cond/branch_0_fun/ppermute | solution.py:564
  69.9 3.5 %collective-permute-start.15 = (bf16[3,256,128]{2,1,0:T(8,128)(2,1)S(1)}, bf16[3,256,128]{2,1,0:T(8,128)(2,1)S(1)}, u32[]{:S(2)}, u32[]{:S(2)}) collective-permute-start(bf16[3,256,128]{2,1,0:T(8,128)(2,1)S(1)} %get-tuple-element.88.refs_1_), channel_id=1, source_target_pairs={{0,1},{1,0},{2,3},{3,2},{4,5},{5,4},{6,7},{7,6},{8,9},{9,8},{10,11... | collective-permute-start | bytes 589832 | tf_op jit(solution)/shard_map/cond/branch_0_fun/ppermute | solution.py:567
  70.0 3.4 %collective-permute-start.16 = (bf16[3,256,128]{2,1,0:T(8,128)(2,1)S(1)}, bf16[3,256,128]{2,1,0:T(8,128)(2,1)S(1)}, u32[]{:S(2)}, u32[]{:S(2)}) collective-permute-start(bf16[3,256,128]{2,1,0:T(8,128)(2,1)S(1)} %get-tuple-element.87.refs_2_), channel_id=1, source_target_pairs={{0,1},{1,0},{2,3},{3,2},{4,5},{5,4},{6,7},{7,6},{8,9},{9,8},{10,11... | collective-permute-start | bytes 589832 | tf_op jit(solution)/shard_map/cond/branch_0_fun/ppermute | solution.py:567
  70.9 2.5 %collective-permute-start.20 = (bf16[5,128,128]{2,1,0:T(8,128)(2,1)S(1)}, bf16[5,128,128]{2,1,0:T(8,128)(2,1)S(1)}, u32[]{:S(2)}, u32[]{:S(2)}) collective-permute-start(bf16[5,128,128]{2,1,0:T(8,128)(2,1)S(1)} %collective-permute-done.17.refs_6_), channel_id=1, source_target_pairs={{0,1},{1,0},{2,3},{3,2},{4,5},{5,4},{6,7},{7,6},{8,9},{9,8},{10,11... | collective-permute-start | bytes 491528 | tf_op jit(solution)/shard_map/cond/branch_0_fun/ppermute | solution.py:567
  70.9 1.5 %collective-permute-start.19 = (bf16[3,128,128]{2,1,0:T(8,128)(2,1)S(1)}, bf16[3,128,128]{2,1,0:T(8,128)(2,1)S(1)}, u32[]{:S(2)}, u32[]{:S(2)}) collective-permute-start(bf16[3,128,128]{2,1,0:T(8,128)(2,1)S(1)} %collective-permute-done.14.refs_1_.refs_4_.refs_5_), channel_id=1, source_target_pairs={{0,1},{1,0},{2,3},{3,2},{4,5},{5,4},{6,7},{7,6},{8,9},{9,8},{10,11... | collective-permute-start | bytes 294920 | tf_op jit(solution)/shard_map/cond/branch_0_fun/ppermute | solution.py:567
  72.0 1.3 %collective-permute-start.21 = (bf16[3,128,128]{2,1,0:T(8,128)(2,1)S(1)}, bf16[3,128,128]{2,1,0:T(8,128)(2,1)S(1)}, u32[]{:S(2)}, u32[]{:S(2)}) collective-permute-start(bf16[3,128,128]{2,1,0:T(8,128)(2,1)S(1)} %collective-permute-done.18.refs_7_), channel_id=1, source_target_pairs={{0,1},{1,0},{2,3},{3,2},{4,5},{5,4},{6,7},{7,6},{8,9},{9,8},{10,11... | collective-permute-start | bytes 294920 | tf_op jit(solution)/shard_map/cond/branch_0_fun/ppermute | solution.py:567

commit v5 on v4

--- a/solution.py
+++ b/solution.py
@@ -118,6 +118,15 @@
     return pltpu.CompilerParams(vmem_limit_bytes=limit)
 
 
+class Rows:
+    def __init__(self, heads):
+        self.strength = 0
+        self.cond = 1
+        self.own = 8
+        self.across = self.own + heads // 2 * len(DISTANCES)
+        self.size = self.across + heads // 2 * len(DISTANCES)
+
+
 class Layout:
     def __init__(self, heads, outs):
         self.mine = 0
@@ -167,13 +176,12 @@
     for out_ref, side in ((kv_ref, 1 - column), (own_ref, column)):
         for j in range(out_ref.shape[0]):
             start = pl.multiple_of(plan_ref[at.order + 2 * j + side] * HD, HD)
-            for k in range(2):
-                copies.append(
-                    pltpu.make_async_copy(
-                        x_ref.at[k + 1, :, pl.ds(start, HD)], out_ref.at[j, k], sems.at[len(copies)]
-                    )
+            copies.append(
+                pltpu.make_async_copy(
+                    x_ref.at[1:3, :, pl.ds(start, HD)], out_ref.at[j], sems.at[len(copies)]
                 )
-                copies[-1].start()
+            )
+            copies[-1].start()
     for j in range(heads // 2):
         plan_ref[at.mine + j] = plan_ref[at.order + 2 * j + column]
         plan_ref[at.theirs + j] = plan_ref[at.order + 2 * j + 1 - column]
@@ -215,17 +223,16 @@
 def pack_kernel(jobs, count_in, plan_ref, x_ref, *refs):
     outs, sems = refs[count_in:-1], refs[-1]
     copies = []
-    for out_ref, (spots, planes) in zip(outs, jobs):
+    for out_ref, (spots, first, last) in zip(outs, jobs):
         for j, spot in enumerate(spots):
             start = pl.multiple_of(plan_ref[spot] * HD, HD)
-            for k, plane in enumerate(planes):
-                copies.append(
-                    pltpu.make_async_copy(
-                        x_ref.at[plane, :, pl.ds(start, HD)],
-                        out_ref.at[j, k],
-                        sems.at[len(copies)],
-                    )
+            copies.append(
+                pltpu.make_async_copy(
+                    x_ref.at[first:last, :, pl.ds(start, HD)],
+                    out_ref.at[j],
+                    sems.at[len(copies)],
                 )
+            )
     for copy in copies:
         copy.start()
     for copy in copies:
@@ -234,20 +241,15 @@
 
 def pack(plan, x3, jobs, after):
     rows = x3.shape[1]
-    total = sum(len(spots) * len(planes) for spots, planes in jobs)
     return pl.pallas_call(
         functools.partial(pack_kernel, jobs, len(after)),
         out_shape=[
-            jax.ShapeDtypeStruct((len(spots), len(planes), rows, HD), x3.dtype)
-            for spots, planes in jobs
+            jax.ShapeDtypeStruct((len(spots), last - first, rows, HD), x3.dtype)
+            for spots, first, last in jobs
         ],
-        grid_spec=pltpu.PrefetchScalarGridSpec(
-            num_scalar_prefetch=1,
-            grid=(1,),
-            in_specs=[whole(pl.ANY)] * (1 + len(after)),
-            out_specs=[whole(pl.ANY)] * len(jobs),
-            scratch_shapes=[pltpu.SemaphoreType.DMA((total,))],
-        ),
+        in_specs=[whole(pltpu.SMEM)] + [whole(pl.ANY)] * (1 + len(after)),
+        out_specs=[whole(pl.ANY)] * len(jobs),
+        scratch_shapes=[pltpu.SemaphoreType.DMA((sum(len(spots) for spots, _, _ in jobs),))],
         compiler_params=params(),
         cost_estimate=cost("pack"),
         name="pack_heads",
@@ -288,113 +290,113 @@
             for e, value in zip(expd, values)
         ],
     )
-    return (mixed / total).astype(BF16)
-
-
-def attend_kernel(spec, plan_ref, q_ref, *refs):
-    count, sources, gathered, heads_at, reach_at, match_at, distances, branch_at, halves = spec
+    return mixed / total
+
+
+def table_kernel(at, rows_at, plan_ref, *refs):
+    table_ref = refs[-1]
+    width = table_ref.shape[1]
+
+    def put(row, value):
+        table_ref[row : row + 1, :] = jnp.full((1, width), value, F32)
+
+    step = jnp.full((1, width), plan_ref[at.step], jnp.int32).astype(F32)
+    table_ref[rows_at.strength : rows_at.strength + 1, :] = 1.0 + 4.0 * step / 999.0
+    put(rows_at.cond, jnp.where(plan_ref[at.branch] == 0, 1.0, 0.0).astype(F32))
+    for first, match_at in ((rows_at.own, at.own_match), (rows_at.across, at.across_match)):
+        for slot in range((rows_at.across - rows_at.own) // len(DISTANCES)):
+            reach = plan_ref[at.my_reach + slot]
+            for k, distance in enumerate(DISTANCES):
+                seen = jnp.logical_and(reach >= distance, plan_ref[match_at + k] != 0)
+                put(
+                    first + slot * len(DISTANCES) + k, jnp.where(seen, 0.0, MASKED).astype(F32)
+                )
+
+
+def make_table(plan, at, rows_at, width, after):
+    return pl.pallas_call(
+        functools.partial(table_kernel, at, rows_at),
+        out_shape=jax.ShapeDtypeStruct((rows_at.size, width), F32),
+        in_specs=[whole(pltpu.SMEM)] + [whole(pl.ANY)] * len(after),
+        out_specs=whole(),
+        compiler_params=params(),
+        cost_estimate=cost("mix"),
+        name="table",
+    )(plan, *after)
+
+
+def local_kernel(count, heads_at, plan_ref, x_ref, *refs):
+    out_ref, held, sems = refs[-3:]
+    copies = []
+    for j in range(count):
+        start = pl.multiple_of(plan_ref[heads_at + j] * HD, HD)
+        copies.append(
+            pltpu.make_async_copy(x_ref.at[:, :, pl.ds(start, HD)], held.at[j], sems.at[j])
+        )
+        copies[-1].start()
+    for copy in copies:
+        copy.wait()
+    for j in range(count):
+        out_ref[j] = softmax_mix(held[j, 0], [held[j, 1]], [held[j, 2]], [None]).astype(BF16)
+
+
+def attend_local(plan, x3, heads_at, count, after):
+    planes, rows, _ = x3.shape
+    return pl.pallas_call(
+        functools.partial(local_kernel, count, heads_at),
+        out_shape=jax.ShapeDtypeStruct((count, rows, HD), BF16),
+        in_specs=[whole(pltpu.SMEM)] + [whole(pl.ANY)] * (1 + len(after)),
+        out_specs=whole(),
+        scratch_shapes=[
+            pltpu.VMEM((count, planes, rows, HD), BF16),
+            pltpu.SemaphoreType.DMA((count,)),
+        ],
+        compiler_params=params(),
+        cost_estimate=cost("local"),
+        name="attend_local",
+    )(plan, x3, *after)
+
+
+def attend_kernel(count, q_offset, offsets, bias_at, cond_at, table_ref, q_ref, *refs):
+    sources = len(offsets)
     kv_refs = refs[:sources]
-    refs = refs[sources:]
-    if gathered:
-        outs, (held, sems) = refs[:-2], refs[-2:]
-        outs = outs[-1:]
-        copies = []
-        planes = held.shape[1]
-        for j in range(count):
-            start = pl.multiple_of(plan_ref[heads_at + j] * HD, HD)
-            for k in range(planes):
-                copies.append(
-                    pltpu.make_async_copy(
-                        q_ref.at[k, :, pl.ds(start, HD)], held.at[j, k], sems.at[j * planes + k]
-                    )
-                )
-        for copy in copies:
-            copy.start()
-        for copy in copies:
-            copy.wait()
-    else:
-        outs = refs[-2:] if halves else refs[-1:]
+    halves = cond_at is not None
+    outs = refs[-2:] if halves else refs[-1:]
     for j in range(count):
-        if gathered:
-            q = held[j, 0]
-        else:
-            q = q_ref[j, 0]
-        if sources:
-            keys = [ref[j, 0] for ref in kv_refs]
-            values = [ref[j, 1] for ref in kv_refs]
-            reach = plan_ref[reach_at + j]
-            biases = []
-            for k, distance in enumerate(distances):
-                seen = jnp.logical_and(reach >= distance, plan_ref[match_at + k] != 0)
-                biases.append(jnp.where(seen, 0.0, MASKED).astype(F32))
-        else:
-            keys, values, biases = [held[j, 1]], [held[j, 2]], [None]
-        out = softmax_mix(q, keys, values, biases)
+        keys = [ref[o + j, 0] for ref, o in zip(kv_refs, offsets)]
+        values = [ref[o + j, 1] for ref, o in zip(kv_refs, offsets)]
+        first = bias_at + j * len(DISTANCES)
+        biases = [table_ref[first + k : first + k + 1, :] for k in range(sources)]
+        out = softmax_mix(q_ref[q_offset + j, 0], keys, values, biases)
         if halves:
             half = out.shape[0] // 2
             low, high = out[:half], out[half:]
-            first = plan_ref[branch_at] == 0
-            outs[0][j] = jnp.where(first, low, high)
-            outs[1][j] = jnp.where(first, high, low)
+            is_first = table_ref[cond_at : cond_at + 1, :HD] > 0.0
+            outs[0][j] = jnp.where(is_first, low, high).astype(BF16)
+            outs[1][j] = jnp.where(is_first, high, low).astype(BF16)
         else:
-            outs[0][j] = out
-
-
-def slot_spec(array, first, count):
-    if array.shape[0] == count:
-        return whole()
-    block = (count, *array.shape[1:])
-    return pl.BlockSpec(
-        tuple(pl.Element(size) for size in block), lambda i, plan: (first, 0, 0, 0)
-    )
-
-
-def attend_slots(plan, at, q, q_offset, sources, heads_at, first, count, match_at, distances, after):
+            outs[0][j] = out.astype(BF16)
+
+
+def attend_slots(table, q, q_offset, sources, count, bias_at, cond_at, after):
     rows = q.shape[-2]
-    gathered = q.ndim == 3
-    spec = (
-        count,
-        len(sources),
-        gathered,
-        heads_at,
-        at.my_reach + first,
-        match_at,
-        distances,
-        at.branch,
-        not gathered,
-    )
-    kv_specs, kvs = [], []
-    for array, offset in sources:
-        kvs.append(array)
-        kv_specs.append(slot_spec(array, offset, count))
-    scratch = []
-    if gathered:
-        planes = 1 if sources else 3
-        scratch = [
-            pltpu.VMEM((count, planes, rows, HD), BF16),
-            pltpu.SemaphoreType.DMA((count * planes,)),
-        ]
+    if cond_at is None:
         out_shape = jax.ShapeDtypeStruct((count, rows, HD), BF16)
         out_specs = whole()
     else:
         out_shape = [jax.ShapeDtypeStruct((count, rows // 2, HD), BF16)] * 2
         out_specs = [whole()] * 2
+    arrays = [array for array, _ in sources]
+    offsets = [offset for _, offset in sources]
     return pl.pallas_call(
-        functools.partial(attend_kernel, spec),
+        functools.partial(attend_kernel, count, q_offset, offsets, bias_at, cond_at),
         out_shape=out_shape,
-        grid_spec=pltpu.PrefetchScalarGridSpec(
-            num_scalar_prefetch=1,
-            grid=(1,),
-            in_specs=[whole(pl.ANY) if gathered else slot_spec(q, q_offset, count)]
-            + kv_specs
-            + [whole(pl.ANY)] * len(after),
-            out_specs=out_specs,
-            scratch_shapes=scratch,
-        ),
+        in_specs=[whole()] * (2 + len(arrays)) + [whole(pl.ANY)] * len(after),
+        out_specs=out_specs,
         compiler_params=params(),
-        cost_estimate=cost("local" if not sources else "own" if gathered else "across"),
+        cost_estimate=cost("own" if cond_at is None else "across"),
         name="attend",
-    )(plan, q, *kvs, *after)
+    )(table, q, *arrays, *after)
 
 
 def blend(cond, uncond, strength):
@@ -403,106 +405,87 @@
     return (uncond + strength * (cond - uncond)).astype(BF16)
 
 
-def strength_of(at, plan_ref):
-    step = jnp.full((1, HD), plan_ref[at.step], jnp.int32).astype(F32)
-    return 1.0 + 4.0 * step / 999.0
-
-
-def mix_kernel(at, plan_ref, mine_ref, other_ref, *refs):
+def mix_branches(rows_at, table_ref, mine, other):
+    strength = table_ref[rows_at.strength : rows_at.strength + 1, :HD]
+    is_cond = table_ref[rows_at.cond : rows_at.cond + 1, :HD] > 0.0
+    mine = mine.astype(F32)
+    other = other.astype(F32)
+    return blend(jnp.where(is_cond, mine, other), jnp.where(is_cond, other, mine), strength)
+
+
+def mix_kernel(rows_at, pieces, table_ref, mine_ref, *refs):
     out_ref = refs[-1]
-    strength = strength_of(at, plan_ref)
-    first = plan_ref[at.branch] == 0
-    for j in range(out_ref.shape[0]):
-        mine, other = mine_ref[j], other_ref[j]
-        out_ref[j] = blend(
-            jnp.where(first, mine, other), jnp.where(first, other, mine), strength
-        )
-
-
-def mix_cores(plan, at, mine, other, after):
+    j = 0
+    for other_ref in refs[:pieces]:
+        for i in range(other_ref.shape[0]):
+            out_ref[j] = mix_branches(rows_at, table_ref, mine_ref[j], other_ref[i])
+            j += 1
+
+
+def mix_cores(table, rows_at, mine, others, after):
     return pl.pallas_call(
-        functools.partial(mix_kernel, at),
+        functools.partial(mix_kernel, rows_at, len(others)),
         out_shape=jax.ShapeDtypeStruct(mine.shape, mine.dtype),
-        in_specs=[whole(pltpu.SMEM)] + [whole()] * 2 + [whole(pl.ANY)] * len(after),
+        in_specs=[whole()] * (2 + len(others)) + [whole(pl.ANY)] * len(after),
         out_specs=whole(),
         compiler_params=params(),
         cost_estimate=cost("mix"),
         name="mix",
-    )(plan, mine, other, *after)
-
-
-def assemble_kernel(at, own_places, raw_places, places, local, plan_ref, *refs):
-    count, own_count, raw_count = len(places), len(own_places), len(raw_places)
-    own, refs = refs[:own_count], refs[own_count:]
-    mine_refs, refs = refs[:raw_count], refs[raw_count:]
-    other_refs, refs = refs[:raw_count], refs[raw_count:]
-    strength = strength_of(at, plan_ref)
-    kept, moved = refs[:count], refs[count : 2 * count]
-    local_ref = refs[2 * count] if local else None
-    out_ref, held, turned, sems = refs[-4:]
-    branch, column = plan_ref[at.branch], plan_ref[at.column]
-    exchanged = 2 * sum(size for _, size in places)
-
-    def one(t, carry):
+    )(table, mine, *others, *after)
+
+
+def assemble_kernel(at, rows_at, sizes, slots, places, plan_in, table_ref, *refs):
+    out_ref, plan_ref, listed, turned, plan_sem, out_sems = refs[-6:]
+    get_plan = pltpu.make_async_copy(plan_in, plan_ref, plan_sem.at[0])
+    get_plan.start()
+    own_count, raw_count, cross_count = sizes
+    refs = list(refs[:-6])
+
+    def take(count):
+        taken = refs[:count]
+        del refs[:count]
+        return taken
+
+    own, raw, raw_other = take(own_count), take(raw_count), take(raw_count)
+    kept, moved, local = take(cross_count), take(cross_count), refs
+    for ref, first in zip(own, places[0]):
+        for j in range(ref.shape[0]):
+            listed[first + j] = ref[j]
+    for ref in local:
+        for j in range(ref.shape[0]):
+            listed[2 * slots + j] = ref[j]
+    for ref, other, first in zip(raw, raw_other, places[1]):
+        for j in range(ref.shape[0]):
+            listed[first + j] = mix_branches(rows_at, table_ref, ref[j], other[j])
+    low_here = table_ref[rows_at.cond : rows_at.cond + 1, :HD] > 0.0
+    for ref, other, first in zip(kept, moved, places[2]):
+        half = ref.shape[1]
+        for j in range(ref.shape[0]):
+            mine, theirs = ref[j].astype(F32), other[j].astype(F32)
+            low = jnp.where(low_here, mine, theirs).astype(BF16)
+            high = jnp.where(low_here, theirs, mine).astype(BF16)
+            listed[slots + first + j, :half] = low
+            listed[slots + first + j, half:] = high
+    get_plan.wait()
+    column = plan_ref[at.column]
+    per_half = turned.shape[1]
+    count = turned.shape[2] // HD * per_half
+    spots = []
+    for t in range(count):
         p = plan_ref[at.pos + t]
         slot = lax.shift_right_logical(p, 1)
-        here = jnp.bitwise_and(p, 1) == column
-        is_local = p >= exchanged
-
-        def place(first, size):
-            inside = jnp.logical_and(slot >= first, slot < first + size)
-            inside = jnp.logical_and(inside, jnp.logical_not(is_local))
-            return inside, jnp.clip(slot - first, 0, size - 1)
-
-        for k, (first, size) in enumerate(own_places):
-            inside, index = place(first, size)
-
-            @pl.when(jnp.logical_and(inside, here))
-            def _(k=k, index=index):
-                held[t] = own[k][index]
-
-        for k, (first, size) in enumerate(raw_places):
-            inside, index = place(first, size)
-
-            @pl.when(jnp.logical_and(inside, here))
-            def _(k=k, index=index):
-                mine, other = mine_refs[k][index], other_refs[k][index]
-                is_cond = branch == 0
-                held[t] = blend(
-                    jnp.where(is_cond, mine, other), jnp.where(is_cond, other, mine), strength
-                )
-
-        for k, (first, size) in enumerate(places):
-            inside, index = place(first, size)
-
-            @pl.when(jnp.logical_and(inside, jnp.logical_not(here)))
-            def _(k=k, index=index):
-                half = kept[k].shape[1]
-                low_here = branch == 0
-                mine, other = kept[k][index], moved[k][index]
-                held[t, :half] = jnp.where(low_here, mine, other)
-                held[t, half:] = jnp.where(low_here, other, mine)
-
-        if local:
-            index = jnp.clip(p - exchanged, 0, local - 1)
-
-            @pl.when(is_local)
-            def _():
-                held[t] = local_ref[index]
-
-        return carry
-
-    lax.fori_loop(0, held.shape[0], one, 0)
-    per_half = turned.shape[1]
-    half = turned.shape[0] // 2
+        paired = jnp.where(jnp.bitwise_and(p, 1) == column, slot, slots + slot)
+        spots.append(jnp.where(p >= 2 * slots, p, paired))
+    parts = 2
+    size = turned.shape[0] // parts
     copies = []
-    for r in range(2):
-        tokens = slice(r * half, (r + 1) * half)
-        for s in range(held.shape[0] // per_half):
-            part = held[s * per_half : (s + 1) * per_half, tokens]
-            turned[tokens, :, s * HD : (s + 1) * HD] = jnp.swapaxes(part, 0, 1)
+    for r in range(parts):
+        tokens = slice(r * size, (r + 1) * size)
+        for s in range(count // per_half):
+            picked = [listed[spots[s * per_half + a], tokens] for a in range(per_half)]
+            turned[tokens, :, s * HD : (s + 1) * HD] = jnp.swapaxes(jnp.stack(picked), 0, 1)
         copies.append(
-            pltpu.make_async_copy(turned.at[tokens], out_ref.at[tokens], sems.at[r])
+            pltpu.make_async_copy(turned.at[tokens], out_ref.at[tokens], out_sems.at[r])
         )
         copies[-1].start()
     for copy in copies:
@@ -518,6 +501,7 @@
     per_half = heads // (seq_count * cfg_count)
     outs = seq_count * per_half
     at = Layout(heads, outs)
+    rows_at = Rows(heads)
     x3 = jnp.transpose(qkv[0], (1, 0, 2))
     lead, base = rungs[0][1] // 2, rungs[0][0] // 2
     plan, rung, kv_lead, kv_base = pl.pallas_call(
@@ -535,7 +519,7 @@
             pltpu.SMEM(segments.shape, jnp.int32),
             pltpu.SMEM(timestep.shape, jnp.int32),
             pltpu.SemaphoreType.DMA((3,)),
-            pltpu.SemaphoreType.DMA((2 * (lead + base),)),
+            pltpu.SemaphoreType.DMA((lead + base,)),
         ],
         compiler_params=params(PLAN_VMEM_BYTES),
         name="plan",
@@ -566,36 +550,36 @@
         def mate(a):
             return lax.ppermute(a, "cfg", SWAP)
 
-        def mix(mine, other, after):
-            return mix_cores(plan, at, mine, other, after)
+        def mix(mine, others, after):
+            return mix_cores(table, rows_at, mine, others, after)
 
         across = [cross(kv_lead)]
         near_base = lax.ppermute(kv_base, grid_axes, apart)
-        (kv_far,) = pack(plan, x3, [(range(at.mine, at.mine + lead), (1, 2))], [kv_base])
+        (kv_far,) = pack(plan, x3, [(range(at.mine, at.mine + lead), 1, 3)], [kv_base])
         far_own = [lax.ppermute(kv_far, grid_axes, onward)]
         split = (lead + base) // 2
-        parts = [(lead, split, 1), (0, lead, 0)]
-        parts += [(lo, hi, k) for k, (lo, hi) in enumerate(bounds) if k > 1] + [(split, base, 1)]
+        parts = [(lead, split, 1), (split, base, 1)]
+        parts += [(lo, hi, k) for k, (lo, hi) in enumerate(bounds) if k > 1] + [(0, lead, 0)]
         later = [slot for lo, hi, _ in parts[1:] for slot in range(lo, hi)]
         jobs = [
-            ([at.theirs + slot for slot in slots_of], (0,))
+            ([at.theirs + slot for slot in slots_of], 0, 1)
             for slots_of in (range(lead, split), later)
         ]
-        jobs += [(range(at.theirs + lo, at.theirs + hi), (1, 2)) for lo, hi in bounds[1:]]
-        jobs += [(range(at.mine + lo, at.mine + hi), (1, 2)) for lo, hi in bounds[2:]]
-        jobs += [(range(at.mine + lead, at.mine + far), (1, 2))] if far > lead else []
-        q_early, q_late, *rest = pack(plan, x3, jobs, [kv_far])
+        jobs += [(range(at.theirs + lo, at.theirs + hi), 1, 3) for lo, hi in bounds[1:]]
+        jobs += [(range(at.mine + lo, at.mine + hi), 1, 3) for lo, hi in bounds[2:]]
+        jobs += [(range(at.mine + lead, at.mine + far), 1, 3)] if far > lead else []
+        jobs.insert(0, (range(at.mine, at.mine + slots), 0, 1))
+        q_own, q_early, q_late, *rest = pack(plan, x3, jobs, [kv_far])
         across += [cross(a) for a in rest[: len(bounds) - 1]]
         more = rest[len(bounds) - 1 :]
         if far > lead:
             far_own.append(lax.ppermute(more.pop(), grid_axes, onward))
         kv_more = more
         near_more = [lax.ppermute(a, grid_axes, apart) for a in kv_more]
-        done = [rest[0]]
+        table = make_table(plan, at, rows_at, rows, [rest[0]])
+        done = [table]
         if local:
-            own_local = attend_slots(
-                plan, at, x3, 0, [], at.order + exchanged, 0, local, 0, (), done
-            )
+            own_local = attend_local(plan, x3, at.order + exchanged, local, done)
             peer_local = mate(own_local)
             done = [own_local]
 
@@ -606,7 +590,7 @@
         done = [q_early]
         q_early = cross(q_early)
         if local:
-            guided = [mix(own_local, peer_local, done)]
+            guided = [mix(own_local, [peer_local], done)]
             done = guided
         (late,) = gate([across[0]], done)
         far_across[0] = lax.ppermute(late, grid_axes, apart)
@@ -621,7 +605,7 @@
             if reaches[k]:
                 far_across[k] = lax.ppermute(across[k], grid_axes, apart)
 
-        def attend_part(k, lo, hi, q, q_offset, names, heads_at, match_at, after):
+        def attend_part(k, lo, hi, q, q_offset, names, bias_at, cond_at, after):
             skip = lo - bounds[k][0]
             arrays = {
                 "O": (kv_more[0], skip) if k > 1 else (kv_base, lo),
@@ -633,36 +617,35 @@
             }
             cut = slice(0, 5) if reaches[k] else slice(1, 4)
             sources = [arrays[name] for name in names[cut]]
-            return attend_slots(
-                plan, at, q, q_offset, sources, heads_at + lo, lo, hi - lo,
-                match_at + cut.start, DISTANCES[cut], after,
-            )
+            bias_at += lo * len(DISTANCES) + cut.start
+            return attend_slots(table, q, q_offset, sources, hi - lo, bias_at, cond_at, after)
 
         def attend_own(k, after):
-            return attend_part(
-                k, *bounds[k], x3, 0, OWN_SOURCES, at.mine, at.own_match, after
-            )
+            lo, hi = bounds[k]
+            return attend_part(k, lo, hi, q_own, lo, OWN_SOURCES, rows_at.own, None, after)
 
         def attend_across(part, after):
             lo, hi, k = parts[part]
             q = q_late if part else q_early
             offset = later.index(lo) if part else 0
             return attend_part(
-                k, lo, hi, q, offset, ACROSS_SOURCES, 0, at.across_match, after
+                k, lo, hi, q, offset, ACROSS_SOURCES, rows_at.across, rows_at.cond, after
             )
 
         own, kept = {}, []
         own[0] = attend_own(0, done)
         keep, send = attend_across(0, [own[0]])
         got = mate(send)
-        end = mix(own[0], mate(own[0]), [keep])
-        mixed = mix(keep, got, [end])
+        end = mix(own[0], [mate(own[0])], [keep])
+        mixed = mix(keep, [got], [end])
         kept.append(cross(mixed))
         waiting = []
         done = [mixed]
         for part in range(1, len(parts)):
             keep, send = attend_across(part, done)
-            waiting.append((keep, mate(send)))
+            middle = send.shape[0] // 2
+            pieces = [send] if part < len(parts) - 1 else [send[:middle], send[middle:]]
+            waiting.append((keep, [mate(piece) for piece in pieces]))
             done = [keep]
         done.append(kept[0])
         for keep, got in waiting:
@@ -676,24 +659,24 @@
             middle = (hi - lo) // 2
             raw += [(lo, own[k][:middle]), (lo + middle, own[k][middle:])]
         others = [mate(a) for _, a in raw]
-        own_places = ((0, lead),)
-        raw_places = tuple((lo, a.shape[0]) for lo, a in raw)
-        arrays = [end, *[a for _, a in raw], *others]
-        arrays += kept + [mate(a) for a in kept] + guided
-        places = tuple((lo, hi - lo) for lo, hi, _ in parts)
+        arrays = [end, *[a for _, a in raw], *others, *kept, *[mate(a) for a in kept], *guided]
+        places = ([0], [lo for lo, _ in raw], [lo for lo, _, _ in parts])
+        sizes = tuple(len(firsts) for firsts in places)
         return pl.pallas_call(
-            functools.partial(assemble_kernel, at, own_places, raw_places, places, local),
+            functools.partial(assemble_kernel, at, rows_at, sizes, slots, places),
             out_shape=pltpu.HBM((rows, per_half, seq_count * HD), BF16),
-            in_specs=[whole(pltpu.SMEM)] + [whole()] * len(arrays),
+            in_specs=[whole(pl.ANY)] + [whole()] * (1 + len(arrays)),
             out_specs=whole(pltpu.HBM),
             scratch_shapes=[
-                pltpu.VMEM((outs, rows, HD), BF16),
+                pltpu.SMEM(plan.shape, plan.dtype),
+                pltpu.VMEM((heads, rows, HD), BF16),
                 pltpu.VMEM((rows, per_half, seq_count * HD), BF16),
+                pltpu.SemaphoreType.DMA((1,)),
                 pltpu.SemaphoreType.DMA((2,)),
             ],
             compiler_params=params(),
             name="assemble",
-        )(plan, *arrays)
+        )(plan, table, *arrays)
 
     return lax.switch(
         rung[0],

time: 77.3 us -> 73.5 us (0.951)
  Pallas kernels: 30.4 us -> 24.3 us
  waiting for transfers between devices: 15.8 us -> 17.6 us
    pallas_call x12 -> x13, Pallas kernels: 23.6 us -> 17.3 us  [the longest x5 11.7 us: attend_slots(): pl.pallas_call(functools.partial(attend_kernel, count, q_offset, offsets,...]
    ppermute x7, waiting for transfers between devices: 8.89 us -> 10.7 us  [cross(): return lax.ppermute(a, 'seq', SWAP)]
    ppermute x10 -> x11, waiting for transfers between devices: 1.53 us -> 2.09 us  [mate(): return lax.ppermute(a, 'cfg', SWAP)]
    ppermute x10 -> x11, starting transfers between devices: 2.41 us -> 2.43 us  [mate(): return lax.ppermute(a, 'cfg', SWAP)]
  transfers between devices with their start and end apart: 22 -> 23, of which waited for: 10 -> 10; matrix products, arithmetic and copies ran while one was open for 0% -> 0% of each run, Pallas kernels for 31% -> 26%
where the time goes in v5:
time: 73.5 us; the launch traced here: 73.2 us
  starting transfers between devices  28.8 us (39%)
  Pallas kernels  24.3 us (33%)
  waiting for transfers between devices  17.6 us (24%)
  between operations  1.53 us (2%)
  loops' own time  0.79 us (1%)
    pallas_call x5, Pallas kernels, attend_slots(): pl.pallas_call(functools.partial(attend_kernel, count, q_offset, offsets,...  11.7 us
    ppermute x7, waiting for transfers between devices, cross(): return lax.ppermute(a, 'seq', SWAP)  10.7 us
    ppermute x7, starting transfers between devices, cross(): return lax.ppermute(a, 'seq', SWAP)  10.4 us
    ppermute x1, starting transfers between devices, attempt(): far_own = [lax.ppermute(kv_far, grid_axes, onward)]  4.72 us
    ppermute x1, starting transfers between devices, attempt(): near_across[k] = lax.ppermute(across[k], grid_axes, onward)  4.6 us
    ppermute x1, starting transfers between devices, attempt(): near_across[0] = lax.ppermute(across[0], grid_axes, onward)  4.08 us
    pallas_call x2, Pallas kernels, pack(): pl.pallas_call(functools.partial(pack_kernel, jobs, len(after)), out_shap...  3.53 us
    ppermute x1, waiting for transfers between devices, attempt(): far_own = [lax.ppermute(kv_far, grid_axes, onward)]  3.48 us
  transfers between devices with their start and end apart: 23, of which 10 were waited for; matrix products, arithmetic and copies ran while one was open for 0% of the time, Pallas kernels for 26%

profile of v5, /device:TPU:0, one launch (start us, length us, event | category | flops | bytes accessed | tf_op | source)
XLA Modules:
  0.0 73.2 jit_solution(18187203380335627061)
XLA Ops:
  0.7 3.4 %plan.1 = (s32[173]{0:T(256)S(1)}, s32[1]{0:T(128)}, bf16[5,2,256,128]{3,2,1,0:T(8,128)(2,1)S(1)}, bf16[11,2,256,128]{3,2,1,0:T(8,128)(2,1)S(1)}) custom-call(s32[32]{0:T(128)} %windows_in.1, s32[8]{0:T(128)} %segments_in.1, s32[1]{0:T(128)S(6)} %copy.49.step_in, bf16[3,256,4096]{2,1,0:T(8,128)(2,1)} %bitcast.4), custom_call_target="tpu_custom_call" | custom-call | tf_op jit(solution)/shard_map/plan/pallas_call | solution.py:507
  4.7 68.2 %conditional.1 = (bf16[256,8,256]{2,1,0:T(8,128)(2,1)}) conditional(s32[]{:T(128)} %bitcast.2, (s32[173]{0:T(256)S(1)}, bf16[3,256,4096]{2,1,0:T(8,128)(2,1)}, bf16[11,2,256,128]{3,2,1,0:T(8,128)(2,1)S(1)}, bf16[5,2,256,128]{3,2,1,0:T(8,128)(2,1)S(1)}) %tuple.24, (s32[173]{0:T(256)S(1)}, bf16[3,256,4096]{2,1,0:T(8,128)(2,1)}, ...), branch_computations={%region_0.0_spmd, %region_1.0_spmd, %region_2.0_spmd} | conditional | flops 48599998464 | bytes 84870480 | solution.py:681
  4.8 3.0 %collective-permute-start.1 = (bf16[5,2,256,128]{3,2,1,0:T(8,128)(2,1)S(1)}, bf16[5,2,256,128]{3,2,1,0:T(8,128)(2,1)S(1)}, u32[]{:S(2)}, u32[]{:S(2)}) collective-permute-start(bf16[5,2,256,128]{3,2,1,0:T(8,128)(2,1)S(1)} %get-tuple-element.38), channel_id=1, source_target_pairs={{0,8},{8,0},{1,9},{9,1},{2,10},{10,2},{3,11},{11,3},{4,12},{12,4},... | collective-permute-start | bytes 1966088 | tf_op jit(solution)/shard_map/cond/branch_0_fun/ppermute | solution.py:548
  7.8 1.3 %collective-permute-start.3 = (bf16[11,2,256,128]{3,2,1,0:T(8,128)(2,1)S(1)}, bf16[11,2,256,128]{3,2,1,0:T(8,128)(2,1)S(1)}, u32[]{:S(2)}, u32[]{:S(2)}) collective-permute-start(bf16[11,2,256,128]{3,2,1,0:T(8,128)(2,1)S(1)} %get-tuple-element.35.refs_0_.refs_2_.refs_1_), channel_id=1, source_target_pairs={{2,0},{4,2},{6,4},{8,10},{10,12},{12,14},{3,1},{5,3},{7,5},{9,11},... | collective-permute-start | bytes 4325384 | tf_op jit(solution)/shard_map/cond/branch_0_fun/ppermute | solution.py:557
  9.1 2.0 %pack_heads.6.refs_0_ = bf16[5,2,256,128]{3,2,1,0:T(8,128)(2,1)S(1)} custom-call(s32[173]{0:T(256)S(1)} %get-tuple-element.32.plan_ref.plan_in, bf16[3,256,4096]{2,1,0:T(8,128)(2,1)} %get-tuple-element.34.x_ref, bf16[11,2,256,128]{3,2,1,0:T(8,128)(2,1)S(1)} %get-tuple-element.35.refs_0_.refs_2_.refs_1_), custom_call_target="tpu_custom_call" | custom-call | flops 10000000000 | bytes 1 | tf_op jit(solution)/shard_map/cond/branch_0_fun/pack_heads/pallas_call | solution.py:244
  11.1 4.7 %collective-permute-start = (bf16[5,2,256,128]{3,2,1,0:T(8,128)(2,1)S(1)}, bf16[5,2,256,128]{3,2,1,0:T(8,128)(2,1)S(1)}, u32[]{:S(2)}, u32[]{:S(2)}) collective-permute-start(bf16[5,2,256,128]{3,2,1,0:T(8,128)(2,1)S(1)} %pack_heads.6.refs_0_), channel_id=1, source_target_pairs={{0,2},{2,4},{4,6},{10,8},{12,10},{14,12},{1,3},{3,5},{5,7},{11,9},... | collective-permute-start | bytes 1966088 | tf_op jit(solution)/shard_map/cond/branch_0_fun/ppermute | solution.py:559
  15.8 1.5 %pack_heads.7 = (bf16[11,1,256,128]{3,2,1,0:T(8,128)(2,1)S(1)}, bf16[3,1,256,128]{3,2,1,0:T(8,128)(2,1)S(1)}, bf16[8,1,256,128]{3,2,1,0:T(8,128)(2,1)S(1)}, bf16[6,2,256,128]{3,2,1,0:T(8,128)(2,1)S(1)}) custom-call(s32[173]{0:T(256)S(1)} %get-tuple-element.32.plan_ref.plan_in, bf16[3,256,4096]{2,1,0:T(8,128)(2,1)S(1)} %copy-done, ...), custom_call_target="tpu_custom_call" | custom-call | flops 10000000000 | bytes 1 | tf_op jit(solution)/shard_map/cond/branch_0_fun/pack_heads/pallas_call | solution.py:244
  18.2 2.5 %attend_local.2.refs_1_.mine_ref = bf16[10,256,128]{2,1,0:T(8,128)(2,1)S(1)} custom-call(s32[173]{0:T(256)S(1)} %get-tuple-element.32.plan_ref.plan_in, bf16[3,256,4096]{2,1,0:T(8,128)(2,1)S(1)} %copy-done, f32[168,256]{1,0:T(8,128)S(1)} %table.3.refs_0_.table_ref), custom_call_target="tpu_custom_call" | custom-call | flops 3000000000 | bytes 1 | tf_op jit(solution)/shard_map/cond/branch_0_fun/attend_local/pallas_call | solution.py:345
  20.7 2.6 %collective-permute-done.1.refs_0_ = bf16[5,2,256,128]{3,2,1,0:T(8,128)(2,1)S(1)} collective-permute-done((bf16[5,2,256,128]{3,2,1,0:T(8,128)(2,1)S(1)}, bf16[5,2,256,128]{3,2,1,0:T(8,128)(2,1)S(1)}, u32[]{:S(2)}, u32[]{:S(2)}) %collective-permute-start.1) | collective-permute-done | bytes 655392 | tf_op jit(solution)/shard_map/cond/branch_0_fun/ppermute | solution.py:548
  23.3 4.1 %collective-permute-start.2 = (bf16[5,2,256,128]{3,2,1,0:T(8,128)(2,1)S(1)}, bf16[5,2,256,128]{3,2,1,0:T(8,128)(2,1)S(1)}, u32[]{:S(2)}, u32[]{:S(2)}) collective-permute-start(bf16[5,2,256,128]{3,2,1,0:T(8,128)(2,1)S(1)} %gate.19.refs_1_.refs_3_.refs_2_), channel_id=1, source_target_pairs={{0,2},{2,4},{4,6},{10,8},{12,10},{14,12},{1,3},{3,5},{5,7},{11,9},... | collective-permute-start | bytes 1966088 | tf_op jit(solution)/shard_map/cond/branch_0_fun/ppermute | solution.py:588
  27.5 3.5 %collective-permute-done.refs_2_.refs_0_ = bf16[5,2,256,128]{3,2,1,0:T(8,128)(2,1)S(1)} collective-permute-done((bf16[5,2,256,128]{3,2,1,0:T(8,128)(2,1)S(1)}, bf16[5,2,256,128]{3,2,1,0:T(8,128)(2,1)S(1)}, u32[]{:S(2)}, u32[]{:S(2)}) %collective-permute-start) | collective-permute-done | bytes 655392 | tf_op jit(solution)/shard_map/cond/branch_0_fun/ppermute | solution.py:559
  30.9 2.7 %collective-permute-start.7 = (bf16[3,1,256,128]{3,2,1,0:T(8,128)(2,1)S(1)}, bf16[3,1,256,128]{3,2,1,0:T(8,128)(2,1)S(1)}, u32[]{:S(2)}, u32[]{:S(2)}) collective-permute-start(bf16[3,1,256,128]{3,2,1,0:T(8,128)(2,1)S(1)} %gate.20.refs_1_), channel_id=1, source_target_pairs={{0,8},{8,0},{1,9},{9,1},{2,10},{10,2},{3,11},{11,3},{4,12},{12,4},... | collective-permute-start | bytes 589832 | tf_op jit(solution)/shard_map/cond/branch_0_fun/ppermute | solution.py:548
  33.9 1.3 %collective-permute-start.10 = (bf16[5,2,256,128]{3,2,1,0:T(8,128)(2,1)S(1)}, bf16[5,2,256,128]{3,2,1,0:T(8,128)(2,1)S(1)}, u32[]{:S(2)}, u32[]{:S(2)}) collective-permute-start(bf16[5,2,256,128]{3,2,1,0:T(8,128)(2,1)S(1)} %gate.21.refs_1_), channel_id=1, source_target_pairs={{2,0},{4,2},{6,4},{8,10},{10,12},{12,14},{3,1},{5,3},{7,5},{9,11},... | collective-permute-start | bytes 1966088 | tf_op jit(solution)/shard_map/cond/branch_0_fun/ppermute | solution.py:596
  35.2 4.9 %collective-permute-done.4.refs_0_ = bf16[6,2,256,128]{3,2,1,0:T(8,128)(2,1)S(1)} collective-permute-done((bf16[6,2,256,128]{3,2,1,0:T(8,128)(2,1)S(1)}, bf16[6,2,256,128]{3,2,1,0:T(8,128)(2,1)S(1)}, u32[]{:S(2)}, u32[]{:S(2)}) %collective-permute-start.4) | collective-permute-done | bytes 786464 | tf_op jit(solution)/shard_map/cond/branch_0_fun/ppermute | solution.py:548
  40.2 2.1 %collective-permute-start.9 = (bf16[8,1,256,128]{3,2,1,0:T(8,128)(2,1)S(1)}, bf16[8,1,256,128]{3,2,1,0:T(8,128)(2,1)S(1)}, u32[]{:S(2)}, u32[]{:S(2)}) collective-permute-start(bf16[8,1,256,128]{3,2,1,0:T(8,128)(2,1)S(1)} %gate.23.refs_2_), channel_id=1, source_target_pairs={{0,8},{8,0},{1,9},{9,1},{2,10},{10,2},{3,11},{11,3},{4,12},{12,4},... | collective-permute-start | bytes 1572872 | tf_op jit(solution)/shard_map/cond/branch_0_fun/ppermute | solution.py:548
  43.2 4.6 %collective-permute-start.8 = (bf16[6,2,256,128]{3,2,1,0:T(8,128)(2,1)S(1)}, bf16[6,2,256,128]{3,2,1,0:T(8,128)(2,1)S(1)}, u32[]{:S(2)}, u32[]{:S(2)}) collective-permute-start(bf16[6,2,256,128]{3,2,1,0:T(8,128)(2,1)S(1)} %gate.24.refs_5_.refs_1_.refs_2_), channel_id=1, source_target_pairs={{0,2},{2,4},{4,6},{10,8},{12,10},{14,12},{1,3},{3,5},{5,7},{11,9},... | collective-permute-start | bytes 2359304 | tf_op jit(solution)/shard_map/cond/branch_0_fun/ppermute | solution.py:604
  47.9 3.1 %attend.17.refs_3_.mine_ref = bf16[5,256,128]{2,1,0:T(8,128)(2,1)S(1)} custom-call(f32[168,256]{1,0:T(8,128)S(1)} %table.3.refs_0_.table_ref, bf16[11,1,256,128]{3,2,1,0:T(8,128)(2,1)S(1)} %get-tuple-element.37.q_ref, bf16[5,2,256,128]{3,2,1,0:T(8,128)(2,1)S(1)} %collective-permute-done.refs_2_.refs_0_, ...), custom_call_target="tpu_custom_call" | custom-call | flops 3000000000 | bytes 1 | tf_op jit(solution)/shard_map/cond/branch_0_fun/attend/pallas_call | solution.py:391
  51.1 1.4 %attend.18 = (bf16[3,128,128]{2,1,0:T(8,128)(2,1)S(1)}, bf16[3,128,128]{2,1,0:T(8,128)(2,1)S(1)}) custom-call(f32[168,256]{1,0:T(8,128)S(1)} %table.3.refs_0_.table_ref, bf16[3,1,256,128]{3,2,1,0:T(8,128)(2,1)S(1)} %collective-permute-done.7.q_ref, bf16[11,2,256,128]{3,2,1,0:T(8,128)(2,1)S(1)} %get-tuple-element.35.refs_0_.refs_2_.refs_1_, ...), custom_call_target="tpu_custom_call" | custom-call | flops 3000000000 | bytes 1 | tf_op jit(solution)/shard_map/cond/branch_0_fun/attend/pallas_call | solution.py:391
  54.8 1.4 %attend.19 = (bf16[3,128,128]{2,1,0:T(8,128)(2,1)S(1)}, bf16[3,128,128]{2,1,0:T(8,128)(2,1)S(1)}) custom-call(f32[168,256]{1,0:T(8,128)S(1)} %table.3.refs_0_.table_ref, bf16[8,1,256,128]{3,2,1,0:T(8,128)(2,1)S(1)} %collective-permute-done.9.q_ref, bf16[11,2,256,128]{3,2,1,0:T(8,128)(2,1)S(1)} %get-tuple-element.35.refs_0_.refs_2_.refs_1_, ...), custom_call_target="tpu_custom_call" | custom-call | flops 3000000000 | bytes 1 | tf_op jit(solution)/shard_map/cond/branch_0_fun/attend/pallas_call | solution.py:391
  56.7 3.1 %attend.20 = (bf16[5,128,128]{2,1,0:T(8,128)(2,1)S(1)}, bf16[5,128,128]{2,1,0:T(8,128)(2,1)S(1)}) custom-call(f32[168,256]{1,0:T(8,128)S(1)} %table.3.refs_0_.table_ref, bf16[8,1,256,128]{3,2,1,0:T(8,128)(2,1)S(1)} %collective-permute-done.9.q_ref, bf16[5,2,256,128]{3,2,1,0:T(8,128)(2,1)S(1)} %collective-permute-done.2.refs_1_.refs_0_, ...), custom_call_target="tpu_custom_call" | custom-call | flops 3000000000 | bytes 1 | tf_op jit(solution)/shard_map/cond/branch_0_fun/attend/pallas_call | solution.py:391
  60.5 1.5 %collective-permute-start.18 = (bf16[3,128,128]{2,1,0:T(8,128)(2,1)S(1)}, bf16[3,128,128]{2,1,0:T(8,128)(2,1)S(1)}, u32[]{:S(2)}, u32[]{:S(2)}) collective-permute-start(bf16[3,128,128]{2,1,0:T(8,128)(2,1)S(1)} %mix.18.refs_2_), channel_id=1, source_target_pairs={{0,8},{8,0},{1,9},{9,1},{2,10},{10,2},{3,11},{11,3},{4,12},{12,4},... | collective-permute-start | bytes 294920 | tf_op jit(solution)/shard_map/cond/branch_0_fun/ppermute | solution.py:548
  63.2 2.6 %attend.21 = bf16[6,256,128]{2,1,0:T(8,128)(2,1)S(1)} custom-call(f32[168,256]{1,0:T(8,128)S(1)} %table.3.refs_0_.table_ref, bf16[11,1,256,128]{3,2,1,0:T(8,128)(2,1)S(1)} %get-tuple-element.37.q_ref, bf16[6,2,256,128]{3,2,1,0:T(8,128)(2,1)S(1)} %collective-permute-done.8.refs_0_, bf16[11,2,256,128]{3,2,1,0:T(8,128)(2,1)S(1)} %get-tuple-element.35.refs_0_.refs_2_.refs_1_, ...), custom_call_target="tpu_custom_call" | custom-call | flops 3000000000 | bytes 1 | tf_op jit(solution)/shard_map/cond/branch_0_fun/attend/pallas_call | solution.py:391
  66.4 2.5 %collective-permute-done.19.refs_7_ = bf16[5,128,128]{2,1,0:T(8,128)(2,1)S(1)} collective-permute-done((bf16[5,128,128]{2,1,0:T(8,128)(2,1)S(1)}, bf16[5,128,128]{2,1,0:T(8,128)(2,1)S(1)}, u32[]{:S(2)}, u32[]{:S(2)}) %collective-permute-start.19) | collective-permute-done | bytes 163872 | tf_op jit(solution)/shard_map/cond/branch_0_fun/ppermute | solution.py:548
  70.7 1.7 %assemble.3 = bf16[256,8,256]{2,1,0:T(8,128)(2,1)} custom-call(s32[173]{0:T(256)S(1)} %get-tuple-element.32.plan_ref.plan_in, f32[168,256]{1,0:T(8,128)S(1)} %table.3.refs_0_.table_ref, bf16[5,256,128]{2,1,0:T(8,128)(2,1)S(1)} %mix.16.refs_1_.refs_0_, bf16[3,256,128]{2,1,0:T(8,128)(2,1)S(1)} %get-tuple-element.91.refs_1_, ...), custom_call_target="tpu_custom_call" | custom-call | tf_op jit(solution)/shard_map/cond/branch_0_fun/assemble/pallas_call | solution.py:665
  (51 shorter events, 9.3 us)
Async XLA Ops:
  4.8 18.6 %collective-permute-start.1 = (bf16[5,2,256,128]{3,2,1,0:T(8,128)(2,1)S(1)}, bf16[5,2,256,128]{3,2,1,0:T(8,128)(2,1)S(1)}, u32[]{:S(2)}, u32[]{:S(2)}) collective-permute-start(bf16[5,2,256,128]{3,2,1,0:T(8,128)(2,1)S(1)} %get-tuple-element.38), channel_id=1, source_target_pairs={{0,8},{8,0},{1,9},{9,1},{2,10},{10,2},{3,11},{11,3},{4,12},{12,4},... | collective-permute-start | bytes 1966088 | tf_op jit(solution)/shard_map/cond/branch_0_fun/ppermute | solution.py:548
  7.8 40.1 %collective-permute-start.3 = (bf16[11,2,256,128]{3,2,1,0:T(8,128)(2,1)S(1)}, bf16[11,2,256,128]{3,2,1,0:T(8,128)(2,1)S(1)}, u32[]{:S(2)}, u32[]{:S(2)}) collective-permute-start(bf16[11,2,256,128]{3,2,1,0:T(8,128)(2,1)S(1)} %get-tuple-element.35.refs_0_.refs_2_.refs_1_), channel_id=1, source_target_pairs={{2,0},{4,2},{6,4},{8,10},{10,12},{12,14},{3,1},{5,3},{7,5},{9,11},... | collective-permute-start | bytes 4325384 | tf_op jit(solution)/shard_map/cond/branch_0_fun/ppermute | solution.py:557
  9.1 6.8 %copy-start = (bf16[3,256,4096]{2,1,0:T(8,128)(2,1)S(1)}, bf16[3,256,4096]{2,1,0:T(8,128)(2,1)}, u32[]{:S(2)}) copy-start(bf16[3,256,4096]{2,1,0:T(8,128)(2,1)} %get-tuple-element.34.x_ref) | copy-start | bytes 18874372 | tf_op jit(solution)/shard_map/cond
  11.1 19.9 %collective-permute-start = (bf16[5,2,256,128]{3,2,1,0:T(8,128)(2,1)S(1)}, bf16[5,2,256,128]{3,2,1,0:T(8,128)(2,1)S(1)}, u32[]{:S(2)}, u32[]{:S(2)}) collective-permute-start(bf16[5,2,256,128]{3,2,1,0:T(8,128)(2,1)S(1)} %pack_heads.6.refs_0_), channel_id=1, source_target_pairs={{0,2},{2,4},{4,6},{10,8},{12,10},{14,12},{1,3},{3,5},{5,7},{11,9},... | collective-permute-start | bytes 1966088 | tf_op jit(solution)/shard_map/cond/branch_0_fun/ppermute | solution.py:559
  17.3 22.8 %collective-permute-start.4 = (bf16[6,2,256,128]{3,2,1,0:T(8,128)(2,1)S(1)}, bf16[6,2,256,128]{3,2,1,0:T(8,128)(2,1)S(1)}, u32[]{:S(2)}, u32[]{:S(2)}) collective-permute-start(bf16[6,2,256,128]{3,2,1,0:T(8,128)(2,1)S(1)} %get-tuple-element.36.refs_0_), channel_id=1, source_target_pairs={{0,8},{8,0},{1,9},{9,1},{2,10},{10,2},{3,11},{11,3},{4,12},{12,4},... | collective-permute-start | bytes 2359304 | tf_op jit(solution)/shard_map/cond/branch_0_fun/ppermute | solution.py:548
  20.7 12.9 %collective-permute-start.5 = (bf16[10,256,128]{2,1,0:T(8,128)(2,1)S(1)}, bf16[10,256,128]{2,1,0:T(8,128)(2,1)S(1)}, u32[]{:S(2)}, u32[]{:S(2)}) collective-permute-start(bf16[10,256,128]{2,1,0:T(8,128)(2,1)S(1)} %attend_local.2.refs_1_.mine_ref), channel_id=1, source_target_pairs={{0,1},{1,0},{2,3},{3,2},{4,5},{5,4},{6,7},{7,6},{8,9},{9,8},{10,11... | collective-permute-start | bytes 1966088 | tf_op jit(solution)/shard_map/cond/branch_0_fun/ppermute | solution.py:551
  23.3 19.9 %collective-permute-start.2 = (bf16[5,2,256,128]{3,2,1,0:T(8,128)(2,1)S(1)}, bf16[5,2,256,128]{3,2,1,0:T(8,128)(2,1)S(1)}, u32[]{:S(2)}, u32[]{:S(2)}) collective-permute-start(bf16[5,2,256,128]{3,2,1,0:T(8,128)(2,1)S(1)} %gate.19.refs_1_.refs_3_.refs_2_), channel_id=1, source_target_pairs={{0,2},{2,4},{4,6},{10,8},{12,10},{14,12},{1,3},{3,5},{5,7},{11,9},... | collective-permute-start | bytes 1966088 | tf_op jit(solution)/shard_map/cond/branch_0_fun/ppermute | solution.py:588
  30.9 20.1 %collective-permute-start.7 = (bf16[3,1,256,128]{3,2,1,0:T(8,128)(2,1)S(1)}, bf16[3,1,256,128]{3,2,1,0:T(8,128)(2,1)S(1)}, u32[]{:S(2)}, u32[]{:S(2)}) collective-permute-start(bf16[3,1,256,128]{3,2,1,0:T(8,128)(2,1)S(1)} %gate.20.refs_1_), channel_id=1, source_target_pairs={{0,8},{8,0},{1,9},{9,1},{2,10},{10,2},{3,11},{11,3},{4,12},{12,4},... | collective-permute-start | bytes 589832 | tf_op jit(solution)/shard_map/cond/branch_0_fun/ppermute | solution.py:548
  33.9 22.8 %collective-permute-start.10 = (bf16[5,2,256,128]{3,2,1,0:T(8,128)(2,1)S(1)}, bf16[5,2,256,128]{3,2,1,0:T(8,128)(2,1)S(1)}, u32[]{:S(2)}, u32[]{:S(2)}) collective-permute-start(bf16[5,2,256,128]{3,2,1,0:T(8,128)(2,1)S(1)} %gate.21.refs_1_), channel_id=1, source_target_pairs={{2,0},{4,2},{6,4},{8,10},{10,12},{12,14},{3,1},{5,3},{7,5},{9,11},... | collective-permute-start | bytes 1966088 | tf_op jit(solution)/shard_map/cond/branch_0_fun/ppermute | solution.py:596
  40.2 14.6 %collective-permute-start.9 = (bf16[8,1,256,128]{3,2,1,0:T(8,128)(2,1)S(1)}, bf16[8,1,256,128]{3,2,1,0:T(8,128)(2,1)S(1)}, u32[]{:S(2)}, u32[]{:S(2)}) collective-permute-start(bf16[8,1,256,128]{3,2,1,0:T(8,128)(2,1)S(1)} %gate.23.refs_2_), channel_id=1, source_target_pairs={{0,8},{8,0},{1,9},{9,1},{2,10},{10,2},{3,11},{11,3},{4,12},{12,4},... | collective-permute-start | bytes 1572872 | tf_op jit(solution)/shard_map/cond/branch_0_fun/ppermute | solution.py:548
  43.2 20.0 %collective-permute-start.8 = (bf16[6,2,256,128]{3,2,1,0:T(8,128)(2,1)S(1)}, bf16[6,2,256,128]{3,2,1,0:T(8,128)(2,1)S(1)}, u32[]{:S(2)}, u32[]{:S(2)}) collective-permute-start(bf16[6,2,256,128]{3,2,1,0:T(8,128)(2,1)S(1)} %gate.24.refs_5_.refs_1_.refs_2_), channel_id=1, source_target_pairs={{0,2},{2,4},{4,6},{10,8},{12,10},{14,12},{1,3},{3,5},{5,7},{11,9},... | collective-permute-start | bytes 2359304 | tf_op jit(solution)/shard_map/cond/branch_0_fun/ppermute | solution.py:604
  51.0 2.1 %collective-permute-start.6 = (bf16[5,256,128]{2,1,0:T(8,128)(2,1)S(1)}, bf16[5,256,128]{2,1,0:T(8,128)(2,1)S(1)}, u32[]{:S(2)}, u32[]{:S(2)}) collective-permute-start(bf16[5,256,128]{2,1,0:T(8,128)(2,1)S(1)} %attend.17.refs_3_.mine_ref), channel_id=1, source_target_pairs={{0,1},{1,0},{2,3},{3,2},{4,5},{5,4},{6,7},{7,6},{8,9},{9,8},{10,11... | collective-permute-start | bytes 983048 | tf_op jit(solution)/shard_map/cond/branch_0_fun/ppermute | solution.py:551
  52.5 1.5 %collective-permute-start.11 = (bf16[3,128,128]{2,1,0:T(8,128)(2,1)S(1)}, bf16[3,128,128]{2,1,0:T(8,128)(2,1)S(1)}, u32[]{:S(2)}, u32[]{:S(2)}) collective-permute-start(bf16[3,128,128]{2,1,0:T(8,128)(2,1)S(1)} %get-tuple-element.42), channel_id=1, source_target_pairs={{0,1},{1,0},{2,3},{3,2},{4,5},{5,4},{6,7},{7,6},{8,9},{9,8},{10,11... | collective-permute-start | bytes 294920 | tf_op jit(solution)/shard_map/cond/branch_0_fun/ppermute | solution.py:551
  54.1 6.4 %collective-permute-start.15 = (bf16[3,128,128]{2,1,0:T(8,128)(2,1)S(1)}, bf16[3,128,128]{2,1,0:T(8,128)(2,1)S(1)}, u32[]{:S(2)}, u32[]{:S(2)}) collective-permute-start(bf16[3,128,128]{2,1,0:T(8,128)(2,1)S(1)} %mix.17.refs_3_), channel_id=1, source_target_pairs={{0,8},{8,0},{1,9},{9,1},{2,10},{10,2},{3,11},{11,3},{4,12},{12,4},... | collective-permute-start | bytes 294920 | tf_op jit(solution)/shard_map/cond/branch_0_fun/ppermute | solution.py:548
  56.2 4.2 %collective-permute-start.14 = (bf16[3,128,128]{2,1,0:T(8,128)(2,1)S(1)}, bf16[3,128,128]{2,1,0:T(8,128)(2,1)S(1)}, u32[]{:S(2)}, u32[]{:S(2)}) collective-permute-start(bf16[3,128,128]{2,1,0:T(8,128)(2,1)S(1)} %get-tuple-element.46), channel_id=1, source_target_pairs={{0,1},{1,0},{2,3},{3,2},{4,5},{5,4},{6,7},{7,6},{8,9},{9,8},{10,11... | collective-permute-start | bytes 294920 | tf_op jit(solution)/shard_map/cond/branch_0_fun/ppermute | solution.py:551
  59.9 2.1 %collective-permute-start.13 = (bf16[3,128,128]{2,1,0:T(8,128)(2,1)S(1)}, bf16[3,128,128]{2,1,0:T(8,128)(2,1)S(1)}, u32[]{:S(2)}, u32[]{:S(2)}) collective-permute-start(bf16[3,128,128]{2,1,0:T(8,128)(2,1)S(1)} %slice.29), channel_id=1, source_target_pairs={{0,1},{1,0},{2,3},{3,2},{4,5},{5,4},{6,7},{7,6},{8,9},{9,8},{10,11... | collective-permute-start | bytes 294920 | tf_op jit(solution)/shard_map/cond/branch_0_fun/ppermute | solution.py:551
  60.0 2.0 %collective-permute-start.12 = (bf16[2,128,128]{2,1,0:T(8,128)(2,1)S(1)}, bf16[2,128,128]{2,1,0:T(8,128)(2,1)S(1)}, u32[]{:S(2)}, u32[]{:S(2)}) collective-permute-start(bf16[2,128,128]{2,1,0:T(8,128)(2,1)S(1)} %slice.28), channel_id=1, source_target_pairs={{0,1},{1,0},{2,3},{3,2},{4,5},{5,4},{6,7},{7,6},{8,9},{9,8},{10,11... | collective-permute-start | bytes 196616 | tf_op jit(solution)/shard_map/cond/branch_0_fun/ppermute | solution.py:551
  60.5 8.9 %collective-permute-start.18 = (bf16[3,128,128]{2,1,0:T(8,128)(2,1)S(1)}, bf16[3,128,128]{2,1,0:T(8,128)(2,1)S(1)}, u32[]{:S(2)}, u32[]{:S(2)}) collective-permute-start(bf16[3,128,128]{2,1,0:T(8,128)(2,1)S(1)} %mix.18.refs_2_), channel_id=1, source_target_pairs={{0,8},{8,0},{1,9},{9,1},{2,10},{10,2},{3,11},{11,3},{4,12},{12,4},... | collective-permute-start | bytes 294920 | tf_op jit(solution)/shard_map/cond/branch_0_fun/ppermute | solution.py:548
  62.1 6.8 %collective-permute-start.19 = (bf16[5,128,128]{2,1,0:T(8,128)(2,1)S(1)}, bf16[5,128,128]{2,1,0:T(8,128)(2,1)S(1)}, u32[]{:S(2)}, u32[]{:S(2)}) collective-permute-start(bf16[5,128,128]{2,1,0:T(8,128)(2,1)S(1)} %mix.19.refs_3_), channel_id=1, source_target_pairs={{0,8},{8,0},{1,9},{9,1},{2,10},{10,2},{3,11},{11,3},{4,12},{12,4},... | collective-permute-start | bytes 491528 | tf_op jit(solution)/shard_map/cond/branch_0_fun/ppermute | solution.py:548
  65.8 4.9 %collective-permute-start.16 = (bf16[3,256,128]{2,1,0:T(8,128)(2,1)S(1)}, bf16[3,256,128]{2,1,0:T(8,128)(2,1)S(1)}, u32[]{:S(2)}, u32[]{:S(2)}) collective-permute-start(bf16[3,256,128]{2,1,0:T(8,128)(2,1)S(1)} %get-tuple-element.91.refs_1_), channel_id=1, source_target_pairs={{0,1},{1,0},{2,3},{3,2},{4,5},{5,4},{6,7},{7,6},{8,9},{9,8},{10,11... | collective-permute-start | bytes 589832 | tf_op jit(solution)/shard_map/cond/branch_0_fun/ppermute | solution.py:551
  65.9 4.8 %collective-permute-start.17 = (bf16[3,256,128]{2,1,0:T(8,128)(2,1)S(1)}, bf16[3,256,128]{2,1,0:T(8,128)(2,1)S(1)}, u32[]{:S(2)}, u32[]{:S(2)}) collective-permute-start(bf16[3,256,128]{2,1,0:T(8,128)(2,1)S(1)} %get-tuple-element.90.refs_2_), channel_id=1, source_target_pairs={{0,1},{1,0},{2,3},{3,2},{4,5},{5,4},{6,7},{7,6},{8,9},{9,8},{10,11... | collective-permute-start | bytes 589832 | tf_op jit(solution)/shard_map/cond/branch_0_fun/ppermute | solution.py:551
  68.9 1.8 %collective-permute-start.22 = (bf16[5,128,128]{2,1,0:T(8,128)(2,1)S(1)}, bf16[5,128,128]{2,1,0:T(8,128)(2,1)S(1)}, u32[]{:S(2)}, u32[]{:S(2)}) collective-permute-start(bf16[5,128,128]{2,1,0:T(8,128)(2,1)S(1)} %collective-permute-done.19.refs_7_), channel_id=1, source_target_pairs={{0,1},{1,0},{2,3},{3,2},{4,5},{5,4},{6,7},{7,6},{8,9},{9,8},{10,11... | collective-permute-start | bytes 491528 | tf_op jit(solution)/shard_map/cond/branch_0_fun/ppermute | solution.py:551
  68.9 1.5 %collective-permute-start.20 = (bf16[3,128,128]{2,1,0:T(8,128)(2,1)S(1)}, bf16[3,128,128]{2,1,0:T(8,128)(2,1)S(1)}, u32[]{:S(2)}, u32[]{:S(2)}) collective-permute-start(bf16[3,128,128]{2,1,0:T(8,128)(2,1)S(1)} %collective-permute-done.15.refs_2_.refs_4_.refs_5_), channel_id=1, source_target_pairs={{0,1},{1,0},{2,3},{3,2},{4,5},{5,4},{6,7},{7,6},{8,9},{9,8},{10,11... | collective-permute-start | bytes 294920 | tf_op jit(solution)/shard_map/cond/branch_0_fun/ppermute | solution.py:551
  69.4 1.3 %collective-permute-start.21 = (bf16[3,128,128]{2,1,0:T(8,128)(2,1)S(1)}, bf16[3,128,128]{2,1,0:T(8,128)(2,1)S(1)}, u32[]{:S(2)}, u32[]{:S(2)}) collective-permute-start(bf16[3,128,128]{2,1,0:T(8,128)(2,1)S(1)} %collective-permute-done.18.refs_6_), channel_id=1, source_target_pairs={{0,1},{1,0},{2,3},{3,2},{4,5},{5,4},{6,7},{7,6},{8,9},{9,8},{10,11... | collective-permute-start | bytes 294920 | tf_op jit(solution)/shard_map/cond/branch_0_fun/ppermute | solution.py:551

commit v6 on v5

--- a/solution.py
+++ b/solution.py
@@ -94,6 +94,7 @@
 
 LOG2E = 1.4426950408889634
 MASKED = -1e30
+UNROLLED_BLOCKS = 25
 BF16 = jnp.bfloat16
 F32 = jnp.float32
 VMEM_BYTES = 32 * 1024 * 1024
@@ -145,8 +146,8 @@
 
 
 def plan_kernel(
-    at, rungs, split, windows_in, segments_in, step_in, x_ref, plan_ref, rung_ref, kv_ref, own_ref,
-    windows_ref, segments_ref, step_ref, in_sems, sems,
+    at, rungs, split, windows_in, segments_in, step_in, x_ref, plan_out, rung_out, kv_ref, own_ref,
+    windows_ref, segments_ref, step_ref, plan_ref, rung_ref, in_sems, out_sems, sems,
 ):
     get_windows = pltpu.make_async_copy(windows_in, windows_ref, in_sems.at[0])
     get_segments = pltpu.make_async_copy(segments_in, segments_ref, in_sems.at[1])
@@ -216,6 +217,9 @@
         fits = jnp.logical_and(many <= rungs[k][0], most <= rungs[k][1])
         index = jnp.where(fits, jnp.int32(k), index)
     rung_ref[0] = index
+    for k, (ref, out) in enumerate(((plan_ref, plan_out), (rung_ref, rung_out))):
+        copies.append(pltpu.make_async_copy(ref, out, out_sems.at[k]))
+        copies[-1].start()
     for copy in copies:
         copy.wait()
 
@@ -362,11 +366,12 @@
     kv_refs = refs[:sources]
     halves = cond_at is not None
     outs = refs[-2:] if halves else refs[-1:]
-    for j in range(count):
+
+    def one(j):
         keys = [ref[o + j, 0] for ref, o in zip(kv_refs, offsets)]
         values = [ref[o + j, 1] for ref, o in zip(kv_refs, offsets)]
         first = bias_at + j * len(DISTANCES)
-        biases = [table_ref[first + k : first + k + 1, :] for k in range(sources)]
+        biases = [table_ref[pl.ds(first + k, 1), :] for k in range(sources)]
         out = softmax_mix(q_ref[q_offset + j, 0], keys, values, biases)
         if halves:
             half = out.shape[0] // 2
@@ -376,6 +381,18 @@
             outs[1][j] = jnp.where(is_first, high, low).astype(BF16)
         else:
             outs[0][j] = out.astype(BF16)
+
+    pairs = 0 if count * sources <= UNROLLED_BLOCKS else count // 2
+
+    def two(i, carry):
+        one(2 * i)
+        one(2 * i + 1)
+        return carry
+
+    if pairs:
+        lax.fori_loop(0, pairs, two, 0)
+    for j in range(2 * pairs, count):
+        one(j)
 
 
 def attend_slots(table, q, q_offset, sources, count, bias_at, cond_at, after):
@@ -513,12 +530,15 @@
             jax.ShapeDtypeStruct((base, 2, rows, HD), BF16),
         ],
         in_specs=[whole(pltpu.HBM)] * 3 + [whole(pl.ANY)],
-        out_specs=[whole(pltpu.SMEM)] * 2 + [whole(pl.ANY)] * 2,
+        out_specs=[whole(pl.ANY)] * 4,
         scratch_shapes=[
             pltpu.SMEM(windows.shape, jnp.int32),
             pltpu.SMEM(segments.shape, jnp.int32),
             pltpu.SMEM(timestep.shape, jnp.int32),
+            pltpu.SMEM((at.size,), jnp.int32),
+            pltpu.SMEM((1,), jnp.int32),
             pltpu.SemaphoreType.DMA((3,)),
+            pltpu.SemaphoreType.DMA((2,)),
             pltpu.SemaphoreType.DMA((lead + base,)),
         ],
         compiler_params=params(PLAN_VMEM_BYTES),
@@ -557,9 +577,12 @@
         near_base = lax.ppermute(kv_base, grid_axes, apart)
         (kv_far,) = pack(plan, x3, [(range(at.mine, at.mine + lead), 1, 3)], [kv_base])
         far_own = [lax.ppermute(kv_far, grid_axes, onward)]
-        split = (lead + base) // 2
+        split = base
+        cut = 0
         parts = [(lead, split, 1), (split, base, 1)]
-        parts += [(lo, hi, k) for k, (lo, hi) in enumerate(bounds) if k > 1] + [(0, lead, 0)]
+        parts += [(lo, hi, k) for k, (lo, hi) in enumerate(bounds) if k > 1]
+        parts += [(0, cut, 0), (cut, lead, 0)]
+        parts = [(lo, hi, k) for lo, hi, k in parts if hi > lo]
         later = [slot for lo, hi, _ in parts[1:] for slot in range(lo, hi)]
         jobs = [
             ([at.theirs + slot for slot in slots_of], 0, 1)

time: 73.5 us -> 72 us (0.980)
  starting transfers between devices: 28.8 us -> 26.1 us
  waiting for transfers between devices: 17.6 us -> 19.8 us
  Pallas kernels: 24.3 us -> 23.5 us
    ppermute x7 -> x6, starting transfers between devices: 10.4 us -> 8.21 us  [cross(): return lax.ppermute(a, 'seq', SWAP)]
    ppermute x11 -> x9, waiting for transfers between devices: 2.09 us -> 3.19 us  [mate(): return lax.ppermute(a, 'cfg', SWAP)]
    ppermute x1, waiting for transfers between devices: 0.42 us -> 1.23 us  [attempt(): far_across[0] = lax.ppermute(late, grid_axes, apart)]
    ppermute x11 -> x9, starting transfers between devices: 2.43 us -> 1.91 us  [mate(): return lax.ppermute(a, 'cfg', SWAP)]
    pallas_call x5 -> x4, Pallas kernels: 11.7 us -> 11.5 us  [attend_slots(): pl.pallas_call(functools.partial(attend_kernel, count, q_offset, offsets,...]
    ppermute x7 -> x6, waiting for transfers between devices: 10.7 us -> 10.9 us  [cross(): return lax.ppermute(a, 'seq', SWAP)]
  transfers between devices with their start and end apart: 23 -> 20, of which waited for: 10 -> 10; matrix products, arithmetic and copies ran while one was open for 0% -> 0% of each run, Pallas kernels for 26% -> 26%
where the time goes in v6:
time: 72 us; the launch traced here: 71.8 us
  starting transfers between devices  26.1 us (36%)
  Pallas kernels  23.5 us (33%)
  waiting for transfers between devices  19.8 us (28%)
  between operations  1.53 us (2%)
  loops' own time  0.79 us (1%)
    pallas_call x4, Pallas kernels, attend_slots(): pl.pallas_call(functools.partial(attend_kernel, count, q_offset, offsets,...  11.5 us
    ppermute x6, waiting for transfers between devices, cross(): return lax.ppermute(a, 'seq', SWAP)  10.9 us
    ppermute x6, starting transfers between devices, cross(): return lax.ppermute(a, 'seq', SWAP)  8.21 us
    ppermute x1, starting transfers between devices, attempt(): far_own = [lax.ppermute(kv_far, grid_axes, onward)]  4.72 us
    ppermute x1, starting transfers between devices, attempt(): near_across[k] = lax.ppermute(across[k], grid_axes, onward)  4.6 us
    ppermute x1, starting transfers between devices, attempt(): near_across[0] = lax.ppermute(across[0], grid_axes, onward)  4.08 us
    pallas_call x2, Pallas kernels, pack(): pl.pallas_call(functools.partial(pack_kernel, jobs, len(after)), out_shap...  3.53 us
    ppermute x1, waiting for transfers between devices, attempt(): far_own = [lax.ppermute(kv_far, grid_axes, onward)]  3.48 us
  transfers between devices with their start and end apart: 20, of which 10 were waited for; matrix products, arithmetic and copies ran while one was open for 0% of the time, Pallas kernels for 26%

profile of v6, /device:TPU:0, one launch (start us, length us, event | category | flops | bytes accessed | tf_op | source)
XLA Modules:
  0.0 71.8 jit_solution(11590361721029568313)
XLA Ops:
  0.7 2.9 %plan.1 = (s32[173]{0:T(256)S(1)}, s32[1]{0:T(128)}, bf16[5,2,256,128]{3,2,1,0:T(8,128)(2,1)S(1)}, bf16[11,2,256,128]{3,2,1,0:T(8,128)(2,1)S(1)}) custom-call(s32[32]{0:T(128)} %windows_in.1, s32[8]{0:T(128)} %segments_in.1, s32[1]{0:T(128)S(6)} %copy.49.step_in, bf16[3,256,4096]{2,1,0:T(8,128)(2,1)} %bitcast.4), custom_call_target="tpu_custom_call" | custom-call | tf_op jit(solution)/shard_map/plan/pallas_call | solution.py:524
  4.2 67.4 %conditional.1 = (bf16[256,8,256]{2,1,0:T(8,128)(2,1)}) conditional(s32[]{:T(128)} %bitcast.2, (s32[173]{0:T(256)S(1)}, bf16[3,256,4096]{2,1,0:T(8,128)(2,1)}, bf16[11,2,256,128]{3,2,1,0:T(8,128)(2,1)S(1)}, bf16[5,2,256,128]{3,2,1,0:T(8,128)(2,1)S(1)}) %tuple.24, (s32[173]{0:T(256)S(1)}, bf16[3,256,4096]{2,1,0:T(8,128)(2,1)}, ...), branch_computations={%region_0.0_spmd, %region_1.0_spmd, %region_2.0_spmd} | conditional | flops 45499998208 | bytes 84870360 | solution.py:704
  4.2 3.0 %collective-permute-start.1 = (bf16[5,2,256,128]{3,2,1,0:T(8,128)(2,1)S(1)}, bf16[5,2,256,128]{3,2,1,0:T(8,128)(2,1)S(1)}, u32[]{:S(2)}, u32[]{:S(2)}) collective-permute-start(bf16[5,2,256,128]{3,2,1,0:T(8,128)(2,1)S(1)} %get-tuple-element.38), channel_id=1, source_target_pairs={{0,8},{8,0},{1,9},{9,1},{2,10},{10,2},{3,11},{11,3},{4,12},{12,4},... | collective-permute-start | bytes 1966088 | tf_op jit(solution)/shard_map/cond/branch_0_fun/ppermute | solution.py:568
  7.2 1.3 %collective-permute-start.3 = (bf16[11,2,256,128]{3,2,1,0:T(8,128)(2,1)S(1)}, bf16[11,2,256,128]{3,2,1,0:T(8,128)(2,1)S(1)}, u32[]{:S(2)}, u32[]{:S(2)}) collective-permute-start(bf16[11,2,256,128]{3,2,1,0:T(8,128)(2,1)S(1)} %get-tuple-element.35.refs_0_.refs_2_.refs_1_), channel_id=1, source_target_pairs={{2,0},{4,2},{6,4},{8,10},{10,12},{12,14},{3,1},{5,3},{7,5},{9,11},... | collective-permute-start | bytes 4325384 | tf_op jit(solution)/shard_map/cond/branch_0_fun/ppermute | solution.py:577
  8.5 2.0 %pack_heads.6.refs_0_ = bf16[5,2,256,128]{3,2,1,0:T(8,128)(2,1)S(1)} custom-call(s32[173]{0:T(256)S(1)} %get-tuple-element.32.plan_ref.plan_in, bf16[3,256,4096]{2,1,0:T(8,128)(2,1)} %get-tuple-element.34.x_ref, bf16[11,2,256,128]{3,2,1,0:T(8,128)(2,1)S(1)} %get-tuple-element.35.refs_0_.refs_2_.refs_1_), custom_call_target="tpu_custom_call" | custom-call | flops 10000000000 | bytes 1 | tf_op jit(solution)/shard_map/cond/branch_0_fun/pack_heads/pallas_call | solution.py:248
  10.5 4.7 %collective-permute-start = (bf16[5,2,256,128]{3,2,1,0:T(8,128)(2,1)S(1)}, bf16[5,2,256,128]{3,2,1,0:T(8,128)(2,1)S(1)}, u32[]{:S(2)}, u32[]{:S(2)}) collective-permute-start(bf16[5,2,256,128]{3,2,1,0:T(8,128)(2,1)S(1)} %pack_heads.6.refs_0_), channel_id=1, source_target_pairs={{0,2},{2,4},{4,6},{10,8},{12,10},{14,12},{1,3},{3,5},{5,7},{11,9},... | collective-permute-start | bytes 1966088 | tf_op jit(solution)/shard_map/cond/branch_0_fun/ppermute | solution.py:579
  15.3 1.5 %pack_heads.7 = (bf16[11,1,256,128]{3,2,1,0:T(8,128)(2,1)S(1)}, bf16[6,1,256,128]{3,2,1,0:T(8,128)(2,1)S(1)}, bf16[5,1,256,128]{3,2,1,0:T(8,128)(2,1)S(1)}, bf16[6,2,256,128]{3,2,1,0:T(8,128)(2,1)S(1)}) custom-call(s32[173]{0:T(256)S(1)} %get-tuple-element.32.plan_ref.plan_in, bf16[3,256,4096]{2,1,0:T(8,128)(2,1)S(1)} %copy-done, ...), custom_call_target="tpu_custom_call" | custom-call | flops 10000000000 | bytes 1 | tf_op jit(solution)/shard_map/cond/branch_0_fun/pack_heads/pallas_call | solution.py:248
  17.6 2.5 %attend_local.2.refs_1_.mine_ref = bf16[10,256,128]{2,1,0:T(8,128)(2,1)S(1)} custom-call(s32[173]{0:T(256)S(1)} %get-tuple-element.32.plan_ref.plan_in, bf16[3,256,4096]{2,1,0:T(8,128)(2,1)S(1)} %copy-done, f32[168,256]{1,0:T(8,128)S(1)} %table.3.refs_0_.table_ref), custom_call_target="tpu_custom_call" | custom-call | flops 3000000000 | bytes 1 | tf_op jit(solution)/shard_map/cond/branch_0_fun/attend_local/pallas_call | solution.py:349
  20.2 2.6 %collective-permute-done.1.refs_0_ = bf16[5,2,256,128]{3,2,1,0:T(8,128)(2,1)S(1)} collective-permute-done((bf16[5,2,256,128]{3,2,1,0:T(8,128)(2,1)S(1)}, bf16[5,2,256,128]{3,2,1,0:T(8,128)(2,1)S(1)}, u32[]{:S(2)}, u32[]{:S(2)}) %collective-permute-start.1) | collective-permute-done | bytes 655392 | tf_op jit(solution)/shard_map/cond/branch_0_fun/ppermute | solution.py:568
  22.8 4.1 %collective-permute-start.2 = (bf16[5,2,256,128]{3,2,1,0:T(8,128)(2,1)S(1)}, bf16[5,2,256,128]{3,2,1,0:T(8,128)(2,1)S(1)}, u32[]{:S(2)}, u32[]{:S(2)}) collective-permute-start(bf16[5,2,256,128]{3,2,1,0:T(8,128)(2,1)S(1)} %gate.19.refs_1_.refs_3_.refs_2_), channel_id=1, source_target_pairs={{0,2},{2,4},{4,6},{10,8},{12,10},{14,12},{1,3},{3,5},{5,7},{11,9},... | collective-permute-start | bytes 1966088 | tf_op jit(solution)/shard_map/cond/branch_0_fun/ppermute | solution.py:611
  26.9 3.5 %collective-permute-done.refs_2_.refs_0_ = bf16[5,2,256,128]{3,2,1,0:T(8,128)(2,1)S(1)} collective-permute-done((bf16[5,2,256,128]{3,2,1,0:T(8,128)(2,1)S(1)}, bf16[5,2,256,128]{3,2,1,0:T(8,128)(2,1)S(1)}, u32[]{:S(2)}, u32[]{:S(2)}) %collective-permute-start) | collective-permute-done | bytes 655392 | tf_op jit(solution)/shard_map/cond/branch_0_fun/ppermute | solution.py:579
  30.4 2.7 %collective-permute-start.7 = (bf16[6,1,256,128]{3,2,1,0:T(8,128)(2,1)S(1)}, bf16[6,1,256,128]{3,2,1,0:T(8,128)(2,1)S(1)}, u32[]{:S(2)}, u32[]{:S(2)}) collective-permute-start(bf16[6,1,256,128]{3,2,1,0:T(8,128)(2,1)S(1)} %gate.20.refs_1_), channel_id=1, source_target_pairs={{0,8},{8,0},{1,9},{9,1},{2,10},{10,2},{3,11},{11,3},{4,12},{12,4},... | collective-permute-start | bytes 1179656 | tf_op jit(solution)/shard_map/cond/branch_0_fun/ppermute | solution.py:568
  33.4 1.3 %collective-permute-start.10 = (bf16[5,2,256,128]{3,2,1,0:T(8,128)(2,1)S(1)}, bf16[5,2,256,128]{3,2,1,0:T(8,128)(2,1)S(1)}, u32[]{:S(2)}, u32[]{:S(2)}) collective-permute-start(bf16[5,2,256,128]{3,2,1,0:T(8,128)(2,1)S(1)} %gate.21.refs_1_), channel_id=1, source_target_pairs={{2,0},{4,2},{6,4},{8,10},{10,12},{12,14},{3,1},{5,3},{7,5},{9,11},... | collective-permute-start | bytes 1966088 | tf_op jit(solution)/shard_map/cond/branch_0_fun/ppermute | solution.py:619
  34.7 4.9 %collective-permute-done.4.refs_0_ = bf16[6,2,256,128]{3,2,1,0:T(8,128)(2,1)S(1)} collective-permute-done((bf16[6,2,256,128]{3,2,1,0:T(8,128)(2,1)S(1)}, bf16[6,2,256,128]{3,2,1,0:T(8,128)(2,1)S(1)}, u32[]{:S(2)}, u32[]{:S(2)}) %collective-permute-start.4) | collective-permute-done | bytes 786464 | tf_op jit(solution)/shard_map/cond/branch_0_fun/ppermute | solution.py:568
  39.6 2.1 %collective-permute-start.9 = (bf16[5,1,256,128]{3,2,1,0:T(8,128)(2,1)S(1)}, bf16[5,1,256,128]{3,2,1,0:T(8,128)(2,1)S(1)}, u32[]{:S(2)}, u32[]{:S(2)}) collective-permute-start(bf16[5,1,256,128]{3,2,1,0:T(8,128)(2,1)S(1)} %gate.23.refs_2_), channel_id=1, source_target_pairs={{0,8},{8,0},{1,9},{9,1},{2,10},{10,2},{3,11},{11,3},{4,12},{12,4},... | collective-permute-start | bytes 983048 | tf_op jit(solution)/shard_map/cond/branch_0_fun/ppermute | solution.py:568
  42.7 4.6 %collective-permute-start.8 = (bf16[6,2,256,128]{3,2,1,0:T(8,128)(2,1)S(1)}, bf16[6,2,256,128]{3,2,1,0:T(8,128)(2,1)S(1)}, u32[]{:S(2)}, u32[]{:S(2)}) collective-permute-start(bf16[6,2,256,128]{3,2,1,0:T(8,128)(2,1)S(1)} %gate.24.refs_5_.refs_1_.refs_2_), channel_id=1, source_target_pairs={{0,2},{2,4},{4,6},{10,8},{12,10},{14,12},{1,3},{3,5},{5,7},{11,9},... | collective-permute-start | bytes 2359304 | tf_op jit(solution)/shard_map/cond/branch_0_fun/ppermute | solution.py:627
  47.3 3.1 %attend.14.refs_3_.mine_ref = bf16[5,256,128]{2,1,0:T(8,128)(2,1)S(1)} custom-call(f32[168,256]{1,0:T(8,128)S(1)} %table.3.refs_0_.table_ref, bf16[11,1,256,128]{3,2,1,0:T(8,128)(2,1)S(1)} %get-tuple-element.37.q_ref, bf16[5,2,256,128]{3,2,1,0:T(8,128)(2,1)S(1)} %collective-permute-done.refs_2_.refs_0_, ...), custom_call_target="tpu_custom_call" | custom-call | flops 3000000000 | bytes 1 | tf_op jit(solution)/shard_map/cond/branch_0_fun/attend/pallas_call | solution.py:408
  50.5 2.6 %attend.15 = (bf16[6,128,128]{2,1,0:T(8,128)(2,1)S(1)}, bf16[6,128,128]{2,1,0:T(8,128)(2,1)S(1)}) custom-call(f32[168,256]{1,0:T(8,128)S(1)} %table.3.refs_0_.table_ref, bf16[6,1,256,128]{3,2,1,0:T(8,128)(2,1)S(1)} %collective-permute-done.7.q_ref, bf16[11,2,256,128]{3,2,1,0:T(8,128)(2,1)S(1)} %get-tuple-element.35.refs_0_.refs_2_.refs_1_, ...), custom_call_target="tpu_custom_call" | custom-call | flops 3000000000 | bytes 1 | tf_op jit(solution)/shard_map/cond/branch_0_fun/attend/pallas_call | solution.py:408
  56.2 3.1 %attend.16 = (bf16[5,128,128]{2,1,0:T(8,128)(2,1)S(1)}, bf16[5,128,128]{2,1,0:T(8,128)(2,1)S(1)}) custom-call(f32[168,256]{1,0:T(8,128)S(1)} %table.3.refs_0_.table_ref, bf16[5,1,256,128]{3,2,1,0:T(8,128)(2,1)S(1)} %collective-permute-done.9.q_ref, bf16[5,2,256,128]{3,2,1,0:T(8,128)(2,1)S(1)} %collective-permute-done.2.refs_1_.refs_0_, ...), custom_call_target="tpu_custom_call" | custom-call | flops 3000000000 | bytes 1 | tf_op jit(solution)/shard_map/cond/branch_0_fun/attend/pallas_call | solution.py:408
  60.8 1.3 %collective-permute-done.14.refs_3_.refs_4_.refs_5_ = bf16[6,128,128]{2,1,0:T(8,128)(2,1)S(1)} collective-permute-done((bf16[6,128,128]{2,1,0:T(8,128)(2,1)S(1)}, bf16[6,128,128]{2,1,0:T(8,128)(2,1)S(1)}, u32[]{:S(2)}, u32[]{:S(2)}) %collective-permute-start.14) | collective-permute-done | bytes 196640 | tf_op jit(solution)/shard_map/cond/branch_0_fun/ppermute | solution.py:568
  62.5 2.6 %attend.17 = bf16[6,256,128]{2,1,0:T(8,128)(2,1)S(1)} custom-call(f32[168,256]{1,0:T(8,128)S(1)} %table.3.refs_0_.table_ref, bf16[11,1,256,128]{3,2,1,0:T(8,128)(2,1)S(1)} %get-tuple-element.37.q_ref, bf16[6,2,256,128]{3,2,1,0:T(8,128)(2,1)S(1)} %collective-permute-done.8.refs_0_, bf16[11,2,256,128]{3,2,1,0:T(8,128)(2,1)S(1)} %get-tuple-element.35.refs_0_.refs_2_.refs_1_, ...), custom_call_target="tpu_custom_call" | custom-call | flops 3000000000 | bytes 1 | tf_op jit(solution)/shard_map/cond/branch_0_fun/attend/pallas_call | solution.py:408
  65.8 2.1 %collective-permute-done.17.refs_6_ = bf16[5,128,128]{2,1,0:T(8,128)(2,1)S(1)} collective-permute-done((bf16[5,128,128]{2,1,0:T(8,128)(2,1)S(1)}, bf16[5,128,128]{2,1,0:T(8,128)(2,1)S(1)}, u32[]{:S(2)}, u32[]{:S(2)}) %collective-permute-start.17) | collective-permute-done | bytes 163872 | tf_op jit(solution)/shard_map/cond/branch_0_fun/ppermute | solution.py:568
  67.9 1.4 %collective-permute-done.19.refs_8_ = bf16[5,128,128]{2,1,0:T(8,128)(2,1)S(1)} collective-permute-done((bf16[5,128,128]{2,1,0:T(8,128)(2,1)S(1)}, bf16[5,128,128]{2,1,0:T(8,128)(2,1)S(1)}, u32[]{:S(2)}, u32[]{:S(2)}) %collective-permute-start.19) | collective-permute-done | bytes 163872 | tf_op jit(solution)/shard_map/cond/branch_0_fun/ppermute | solution.py:571
  69.3 1.7 %assemble.3 = bf16[256,8,256]{2,1,0:T(8,128)(2,1)} custom-call(s32[173]{0:T(256)S(1)} %get-tuple-element.32.plan_ref.plan_in, f32[168,256]{1,0:T(8,128)S(1)} %table.3.refs_0_.table_ref, bf16[5,256,128]{2,1,0:T(8,128)(2,1)S(1)} %mix.13.refs_1_.refs_0_, bf16[3,256,128]{2,1,0:T(8,128)(2,1)S(1)} %get-tuple-element.85.refs_1_, ...), custom_call_target="tpu_custom_call" | custom-call | tf_op jit(solution)/shard_map/cond/branch_0_fun/assemble/pallas_call | solution.py:688
  (43 shorter events, 7.9 us)
Async XLA Ops:
  4.2 18.6 %collective-permute-start.1 = (bf16[5,2,256,128]{3,2,1,0:T(8,128)(2,1)S(1)}, bf16[5,2,256,128]{3,2,1,0:T(8,128)(2,1)S(1)}, u32[]{:S(2)}, u32[]{:S(2)}) collective-permute-start(bf16[5,2,256,128]{3,2,1,0:T(8,128)(2,1)S(1)} %get-tuple-element.38), channel_id=1, source_target_pairs={{0,8},{8,0},{1,9},{9,1},{2,10},{10,2},{3,11},{11,3},{4,12},{12,4},... | collective-permute-start | bytes 1966088 | tf_op jit(solution)/shard_map/cond/branch_0_fun/ppermute | solution.py:568
  7.2 40.1 %collective-permute-start.3 = (bf16[11,2,256,128]{3,2,1,0:T(8,128)(2,1)S(1)}, bf16[11,2,256,128]{3,2,1,0:T(8,128)(2,1)S(1)}, u32[]{:S(2)}, u32[]{:S(2)}) collective-permute-start(bf16[11,2,256,128]{3,2,1,0:T(8,128)(2,1)S(1)} %get-tuple-element.35.refs_0_.refs_2_.refs_1_), channel_id=1, source_target_pairs={{2,0},{4,2},{6,4},{8,10},{10,12},{12,14},{3,1},{5,3},{7,5},{9,11},... | collective-permute-start | bytes 4325384 | tf_op jit(solution)/shard_map/cond/branch_0_fun/ppermute | solution.py:577
  8.5 6.8 %copy-start = (bf16[3,256,4096]{2,1,0:T(8,128)(2,1)S(1)}, bf16[3,256,4096]{2,1,0:T(8,128)(2,1)}, u32[]{:S(2)}) copy-start(bf16[3,256,4096]{2,1,0:T(8,128)(2,1)} %get-tuple-element.34.x_ref) | copy-start | bytes 18874372 | tf_op jit(solution)/shard_map/cond
  10.5 19.9 %collective-permute-start = (bf16[5,2,256,128]{3,2,1,0:T(8,128)(2,1)S(1)}, bf16[5,2,256,128]{3,2,1,0:T(8,128)(2,1)S(1)}, u32[]{:S(2)}, u32[]{:S(2)}) collective-permute-start(bf16[5,2,256,128]{3,2,1,0:T(8,128)(2,1)S(1)} %pack_heads.6.refs_0_), channel_id=1, source_target_pairs={{0,2},{2,4},{4,6},{10,8},{12,10},{14,12},{1,3},{3,5},{5,7},{11,9},... | collective-permute-start | bytes 1966088 | tf_op jit(solution)/shard_map/cond/branch_0_fun/ppermute | solution.py:579
  16.8 22.8 %collective-permute-start.4 = (bf16[6,2,256,128]{3,2,1,0:T(8,128)(2,1)S(1)}, bf16[6,2,256,128]{3,2,1,0:T(8,128)(2,1)S(1)}, u32[]{:S(2)}, u32[]{:S(2)}) collective-permute-start(bf16[6,2,256,128]{3,2,1,0:T(8,128)(2,1)S(1)} %get-tuple-element.36.refs_0_), channel_id=1, source_target_pairs={{0,8},{8,0},{1,9},{9,1},{2,10},{10,2},{3,11},{11,3},{4,12},{12,4},... | collective-permute-start | bytes 2359304 | tf_op jit(solution)/shard_map/cond/branch_0_fun/ppermute | solution.py:568
  20.1 12.9 %collective-permute-start.5 = (bf16[10,256,128]{2,1,0:T(8,128)(2,1)S(1)}, bf16[10,256,128]{2,1,0:T(8,128)(2,1)S(1)}, u32[]{:S(2)}, u32[]{:S(2)}) collective-permute-start(bf16[10,256,128]{2,1,0:T(8,128)(2,1)S(1)} %attend_local.2.refs_1_.mine_ref), channel_id=1, source_target_pairs={{0,1},{1,0},{2,3},{3,2},{4,5},{5,4},{6,7},{7,6},{8,9},{9,8},{10,11... | collective-permute-start | bytes 1966088 | tf_op jit(solution)/shard_map/cond/branch_0_fun/ppermute | solution.py:571
  22.8 19.9 %collective-permute-start.2 = (bf16[5,2,256,128]{3,2,1,0:T(8,128)(2,1)S(1)}, bf16[5,2,256,128]{3,2,1,0:T(8,128)(2,1)S(1)}, u32[]{:S(2)}, u32[]{:S(2)}) collective-permute-start(bf16[5,2,256,128]{3,2,1,0:T(8,128)(2,1)S(1)} %gate.19.refs_1_.refs_3_.refs_2_), channel_id=1, source_target_pairs={{0,2},{2,4},{4,6},{10,8},{12,10},{14,12},{1,3},{3,5},{5,7},{11,9},... | collective-permute-start | bytes 1966088 | tf_op jit(solution)/shard_map/cond/branch_0_fun/ppermute | solution.py:611
  30.4 20.1 %collective-permute-start.7 = (bf16[6,1,256,128]{3,2,1,0:T(8,128)(2,1)S(1)}, bf16[6,1,256,128]{3,2,1,0:T(8,128)(2,1)S(1)}, u32[]{:S(2)}, u32[]{:S(2)}) collective-permute-start(bf16[6,1,256,128]{3,2,1,0:T(8,128)(2,1)S(1)} %gate.20.refs_1_), channel_id=1, source_target_pairs={{0,8},{8,0},{1,9},{9,1},{2,10},{10,2},{3,11},{11,3},{4,12},{12,4},... | collective-permute-start | bytes 1179656 | tf_op jit(solution)/shard_map/cond/branch_0_fun/ppermute | solution.py:568
  33.4 22.8 %collective-permute-start.10 = (bf16[5,2,256,128]{3,2,1,0:T(8,128)(2,1)S(1)}, bf16[5,2,256,128]{3,2,1,0:T(8,128)(2,1)S(1)}, u32[]{:S(2)}, u32[]{:S(2)}) collective-permute-start(bf16[5,2,256,128]{3,2,1,0:T(8,128)(2,1)S(1)} %gate.21.refs_1_), channel_id=1, source_target_pairs={{2,0},{4,2},{6,4},{8,10},{10,12},{12,14},{3,1},{5,3},{7,5},{9,11},... | collective-permute-start | bytes 1966088 | tf_op jit(solution)/shard_map/cond/branch_0_fun/ppermute | solution.py:619
  39.6 15.3 %collective-permute-start.9 = (bf16[5,1,256,128]{3,2,1,0:T(8,128)(2,1)S(1)}, bf16[5,1,256,128]{3,2,1,0:T(8,128)(2,1)S(1)}, u32[]{:S(2)}, u32[]{:S(2)}) collective-permute-start(bf16[5,1,256,128]{3,2,1,0:T(8,128)(2,1)S(1)} %gate.23.refs_2_), channel_id=1, source_target_pairs={{0,8},{8,0},{1,9},{9,1},{2,10},{10,2},{3,11},{11,3},{4,12},{12,4},... | collective-permute-start | bytes 983048 | tf_op jit(solution)/shard_map/cond/branch_0_fun/ppermute | solution.py:568
  42.7 19.9 %collective-permute-start.8 = (bf16[6,2,256,128]{3,2,1,0:T(8,128)(2,1)S(1)}, bf16[6,2,256,128]{3,2,1,0:T(8,128)(2,1)S(1)}, u32[]{:S(2)}, u32[]{:S(2)}) collective-permute-start(bf16[6,2,256,128]{3,2,1,0:T(8,128)(2,1)S(1)} %gate.24.refs_5_.refs_1_.refs_2_), channel_id=1, source_target_pairs={{0,2},{2,4},{4,6},{10,8},{12,10},{14,12},{1,3},{3,5},{5,7},{11,9},... | collective-permute-start | bytes 2359304 | tf_op jit(solution)/shard_map/cond/branch_0_fun/ppermute | solution.py:627
  50.4 3.3 %collective-permute-start.6 = (bf16[5,256,128]{2,1,0:T(8,128)(2,1)S(1)}, bf16[5,256,128]{2,1,0:T(8,128)(2,1)S(1)}, u32[]{:S(2)}, u32[]{:S(2)}) collective-permute-start(bf16[5,256,128]{2,1,0:T(8,128)(2,1)S(1)} %attend.14.refs_3_.mine_ref), channel_id=1, source_target_pairs={{0,1},{1,0},{2,3},{3,2},{4,5},{5,4},{6,7},{7,6},{8,9},{9,8},{10,11... | collective-permute-start | bytes 983048 | tf_op jit(solution)/shard_map/cond/branch_0_fun/ppermute | solution.py:571
  53.1 1.6 %collective-permute-start.11 = (bf16[6,128,128]{2,1,0:T(8,128)(2,1)S(1)}, bf16[6,128,128]{2,1,0:T(8,128)(2,1)S(1)}, u32[]{:S(2)}, u32[]{:S(2)}) collective-permute-start(bf16[6,128,128]{2,1,0:T(8,128)(2,1)S(1)} %get-tuple-element.42), channel_id=1, source_target_pairs={{0,1},{1,0},{2,3},{3,2},{4,5},{5,4},{6,7},{7,6},{8,9},{9,8},{10,11... | collective-permute-start | bytes 589832 | tf_op jit(solution)/shard_map/cond/branch_0_fun/ppermute | solution.py:571
  54.9 7.2 %collective-permute-start.14 = (bf16[6,128,128]{2,1,0:T(8,128)(2,1)S(1)}, bf16[6,128,128]{2,1,0:T(8,128)(2,1)S(1)}, u32[]{:S(2)}, u32[]{:S(2)}) collective-permute-start(bf16[6,128,128]{2,1,0:T(8,128)(2,1)S(1)} %mix.14.refs_5_), channel_id=1, source_target_pairs={{0,8},{8,0},{1,9},{9,1},{2,10},{10,2},{3,11},{11,3},{4,12},{12,4},... | collective-permute-start | bytes 589832 | tf_op jit(solution)/shard_map/cond/branch_0_fun/ppermute | solution.py:568
  59.3 1.5 %collective-permute-start.13 = (bf16[3,128,128]{2,1,0:T(8,128)(2,1)S(1)}, bf16[3,128,128]{2,1,0:T(8,128)(2,1)S(1)}, u32[]{:S(2)}, u32[]{:S(2)}) collective-permute-start(bf16[3,128,128]{2,1,0:T(8,128)(2,1)S(1)} %slice.29), channel_id=1, source_target_pairs={{0,1},{1,0},{2,3},{3,2},{4,5},{5,4},{6,7},{7,6},{8,9},{9,8},{10,11... | collective-permute-start | bytes 294920 | tf_op jit(solution)/shard_map/cond/branch_0_fun/ppermute | solution.py:571
  59.4 1.4 %collective-permute-start.12 = (bf16[2,128,128]{2,1,0:T(8,128)(2,1)S(1)}, bf16[2,128,128]{2,1,0:T(8,128)(2,1)S(1)}, u32[]{:S(2)}, u32[]{:S(2)}) collective-permute-start(bf16[2,128,128]{2,1,0:T(8,128)(2,1)S(1)} %slice.28), channel_id=1, source_target_pairs={{0,1},{1,0},{2,3},{3,2},{4,5},{5,4},{6,7},{7,6},{8,9},{9,8},{10,11... | collective-permute-start | bytes 196616 | tf_op jit(solution)/shard_map/cond/branch_0_fun/ppermute | solution.py:571
  62.2 5.7 %collective-permute-start.17 = (bf16[5,128,128]{2,1,0:T(8,128)(2,1)S(1)}, bf16[5,128,128]{2,1,0:T(8,128)(2,1)S(1)}, u32[]{:S(2)}, u32[]{:S(2)}) collective-permute-start(bf16[5,128,128]{2,1,0:T(8,128)(2,1)S(1)} %mix.15.refs_3_), channel_id=1, source_target_pairs={{0,8},{8,0},{1,9},{9,1},{2,10},{10,2},{3,11},{11,3},{4,12},{12,4},... | collective-permute-start | bytes 491528 | tf_op jit(solution)/shard_map/cond/branch_0_fun/ppermute | solution.py:568
  62.5 5.4 %collective-permute-start.18 = (bf16[6,128,128]{2,1,0:T(8,128)(2,1)S(1)}, bf16[6,128,128]{2,1,0:T(8,128)(2,1)S(1)}, u32[]{:S(2)}, u32[]{:S(2)}) collective-permute-start(bf16[6,128,128]{2,1,0:T(8,128)(2,1)S(1)} %collective-permute-done.14.refs_3_.refs_4_.refs_5_), channel_id=1, source_target_pairs={{0,1},{1,0},{2,3},{3,2},{4,5},{5,4},{6,7},{7,6},{8,9},{9,8},{10,11... | collective-permute-start | bytes 589832 | tf_op jit(solution)/shard_map/cond/branch_0_fun/ppermute | solution.py:571
  65.2 2.7 %collective-permute-start.15 = (bf16[3,256,128]{2,1,0:T(8,128)(2,1)S(1)}, bf16[3,256,128]{2,1,0:T(8,128)(2,1)S(1)}, u32[]{:S(2)}, u32[]{:S(2)}) collective-permute-start(bf16[3,256,128]{2,1,0:T(8,128)(2,1)S(1)} %get-tuple-element.85.refs_1_), channel_id=1, source_target_pairs={{0,1},{1,0},{2,3},{3,2},{4,5},{5,4},{6,7},{7,6},{8,9},{9,8},{10,11... | collective-permute-start | bytes 589832 | tf_op jit(solution)/shard_map/cond/branch_0_fun/ppermute | solution.py:571
  65.7 2.2 %collective-permute-start.16 = (bf16[3,256,128]{2,1,0:T(8,128)(2,1)S(1)}, bf16[3,256,128]{2,1,0:T(8,128)(2,1)S(1)}, u32[]{:S(2)}, u32[]{:S(2)}) collective-permute-start(bf16[3,256,128]{2,1,0:T(8,128)(2,1)S(1)} %get-tuple-element.84.refs_2_), channel_id=1, source_target_pairs={{0,1},{1,0},{2,3},{3,2},{4,5},{5,4},{6,7},{7,6},{8,9},{9,8},{10,11... | collective-permute-start | bytes 589832 | tf_op jit(solution)/shard_map/cond/branch_0_fun/ppermute | solution.py:571
  67.9 1.4 %collective-permute-start.19 = (bf16[5,128,128]{2,1,0:T(8,128)(2,1)S(1)}, bf16[5,128,128]{2,1,0:T(8,128)(2,1)S(1)}, u32[]{:S(2)}, u32[]{:S(2)}) collective-permute-start(bf16[5,128,128]{2,1,0:T(8,128)(2,1)S(1)} %collective-permute-done.17.refs_6_), channel_id=1, source_target_pairs={{0,1},{1,0},{2,3},{3,2},{4,5},{5,4},{6,7},{7,6},{8,9},{9,8},{10,11... | collective-permute-start | bytes 491528 | tf_op jit(solution)/shard_map/cond/branch_0_fun/ppermute | solution.py:571

commit v7 on v6

--- a/solution.py
+++ b/solution.py
@@ -252,7 +252,7 @@
             for spots, first, last in jobs
         ],
         in_specs=[whole(pltpu.SMEM)] + [whole(pl.ANY)] * (1 + len(after)),
-        out_specs=[whole(pl.ANY)] * len(jobs),
+        out_specs=[whole()] * len(jobs),
         scratch_shapes=[pltpu.SemaphoreType.DMA((sum(len(spots) for spots, _, _ in jobs),))],
         compiler_params=params(),
         cost_estimate=cost("pack"),
@@ -361,7 +361,7 @@
     )(plan, x3, *after)
 
 
-def attend_kernel(count, q_offset, offsets, bias_at, cond_at, table_ref, q_ref, *refs):
+def attend_kernel(count, q_offset, offsets, always, bias_at, cond_at, table_ref, q_ref, *refs):
     sources = len(offsets)
     kv_refs = refs[:sources]
     halves = cond_at is not None
@@ -371,7 +371,9 @@
         keys = [ref[o + j, 0] for ref, o in zip(kv_refs, offsets)]
         values = [ref[o + j, 1] for ref, o in zip(kv_refs, offsets)]
         first = bias_at + j * len(DISTANCES)
-        biases = [table_ref[pl.ds(first + k, 1), :] for k in range(sources)]
+        biases = [
+            None if k == always else table_ref[pl.ds(first + k, 1), :] for k in range(sources)
+        ]
         out = softmax_mix(q_ref[q_offset + j, 0], keys, values, biases)
         if halves:
             half = out.shape[0] // 2
@@ -395,7 +397,7 @@
         one(j)
 
 
-def attend_slots(table, q, q_offset, sources, count, bias_at, cond_at, after):
+def attend_slots(table, q, q_offset, sources, always, count, bias_at, cond_at, after):
     rows = q.shape[-2]
     if cond_at is None:
         out_shape = jax.ShapeDtypeStruct((count, rows, HD), BF16)
@@ -406,7 +408,7 @@
     arrays = [array for array, _ in sources]
     offsets = [offset for _, offset in sources]
     return pl.pallas_call(
-        functools.partial(attend_kernel, count, q_offset, offsets, bias_at, cond_at),
+        functools.partial(attend_kernel, count, q_offset, offsets, always, bias_at, cond_at),
         out_shape=out_shape,
         in_specs=[whole()] * (2 + len(arrays)) + [whole(pl.ANY)] * len(after),
         out_specs=out_specs,
@@ -474,17 +476,15 @@
     for ref, other, first in zip(raw, raw_other, places[1]):
         for j in range(ref.shape[0]):
             listed[first + j] = mix_branches(rows_at, table_ref, ref[j], other[j])
-    low_here = table_ref[rows_at.cond : rows_at.cond + 1, :HD] > 0.0
+    get_plan.wait()
+    column, branch = plan_ref[at.column], plan_ref[at.branch]
     for ref, other, first in zip(kept, moved, places[2]):
         half = ref.shape[1]
+        here = pl.multiple_of(branch * half, half)
+        there = pl.multiple_of((1 - branch) * half, half)
         for j in range(ref.shape[0]):
-            mine, theirs = ref[j].astype(F32), other[j].astype(F32)
-            low = jnp.where(low_here, mine, theirs).astype(BF16)
-            high = jnp.where(low_here, theirs, mine).astype(BF16)
-            listed[slots + first + j, :half] = low
-            listed[slots + first + j, half:] = high
-    get_plan.wait()
-    column = plan_ref[at.column]
+            listed[slots + first + j, pl.ds(here, half)] = ref[j]
+            listed[slots + first + j, pl.ds(there, half)] = other[j]
     per_half = turned.shape[1]
     count = turned.shape[2] // HD * per_half
     spots = []
@@ -493,7 +493,7 @@
         slot = lax.shift_right_logical(p, 1)
         paired = jnp.where(jnp.bitwise_and(p, 1) == column, slot, slots + slot)
         spots.append(jnp.where(p >= 2 * slots, p, paired))
-    parts = 2
+    parts = out_sems.shape[0]
     size = turned.shape[0] // parts
     copies = []
     for r in range(parts):
@@ -530,7 +530,7 @@
             jax.ShapeDtypeStruct((base, 2, rows, HD), BF16),
         ],
         in_specs=[whole(pltpu.HBM)] * 3 + [whole(pl.ANY)],
-        out_specs=[whole(pl.ANY)] * 4,
+        out_specs=[whole(pl.ANY)] * 2 + [whole()] * 2,
         scratch_shapes=[
             pltpu.SMEM(windows.shape, jnp.int32),
             pltpu.SMEM(segments.shape, jnp.int32),
@@ -618,15 +618,17 @@
         (late,) = gate([across[0]], done)
         far_across[0] = lax.ppermute(late, grid_axes, apart)
         (across[1],) = gate([across[1]], [late, *done])
-        (q_late,) = gate([q_late], [across[1]])
-        done = [near_across[0], q_late]
-        q_late = cross(q_late)
+        done = [across[1]]
         for k in chunks[1:]:
-            (across[k],) = gate([across[k]], done)
+            if k > 1:
+                (across[k],) = gate([across[k]], done)
             done = [across[k]]
             near_across[k] = lax.ppermute(across[k], grid_axes, onward)
             if reaches[k]:
                 far_across[k] = lax.ppermute(across[k], grid_axes, apart)
+        (q_late,) = gate([q_late], [*done, near_across[0]])
+        done = [q_late]
+        q_late = cross(q_late)
 
         def attend_part(k, lo, hi, q, q_offset, names, bias_at, cond_at, after):
             skip = lo - bounds[k][0]
@@ -641,7 +643,10 @@
             cut = slice(0, 5) if reaches[k] else slice(1, 4)
             sources = [arrays[name] for name in names[cut]]
             bias_at += lo * len(DISTANCES) + cut.start
-            return attend_slots(table, q, q_offset, sources, hi - lo, bias_at, cond_at, after)
+            always = DISTANCES[cut].index(0)
+            return attend_slots(
+                table, q, q_offset, sources, always, hi - lo, bias_at, cond_at, after
+            )
 
         def attend_own(k, after):
             lo, hi = bounds[k]
@@ -695,7 +700,7 @@
                 pltpu.VMEM((heads, rows, HD), BF16),
                 pltpu.VMEM((rows, per_half, seq_count * HD), BF16),
                 pltpu.SemaphoreType.DMA((1,)),
-                pltpu.SemaphoreType.DMA((2,)),
+                pltpu.SemaphoreType.DMA((4,)),
             ],
             compiler_params=params(),
             name="assemble",

time: 72 us -> 71.5 us (level)
  waiting for transfers between devices: 19.8 us -> 18.9 us
    ppermute x1, waiting for transfers between devices: 0.99 us -> 0.01 us  [attempt(): near_across[0] = lax.ppermute(across[0], grid_axes, onward)]
    ppermute x6, starting transfers between devices: 8.21 us -> 9.06 us  [cross(): return lax.ppermute(a, 'seq', SWAP)]
  transfers between devices with their start and end apart: 20 -> 20, of which waited for: 10 -> 9; matrix products, arithmetic and copies ran while one was open for 0% -> 0% of each run, Pallas kernels for 26% -> 26%
where the time goes in v7:
time: 71.5 us; the launch traced here: 71.2 us
  starting transfers between devices  26.6 us (37%)
  Pallas kernels  23.3 us (33%)
  waiting for transfers between devices  18.9 us (26%)
  between operations  1.53 us (2%)
  loops' own time  0.79 us (1%)
    pallas_call x4, Pallas kernels, attend_slots(): pl.pallas_call(functools.partial(attend_kernel, count, q_offset, offsets,...  11.4 us
    ppermute x6, waiting for transfers between devices, cross(): return lax.ppermute(a, 'seq', SWAP)  10.4 us
    ppermute x6, starting transfers between devices, cross(): return lax.ppermute(a, 'seq', SWAP)  9.06 us
    ppermute x1, starting transfers between devices, attempt(): far_own = [lax.ppermute(kv_far, grid_axes, onward)]  4.72 us
    ppermute x1, starting transfers between devices, attempt(): near_across[k] = lax.ppermute(across[k], grid_axes, onward)  4.27 us
    ppermute x1, starting transfers between devices, attempt(): near_across[0] = lax.ppermute(across[0], grid_axes, onward)  4.08 us
    pallas_call x2, Pallas kernels, pack(): pl.pallas_call(functools.partial(pack_kernel, jobs, len(after)), out_shap...  3.53 us
    ppermute x1, waiting for transfers between devices, attempt(): far_own = [lax.ppermute(kv_far, grid_axes, onward)]  3.48 us
  transfers between devices with their start and end apart: 20, of which 9 were waited for; matrix products, arithmetic and copies ran while one was open for 0% of the time, Pallas kernels for 26%

profile of v7, /device:TPU:0, one launch (start us, length us, event | category | flops | bytes accessed | tf_op | source)
XLA Modules:
  0.0 71.2 jit_solution(317468039998727238)
XLA Ops:
  0.7 2.9 %plan.1 = (s32[173]{0:T(256)S(1)}, s32[1]{0:T(128)}, bf16[5,2,256,128]{3,2,1,0:T(8,128)(2,1)S(1)}, bf16[11,2,256,128]{3,2,1,0:T(8,128)(2,1)S(1)}) custom-call(s32[32]{0:T(128)} %windows_in.1, s32[8]{0:T(128)} %segments_in.1, s32[1]{0:T(128)S(6)} %copy.43.step_in, bf16[3,256,4096]{2,1,0:T(8,128)(2,1)} %bitcast.4), custom_call_target="tpu_custom_call" | custom-call | tf_op jit(solution)/shard_map/plan/pallas_call | solution.py:524
  4.2 66.8 %conditional.1 = (bf16[256,8,256]{2,1,0:T(8,128)(2,1)}) conditional(s32[]{:T(128)} %bitcast.2, (s32[173]{0:T(256)S(1)}, bf16[3,256,4096]{2,1,0:T(8,128)(2,1)}, bf16[11,2,256,128]{3,2,1,0:T(8,128)(2,1)S(1)}, bf16[5,2,256,128]{3,2,1,0:T(8,128)(2,1)S(1)}) %tuple.24, (s32[173]{0:T(256)S(1)}, bf16[3,256,4096]{2,1,0:T(8,128)(2,1)}, ...), branch_computations={%region_0.0_spmd, %region_1.0_spmd, %region_2.0_spmd} | conditional | flops 44499996672 | bytes 84870360 | solution.py:709
  4.2 3.0 %collective-permute-start.1 = (bf16[5,2,256,128]{3,2,1,0:T(8,128)(2,1)S(1)}, bf16[5,2,256,128]{3,2,1,0:T(8,128)(2,1)S(1)}, u32[]{:S(2)}, u32[]{:S(2)}) collective-permute-start(bf16[5,2,256,128]{3,2,1,0:T(8,128)(2,1)S(1)} %get-tuple-element.38), channel_id=1, source_target_pairs={{0,8},{8,0},{1,9},{9,1},{2,10},{10,2},{3,11},{11,3},{4,12},{12,4},... | collective-permute-start | bytes 1966088 | tf_op jit(solution)/shard_map/cond/branch_0_fun/ppermute | solution.py:568
  7.2 1.3 %collective-permute-start.3 = (bf16[11,2,256,128]{3,2,1,0:T(8,128)(2,1)S(1)}, bf16[11,2,256,128]{3,2,1,0:T(8,128)(2,1)S(1)}, u32[]{:S(2)}, u32[]{:S(2)}) collective-permute-start(bf16[11,2,256,128]{3,2,1,0:T(8,128)(2,1)S(1)} %get-tuple-element.35.refs_0_.refs_2_.refs_1_), channel_id=1, source_target_pairs={{2,0},{4,2},{6,4},{8,10},{10,12},{12,14},{3,1},{5,3},{7,5},{9,11},... | collective-permute-start | bytes 4325384 | tf_op jit(solution)/shard_map/cond/branch_0_fun/ppermute | solution.py:577
  8.5 2.0 %pack_heads.6.refs_0_ = bf16[5,2,256,128]{3,2,1,0:T(8,128)(2,1)S(1)} custom-call(s32[173]{0:T(256)S(1)} %get-tuple-element.32.plan_ref.plan_in, bf16[3,256,4096]{2,1,0:T(8,128)(2,1)} %get-tuple-element.34.x_ref, bf16[11,2,256,128]{3,2,1,0:T(8,128)(2,1)S(1)} %get-tuple-element.35.refs_0_.refs_2_.refs_1_), custom_call_target="tpu_custom_call" | custom-call | flops 10000000000 | bytes 1 | tf_op jit(solution)/shard_map/cond/branch_0_fun/pack_heads/pallas_call | solution.py:248
  10.5 4.7 %collective-permute-start = (bf16[5,2,256,128]{3,2,1,0:T(8,128)(2,1)S(1)}, bf16[5,2,256,128]{3,2,1,0:T(8,128)(2,1)S(1)}, u32[]{:S(2)}, u32[]{:S(2)}) collective-permute-start(bf16[5,2,256,128]{3,2,1,0:T(8,128)(2,1)S(1)} %pack_heads.6.refs_0_), channel_id=1, source_target_pairs={{0,2},{2,4},{4,6},{10,8},{12,10},{14,12},{1,3},{3,5},{5,7},{11,9},... | collective-permute-start | bytes 1966088 | tf_op jit(solution)/shard_map/cond/branch_0_fun/ppermute | solution.py:579
  15.3 1.5 %pack_heads.7 = (bf16[11,1,256,128]{3,2,1,0:T(8,128)(2,1)S(1)}, bf16[6,1,256,128]{3,2,1,0:T(8,128)(2,1)S(1)}, bf16[5,1,256,128]{3,2,1,0:T(8,128)(2,1)S(1)}, bf16[6,2,256,128]{3,2,1,0:T(8,128)(2,1)S(1)}) custom-call(s32[173]{0:T(256)S(1)} %get-tuple-element.32.plan_ref.plan_in, bf16[3,256,4096]{2,1,0:T(8,128)(2,1)S(1)} %copy-done, ...), custom_call_target="tpu_custom_call" | custom-call | flops 10000000000 | bytes 1 | tf_op jit(solution)/shard_map/cond/branch_0_fun/pack_heads/pallas_call | solution.py:248
  17.6 2.5 %attend_local.2.refs_1_.mine_ref = bf16[10,256,128]{2,1,0:T(8,128)(2,1)S(1)} custom-call(s32[173]{0:T(256)S(1)} %get-tuple-element.32.plan_ref.plan_in, bf16[3,256,4096]{2,1,0:T(8,128)(2,1)S(1)} %copy-done, f32[168,256]{1,0:T(8,128)S(1)} %table.3.refs_0_.table_ref), custom_call_target="tpu_custom_call" | custom-call | flops 3000000000 | bytes 1 | tf_op jit(solution)/shard_map/cond/branch_0_fun/attend_local/pallas_call | solution.py:349
  20.2 2.6 %collective-permute-done.1.refs_0_ = bf16[5,2,256,128]{3,2,1,0:T(8,128)(2,1)S(1)} collective-permute-done((bf16[5,2,256,128]{3,2,1,0:T(8,128)(2,1)S(1)}, bf16[5,2,256,128]{3,2,1,0:T(8,128)(2,1)S(1)}, u32[]{:S(2)}, u32[]{:S(2)}) %collective-permute-start.1) | collective-permute-done | bytes 655392 | tf_op jit(solution)/shard_map/cond/branch_0_fun/ppermute | solution.py:568
  22.8 4.1 %collective-permute-start.2 = (bf16[5,2,256,128]{3,2,1,0:T(8,128)(2,1)S(1)}, bf16[5,2,256,128]{3,2,1,0:T(8,128)(2,1)S(1)}, u32[]{:S(2)}, u32[]{:S(2)}) collective-permute-start(bf16[5,2,256,128]{3,2,1,0:T(8,128)(2,1)S(1)} %gate.16.refs_1_.refs_3_.refs_2_), channel_id=1, source_target_pairs={{0,2},{2,4},{4,6},{10,8},{12,10},{14,12},{1,3},{3,5},{5,7},{11,9},... | collective-permute-start | bytes 1966088 | tf_op jit(solution)/shard_map/cond/branch_0_fun/ppermute | solution.py:611
  26.9 3.5 %collective-permute-done.refs_2_.refs_0_ = bf16[5,2,256,128]{3,2,1,0:T(8,128)(2,1)S(1)} collective-permute-done((bf16[5,2,256,128]{3,2,1,0:T(8,128)(2,1)S(1)}, bf16[5,2,256,128]{3,2,1,0:T(8,128)(2,1)S(1)}, u32[]{:S(2)}, u32[]{:S(2)}) %collective-permute-start) | collective-permute-done | bytes 655392 | tf_op jit(solution)/shard_map/cond/branch_0_fun/ppermute | solution.py:579
  30.4 2.7 %collective-permute-start.7 = (bf16[6,1,256,128]{3,2,1,0:T(8,128)(2,1)S(1)}, bf16[6,1,256,128]{3,2,1,0:T(8,128)(2,1)S(1)}, u32[]{:S(2)}, u32[]{:S(2)}) collective-permute-start(bf16[6,1,256,128]{3,2,1,0:T(8,128)(2,1)S(1)} %gate.17.refs_1_), channel_id=1, source_target_pairs={{0,8},{8,0},{1,9},{9,1},{2,10},{10,2},{3,11},{11,3},{4,12},{12,4},... | collective-permute-start | bytes 1179656 | tf_op jit(solution)/shard_map/cond/branch_0_fun/ppermute | solution.py:568
  33.4 1.3 %collective-permute-start.10 = (bf16[5,2,256,128]{3,2,1,0:T(8,128)(2,1)S(1)}, bf16[5,2,256,128]{3,2,1,0:T(8,128)(2,1)S(1)}, u32[]{:S(2)}, u32[]{:S(2)}) collective-permute-start(bf16[5,2,256,128]{3,2,1,0:T(8,128)(2,1)S(1)} %gate.18.refs_1_), channel_id=1, source_target_pairs={{2,0},{4,2},{6,4},{8,10},{10,12},{12,14},{3,1},{5,3},{7,5},{9,11},... | collective-permute-start | bytes 1966088 | tf_op jit(solution)/shard_map/cond/branch_0_fun/ppermute | solution.py:619
  34.7 4.9 %collective-permute-done.4.refs_0_ = bf16[6,2,256,128]{3,2,1,0:T(8,128)(2,1)S(1)} collective-permute-done((bf16[6,2,256,128]{3,2,1,0:T(8,128)(2,1)S(1)}, bf16[6,2,256,128]{3,2,1,0:T(8,128)(2,1)S(1)}, u32[]{:S(2)}, u32[]{:S(2)}) %collective-permute-start.4) | collective-permute-done | bytes 786464 | tf_op jit(solution)/shard_map/cond/branch_0_fun/ppermute | solution.py:568
  39.6 4.3 %collective-permute-start.8 = (bf16[6,2,256,128]{3,2,1,0:T(8,128)(2,1)S(1)}, bf16[6,2,256,128]{3,2,1,0:T(8,128)(2,1)S(1)}, u32[]{:S(2)}, u32[]{:S(2)}) collective-permute-start(bf16[6,2,256,128]{3,2,1,0:T(8,128)(2,1)S(1)} %gate.19.refs_1_.refs_2_), channel_id=1, source_target_pairs={{0,2},{2,4},{4,6},{10,8},{12,10},{14,12},{1,3},{3,5},{5,7},{11,9},... | collective-permute-start | bytes 2359304 | tf_op jit(solution)/shard_map/cond/branch_0_fun/ppermute | solution.py:626
  43.9 2.7 %collective-permute-start.9 = (bf16[5,1,256,128]{3,2,1,0:T(8,128)(2,1)S(1)}, bf16[5,1,256,128]{3,2,1,0:T(8,128)(2,1)S(1)}, u32[]{:S(2)}, u32[]{:S(2)}) collective-permute-start(bf16[5,1,256,128]{3,2,1,0:T(8,128)(2,1)S(1)} %gate.20.refs_5_), channel_id=1, source_target_pairs={{0,8},{8,0},{1,9},{9,1},{2,10},{10,2},{3,11},{11,3},{4,12},{12,4},... | collective-permute-start | bytes 983048 | tf_op jit(solution)/shard_map/cond/branch_0_fun/ppermute | solution.py:568
  46.6 3.1 %attend.14.refs_3_.mine_ref = bf16[5,256,128]{2,1,0:T(8,128)(2,1)S(1)} custom-call(f32[168,256]{1,0:T(8,128)S(1)} %table.3.refs_0_.table_ref, bf16[11,1,256,128]{3,2,1,0:T(8,128)(2,1)S(1)} %get-tuple-element.37.q_ref, bf16[5,2,256,128]{3,2,1,0:T(8,128)(2,1)S(1)} %collective-permute-done.refs_2_.refs_0_, ...), custom_call_target="tpu_custom_call" | custom-call | flops 3000000000 | bytes 1 | tf_op jit(solution)/shard_map/cond/branch_0_fun/attend/pallas_call | solution.py:410
  49.8 2.6 %attend.15 = (bf16[6,128,128]{2,1,0:T(8,128)(2,1)S(1)}, bf16[6,128,128]{2,1,0:T(8,128)(2,1)S(1)}) custom-call(f32[168,256]{1,0:T(8,128)S(1)} %table.3.refs_0_.table_ref, bf16[6,1,256,128]{3,2,1,0:T(8,128)(2,1)S(1)} %collective-permute-done.7.q_ref, bf16[11,2,256,128]{3,2,1,0:T(8,128)(2,1)S(1)} %get-tuple-element.35.refs_0_.refs_2_.refs_1_, ...), custom_call_target="tpu_custom_call" | custom-call | flops 3000000000 | bytes 1 | tf_op jit(solution)/shard_map/cond/branch_0_fun/attend/pallas_call | solution.py:410
  54.4 1.8 %collective-permute-done.10.refs_4_ = bf16[5,2,256,128]{3,2,1,0:T(8,128)(2,1)S(1)} collective-permute-done((bf16[5,2,256,128]{3,2,1,0:T(8,128)(2,1)S(1)}, bf16[5,2,256,128]{3,2,1,0:T(8,128)(2,1)S(1)}, u32[]{:S(2)}, u32[]{:S(2)}) %collective-permute-start.10) | collective-permute-done | bytes 655392 | tf_op jit(solution)/shard_map/cond/branch_0_fun/ppermute | solution.py:619
  56.2 3.1 %attend.16 = (bf16[5,128,128]{2,1,0:T(8,128)(2,1)S(1)}, bf16[5,128,128]{2,1,0:T(8,128)(2,1)S(1)}) custom-call(f32[168,256]{1,0:T(8,128)S(1)} %table.3.refs_0_.table_ref, bf16[5,1,256,128]{3,2,1,0:T(8,128)(2,1)S(1)} %collective-permute-done.9.q_ref, bf16[5,2,256,128]{3,2,1,0:T(8,128)(2,1)S(1)} %collective-permute-done.2.refs_2_.refs_1_.refs_0_, ...), custom_call_target="tpu_custom_call" | custom-call | flops 3000000000 | bytes 1 | tf_op jit(solution)/shard_map/cond/branch_0_fun/attend/pallas_call | solution.py:410
  61.8 2.6 %attend.17 = bf16[6,256,128]{2,1,0:T(8,128)(2,1)S(1)} custom-call(f32[168,256]{1,0:T(8,128)S(1)} %table.3.refs_0_.table_ref, bf16[11,1,256,128]{3,2,1,0:T(8,128)(2,1)S(1)} %get-tuple-element.37.q_ref, bf16[6,2,256,128]{3,2,1,0:T(8,128)(2,1)S(1)} %collective-permute-done.8.refs_0_, bf16[11,2,256,128]{3,2,1,0:T(8,128)(2,1)S(1)} %get-tuple-element.35.refs_0_.refs_2_.refs_1_, ...), custom_call_target="tpu_custom_call" | custom-call | flops 3000000000 | bytes 1 | tf_op jit(solution)/shard_map/cond/branch_0_fun/attend/pallas_call | solution.py:410
  65.1 2.3 %collective-permute-done.17.refs_6_ = bf16[5,128,128]{2,1,0:T(8,128)(2,1)S(1)} collective-permute-done((bf16[5,128,128]{2,1,0:T(8,128)(2,1)S(1)}, bf16[5,128,128]{2,1,0:T(8,128)(2,1)S(1)}, u32[]{:S(2)}, u32[]{:S(2)}) %collective-permute-start.17) | collective-permute-done | bytes 163872 | tf_op jit(solution)/shard_map/cond/branch_0_fun/ppermute | solution.py:568
  67.4 1.4 %collective-permute-done.19.refs_8_ = bf16[5,128,128]{2,1,0:T(8,128)(2,1)S(1)} collective-permute-done((bf16[5,128,128]{2,1,0:T(8,128)(2,1)S(1)}, bf16[5,128,128]{2,1,0:T(8,128)(2,1)S(1)}, u32[]{:S(2)}, u32[]{:S(2)}) %collective-permute-start.19) | collective-permute-done | bytes 163872 | tf_op jit(solution)/shard_map/cond/branch_0_fun/ppermute | solution.py:571
  68.8 1.7 %assemble.3 = bf16[256,8,256]{2,1,0:T(8,128)(2,1)} custom-call(s32[173]{0:T(256)S(1)} %get-tuple-element.32.plan_ref.plan_in, f32[168,256]{1,0:T(8,128)S(1)} %table.3.refs_0_.table_ref, bf16[5,256,128]{2,1,0:T(8,128)(2,1)S(1)} %mix.13.refs_1_.refs_0_, bf16[3,256,128]{2,1,0:T(8,128)(2,1)S(1)} %get-tuple-element.85.refs_1_, ...), custom_call_target="tpu_custom_call" | custom-call | tf_op jit(solution)/shard_map/cond/branch_0_fun/assemble/pallas_call | solution.py:693
  (42 shorter events, 6.5 us)
Async XLA Ops:
  4.2 18.6 %collective-permute-start.1 = (bf16[5,2,256,128]{3,2,1,0:T(8,128)(2,1)S(1)}, bf16[5,2,256,128]{3,2,1,0:T(8,128)(2,1)S(1)}, u32[]{:S(2)}, u32[]{:S(2)}) collective-permute-start(bf16[5,2,256,128]{3,2,1,0:T(8,128)(2,1)S(1)} %get-tuple-element.38), channel_id=1, source_target_pairs={{0,8},{8,0},{1,9},{9,1},{2,10},{10,2},{3,11},{11,3},{4,12},{12,4},... | collective-permute-start | bytes 1966088 | tf_op jit(solution)/shard_map/cond/branch_0_fun/ppermute | solution.py:568
  7.2 39.4 %collective-permute-start.3 = (bf16[11,2,256,128]{3,2,1,0:T(8,128)(2,1)S(1)}, bf16[11,2,256,128]{3,2,1,0:T(8,128)(2,1)S(1)}, u32[]{:S(2)}, u32[]{:S(2)}) collective-permute-start(bf16[11,2,256,128]{3,2,1,0:T(8,128)(2,1)S(1)} %get-tuple-element.35.refs_0_.refs_2_.refs_1_), channel_id=1, source_target_pairs={{2,0},{4,2},{6,4},{8,10},{10,12},{12,14},{3,1},{5,3},{7,5},{9,11},... | collective-permute-start | bytes 4325384 | tf_op jit(solution)/shard_map/cond/branch_0_fun/ppermute | solution.py:577
  8.5 6.8 %copy-start = (bf16[3,256,4096]{2,1,0:T(8,128)(2,1)S(1)}, bf16[3,256,4096]{2,1,0:T(8,128)(2,1)}, u32[]{:S(2)}) copy-start(bf16[3,256,4096]{2,1,0:T(8,128)(2,1)} %get-tuple-element.34.x_ref) | copy-start | bytes 18874372 | tf_op jit(solution)/shard_map/cond
  10.5 19.9 %collective-permute-start = (bf16[5,2,256,128]{3,2,1,0:T(8,128)(2,1)S(1)}, bf16[5,2,256,128]{3,2,1,0:T(8,128)(2,1)S(1)}, u32[]{:S(2)}, u32[]{:S(2)}) collective-permute-start(bf16[5,2,256,128]{3,2,1,0:T(8,128)(2,1)S(1)} %pack_heads.6.refs_0_), channel_id=1, source_target_pairs={{0,2},{2,4},{4,6},{10,8},{12,10},{14,12},{1,3},{3,5},{5,7},{11,9},... | collective-permute-start | bytes 1966088 | tf_op jit(solution)/shard_map/cond/branch_0_fun/ppermute | solution.py:579
  16.8 22.8 %collective-permute-start.4 = (bf16[6,2,256,128]{3,2,1,0:T(8,128)(2,1)S(1)}, bf16[6,2,256,128]{3,2,1,0:T(8,128)(2,1)S(1)}, u32[]{:S(2)}, u32[]{:S(2)}) collective-permute-start(bf16[6,2,256,128]{3,2,1,0:T(8,128)(2,1)S(1)} %get-tuple-element.36.refs_0_), channel_id=1, source_target_pairs={{0,8},{8,0},{1,9},{9,1},{2,10},{10,2},{3,11},{11,3},{4,12},{12,4},... | collective-permute-start | bytes 2359304 | tf_op jit(solution)/shard_map/cond/branch_0_fun/ppermute | solution.py:568
  20.1 12.9 %collective-permute-start.5 = (bf16[10,256,128]{2,1,0:T(8,128)(2,1)S(1)}, bf16[10,256,128]{2,1,0:T(8,128)(2,1)S(1)}, u32[]{:S(2)}, u32[]{:S(2)}) collective-permute-start(bf16[10,256,128]{2,1,0:T(8,128)(2,1)S(1)} %attend_local.2.refs_1_.mine_ref), channel_id=1, source_target_pairs={{0,1},{1,0},{2,3},{3,2},{4,5},{5,4},{6,7},{7,6},{8,9},{9,8},{10,11... | collective-permute-start | bytes 1966088 | tf_op jit(solution)/shard_map/cond/branch_0_fun/ppermute | solution.py:571
  22.8 21.1 %collective-permute-start.2 = (bf16[5,2,256,128]{3,2,1,0:T(8,128)(2,1)S(1)}, bf16[5,2,256,128]{3,2,1,0:T(8,128)(2,1)S(1)}, u32[]{:S(2)}, u32[]{:S(2)}) collective-permute-start(bf16[5,2,256,128]{3,2,1,0:T(8,128)(2,1)S(1)} %gate.16.refs_1_.refs_3_.refs_2_), channel_id=1, source_target_pairs={{0,2},{2,4},{4,6},{10,8},{12,10},{14,12},{1,3},{3,5},{5,7},{11,9},... | collective-permute-start | bytes 1966088 | tf_op jit(solution)/shard_map/cond/branch_0_fun/ppermute | solution.py:611
  30.4 19.4 %collective-permute-start.7 = (bf16[6,1,256,128]{3,2,1,0:T(8,128)(2,1)S(1)}, bf16[6,1,256,128]{3,2,1,0:T(8,128)(2,1)S(1)}, u32[]{:S(2)}, u32[]{:S(2)}) collective-permute-start(bf16[6,1,256,128]{3,2,1,0:T(8,128)(2,1)S(1)} %gate.17.refs_1_), channel_id=1, source_target_pairs={{0,8},{8,0},{1,9},{9,1},{2,10},{10,2},{3,11},{11,3},{4,12},{12,4},... | collective-permute-start | bytes 1179656 | tf_op jit(solution)/shard_map/cond/branch_0_fun/ppermute | solution.py:568
  33.4 22.8 %collective-permute-start.10 = (bf16[5,2,256,128]{3,2,1,0:T(8,128)(2,1)S(1)}, bf16[5,2,256,128]{3,2,1,0:T(8,128)(2,1)S(1)}, u32[]{:S(2)}, u32[]{:S(2)}) collective-permute-start(bf16[5,2,256,128]{3,2,1,0:T(8,128)(2,1)S(1)} %gate.18.refs_1_), channel_id=1, source_target_pairs={{2,0},{4,2},{6,4},{8,10},{10,12},{12,14},{3,1},{5,3},{7,5},{9,11},... | collective-permute-start | bytes 1966088 | tf_op jit(solution)/shard_map/cond/branch_0_fun/ppermute | solution.py:619
  39.6 22.2 %collective-permute-start.8 = (bf16[6,2,256,128]{3,2,1,0:T(8,128)(2,1)S(1)}, bf16[6,2,256,128]{3,2,1,0:T(8,128)(2,1)S(1)}, u32[]{:S(2)}, u32[]{:S(2)}) collective-permute-start(bf16[6,2,256,128]{3,2,1,0:T(8,128)(2,1)S(1)} %gate.19.refs_1_.refs_2_), channel_id=1, source_target_pairs={{0,2},{2,4},{4,6},{10,8},{12,10},{14,12},{1,3},{3,5},{5,7},{11,9},... | collective-permute-start | bytes 2359304 | tf_op jit(solution)/shard_map/cond/branch_0_fun/ppermute | solution.py:626
  43.9 12.3 %collective-permute-start.9 = (bf16[5,1,256,128]{3,2,1,0:T(8,128)(2,1)S(1)}, bf16[5,1,256,128]{3,2,1,0:T(8,128)(2,1)S(1)}, u32[]{:S(2)}, u32[]{:S(2)}) collective-permute-start(bf16[5,1,256,128]{3,2,1,0:T(8,128)(2,1)S(1)} %gate.20.refs_5_), channel_id=1, source_target_pairs={{0,8},{8,0},{1,9},{9,1},{2,10},{10,2},{3,11},{11,3},{4,12},{12,4},... | collective-permute-start | bytes 983048 | tf_op jit(solution)/shard_map/cond/branch_0_fun/ppermute | solution.py:568
  49.7 3.3 %collective-permute-start.6 = (bf16[5,256,128]{2,1,0:T(8,128)(2,1)S(1)}, bf16[5,256,128]{2,1,0:T(8,128)(2,1)S(1)}, u32[]{:S(2)}, u32[]{:S(2)}) collective-permute-start(bf16[5,256,128]{2,1,0:T(8,128)(2,1)S(1)} %attend.14.refs_3_.mine_ref), channel_id=1, source_target_pairs={{0,1},{1,0},{2,3},{3,2},{4,5},{5,4},{6,7},{7,6},{8,9},{9,8},{10,11... | collective-permute-start | bytes 983048 | tf_op jit(solution)/shard_map/cond/branch_0_fun/ppermute | solution.py:571
  52.4 1.6 %collective-permute-start.11 = (bf16[6,128,128]{2,1,0:T(8,128)(2,1)S(1)}, bf16[6,128,128]{2,1,0:T(8,128)(2,1)S(1)}, u32[]{:S(2)}, u32[]{:S(2)}) collective-permute-start(bf16[6,128,128]{2,1,0:T(8,128)(2,1)S(1)} %get-tuple-element.42), channel_id=1, source_target_pairs={{0,1},{1,0},{2,3},{3,2},{4,5},{5,4},{6,7},{7,6},{8,9},{9,8},{10,11... | collective-permute-start | bytes 589832 | tf_op jit(solution)/shard_map/cond/branch_0_fun/ppermute | solution.py:571
  54.1 7.2 %collective-permute-start.14 = (bf16[6,128,128]{2,1,0:T(8,128)(2,1)S(1)}, bf16[6,128,128]{2,1,0:T(8,128)(2,1)S(1)}, u32[]{:S(2)}, u32[]{:S(2)}) collective-permute-start(bf16[6,128,128]{2,1,0:T(8,128)(2,1)S(1)} %mix.14.refs_5_), channel_id=1, source_target_pairs={{0,8},{8,0},{1,9},{9,1},{2,10},{10,2},{3,11},{11,3},{4,12},{12,4},... | collective-permute-start | bytes 589832 | tf_op jit(solution)/shard_map/cond/branch_0_fun/ppermute | solution.py:568
  59.3 1.5 %collective-permute-start.13 = (bf16[3,128,128]{2,1,0:T(8,128)(2,1)S(1)}, bf16[3,128,128]{2,1,0:T(8,128)(2,1)S(1)}, u32[]{:S(2)}, u32[]{:S(2)}) collective-permute-start(bf16[3,128,128]{2,1,0:T(8,128)(2,1)S(1)} %slice.29), channel_id=1, source_target_pairs={{0,1},{1,0},{2,3},{3,2},{4,5},{5,4},{6,7},{7,6},{8,9},{9,8},{10,11... | collective-permute-start | bytes 294920 | tf_op jit(solution)/shard_map/cond/branch_0_fun/ppermute | solution.py:571
  59.4 1.4 %collective-permute-start.12 = (bf16[2,128,128]{2,1,0:T(8,128)(2,1)S(1)}, bf16[2,128,128]{2,1,0:T(8,128)(2,1)S(1)}, u32[]{:S(2)}, u32[]{:S(2)}) collective-permute-start(bf16[2,128,128]{2,1,0:T(8,128)(2,1)S(1)} %slice.28), channel_id=1, source_target_pairs={{0,1},{1,0},{2,3},{3,2},{4,5},{5,4},{6,7},{7,6},{8,9},{9,8},{10,11... | collective-permute-start | bytes 196616 | tf_op jit(solution)/shard_map/cond/branch_0_fun/ppermute | solution.py:571
  61.4 5.9 %collective-permute-start.17 = (bf16[5,128,128]{2,1,0:T(8,128)(2,1)S(1)}, bf16[5,128,128]{2,1,0:T(8,128)(2,1)S(1)}, u32[]{:S(2)}, u32[]{:S(2)}) collective-permute-start(bf16[5,128,128]{2,1,0:T(8,128)(2,1)S(1)} %mix.15.refs_3_), channel_id=1, source_target_pairs={{0,8},{8,0},{1,9},{9,1},{2,10},{10,2},{3,11},{11,3},{4,12},{12,4},... | collective-permute-start | bytes 491528 | tf_op jit(solution)/shard_map/cond/branch_0_fun/ppermute | solution.py:568
  64.4 2.9 %collective-permute-start.15 = (bf16[3,256,128]{2,1,0:T(8,128)(2,1)S(1)}, bf16[3,256,128]{2,1,0:T(8,128)(2,1)S(1)}, u32[]{:S(2)}, u32[]{:S(2)}) collective-permute-start(bf16[3,256,128]{2,1,0:T(8,128)(2,1)S(1)} %get-tuple-element.85.refs_1_), channel_id=1, source_target_pairs={{0,1},{1,0},{2,3},{3,2},{4,5},{5,4},{6,7},{7,6},{8,9},{9,8},{10,11... | collective-permute-start | bytes 589832 | tf_op jit(solution)/shard_map/cond/branch_0_fun/ppermute | solution.py:571
  64.5 2.9 %collective-permute-start.16 = (bf16[3,256,128]{2,1,0:T(8,128)(2,1)S(1)}, bf16[3,256,128]{2,1,0:T(8,128)(2,1)S(1)}, u32[]{:S(2)}, u32[]{:S(2)}) collective-permute-start(bf16[3,256,128]{2,1,0:T(8,128)(2,1)S(1)} %get-tuple-element.84.refs_2_), channel_id=1, source_target_pairs={{0,1},{1,0},{2,3},{3,2},{4,5},{5,4},{6,7},{7,6},{8,9},{9,8},{10,11... | collective-permute-start | bytes 589832 | tf_op jit(solution)/shard_map/cond/branch_0_fun/ppermute | solution.py:571
  65.0 2.4 %collective-permute-start.18 = (bf16[6,128,128]{2,1,0:T(8,128)(2,1)S(1)}, bf16[6,128,128]{2,1,0:T(8,128)(2,1)S(1)}, u32[]{:S(2)}, u32[]{:S(2)}) collective-permute-start(bf16[6,128,128]{2,1,0:T(8,128)(2,1)S(1)} %collective-permute-done.14.refs_3_.refs_4_.refs_5_), channel_id=1, source_target_pairs={{0,1},{1,0},{2,3},{3,2},{4,5},{5,4},{6,7},{7,6},{8,9},{9,8},{10,11... | collective-permute-start | bytes 589832 | tf_op jit(solution)/shard_map/cond/branch_0_fun/ppermute | solution.py:571
  67.4 1.4 %collective-permute-start.19 = (bf16[5,128,128]{2,1,0:T(8,128)(2,1)S(1)}, bf16[5,128,128]{2,1,0:T(8,128)(2,1)S(1)}, u32[]{:S(2)}, u32[]{:S(2)}) collective-permute-start(bf16[5,128,128]{2,1,0:T(8,128)(2,1)S(1)} %collective-permute-done.17.refs_6_), channel_id=1, source_target_pairs={{0,1},{1,0},{2,3},{3,2},{4,5},{5,4},{6,7},{7,6},{8,9},{9,8},{10,11... | collective-permute-start | bytes 491528 | tf_op jit(solution)/shard_map/cond/branch_0_fun/ppermute | solution.py:571

commit v8 on v7

--- a/solution.py
+++ b/solution.py
@@ -94,7 +94,6 @@
 
 LOG2E = 1.4426950408889634
 MASKED = -1e30
-UNROLLED_BLOCKS = 25
 BF16 = jnp.bfloat16
 F32 = jnp.float32
 VMEM_BYTES = 32 * 1024 * 1024
@@ -361,7 +360,9 @@
     )(plan, x3, *after)
 
 
-def attend_kernel(count, q_offset, offsets, always, bias_at, cond_at, table_ref, q_ref, *refs):
+def attend_kernel(
+    count, q_offset, offsets, always, bias_at, cond_at, written_out, table_ref, q_ref, *refs
+):
     sources = len(offsets)
     kv_refs = refs[:sources]
     halves = cond_at is not None
@@ -384,7 +385,7 @@
         else:
             outs[0][j] = out.astype(BF16)
 
-    pairs = 0 if count * sources <= UNROLLED_BLOCKS else count // 2
+    pairs = 0 if written_out else count // 2
 
     def two(i, carry):
         one(2 * i)
@@ -397,7 +398,9 @@
         one(j)
 
 
-def attend_slots(table, q, q_offset, sources, always, count, bias_at, cond_at, after):
+def attend_slots(
+    table, q, q_offset, sources, always, count, bias_at, cond_at, written_out, after
+):
     rows = q.shape[-2]
     if cond_at is None:
         out_shape = jax.ShapeDtypeStruct((count, rows, HD), BF16)
@@ -408,7 +411,9 @@
     arrays = [array for array, _ in sources]
     offsets = [offset for _, offset in sources]
     return pl.pallas_call(
-        functools.partial(attend_kernel, count, q_offset, offsets, always, bias_at, cond_at),
+        functools.partial(
+            attend_kernel, count, q_offset, offsets, always, bias_at, cond_at, written_out
+        ),
         out_shape=out_shape,
         in_specs=[whole()] * (2 + len(arrays)) + [whole(pl.ANY)] * len(after),
         out_specs=out_specs,
@@ -645,7 +650,7 @@
             bias_at += lo * len(DISTANCES) + cut.start
             always = DISTANCES[cut].index(0)
             return attend_slots(
-                table, q, q_offset, sources, always, hi - lo, bias_at, cond_at, after
+                table, q, q_offset, sources, always, hi - lo, bias_at, cond_at, rung == rungs[0], after
             )
 
         def attend_own(k, after):
@@ -675,7 +680,6 @@
             pieces = [send] if part < len(parts) - 1 else [send[:middle], send[middle:]]
             waiting.append((keep, [mate(piece) for piece in pieces]))
             done = [keep]
-        done.append(kept[0])
         for keep, got in waiting:
             mixed = mix(keep, got, done)
             kept.append(cross(mixed))

time: 71.5 us -> 71.5 us (level)
  no operation moved by 1% of the time
where the time goes in v8:
time: 71.5 us; the launch traced here: 71.2 us
  starting transfers between devices  26.4 us (37%)
  Pallas kernels  23.3 us (33%)
  waiting for transfers between devices  19.1 us (27%)
  between operations  1.53 us (2%)
  loops' own time  0.79 us (1%)
    pallas_call x4, Pallas kernels, attend_slots(): pl.pallas_call(functools.partial(attend_kernel, count, q_offset, offsets,...  11.3 us
    ppermute x6, waiting for transfers between devices, cross(): return lax.ppermute(a, 'seq', SWAP)  10.6 us
    ppermute x6, starting transfers between devices, cross(): return lax.ppermute(a, 'seq', SWAP)  8.82 us
    ppermute x1, starting transfers between devices, attempt(): far_own = [lax.ppermute(kv_far, grid_axes, onward)]  4.72 us
    ppermute x1, starting transfers between devices, attempt(): near_across[k] = lax.ppermute(across[k], grid_axes, onward)  4.27 us
    ppermute x1, starting transfers between devices, attempt(): near_across[0] = lax.ppermute(across[0], grid_axes, onward)  4.08 us
    pallas_call x2, Pallas kernels, pack(): pl.pallas_call(functools.partial(pack_kernel, jobs, len(after)), out_shap...  3.53 us
    ppermute x1, waiting for transfers between devices, attempt(): far_own = [lax.ppermute(kv_far, grid_axes, onward)]  3.48 us
  transfers between devices with their start and end apart: 20, of which 9 were waited for; matrix products, arithmetic and copies ran while one was open for 0% of the time, Pallas kernels for 26%

profile of v8, /device:TPU:0, one launch (start us, length us, event | category | flops | bytes accessed | tf_op | source)
XLA Modules:
  0.0 71.2 jit_solution(8900661337355731661)
XLA Ops:
  0.7 2.9 %plan.1 = (s32[173]{0:T(256)S(1)}, s32[1]{0:T(128)}, bf16[5,2,256,128]{3,2,1,0:T(8,128)(2,1)S(1)}, bf16[11,2,256,128]{3,2,1,0:T(8,128)(2,1)S(1)}) custom-call(s32[32]{0:T(128)} %windows_in.1, s32[8]{0:T(128)} %segments_in.1, s32[1]{0:T(128)S(6)} %copy.43.step_in, bf16[3,256,4096]{2,1,0:T(8,128)(2,1)} %bitcast.4), custom_call_target="tpu_custom_call" | custom-call | tf_op jit(solution)/shard_map/plan/pallas_call | solution.py:529
  4.2 66.8 %conditional.1 = (bf16[256,8,256]{2,1,0:T(8,128)(2,1)}) conditional(s32[]{:T(128)} %bitcast.2, (s32[173]{0:T(256)S(1)}, bf16[3,256,4096]{2,1,0:T(8,128)(2,1)}, bf16[11,2,256,128]{3,2,1,0:T(8,128)(2,1)S(1)}, bf16[5,2,256,128]{3,2,1,0:T(8,128)(2,1)S(1)}) %tuple.24, (s32[173]{0:T(256)S(1)}, bf16[3,256,4096]{2,1,0:T(8,128)(2,1)}, ...), branch_computations={%region_0.0_spmd, %region_1.0_spmd, %region_2.0_spmd} | conditional | flops 44499996672 | bytes 84870360 | solution.py:713
  4.2 3.0 %collective-permute-start.1 = (bf16[5,2,256,128]{3,2,1,0:T(8,128)(2,1)S(1)}, bf16[5,2,256,128]{3,2,1,0:T(8,128)(2,1)S(1)}, u32[]{:S(2)}, u32[]{:S(2)}) collective-permute-start(bf16[5,2,256,128]{3,2,1,0:T(8,128)(2,1)S(1)} %get-tuple-element.38), channel_id=1, source_target_pairs={{0,8},{8,0},{1,9},{9,1},{2,10},{10,2},{3,11},{11,3},{4,12},{12,4},... | collective-permute-start | bytes 1966088 | tf_op jit(solution)/shard_map/cond/branch_0_fun/ppermute | solution.py:573
  7.2 1.3 %collective-permute-start.3 = (bf16[11,2,256,128]{3,2,1,0:T(8,128)(2,1)S(1)}, bf16[11,2,256,128]{3,2,1,0:T(8,128)(2,1)S(1)}, u32[]{:S(2)}, u32[]{:S(2)}) collective-permute-start(bf16[11,2,256,128]{3,2,1,0:T(8,128)(2,1)S(1)} %get-tuple-element.35.refs_0_.refs_2_.refs_1_), channel_id=1, source_target_pairs={{2,0},{4,2},{6,4},{8,10},{10,12},{12,14},{3,1},{5,3},{7,5},{9,11},... | collective-permute-start | bytes 4325384 | tf_op jit(solution)/shard_map/cond/branch_0_fun/ppermute | solution.py:582
  8.5 2.0 %pack_heads.6.refs_0_ = bf16[5,2,256,128]{3,2,1,0:T(8,128)(2,1)S(1)} custom-call(s32[173]{0:T(256)S(1)} %get-tuple-element.32.plan_ref.plan_in, bf16[3,256,4096]{2,1,0:T(8,128)(2,1)} %get-tuple-element.34.x_ref, bf16[11,2,256,128]{3,2,1,0:T(8,128)(2,1)S(1)} %get-tuple-element.35.refs_0_.refs_2_.refs_1_), custom_call_target="tpu_custom_call" | custom-call | flops 10000000000 | bytes 1 | tf_op jit(solution)/shard_map/cond/branch_0_fun/pack_heads/pallas_call | solution.py:247
  10.5 4.7 %collective-permute-start = (bf16[5,2,256,128]{3,2,1,0:T(8,128)(2,1)S(1)}, bf16[5,2,256,128]{3,2,1,0:T(8,128)(2,1)S(1)}, u32[]{:S(2)}, u32[]{:S(2)}) collective-permute-start(bf16[5,2,256,128]{3,2,1,0:T(8,128)(2,1)S(1)} %pack_heads.6.refs_0_), channel_id=1, source_target_pairs={{0,2},{2,4},{4,6},{10,8},{12,10},{14,12},{1,3},{3,5},{5,7},{11,9},... | collective-permute-start | bytes 1966088 | tf_op jit(solution)/shard_map/cond/branch_0_fun/ppermute | solution.py:584
  15.3 1.5 %pack_heads.7 = (bf16[11,1,256,128]{3,2,1,0:T(8,128)(2,1)S(1)}, bf16[6,1,256,128]{3,2,1,0:T(8,128)(2,1)S(1)}, bf16[5,1,256,128]{3,2,1,0:T(8,128)(2,1)S(1)}, bf16[6,2,256,128]{3,2,1,0:T(8,128)(2,1)S(1)}) custom-call(s32[173]{0:T(256)S(1)} %get-tuple-element.32.plan_ref.plan_in, bf16[3,256,4096]{2,1,0:T(8,128)(2,1)S(1)} %copy-done, ...), custom_call_target="tpu_custom_call" | custom-call | flops 10000000000 | bytes 1 | tf_op jit(solution)/shard_map/cond/branch_0_fun/pack_heads/pallas_call | solution.py:247
  17.6 2.5 %attend_local.2.refs_1_.mine_ref = bf16[10,256,128]{2,1,0:T(8,128)(2,1)S(1)} custom-call(s32[173]{0:T(256)S(1)} %get-tuple-element.32.plan_ref.plan_in, bf16[3,256,4096]{2,1,0:T(8,128)(2,1)S(1)} %copy-done, f32[168,256]{1,0:T(8,128)S(1)} %table.3.refs_0_.table_ref), custom_call_target="tpu_custom_call" | custom-call | flops 3000000000 | bytes 1 | tf_op jit(solution)/shard_map/cond/branch_0_fun/attend_local/pallas_call | solution.py:348
  20.2 2.6 %collective-permute-done.1.refs_0_ = bf16[5,2,256,128]{3,2,1,0:T(8,128)(2,1)S(1)} collective-permute-done((bf16[5,2,256,128]{3,2,1,0:T(8,128)(2,1)S(1)}, bf16[5,2,256,128]{3,2,1,0:T(8,128)(2,1)S(1)}, u32[]{:S(2)}, u32[]{:S(2)}) %collective-permute-start.1) | collective-permute-done | bytes 655392 | tf_op jit(solution)/shard_map/cond/branch_0_fun/ppermute | solution.py:573
  22.8 4.1 %collective-permute-start.2 = (bf16[5,2,256,128]{3,2,1,0:T(8,128)(2,1)S(1)}, bf16[5,2,256,128]{3,2,1,0:T(8,128)(2,1)S(1)}, u32[]{:S(2)}, u32[]{:S(2)}) collective-permute-start(bf16[5,2,256,128]{3,2,1,0:T(8,128)(2,1)S(1)} %gate.16.refs_1_.refs_3_.refs_2_), channel_id=1, source_target_pairs={{0,2},{2,4},{4,6},{10,8},{12,10},{14,12},{1,3},{3,5},{5,7},{11,9},... | collective-permute-start | bytes 1966088 | tf_op jit(solution)/shard_map/cond/branch_0_fun/ppermute | solution.py:616
  26.9 3.5 %collective-permute-done.refs_2_.refs_0_ = bf16[5,2,256,128]{3,2,1,0:T(8,128)(2,1)S(1)} collective-permute-done((bf16[5,2,256,128]{3,2,1,0:T(8,128)(2,1)S(1)}, bf16[5,2,256,128]{3,2,1,0:T(8,128)(2,1)S(1)}, u32[]{:S(2)}, u32[]{:S(2)}) %collective-permute-start) | collective-permute-done | bytes 655392 | tf_op jit(solution)/shard_map/cond/branch_0_fun/ppermute | solution.py:584
  30.4 2.7 %collective-permute-start.7 = (bf16[6,1,256,128]{3,2,1,0:T(8,128)(2,1)S(1)}, bf16[6,1,256,128]{3,2,1,0:T(8,128)(2,1)S(1)}, u32[]{:S(2)}, u32[]{:S(2)}) collective-permute-start(bf16[6,1,256,128]{3,2,1,0:T(8,128)(2,1)S(1)} %gate.17.refs_1_), channel_id=1, source_target_pairs={{0,8},{8,0},{1,9},{9,1},{2,10},{10,2},{3,11},{11,3},{4,12},{12,4},... | collective-permute-start | bytes 1179656 | tf_op jit(solution)/shard_map/cond/branch_0_fun/ppermute | solution.py:573
  33.4 1.3 %collective-permute-start.10 = (bf16[5,2,256,128]{3,2,1,0:T(8,128)(2,1)S(1)}, bf16[5,2,256,128]{3,2,1,0:T(8,128)(2,1)S(1)}, u32[]{:S(2)}, u32[]{:S(2)}) collective-permute-start(bf16[5,2,256,128]{3,2,1,0:T(8,128)(2,1)S(1)} %gate.18.refs_1_), channel_id=1, source_target_pairs={{2,0},{4,2},{6,4},{8,10},{10,12},{12,14},{3,1},{5,3},{7,5},{9,11},... | collective-permute-start | bytes 1966088 | tf_op jit(solution)/shard_map/cond/branch_0_fun/ppermute | solution.py:624
  34.7 4.9 %collective-permute-done.4.refs_0_ = bf16[6,2,256,128]{3,2,1,0:T(8,128)(2,1)S(1)} collective-permute-done((bf16[6,2,256,128]{3,2,1,0:T(8,128)(2,1)S(1)}, bf16[6,2,256,128]{3,2,1,0:T(8,128)(2,1)S(1)}, u32[]{:S(2)}, u32[]{:S(2)}) %collective-permute-start.4) | collective-permute-done | bytes 786464 | tf_op jit(solution)/shard_map/cond/branch_0_fun/ppermute | solution.py:573
  39.6 4.3 %collective-permute-start.8 = (bf16[6,2,256,128]{3,2,1,0:T(8,128)(2,1)S(1)}, bf16[6,2,256,128]{3,2,1,0:T(8,128)(2,1)S(1)}, u32[]{:S(2)}, u32[]{:S(2)}) collective-permute-start(bf16[6,2,256,128]{3,2,1,0:T(8,128)(2,1)S(1)} %gate.19.refs_1_.refs_2_), channel_id=1, source_target_pairs={{0,2},{2,4},{4,6},{10,8},{12,10},{14,12},{1,3},{3,5},{5,7},{11,9},... | collective-permute-start | bytes 2359304 | tf_op jit(solution)/shard_map/cond/branch_0_fun/ppermute | solution.py:631
  43.9 2.7 %collective-permute-start.9 = (bf16[5,1,256,128]{3,2,1,0:T(8,128)(2,1)S(1)}, bf16[5,1,256,128]{3,2,1,0:T(8,128)(2,1)S(1)}, u32[]{:S(2)}, u32[]{:S(2)}) collective-permute-start(bf16[5,1,256,128]{3,2,1,0:T(8,128)(2,1)S(1)} %gate.20.refs_5_), channel_id=1, source_target_pairs={{0,8},{8,0},{1,9},{9,1},{2,10},{10,2},{3,11},{11,3},{4,12},{12,4},... | collective-permute-start | bytes 983048 | tf_op jit(solution)/shard_map/cond/branch_0_fun/ppermute | solution.py:573
  46.6 3.1 %attend.14.refs_3_.mine_ref = bf16[5,256,128]{2,1,0:T(8,128)(2,1)S(1)} custom-call(f32[168,256]{1,0:T(8,128)S(1)} %table.3.refs_0_.table_ref, bf16[11,1,256,128]{3,2,1,0:T(8,128)(2,1)S(1)} %get-tuple-element.37.q_ref, bf16[5,2,256,128]{3,2,1,0:T(8,128)(2,1)S(1)} %collective-permute-done.refs_2_.refs_0_, ...), custom_call_target="tpu_custom_call" | custom-call | flops 3000000000 | bytes 1 | tf_op jit(solution)/shard_map/cond/branch_0_fun/attend/pallas_call | solution.py:413
  49.8 2.6 %attend.15 = (bf16[6,128,128]{2,1,0:T(8,128)(2,1)S(1)}, bf16[6,128,128]{2,1,0:T(8,128)(2,1)S(1)}) custom-call(f32[168,256]{1,0:T(8,128)S(1)} %table.3.refs_0_.table_ref, bf16[6,1,256,128]{3,2,1,0:T(8,128)(2,1)S(1)} %collective-permute-done.7.q_ref, bf16[11,2,256,128]{3,2,1,0:T(8,128)(2,1)S(1)} %get-tuple-element.35.refs_0_.refs_2_.refs_1_, ...), custom_call_target="tpu_custom_call" | custom-call | flops 3000000000 | bytes 1 | tf_op jit(solution)/shard_map/cond/branch_0_fun/attend/pallas_call | solution.py:413
  54.4 1.8 %collective-permute-done.10.refs_4_ = bf16[5,2,256,128]{3,2,1,0:T(8,128)(2,1)S(1)} collective-permute-done((bf16[5,2,256,128]{3,2,1,0:T(8,128)(2,1)S(1)}, bf16[5,2,256,128]{3,2,1,0:T(8,128)(2,1)S(1)}, u32[]{:S(2)}, u32[]{:S(2)}) %collective-permute-start.10) | collective-permute-done | bytes 655392 | tf_op jit(solution)/shard_map/cond/branch_0_fun/ppermute | solution.py:624
  56.2 3.1 %attend.16 = (bf16[5,128,128]{2,1,0:T(8,128)(2,1)S(1)}, bf16[5,128,128]{2,1,0:T(8,128)(2,1)S(1)}) custom-call(f32[168,256]{1,0:T(8,128)S(1)} %table.3.refs_0_.table_ref, bf16[5,1,256,128]{3,2,1,0:T(8,128)(2,1)S(1)} %collective-permute-done.9.q_ref, bf16[5,2,256,128]{3,2,1,0:T(8,128)(2,1)S(1)} %collective-permute-done.2.refs_2_.refs_1_.refs_0_, ...), custom_call_target="tpu_custom_call" | custom-call | flops 3000000000 | bytes 1 | tf_op jit(solution)/shard_map/cond/branch_0_fun/attend/pallas_call | solution.py:413
  61.4 2.6 %attend.17 = bf16[6,256,128]{2,1,0:T(8,128)(2,1)S(1)} custom-call(f32[168,256]{1,0:T(8,128)S(1)} %table.3.refs_0_.table_ref, bf16[11,1,256,128]{3,2,1,0:T(8,128)(2,1)S(1)} %get-tuple-element.37.q_ref, bf16[6,2,256,128]{3,2,1,0:T(8,128)(2,1)S(1)} %collective-permute-done.8.refs_0_, bf16[11,2,256,128]{3,2,1,0:T(8,128)(2,1)S(1)} %get-tuple-element.35.refs_0_.refs_2_.refs_1_, ...), custom_call_target="tpu_custom_call" | custom-call | flops 3000000000 | bytes 1 | tf_op jit(solution)/shard_map/cond/branch_0_fun/attend/pallas_call | solution.py:413
  64.6 2.7 %collective-permute-done.17.refs_6_ = bf16[5,128,128]{2,1,0:T(8,128)(2,1)S(1)} collective-permute-done((bf16[5,128,128]{2,1,0:T(8,128)(2,1)S(1)}, bf16[5,128,128]{2,1,0:T(8,128)(2,1)S(1)}, u32[]{:S(2)}, u32[]{:S(2)}) %collective-permute-start.17) | collective-permute-done | bytes 163872 | tf_op jit(solution)/shard_map/cond/branch_0_fun/ppermute | solution.py:573
  67.4 1.4 %collective-permute-done.19.refs_8_ = bf16[5,128,128]{2,1,0:T(8,128)(2,1)S(1)} collective-permute-done((bf16[5,128,128]{2,1,0:T(8,128)(2,1)S(1)}, bf16[5,128,128]{2,1,0:T(8,128)(2,1)S(1)}, u32[]{:S(2)}, u32[]{:S(2)}) %collective-permute-start.19) | collective-permute-done | bytes 163872 | tf_op jit(solution)/shard_map/cond/branch_0_fun/ppermute | solution.py:576
  68.8 1.7 %assemble.3 = bf16[256,8,256]{2,1,0:T(8,128)(2,1)} custom-call(s32[173]{0:T(256)S(1)} %get-tuple-element.32.plan_ref.plan_in, f32[168,256]{1,0:T(8,128)S(1)} %table.3.refs_0_.table_ref, bf16[5,256,128]{2,1,0:T(8,128)(2,1)S(1)} %mix.13.refs_1_.refs_0_, bf16[3,256,128]{2,1,0:T(8,128)(2,1)S(1)} %get-tuple-element.85.refs_1_, ...), custom_call_target="tpu_custom_call" | custom-call | tf_op jit(solution)/shard_map/cond/branch_0_fun/assemble/pallas_call | solution.py:697
  (42 shorter events, 6.1 us)
Async XLA Ops:
  4.2 18.6 %collective-permute-start.1 = (bf16[5,2,256,128]{3,2,1,0:T(8,128)(2,1)S(1)}, bf16[5,2,256,128]{3,2,1,0:T(8,128)(2,1)S(1)}, u32[]{:S(2)}, u32[]{:S(2)}) collective-permute-start(bf16[5,2,256,128]{3,2,1,0:T(8,128)(2,1)S(1)} %get-tuple-element.38), channel_id=1, source_target_pairs={{0,8},{8,0},{1,9},{9,1},{2,10},{10,2},{3,11},{11,3},{4,12},{12,4},... | collective-permute-start | bytes 1966088 | tf_op jit(solution)/shard_map/cond/branch_0_fun/ppermute | solution.py:573
  7.2 39.4 %collective-permute-start.3 = (bf16[11,2,256,128]{3,2,1,0:T(8,128)(2,1)S(1)}, bf16[11,2,256,128]{3,2,1,0:T(8,128)(2,1)S(1)}, u32[]{:S(2)}, u32[]{:S(2)}) collective-permute-start(bf16[11,2,256,128]{3,2,1,0:T(8,128)(2,1)S(1)} %get-tuple-element.35.refs_0_.refs_2_.refs_1_), channel_id=1, source_target_pairs={{2,0},{4,2},{6,4},{8,10},{10,12},{12,14},{3,1},{5,3},{7,5},{9,11},... | collective-permute-start | bytes 4325384 | tf_op jit(solution)/shard_map/cond/branch_0_fun/ppermute | solution.py:582
  8.5 6.8 %copy-start = (bf16[3,256,4096]{2,1,0:T(8,128)(2,1)S(1)}, bf16[3,256,4096]{2,1,0:T(8,128)(2,1)}, u32[]{:S(2)}) copy-start(bf16[3,256,4096]{2,1,0:T(8,128)(2,1)} %get-tuple-element.34.x_ref) | copy-start | bytes 18874372 | tf_op jit(solution)/shard_map/cond
  10.5 19.9 %collective-permute-start = (bf16[5,2,256,128]{3,2,1,0:T(8,128)(2,1)S(1)}, bf16[5,2,256,128]{3,2,1,0:T(8,128)(2,1)S(1)}, u32[]{:S(2)}, u32[]{:S(2)}) collective-permute-start(bf16[5,2,256,128]{3,2,1,0:T(8,128)(2,1)S(1)} %pack_heads.6.refs_0_), channel_id=1, source_target_pairs={{0,2},{2,4},{4,6},{10,8},{12,10},{14,12},{1,3},{3,5},{5,7},{11,9},... | collective-permute-start | bytes 1966088 | tf_op jit(solution)/shard_map/cond/branch_0_fun/ppermute | solution.py:584
  16.8 22.8 %collective-permute-start.4 = (bf16[6,2,256,128]{3,2,1,0:T(8,128)(2,1)S(1)}, bf16[6,2,256,128]{3,2,1,0:T(8,128)(2,1)S(1)}, u32[]{:S(2)}, u32[]{:S(2)}) collective-permute-start(bf16[6,2,256,128]{3,2,1,0:T(8,128)(2,1)S(1)} %get-tuple-element.36.refs_0_), channel_id=1, source_target_pairs={{0,8},{8,0},{1,9},{9,1},{2,10},{10,2},{3,11},{11,3},{4,12},{12,4},... | collective-permute-start | bytes 2359304 | tf_op jit(solution)/shard_map/cond/branch_0_fun/ppermute | solution.py:573
  20.1 12.9 %collective-permute-start.5 = (bf16[10,256,128]{2,1,0:T(8,128)(2,1)S(1)}, bf16[10,256,128]{2,1,0:T(8,128)(2,1)S(1)}, u32[]{:S(2)}, u32[]{:S(2)}) collective-permute-start(bf16[10,256,128]{2,1,0:T(8,128)(2,1)S(1)} %attend_local.2.refs_1_.mine_ref), channel_id=1, source_target_pairs={{0,1},{1,0},{2,3},{3,2},{4,5},{5,4},{6,7},{7,6},{8,9},{9,8},{10,11... | collective-permute-start | bytes 1966088 | tf_op jit(solution)/shard_map/cond/branch_0_fun/ppermute | solution.py:576
  22.8 21.1 %collective-permute-start.2 = (bf16[5,2,256,128]{3,2,1,0:T(8,128)(2,1)S(1)}, bf16[5,2,256,128]{3,2,1,0:T(8,128)(2,1)S(1)}, u32[]{:S(2)}, u32[]{:S(2)}) collective-permute-start(bf16[5,2,256,128]{3,2,1,0:T(8,128)(2,1)S(1)} %gate.16.refs_1_.refs_3_.refs_2_), channel_id=1, source_target_pairs={{0,2},{2,4},{4,6},{10,8},{12,10},{14,12},{1,3},{3,5},{5,7},{11,9},... | collective-permute-start | bytes 1966088 | tf_op jit(solution)/shard_map/cond/branch_0_fun/ppermute | solution.py:616
  30.4 19.4 %collective-permute-start.7 = (bf16[6,1,256,128]{3,2,1,0:T(8,128)(2,1)S(1)}, bf16[6,1,256,128]{3,2,1,0:T(8,128)(2,1)S(1)}, u32[]{:S(2)}, u32[]{:S(2)}) collective-permute-start(bf16[6,1,256,128]{3,2,1,0:T(8,128)(2,1)S(1)} %gate.17.refs_1_), channel_id=1, source_target_pairs={{0,8},{8,0},{1,9},{9,1},{2,10},{10,2},{3,11},{11,3},{4,12},{12,4},... | collective-permute-start | bytes 1179656 | tf_op jit(solution)/shard_map/cond/branch_0_fun/ppermute | solution.py:573
  33.4 22.8 %collective-permute-start.10 = (bf16[5,2,256,128]{3,2,1,0:T(8,128)(2,1)S(1)}, bf16[5,2,256,128]{3,2,1,0:T(8,128)(2,1)S(1)}, u32[]{:S(2)}, u32[]{:S(2)}) collective-permute-start(bf16[5,2,256,128]{3,2,1,0:T(8,128)(2,1)S(1)} %gate.18.refs_1_), channel_id=1, source_target_pairs={{2,0},{4,2},{6,4},{8,10},{10,12},{12,14},{3,1},{5,3},{7,5},{9,11},... | collective-permute-start | bytes 1966088 | tf_op jit(solution)/shard_map/cond/branch_0_fun/ppermute | solution.py:624
  39.6 21.4 %collective-permute-start.8 = (bf16[6,2,256,128]{3,2,1,0:T(8,128)(2,1)S(1)}, bf16[6,2,256,128]{3,2,1,0:T(8,128)(2,1)S(1)}, u32[]{:S(2)}, u32[]{:S(2)}) collective-permute-start(bf16[6,2,256,128]{3,2,1,0:T(8,128)(2,1)S(1)} %gate.19.refs_1_.refs_2_), channel_id=1, source_target_pairs={{0,2},{2,4},{4,6},{10,8},{12,10},{14,12},{1,3},{3,5},{5,7},{11,9},... | collective-permute-start | bytes 2359304 | tf_op jit(solution)/shard_map/cond/branch_0_fun/ppermute | solution.py:631
  43.9 12.3 %collective-permute-start.9 = (bf16[5,1,256,128]{3,2,1,0:T(8,128)(2,1)S(1)}, bf16[5,1,256,128]{3,2,1,0:T(8,128)(2,1)S(1)}, u32[]{:S(2)}, u32[]{:S(2)}) collective-permute-start(bf16[5,1,256,128]{3,2,1,0:T(8,128)(2,1)S(1)} %gate.20.refs_5_), channel_id=1, source_target_pairs={{0,8},{8,0},{1,9},{9,1},{2,10},{10,2},{3,11},{11,3},{4,12},{12,4},... | collective-permute-start | bytes 983048 | tf_op jit(solution)/shard_map/cond/branch_0_fun/ppermute | solution.py:573
  49.7 3.3 %collective-permute-start.6 = (bf16[5,256,128]{2,1,0:T(8,128)(2,1)S(1)}, bf16[5,256,128]{2,1,0:T(8,128)(2,1)S(1)}, u32[]{:S(2)}, u32[]{:S(2)}) collective-permute-start(bf16[5,256,128]{2,1,0:T(8,128)(2,1)S(1)} %attend.14.refs_3_.mine_ref), channel_id=1, source_target_pairs={{0,1},{1,0},{2,3},{3,2},{4,5},{5,4},{6,7},{7,6},{8,9},{9,8},{10,11... | collective-permute-start | bytes 983048 | tf_op jit(solution)/shard_map/cond/branch_0_fun/ppermute | solution.py:576
  52.4 1.6 %collective-permute-start.11 = (bf16[6,128,128]{2,1,0:T(8,128)(2,1)S(1)}, bf16[6,128,128]{2,1,0:T(8,128)(2,1)S(1)}, u32[]{:S(2)}, u32[]{:S(2)}) collective-permute-start(bf16[6,128,128]{2,1,0:T(8,128)(2,1)S(1)} %get-tuple-element.42), channel_id=1, source_target_pairs={{0,1},{1,0},{2,3},{3,2},{4,5},{5,4},{6,7},{7,6},{8,9},{9,8},{10,11... | collective-permute-start | bytes 589832 | tf_op jit(solution)/shard_map/cond/branch_0_fun/ppermute | solution.py:576
  54.1 7.2 %collective-permute-start.14 = (bf16[6,128,128]{2,1,0:T(8,128)(2,1)S(1)}, bf16[6,128,128]{2,1,0:T(8,128)(2,1)S(1)}, u32[]{:S(2)}, u32[]{:S(2)}) collective-permute-start(bf16[6,128,128]{2,1,0:T(8,128)(2,1)S(1)} %mix.14.refs_5_), channel_id=1, source_target_pairs={{0,8},{8,0},{1,9},{9,1},{2,10},{10,2},{3,11},{11,3},{4,12},{12,4},... | collective-permute-start | bytes 589832 | tf_op jit(solution)/shard_map/cond/branch_0_fun/ppermute | solution.py:573
  59.3 1.5 %collective-permute-start.13 = (bf16[3,128,128]{2,1,0:T(8,128)(2,1)S(1)}, bf16[3,128,128]{2,1,0:T(8,128)(2,1)S(1)}, u32[]{:S(2)}, u32[]{:S(2)}) collective-permute-start(bf16[3,128,128]{2,1,0:T(8,128)(2,1)S(1)} %slice.29), channel_id=1, source_target_pairs={{0,1},{1,0},{2,3},{3,2},{4,5},{5,4},{6,7},{7,6},{8,9},{9,8},{10,11... | collective-permute-start | bytes 294920 | tf_op jit(solution)/shard_map/cond/branch_0_fun/ppermute | solution.py:576
  59.4 1.4 %collective-permute-start.12 = (bf16[2,128,128]{2,1,0:T(8,128)(2,1)S(1)}, bf16[2,128,128]{2,1,0:T(8,128)(2,1)S(1)}, u32[]{:S(2)}, u32[]{:S(2)}) collective-permute-start(bf16[2,128,128]{2,1,0:T(8,128)(2,1)S(1)} %slice.28), channel_id=1, source_target_pairs={{0,1},{1,0},{2,3},{3,2},{4,5},{5,4},{6,7},{7,6},{8,9},{9,8},{10,11... | collective-permute-start | bytes 196616 | tf_op jit(solution)/shard_map/cond/branch_0_fun/ppermute | solution.py:576
  60.8 6.5 %collective-permute-start.17 = (bf16[5,128,128]{2,1,0:T(8,128)(2,1)S(1)}, bf16[5,128,128]{2,1,0:T(8,128)(2,1)S(1)}, u32[]{:S(2)}, u32[]{:S(2)}) collective-permute-start(bf16[5,128,128]{2,1,0:T(8,128)(2,1)S(1)} %mix.15.refs_3_), channel_id=1, source_target_pairs={{0,8},{8,0},{1,9},{9,1},{2,10},{10,2},{3,11},{11,3},{4,12},{12,4},... | collective-permute-start | bytes 491528 | tf_op jit(solution)/shard_map/cond/branch_0_fun/ppermute | solution.py:573
  64.0 3.4 %collective-permute-start.15 = (bf16[3,256,128]{2,1,0:T(8,128)(2,1)S(1)}, bf16[3,256,128]{2,1,0:T(8,128)(2,1)S(1)}, u32[]{:S(2)}, u32[]{:S(2)}) collective-permute-start(bf16[3,256,128]{2,1,0:T(8,128)(2,1)S(1)} %get-tuple-element.85.refs_1_), channel_id=1, source_target_pairs={{0,1},{1,0},{2,3},{3,2},{4,5},{5,4},{6,7},{7,6},{8,9},{9,8},{10,11... | collective-permute-start | bytes 589832 | tf_op jit(solution)/shard_map/cond/branch_0_fun/ppermute | solution.py:576
  64.1 3.3 %collective-permute-start.16 = (bf16[3,256,128]{2,1,0:T(8,128)(2,1)S(1)}, bf16[3,256,128]{2,1,0:T(8,128)(2,1)S(1)}, u32[]{:S(2)}, u32[]{:S(2)}) collective-permute-start(bf16[3,256,128]{2,1,0:T(8,128)(2,1)S(1)} %get-tuple-element.84.refs_2_), channel_id=1, source_target_pairs={{0,1},{1,0},{2,3},{3,2},{4,5},{5,4},{6,7},{7,6},{8,9},{9,8},{10,11... | collective-permute-start | bytes 589832 | tf_op jit(solution)/shard_map/cond/branch_0_fun/ppermute | solution.py:576
  64.6 2.8 %collective-permute-start.18 = (bf16[6,128,128]{2,1,0:T(8,128)(2,1)S(1)}, bf16[6,128,128]{2,1,0:T(8,128)(2,1)S(1)}, u32[]{:S(2)}, u32[]{:S(2)}) collective-permute-start(bf16[6,128,128]{2,1,0:T(8,128)(2,1)S(1)} %collective-permute-done.14.refs_4_.refs_5_), channel_id=1, source_target_pairs={{0,1},{1,0},{2,3},{3,2},{4,5},{5,4},{6,7},{7,6},{8,9},{9,8},{10,11... | collective-permute-start | bytes 589832 | tf_op jit(solution)/shard_map/cond/branch_0_fun/ppermute | solution.py:576
  67.4 1.4 %collective-permute-start.19 = (bf16[5,128,128]{2,1,0:T(8,128)(2,1)S(1)}, bf16[5,128,128]{2,1,0:T(8,128)(2,1)S(1)}, u32[]{:S(2)}, u32[]{:S(2)}) collective-permute-start(bf16[5,128,128]{2,1,0:T(8,128)(2,1)S(1)} %collective-permute-done.17.refs_6_), channel_id=1, source_target_pairs={{0,1},{1,0},{2,3},{3,2},{4,5},{5,4},{6,7},{7,6},{8,9},{9,8},{10,11... | collective-permute-start | bytes 491528 | tf_op jit(solution)/shard_map/cond/branch_0_fun/ppermute | solution.py:576

commit v9 on v7

--- a/solution.py
+++ b/solution.py
@@ -519,7 +519,7 @@
     outs = seq_count * per_half
     at = Layout(heads, outs)
     rows_at = Rows(heads)
-    x3 = jnp.transpose(qkv[0], (1, 0, 2))
+    x3 = pltpu.with_memory_space_constraint(jnp.transpose(qkv[0], (1, 0, 2)), pltpu.HBM)
     lead, base = rungs[0][1] // 2, rungs[0][0] // 2
     plan, rung, kv_lead, kv_base = pl.pallas_call(
         functools.partial(plan_kernel, at, rungs, (seq_count, cfg_count)),

time: 71.5 us -> 71.6 us (level)
  waiting for transfers between devices: 18.9 us -> 16.8 us
  Pallas kernels: 23.3 us -> 25.2 us
    ppermute x6, waiting for transfers between devices: 10.4 us -> 8.82 us  [cross(): return lax.ppermute(a, 'seq', SWAP)]
    pallas_call x1, Pallas kernels: 2.5 us -> 3.56 us  [attend_local(): pl.pallas_call(functools.partial(local_kernel, count, heads_at), out_shap...]
    pallas_call x2, Pallas kernels: 3.53 us -> 4.3 us  [pack(): pl.pallas_call(functools.partial(pack_kernel, jobs, len(after)), out_shap...]
  transfers between devices with their start and end apart: 20 -> 20, of which waited for: 9 -> 8; matrix products, arithmetic and copies ran while one was open for 0% -> 0% of each run, Pallas kernels for 26% -> 29%
where the time goes in v9:
time: 71.6 us; the launch traced here: 71.2 us
  starting transfers between devices  26.8 us (37%)
  Pallas kernels  25.2 us (35%)
  waiting for transfers between devices  16.8 us (23%)
  between operations  1.53 us (2%)
  loops' own time  0.77 us (1%)
    pallas_call x4, Pallas kernels, attend_slots(): pl.pallas_call(functools.partial(attend_kernel, count, q_offset, offsets,...  11.4 us
    ppermute x6, starting transfers between devices, cross(): return lax.ppermute(a, 'seq', SWAP)  9.43 us
    ppermute x6, waiting for transfers between devices, cross(): return lax.ppermute(a, 'seq', SWAP)  8.82 us
    ppermute x1, starting transfers between devices, attempt(): far_own = [lax.ppermute(kv_far, grid_axes, onward)]  4.59 us
    pallas_call x2, Pallas kernels, pack(): pl.pallas_call(functools.partial(pack_kernel, jobs, len(after)), out_shap...  4.3 us
    ppermute x1, starting transfers between devices, attempt(): near_across[k] = lax.ppermute(across[k], grid_axes, onward)  4.27 us
    ppermute x1, starting transfers between devices, attempt(): near_across[0] = lax.ppermute(across[0], grid_axes, onward)  4.08 us
    pallas_call x1, Pallas kernels, attend_local(): pl.pallas_call(functools.partial(local_kernel, count, heads_at), out_shap...  3.56 us
  transfers between devices with their start and end apart: 20, of which 8 were waited for; matrix products, arithmetic and copies ran while one was open for 0% of the time, Pallas kernels for 29%

profile of v9, /device:TPU:0, one launch (start us, length us, event | category | flops | bytes accessed | tf_op | source)
XLA Modules:
  0.0 71.2 jit_solution(1096069064626923308)
XLA Ops:
  0.7 2.9 %plan.1 = (s32[173]{0:T(256)S(1)}, s32[1]{0:T(128)}, bf16[5,2,256,128]{3,2,1,0:T(8,128)(2,1)S(1)}, bf16[11,2,256,128]{3,2,1,0:T(8,128)(2,1)S(1)}) custom-call(s32[32]{0:T(128)} %windows_in.1, s32[8]{0:T(128)} %segments_in.1, s32[1]{0:T(128)S(6)} %copy.43.step_in, bf16[3,256,4096]{2,1,0:T(8,128)(2,1)} %bitcast.4), custom_call_target="tpu_custom_call" | custom-call | tf_op jit(solution)/shard_map/plan/pallas_call | solution.py:524
  4.2 66.8 %conditional.1 = (bf16[256,8,256]{2,1,0:T(8,128)(2,1)}) conditional(s32[]{:T(128)} %bitcast.2, (s32[173]{0:T(256)S(1)}, bf16[3,256,4096]{2,1,0:T(8,128)(2,1)}, bf16[11,2,256,128]{3,2,1,0:T(8,128)(2,1)S(1)}, bf16[5,2,256,128]{3,2,1,0:T(8,128)(2,1)S(1)}) %tuple.24, (s32[173]{0:T(256)S(1)}, bf16[3,256,4096]{2,1,0:T(8,128)(2,1)}, ...), branch_computations={%region_0.0_spmd, %region_1.0_spmd, %region_2.0_spmd} | conditional | flops 44499996672 | bytes 59704508 | solution.py:709
  4.2 3.0 %collective-permute-start.1 = (bf16[5,2,256,128]{3,2,1,0:T(8,128)(2,1)S(1)}, bf16[5,2,256,128]{3,2,1,0:T(8,128)(2,1)S(1)}, u32[]{:S(2)}, u32[]{:S(2)}) collective-permute-start(bf16[5,2,256,128]{3,2,1,0:T(8,128)(2,1)S(1)} %get-tuple-element.38), channel_id=1, source_target_pairs={{0,8},{8,0},{1,9},{9,1},{2,10},{10,2},{3,11},{11,3},{4,12},{12,4},... | collective-permute-start | bytes 1966088 | tf_op jit(solution)/shard_map/cond/branch_0_fun/ppermute | solution.py:568
  7.2 1.3 %collective-permute-start.3 = (bf16[11,2,256,128]{3,2,1,0:T(8,128)(2,1)S(1)}, bf16[11,2,256,128]{3,2,1,0:T(8,128)(2,1)S(1)}, u32[]{:S(2)}, u32[]{:S(2)}) collective-permute-start(bf16[11,2,256,128]{3,2,1,0:T(8,128)(2,1)S(1)} %get-tuple-element.35.refs_0_.refs_2_.refs_1_), channel_id=1, source_target_pairs={{2,0},{4,2},{6,4},{8,10},{10,12},{12,14},{3,1},{5,3},{7,5},{9,11},... | collective-permute-start | bytes 4325384 | tf_op jit(solution)/shard_map/cond/branch_0_fun/ppermute | solution.py:577
  8.5 1.8 %pack_heads.6.refs_0_ = bf16[5,2,256,128]{3,2,1,0:T(8,128)(2,1)S(1)} custom-call(s32[173]{0:T(256)S(1)} %get-tuple-element.32.plan_ref.plan_in, bf16[3,256,4096]{2,1,0:T(8,128)(2,1)} %get-tuple-element.34.x_ref, bf16[11,2,256,128]{3,2,1,0:T(8,128)(2,1)S(1)} %get-tuple-element.35.refs_0_.refs_2_.refs_1_), custom_call_target="tpu_custom_call" | custom-call | flops 10000000000 | bytes 1 | tf_op jit(solution)/shard_map/cond/branch_0_fun/pack_heads/pallas_call | solution.py:248
  10.3 4.6 %collective-permute-start = (bf16[5,2,256,128]{3,2,1,0:T(8,128)(2,1)S(1)}, bf16[5,2,256,128]{3,2,1,0:T(8,128)(2,1)S(1)}, u32[]{:S(2)}, u32[]{:S(2)}) collective-permute-start(bf16[5,2,256,128]{3,2,1,0:T(8,128)(2,1)S(1)} %pack_heads.6.refs_0_), channel_id=1, source_target_pairs={{0,2},{2,4},{4,6},{10,8},{12,10},{14,12},{1,3},{3,5},{5,7},{11,9},... | collective-permute-start | bytes 1966088 | tf_op jit(solution)/shard_map/cond/branch_0_fun/ppermute | solution.py:579
  14.9 2.5 %pack_heads.7 = (bf16[11,1,256,128]{3,2,1,0:T(8,128)(2,1)S(1)}, bf16[6,1,256,128]{3,2,1,0:T(8,128)(2,1)S(1)}, bf16[5,1,256,128]{3,2,1,0:T(8,128)(2,1)S(1)}, bf16[6,2,256,128]{3,2,1,0:T(8,128)(2,1)S(1)}) custom-call(s32[173]{0:T(256)S(1)} %get-tuple-element.32.plan_ref.plan_in, bf16[3,256,4096]{2,1,0:T(8,128)(2,1)} %get-tuple-element.34.x_ref, ...), custom_call_target="tpu_custom_call" | custom-call | flops 10000000000 | bytes 1 | tf_op jit(solution)/shard_map/cond/branch_0_fun/pack_heads/pallas_call | solution.py:248
  18.2 3.6 %attend_local.2.refs_1_.mine_ref = bf16[10,256,128]{2,1,0:T(8,128)(2,1)S(1)} custom-call(s32[173]{0:T(256)S(1)} %get-tuple-element.32.plan_ref.plan_in, bf16[3,256,4096]{2,1,0:T(8,128)(2,1)} %get-tuple-element.34.x_ref, f32[168,256]{1,0:T(8,128)S(1)} %table.3.refs_0_.table_ref), custom_call_target="tpu_custom_call" | custom-call | flops 3000000000 | bytes 1 | tf_op jit(solution)/shard_map/cond/branch_0_fun/attend_local/pallas_call | solution.py:349
  22.8 4.1 %collective-permute-start.2 = (bf16[5,2,256,128]{3,2,1,0:T(8,128)(2,1)S(1)}, bf16[5,2,256,128]{3,2,1,0:T(8,128)(2,1)S(1)}, u32[]{:S(2)}, u32[]{:S(2)}) collective-permute-start(bf16[5,2,256,128]{3,2,1,0:T(8,128)(2,1)S(1)} %gate.16.refs_1_.refs_3_.refs_2_), channel_id=1, source_target_pairs={{0,2},{2,4},{4,6},{10,8},{12,10},{14,12},{1,3},{3,5},{5,7},{11,9},... | collective-permute-start | bytes 1966088 | tf_op jit(solution)/shard_map/cond/branch_0_fun/ppermute | solution.py:611
  26.9 3.0 %collective-permute-done.refs_2_.refs_0_ = bf16[5,2,256,128]{3,2,1,0:T(8,128)(2,1)S(1)} collective-permute-done((bf16[5,2,256,128]{3,2,1,0:T(8,128)(2,1)S(1)}, bf16[5,2,256,128]{3,2,1,0:T(8,128)(2,1)S(1)}, u32[]{:S(2)}, u32[]{:S(2)}) %collective-permute-start) | collective-permute-done | bytes 655392 | tf_op jit(solution)/shard_map/cond/branch_0_fun/ppermute | solution.py:579
  29.9 2.7 %collective-permute-start.7 = (bf16[6,1,256,128]{3,2,1,0:T(8,128)(2,1)S(1)}, bf16[6,1,256,128]{3,2,1,0:T(8,128)(2,1)S(1)}, u32[]{:S(2)}, u32[]{:S(2)}) collective-permute-start(bf16[6,1,256,128]{3,2,1,0:T(8,128)(2,1)S(1)} %gate.17.refs_1_), channel_id=1, source_target_pairs={{0,8},{8,0},{1,9},{9,1},{2,10},{10,2},{3,11},{11,3},{4,12},{12,4},... | collective-permute-start | bytes 1179656 | tf_op jit(solution)/shard_map/cond/branch_0_fun/ppermute | solution.py:568
  33.0 1.3 %collective-permute-start.10 = (bf16[5,2,256,128]{3,2,1,0:T(8,128)(2,1)S(1)}, bf16[5,2,256,128]{3,2,1,0:T(8,128)(2,1)S(1)}, u32[]{:S(2)}, u32[]{:S(2)}) collective-permute-start(bf16[5,2,256,128]{3,2,1,0:T(8,128)(2,1)S(1)} %gate.18.refs_1_), channel_id=1, source_target_pairs={{2,0},{4,2},{6,4},{8,10},{10,12},{12,14},{3,1},{5,3},{7,5},{9,11},... | collective-permute-start | bytes 1966088 | tf_op jit(solution)/shard_map/cond/branch_0_fun/ppermute | solution.py:619
  34.3 5.3 %collective-permute-done.4.refs_0_ = bf16[6,2,256,128]{3,2,1,0:T(8,128)(2,1)S(1)} collective-permute-done((bf16[6,2,256,128]{3,2,1,0:T(8,128)(2,1)S(1)}, bf16[6,2,256,128]{3,2,1,0:T(8,128)(2,1)S(1)}, u32[]{:S(2)}, u32[]{:S(2)}) %collective-permute-start.4) | collective-permute-done | bytes 786464 | tf_op jit(solution)/shard_map/cond/branch_0_fun/ppermute | solution.py:568
  39.6 4.3 %collective-permute-start.8 = (bf16[6,2,256,128]{3,2,1,0:T(8,128)(2,1)S(1)}, bf16[6,2,256,128]{3,2,1,0:T(8,128)(2,1)S(1)}, u32[]{:S(2)}, u32[]{:S(2)}) collective-permute-start(bf16[6,2,256,128]{3,2,1,0:T(8,128)(2,1)S(1)} %gate.19.refs_1_.refs_2_), channel_id=1, source_target_pairs={{0,2},{2,4},{4,6},{10,8},{12,10},{14,12},{1,3},{3,5},{5,7},{11,9},... | collective-permute-start | bytes 2359304 | tf_op jit(solution)/shard_map/cond/branch_0_fun/ppermute | solution.py:626
  43.9 1.9 %collective-permute-start.9 = (bf16[5,1,256,128]{3,2,1,0:T(8,128)(2,1)S(1)}, bf16[5,1,256,128]{3,2,1,0:T(8,128)(2,1)S(1)}, u32[]{:S(2)}, u32[]{:S(2)}) collective-permute-start(bf16[5,1,256,128]{3,2,1,0:T(8,128)(2,1)S(1)} %gate.20.refs_5_), channel_id=1, source_target_pairs={{0,8},{8,0},{1,9},{9,1},{2,10},{10,2},{3,11},{11,3},{4,12},{12,4},... | collective-permute-start | bytes 983048 | tf_op jit(solution)/shard_map/cond/branch_0_fun/ppermute | solution.py:568
  45.8 3.1 %attend.14.refs_3_.mine_ref = bf16[5,256,128]{2,1,0:T(8,128)(2,1)S(1)} custom-call(f32[168,256]{1,0:T(8,128)S(1)} %table.3.refs_0_.table_ref, bf16[11,1,256,128]{3,2,1,0:T(8,128)(2,1)S(1)} %get-tuple-element.37.q_ref, bf16[5,2,256,128]{3,2,1,0:T(8,128)(2,1)S(1)} %collective-permute-done.refs_2_.refs_0_, ...), custom_call_target="tpu_custom_call" | custom-call | flops 3000000000 | bytes 1 | tf_op jit(solution)/shard_map/cond/branch_0_fun/attend/pallas_call | solution.py:410
  49.0 2.6 %attend.15 = (bf16[6,128,128]{2,1,0:T(8,128)(2,1)S(1)}, bf16[6,128,128]{2,1,0:T(8,128)(2,1)S(1)}) custom-call(f32[168,256]{1,0:T(8,128)S(1)} %table.3.refs_0_.table_ref, bf16[6,1,256,128]{3,2,1,0:T(8,128)(2,1)S(1)} %collective-permute-done.7.q_ref, bf16[11,2,256,128]{3,2,1,0:T(8,128)(2,1)S(1)} %get-tuple-element.35.refs_0_.refs_2_.refs_1_, ...), custom_call_target="tpu_custom_call" | custom-call | flops 3000000000 | bytes 1 | tf_op jit(solution)/shard_map/cond/branch_0_fun/attend/pallas_call | solution.py:410
  53.4 1.0 %collective-permute-start.14 = (bf16[6,128,128]{2,1,0:T(8,128)(2,1)S(1)}, bf16[6,128,128]{2,1,0:T(8,128)(2,1)S(1)}, u32[]{:S(2)}, u32[]{:S(2)}) collective-permute-start(bf16[6,128,128]{2,1,0:T(8,128)(2,1)S(1)} %mix.14.refs_5_), channel_id=1, source_target_pairs={{0,8},{8,0},{1,9},{9,1},{2,10},{10,2},{3,11},{11,3},{4,12},{12,4},... | collective-permute-start | bytes 589832 | tf_op jit(solution)/shard_map/cond/branch_0_fun/ppermute | solution.py:568
  54.4 1.8 %collective-permute-done.10.refs_4_ = bf16[5,2,256,128]{3,2,1,0:T(8,128)(2,1)S(1)} collective-permute-done((bf16[5,2,256,128]{3,2,1,0:T(8,128)(2,1)S(1)}, bf16[5,2,256,128]{3,2,1,0:T(8,128)(2,1)S(1)}, u32[]{:S(2)}, u32[]{:S(2)}) %collective-permute-start.10) | collective-permute-done | bytes 655392 | tf_op jit(solution)/shard_map/cond/branch_0_fun/ppermute | solution.py:619
  56.2 3.1 %attend.16 = (bf16[5,128,128]{2,1,0:T(8,128)(2,1)S(1)}, bf16[5,128,128]{2,1,0:T(8,128)(2,1)S(1)}) custom-call(f32[168,256]{1,0:T(8,128)S(1)} %table.3.refs_0_.table_ref, bf16[5,1,256,128]{3,2,1,0:T(8,128)(2,1)S(1)} %collective-permute-done.9.q_ref, bf16[5,2,256,128]{3,2,1,0:T(8,128)(2,1)S(1)} %collective-permute-done.2.refs_2_.refs_1_.refs_0_, ...), custom_call_target="tpu_custom_call" | custom-call | flops 3000000000 | bytes 1 | tf_op jit(solution)/shard_map/cond/branch_0_fun/attend/pallas_call | solution.py:410
  61.5 2.6 %attend.17 = bf16[6,256,128]{2,1,0:T(8,128)(2,1)S(1)} custom-call(f32[168,256]{1,0:T(8,128)S(1)} %table.3.refs_0_.table_ref, bf16[11,1,256,128]{3,2,1,0:T(8,128)(2,1)S(1)} %get-tuple-element.37.q_ref, bf16[6,2,256,128]{3,2,1,0:T(8,128)(2,1)S(1)} %collective-permute-done.8.refs_0_, bf16[11,2,256,128]{3,2,1,0:T(8,128)(2,1)S(1)} %get-tuple-element.35.refs_0_.refs_2_.refs_1_, ...), custom_call_target="tpu_custom_call" | custom-call | flops 3000000000 | bytes 1 | tf_op jit(solution)/shard_map/cond/branch_0_fun/attend/pallas_call | solution.py:410
  64.8 2.6 %collective-permute-done.17.refs_6_ = bf16[5,128,128]{2,1,0:T(8,128)(2,1)S(1)} collective-permute-done((bf16[5,128,128]{2,1,0:T(8,128)(2,1)S(1)}, bf16[5,128,128]{2,1,0:T(8,128)(2,1)S(1)}, u32[]{:S(2)}, u32[]{:S(2)}) %collective-permute-start.17) | collective-permute-done | bytes 163872 | tf_op jit(solution)/shard_map/cond/branch_0_fun/ppermute | solution.py:568
  67.4 1.4 %collective-permute-done.19.refs_8_ = bf16[5,128,128]{2,1,0:T(8,128)(2,1)S(1)} collective-permute-done((bf16[5,128,128]{2,1,0:T(8,128)(2,1)S(1)}, bf16[5,128,128]{2,1,0:T(8,128)(2,1)S(1)}, u32[]{:S(2)}, u32[]{:S(2)}) %collective-permute-start.19) | collective-permute-done | bytes 163872 | tf_op jit(solution)/shard_map/cond/branch_0_fun/ppermute | solution.py:571
  68.8 1.7 %assemble.3 = bf16[256,8,256]{2,1,0:T(8,128)(2,1)} custom-call(s32[173]{0:T(256)S(1)} %get-tuple-element.32.plan_ref.plan_in, f32[168,256]{1,0:T(8,128)S(1)} %table.3.refs_0_.table_ref, bf16[5,256,128]{2,1,0:T(8,128)(2,1)S(1)} %mix.13.refs_1_.refs_0_, bf16[3,256,128]{2,1,0:T(8,128)(2,1)S(1)} %get-tuple-element.85.refs_1_, ...), custom_call_target="tpu_custom_call" | custom-call | tf_op jit(solution)/shard_map/cond/branch_0_fun/assemble/pallas_call | solution.py:693
  (40 shorter events, 6.9 us)
Async XLA Ops:
  4.2 18.6 %collective-permute-start.1 = (bf16[5,2,256,128]{3,2,1,0:T(8,128)(2,1)S(1)}, bf16[5,2,256,128]{3,2,1,0:T(8,128)(2,1)S(1)}, u32[]{:S(2)}, u32[]{:S(2)}) collective-permute-start(bf16[5,2,256,128]{3,2,1,0:T(8,128)(2,1)S(1)} %get-tuple-element.38), channel_id=1, source_target_pairs={{0,8},{8,0},{1,9},{9,1},{2,10},{10,2},{3,11},{11,3},{4,12},{12,4},... | collective-permute-start | bytes 1966088 | tf_op jit(solution)/shard_map/cond/branch_0_fun/ppermute | solution.py:568
  7.2 38.6 %collective-permute-start.3 = (bf16[11,2,256,128]{3,2,1,0:T(8,128)(2,1)S(1)}, bf16[11,2,256,128]{3,2,1,0:T(8,128)(2,1)S(1)}, u32[]{:S(2)}, u32[]{:S(2)}) collective-permute-start(bf16[11,2,256,128]{3,2,1,0:T(8,128)(2,1)S(1)} %get-tuple-element.35.refs_0_.refs_2_.refs_1_), channel_id=1, source_target_pairs={{2,0},{4,2},{6,4},{8,10},{10,12},{12,14},{3,1},{5,3},{7,5},{9,11},... | collective-permute-start | bytes 4325384 | tf_op jit(solution)/shard_map/cond/branch_0_fun/ppermute | solution.py:577
  10.3 19.7 %collective-permute-start = (bf16[5,2,256,128]{3,2,1,0:T(8,128)(2,1)S(1)}, bf16[5,2,256,128]{3,2,1,0:T(8,128)(2,1)S(1)}, u32[]{:S(2)}, u32[]{:S(2)}) collective-permute-start(bf16[5,2,256,128]{3,2,1,0:T(8,128)(2,1)S(1)} %pack_heads.6.refs_0_), channel_id=1, source_target_pairs={{0,2},{2,4},{4,6},{10,8},{12,10},{14,12},{1,3},{3,5},{5,7},{11,9},... | collective-permute-start | bytes 1966088 | tf_op jit(solution)/shard_map/cond/branch_0_fun/ppermute | solution.py:579
  17.4 22.2 %collective-permute-start.4 = (bf16[6,2,256,128]{3,2,1,0:T(8,128)(2,1)S(1)}, bf16[6,2,256,128]{3,2,1,0:T(8,128)(2,1)S(1)}, u32[]{:S(2)}, u32[]{:S(2)}) collective-permute-start(bf16[6,2,256,128]{3,2,1,0:T(8,128)(2,1)S(1)} %get-tuple-element.36.refs_0_), channel_id=1, source_target_pairs={{0,8},{8,0},{1,9},{9,1},{2,10},{10,2},{3,11},{11,3},{4,12},{12,4},... | collective-permute-start | bytes 2359304 | tf_op jit(solution)/shard_map/cond/branch_0_fun/ppermute | solution.py:568
  21.8 10.9 %collective-permute-start.5 = (bf16[10,256,128]{2,1,0:T(8,128)(2,1)S(1)}, bf16[10,256,128]{2,1,0:T(8,128)(2,1)S(1)}, u32[]{:S(2)}, u32[]{:S(2)}) collective-permute-start(bf16[10,256,128]{2,1,0:T(8,128)(2,1)S(1)} %attend_local.2.refs_1_.mine_ref), channel_id=1, source_target_pairs={{0,1},{1,0},{2,3},{3,2},{4,5},{5,4},{6,7},{7,6},{8,9},{9,8},{10,11... | collective-permute-start | bytes 1966088 | tf_op jit(solution)/shard_map/cond/branch_0_fun/ppermute | solution.py:571
  22.8 21.1 %collective-permute-start.2 = (bf16[5,2,256,128]{3,2,1,0:T(8,128)(2,1)S(1)}, bf16[5,2,256,128]{3,2,1,0:T(8,128)(2,1)S(1)}, u32[]{:S(2)}, u32[]{:S(2)}) collective-permute-start(bf16[5,2,256,128]{3,2,1,0:T(8,128)(2,1)S(1)} %gate.16.refs_1_.refs_3_.refs_2_), channel_id=1, source_target_pairs={{0,2},{2,4},{4,6},{10,8},{12,10},{14,12},{1,3},{3,5},{5,7},{11,9},... | collective-permute-start | bytes 1966088 | tf_op jit(solution)/shard_map/cond/branch_0_fun/ppermute | solution.py:611
  29.9 19.1 %collective-permute-start.7 = (bf16[6,1,256,128]{3,2,1,0:T(8,128)(2,1)S(1)}, bf16[6,1,256,128]{3,2,1,0:T(8,128)(2,1)S(1)}, u32[]{:S(2)}, u32[]{:S(2)}) collective-permute-start(bf16[6,1,256,128]{3,2,1,0:T(8,128)(2,1)S(1)} %gate.17.refs_1_), channel_id=1, source_target_pairs={{0,8},{8,0},{1,9},{9,1},{2,10},{10,2},{3,11},{11,3},{4,12},{12,4},... | collective-permute-start | bytes 1179656 | tf_op jit(solution)/shard_map/cond/branch_0_fun/ppermute | solution.py:568
  33.0 23.2 %collective-permute-start.10 = (bf16[5,2,256,128]{3,2,1,0:T(8,128)(2,1)S(1)}, bf16[5,2,256,128]{3,2,1,0:T(8,128)(2,1)S(1)}, u32[]{:S(2)}, u32[]{:S(2)}) collective-permute-start(bf16[5,2,256,128]{3,2,1,0:T(8,128)(2,1)S(1)} %gate.18.refs_1_), channel_id=1, source_target_pairs={{2,0},{4,2},{6,4},{8,10},{10,12},{12,14},{3,1},{5,3},{7,5},{9,11},... | collective-permute-start | bytes 1966088 | tf_op jit(solution)/shard_map/cond/branch_0_fun/ppermute | solution.py:619
  39.6 21.9 %collective-permute-start.8 = (bf16[6,2,256,128]{3,2,1,0:T(8,128)(2,1)S(1)}, bf16[6,2,256,128]{3,2,1,0:T(8,128)(2,1)S(1)}, u32[]{:S(2)}, u32[]{:S(2)}) collective-permute-start(bf16[6,2,256,128]{3,2,1,0:T(8,128)(2,1)S(1)} %gate.19.refs_1_.refs_2_), channel_id=1, source_target_pairs={{0,2},{2,4},{4,6},{10,8},{12,10},{14,12},{1,3},{3,5},{5,7},{11,9},... | collective-permute-start | bytes 2359304 | tf_op jit(solution)/shard_map/cond/branch_0_fun/ppermute | solution.py:626
  43.9 12.3 %collective-permute-start.9 = (bf16[5,1,256,128]{3,2,1,0:T(8,128)(2,1)S(1)}, bf16[5,1,256,128]{3,2,1,0:T(8,128)(2,1)S(1)}, u32[]{:S(2)}, u32[]{:S(2)}) collective-permute-start(bf16[5,1,256,128]{3,2,1,0:T(8,128)(2,1)S(1)} %gate.20.refs_5_), channel_id=1, source_target_pairs={{0,8},{8,0},{1,9},{9,1},{2,10},{10,2},{3,11},{11,3},{4,12},{12,4},... | collective-permute-start | bytes 983048 | tf_op jit(solution)/shard_map/cond/branch_0_fun/ppermute | solution.py:568
  48.9 3.3 %collective-permute-start.6 = (bf16[5,256,128]{2,1,0:T(8,128)(2,1)S(1)}, bf16[5,256,128]{2,1,0:T(8,128)(2,1)S(1)}, u32[]{:S(2)}, u32[]{:S(2)}) collective-permute-start(bf16[5,256,128]{2,1,0:T(8,128)(2,1)S(1)} %attend.14.refs_3_.mine_ref), channel_id=1, source_target_pairs={{0,1},{1,0},{2,3},{3,2},{4,5},{5,4},{6,7},{7,6},{8,9},{9,8},{10,11... | collective-permute-start | bytes 983048 | tf_op jit(solution)/shard_map/cond/branch_0_fun/ppermute | solution.py:571
  51.6 1.6 %collective-permute-start.11 = (bf16[6,128,128]{2,1,0:T(8,128)(2,1)S(1)}, bf16[6,128,128]{2,1,0:T(8,128)(2,1)S(1)}, u32[]{:S(2)}, u32[]{:S(2)}) collective-permute-start(bf16[6,128,128]{2,1,0:T(8,128)(2,1)S(1)} %get-tuple-element.42), channel_id=1, source_target_pairs={{0,1},{1,0},{2,3},{3,2},{4,5},{5,4},{6,7},{7,6},{8,9},{9,8},{10,11... | collective-permute-start | bytes 589832 | tf_op jit(solution)/shard_map/cond/branch_0_fun/ppermute | solution.py:571
  53.4 7.4 %collective-permute-start.14 = (bf16[6,128,128]{2,1,0:T(8,128)(2,1)S(1)}, bf16[6,128,128]{2,1,0:T(8,128)(2,1)S(1)}, u32[]{:S(2)}, u32[]{:S(2)}) collective-permute-start(bf16[6,128,128]{2,1,0:T(8,128)(2,1)S(1)} %mix.14.refs_5_), channel_id=1, source_target_pairs={{0,8},{8,0},{1,9},{9,1},{2,10},{10,2},{3,11},{11,3},{4,12},{12,4},... | collective-permute-start | bytes 589832 | tf_op jit(solution)/shard_map/cond/branch_0_fun/ppermute | solution.py:568
  59.3 1.5 %collective-permute-start.13 = (bf16[3,128,128]{2,1,0:T(8,128)(2,1)S(1)}, bf16[3,128,128]{2,1,0:T(8,128)(2,1)S(1)}, u32[]{:S(2)}, u32[]{:S(2)}) collective-permute-start(bf16[3,128,128]{2,1,0:T(8,128)(2,1)S(1)} %slice.29), channel_id=1, source_target_pairs={{0,1},{1,0},{2,3},{3,2},{4,5},{5,4},{6,7},{7,6},{8,9},{9,8},{10,11... | collective-permute-start | bytes 294920 | tf_op jit(solution)/shard_map/cond/branch_0_fun/ppermute | solution.py:571
  59.4 1.4 %collective-permute-start.12 = (bf16[2,128,128]{2,1,0:T(8,128)(2,1)S(1)}, bf16[2,128,128]{2,1,0:T(8,128)(2,1)S(1)}, u32[]{:S(2)}, u32[]{:S(2)}) collective-permute-start(bf16[2,128,128]{2,1,0:T(8,128)(2,1)S(1)} %slice.28), channel_id=1, source_target_pairs={{0,1},{1,0},{2,3},{3,2},{4,5},{5,4},{6,7},{7,6},{8,9},{9,8},{10,11... | collective-permute-start | bytes 196616 | tf_op jit(solution)/shard_map/cond/branch_0_fun/ppermute | solution.py:571
  60.9 6.5 %collective-permute-start.17 = (bf16[5,128,128]{2,1,0:T(8,128)(2,1)S(1)}, bf16[5,128,128]{2,1,0:T(8,128)(2,1)S(1)}, u32[]{:S(2)}, u32[]{:S(2)}) collective-permute-start(bf16[5,128,128]{2,1,0:T(8,128)(2,1)S(1)} %mix.15.refs_3_), channel_id=1, source_target_pairs={{0,8},{8,0},{1,9},{9,1},{2,10},{10,2},{3,11},{11,3},{4,12},{12,4},... | collective-permute-start | bytes 491528 | tf_op jit(solution)/shard_map/cond/branch_0_fun/ppermute | solution.py:568
  64.1 3.2 %collective-permute-start.15 = (bf16[3,256,128]{2,1,0:T(8,128)(2,1)S(1)}, bf16[3,256,128]{2,1,0:T(8,128)(2,1)S(1)}, u32[]{:S(2)}, u32[]{:S(2)}) collective-permute-start(bf16[3,256,128]{2,1,0:T(8,128)(2,1)S(1)} %get-tuple-element.85.refs_1_), channel_id=1, source_target_pairs={{0,1},{1,0},{2,3},{3,2},{4,5},{5,4},{6,7},{7,6},{8,9},{9,8},{10,11... | collective-permute-start | bytes 589832 | tf_op jit(solution)/shard_map/cond/branch_0_fun/ppermute | solution.py:571
  64.2 3.2 %collective-permute-start.16 = (bf16[3,256,128]{2,1,0:T(8,128)(2,1)S(1)}, bf16[3,256,128]{2,1,0:T(8,128)(2,1)S(1)}, u32[]{:S(2)}, u32[]{:S(2)}) collective-permute-start(bf16[3,256,128]{2,1,0:T(8,128)(2,1)S(1)} %get-tuple-element.84.refs_2_), channel_id=1, source_target_pairs={{0,1},{1,0},{2,3},{3,2},{4,5},{5,4},{6,7},{7,6},{8,9},{9,8},{10,11... | collective-permute-start | bytes 589832 | tf_op jit(solution)/shard_map/cond/branch_0_fun/ppermute | solution.py:571
  64.7 2.7 %collective-permute-start.18 = (bf16[6,128,128]{2,1,0:T(8,128)(2,1)S(1)}, bf16[6,128,128]{2,1,0:T(8,128)(2,1)S(1)}, u32[]{:S(2)}, u32[]{:S(2)}) collective-permute-start(bf16[6,128,128]{2,1,0:T(8,128)(2,1)S(1)} %collective-permute-done.14.refs_3_.refs_4_.refs_5_), channel_id=1, source_target_pairs={{0,1},{1,0},{2,3},{3,2},{4,5},{5,4},{6,7},{7,6},{8,9},{9,8},{10,11... | collective-permute-start | bytes 589832 | tf_op jit(solution)/shard_map/cond/branch_0_fun/ppermute | solution.py:571
  67.4 1.4 %collective-permute-start.19 = (bf16[5,128,128]{2,1,0:T(8,128)(2,1)S(1)}, bf16[5,128,128]{2,1,0:T(8,128)(2,1)S(1)}, u32[]{:S(2)}, u32[]{:S(2)}) collective-permute-start(bf16[5,128,128]{2,1,0:T(8,128)(2,1)S(1)} %collective-permute-done.17.refs_6_), channel_id=1, source_target_pairs={{0,1},{1,0},{2,3},{3,2},{4,5},{5,4},{6,7},{7,6},{8,9},{9,8},{10,11... | collective-permute-start | bytes 491528 | tf_op jit(solution)/shard_map/cond/branch_0_fun/ppermute | solution.py:571
